TPU v7x, 32 devices: a whole 2x2x4 slice. The times are simulated.
32 devices in a mesh: rows: 4 (over z), seq: 8 (over y, x, core).
Axes of the slice: x: 2, y: 2, z: 4, core: 2. Of those that a mesh axis runs over, the one named last changes fastest.
Arguments:
- tokens: bfloat16 [4, 2048, 512], P('rows', 'seq'), may hold values from -6 to 6
- norm_attn: bfloat16 [512], replicated, may hold values from 0.099609375 to 1.8984375
- query_weight: bfloat16 [512, 384], replicated, may hold values from -0.0625 to 0.0625
- key_weight: bfloat16 [512, 384], replicated, may hold values from -0.25 to 0.25
- value_weight: bfloat16 [512, 384], replicated, may hold values from -0.25 to 0.25
- out_weight: bfloat16 [384, 512], replicated, may hold values from -1.25 to 1.25
- bucket_bias_table: bfloat16 [32, 6], replicated, may hold values from -4 to 4
- norm_ffn: bfloat16 [512], replicated, may hold values from 0.099609375 to 1.8984375
- gate_weight: bfloat16 [512, 1024], replicated, may hold values from -0.25 to 0.25
- expansion_matrix: bfloat16 [512, 1024], replicated, may hold values from -0.25 to 0.25
- down_weight: bfloat16 [1024, 512], replicated, may hold values from -0.25 to 0.25
- lengths: int32 [4, 16], P('rows'), may hold values from 0 to 2048, as said below
- cotangent: bfloat16 [4, 2048, 512], P('rows', 'seq'), may hold values from -6 to 6
Outputs:
- output: bfloat16 [4, 2048, 512], P('rows', 'seq')
- grad_tokens: float32 [4, 2048, 512], P('rows', 'seq')
- grad_norm_attn: float32 [512], replicated
- grad_query_weight: float32 [512, 384], replicated
- key_weight_gradient: float32 [512, 384], replicated
- grad_value_weight: float32 [512, 384], replicated
- grad_out_weight: float32 [384, 512], replicated
- grad_bias_table: float32 [32, 6], replicated
- grad_norm_ffn: float32 [512], replicated
- grad_gate_weight: float32 [512, 1024], replicated
- grad_up_weight: float32 [512, 1024], replicated
- grad_down_weight: float32 [1024, 512], replicated
Inputs may be any that keep to these rules, and one draw needn't show every extreme that they name: Each row's lengths sum to at most 2048; bytes past the sum are padding. In every draw some row is one segment of 2048 bytes.
All inputs are finite; a program needn't handle non-finite values.
Results may differ from a plain program's by a relative error of at most 0.03.
Values may be sent and summed in bfloat16 or wider, within the bound.
No kernel may reach another device: no remote copies, remote signals or barrier semaphores. Data moves between devices by JAX's collectives and lax.ppermute only.
A program may use at most 128 MiB of HBM per device.

v0:
```python
from functools import partial
import math

import jax
import jax.numpy as jnp
from jax import lax
from jax.sharding import PartitionSpec as P

H = 6
BUCKETS = 32
MAXDIST = 128


norm_epsilon = 1e-06
masked_score = -1000000000.0
initial_max = -1e30


def bucket_thresholds(bucket_count, max_distance):
    half_count = bucket_count // 2
    exact_count = half_count // 2
    log_range = half_count - exact_count
    thresholds = list(range(1, exact_count))
    for power_step in range(log_range):
        target = exact_count ** (log_range - power_step) * max_distance**power_step
        candidate = exact_count
        while candidate**log_range < target:
            candidate += 1
        thresholds.append(candidate)
    return thresholds


def relative_bucket(query_pos, key_pos):
    offsets = key_pos[None, :] - query_pos[:, None]
    distance = jnp.abs(offsets)
    bucket = (offsets > 0).astype(jnp.int32) * (BUCKETS // 2)
    for threshold in bucket_thresholds(BUCKETS, MAXDIST):
        bucket = bucket + (distance >= threshold).astype(jnp.int32)
    return bucket


def rms_norm(values, gain_vec):
    return (
        values
        * lax.rsqrt(jnp.mean(values * values, axis=-1, keepdims=True) + norm_epsilon)
        * gain_vec
    )


def project(left_side, right_side):
    return jnp.einsum("rtd,de->rte", left_side, right_side, preferred_element_type=jnp.float32)


def project_back(left_side, right_side):
    return jnp.einsum("rte,de->rtd", left_side, right_side, preferred_element_type=jnp.float32)


def weight_grad(left_side, right_side):
    return jnp.einsum("rtd,rte->de", left_side, right_side, preferred_element_type=jnp.float32)


def split_heads(values):
    return values.reshape(values.shape[0], values.shape[1], H, values.shape[2] // H)


def bias_pieces(bucket_bias_table, query_pos, key_pos):
    bucket = relative_bucket(query_pos, key_pos)
    distance_class_onehot = (
        jnp.arange(bucket_bias_table.shape[0], dtype=jnp.int32)[:, None, None] == bucket[None]
    ).astype(jnp.bfloat16)
    position_bias_term = jnp.einsum(
        "xpt,xn->npt", distance_class_onehot, bucket_bias_table, preferred_element_type=jnp.float32
    )
    return (distance_class_onehot, position_bias_term)


def masked_scores(heads_of_query, key_heads, position_bias_term, allowed):
    scores = (
        jnp.einsum("rqhd,rkhd->rhqk", heads_of_query, key_heads, preferred_element_type=jnp.float32)
        + position_bias_term[None]
    )
    return jnp.where(allowed[:, None], scores, masked_score)


def over_blocks(step_fn, running, arrays):
    piece_len = arrays[0].shape[1]
    block_len = math.gcd(piece_len, 512)

    def inner_step(block_index, state_now):
        offset = block_index * block_len
        item_list = tuple(
            (lax.dynamic_slice_in_dim(array_one, offset, block_len, 1) for array_one in arrays)
        )
        return step_fn(state_now, item_list, offset)

    return lax.fori_loop(0, piece_len // block_len, inner_step, running)


def shards(
    tokens,
    norm_attn,
    query_weight,
    key_weight,
    value_weight,
    out_weight,
    bucket_bias_table,
    norm_ffn,
    gate_weight,
    expansion_matrix,
    down_weight,
    lengths,
    cotangent,
):
    rows_here = tokens.shape[0]
    block_len = tokens.shape[1]
    row_len = block_len * lax.axis_size("seq")
    first_pos = lax.axis_index("seq") * block_len
    segment_ends = jnp.cumsum(lengths, axis=1)
    all_pos = jnp.arange(row_len, dtype=jnp.int32)
    segment_all = jnp.sum(
        (all_pos[None, :, None] >= segment_ends[:, None, :]).astype(jnp.int32), axis=2
    )
    my_pos = first_pos + jnp.arange(block_len, dtype=jnp.int32)
    my_segment = lax.dynamic_slice_in_dim(segment_all, first_pos, block_len, 1)
    valid_mask = (my_pos[None, :] < segment_ends[:, -1:]).astype(jnp.float32)
    inputs = tokens.astype(jnp.float32)
    gain_one = norm_attn.astype(jnp.float32)
    normed_one = rms_norm(inputs, gain_one)
    normed_low = normed_one.astype(jnp.bfloat16)
    query_low = project(normed_low, query_weight).astype(jnp.bfloat16)
    key_low = project(normed_low, key_weight).astype(jnp.bfloat16)
    value_low = project(normed_low, value_weight).astype(jnp.bfloat16)
    heads_of_query = split_heads(query_low)

    def attend(running, pieces, begin_at):
        key_heads = split_heads(pieces[0])
        value_heads = split_heads(pieces[1])
        piece_len = pieces[0].shape[1]
        key_pos = begin_at + jnp.arange(piece_len, dtype=jnp.int32)
        distance_class_onehot, position_bias_term = bias_pieces(bucket_bias_table, my_pos, key_pos)
        allowed = (
            my_segment[:, :, None]
            == lax.dynamic_slice_in_dim(segment_all, begin_at, piece_len, 1)[:, None, :]
        )
        scores = masked_scores(heads_of_query, key_heads, position_bias_term, allowed)
        old_max, old_total, weighted = running
        new_max = jnp.maximum(old_max, jnp.max(scores, axis=-1))
        factor = jnp.exp(old_max - new_max)
        raised = jnp.exp(scores - new_max[..., None])
        new_total = old_total * factor + jnp.sum(raised, axis=-1)
        weighted = weighted * factor[..., None] + jnp.einsum(
            "rhqk,rkhd->rhqd",
            raised.astype(jnp.bfloat16),
            value_heads,
            preferred_element_type=jnp.float32,
        )
        return (new_max, new_total, weighted)

    head_size = query_low.shape[2] // H
    start_state = (
        jnp.full((rows_here, H, block_len), initial_max, jnp.float32),
        jnp.zeros((rows_here, H, block_len), jnp.float32),
        jnp.zeros((rows_here, H, block_len, head_size), jnp.float32),
    )
    closing_running_peak, final_total, weighted = over_blocks(
        attend,
        start_state,
        (
            lax.all_gather(key_low, "seq", axis=1, tiled=True),
            lax.all_gather(value_low, "seq", axis=1, tiled=True),
        ),
    )
    log_sum = closing_running_peak + jnp.log(final_total)
    blended_attention_output = jnp.transpose(weighted / final_total[..., None], (0, 2, 1, 3))
    mixed_out = blended_attention_output.reshape(rows_here, block_len, H * head_size)
    mixed_low = mixed_out.astype(jnp.bfloat16)
    hidden = inputs + project(mixed_low, out_weight)
    gain_two = norm_ffn.astype(jnp.float32)
    normed_two = rms_norm(hidden, gain_two)
    normed_two_low = normed_two.astype(jnp.bfloat16)
    gate_val = project(normed_two_low, gate_weight)
    up_val = project(normed_two_low, expansion_matrix)
    activated, gelu_back = jax.vjp(partial(jax.nn.gelu, approximate=True), gate_val)
    inner_low = (activated * up_val).astype(jnp.bfloat16)
    output = (hidden + project(inner_low, down_weight)).astype(jnp.bfloat16)
    grad_out = cotangent.astype(jnp.float32) * valid_mask[..., None]
    grad_out_low = grad_out.astype(jnp.bfloat16)
    grad_down = weight_grad(inner_low, grad_out_low)
    grad_inner = project_back(grad_out_low, down_weight).astype(jnp.bfloat16).astype(jnp.float32)
    grad_gate_low = gelu_back(grad_inner * up_val)[0].astype(jnp.bfloat16)
    grad_up_low = (grad_inner * activated).astype(jnp.bfloat16)
    grad_gate = weight_grad(normed_two_low, grad_gate_low)
    grad_up = weight_grad(normed_two_low, grad_up_low)
    grad_normed_two = project_back(grad_gate_low, gate_weight) + project_back(
        grad_up_low, expansion_matrix
    )
    _, norm_two_back = jax.vjp(rms_norm, hidden, gain_two)
    grad_hidden_norm, grad_gain_two = norm_two_back(grad_normed_two)
    grad_hidden = grad_out + grad_hidden_norm
    grad_hidden_low = grad_hidden.astype(jnp.bfloat16)
    grad_out_proj = weight_grad(mixed_low, grad_hidden_low)
    grad_mixed_low = project_back(grad_hidden_low, out_weight).astype(jnp.bfloat16)
    grad_mixed_heads = split_heads(grad_mixed_low)
    delta_sum = jnp.transpose(
        jnp.sum(grad_mixed_heads.astype(jnp.float32) * blended_attention_output, axis=-1), (0, 2, 1)
    )

    def backward_block(running, pieces, begin_at, with_keys):
        key_heads = split_heads(pieces[0])
        value_heads = split_heads(pieces[1])
        piece_len = pieces[0].shape[1]
        key_pos = begin_at + jnp.arange(piece_len, dtype=jnp.int32)
        distance_class_onehot, position_bias_term = bias_pieces(bucket_bias_table, my_pos, key_pos)
        allowed = (
            my_segment[:, :, None]
            == lax.dynamic_slice_in_dim(segment_all, begin_at, piece_len, 1)[:, None, :]
        )
        scores = masked_scores(heads_of_query, key_heads, position_bias_term, allowed)
        probs_full = jnp.exp(scores - log_sum[..., None])
        grad_probs = jnp.einsum(
            "rqhd,rkhd->rhqk", grad_mixed_heads, value_heads, preferred_element_type=jnp.float32
        )
        logit_derivative = (probs_full * (grad_probs - delta_sum[..., None])).astype(jnp.bfloat16)
        grad_query = running[0] + jnp.einsum(
            "rhqk,rkhd->rqhd", logit_derivative, key_heads, preferred_element_type=jnp.float32
        )
        grad_bias = running[1] + jnp.einsum(
            "uvxr,yxr->yv",
            logit_derivative,
            distance_class_onehot,
            preferred_element_type=jnp.float32,
        )
        key_term = jnp.einsum(
            "rhqk,rqhd->rkhd", logit_derivative, heads_of_query, preferred_element_type=jnp.float32
        ).reshape(rows_here, piece_len, -1)
        value_term = jnp.einsum(
            "rhqk,rqhd->rkhd",
            probs_full.astype(jnp.bfloat16),
            grad_mixed_heads,
            preferred_element_type=jnp.float32,
        ).reshape(rows_here, piece_len, -1)
        key_buffer = lax.dynamic_update_slice_in_dim(
            running[2],
            lax.dynamic_slice_in_dim(running[2], begin_at, piece_len, 1) + key_term,
            begin_at,
            1,
        )
        value_buffer = lax.dynamic_update_slice_in_dim(
            running[3],
            lax.dynamic_slice_in_dim(running[3], begin_at, piece_len, 1) + value_term,
            begin_at,
            1,
        )
        return (grad_query, grad_bias, key_buffer, value_buffer)

    query_zero = jnp.zeros((rows_here, block_len, H, head_size), jnp.float32)
    bias_zero = jnp.zeros(bucket_bias_table.shape, jnp.float32)
    buffer_zero = jnp.zeros((rows_here, row_len, H * head_size), jnp.float32)
    backward_starting = (query_zero, bias_zero, buffer_zero, buffer_zero)
    backward_result = over_blocks(
        partial(backward_block, with_keys=True),
        backward_starting,
        (
            lax.all_gather(key_low, "seq", axis=1, tiled=True),
            lax.all_gather(value_low, "seq", axis=1, tiled=True),
        ),
    )
    asker_side_derivative_total = backward_result[0]
    grad_bias = backward_result[1]
    grad_key_sum, grad_value_sum = (
        lax.psum_scatter(
            backward_result[2].astype(jnp.bfloat16), "seq", scatter_dimension=1, tiled=True
        ).astype(jnp.float32),
        lax.psum_scatter(
            backward_result[3].astype(jnp.bfloat16), "seq", scatter_dimension=1, tiled=True
        ).astype(jnp.float32),
    )
    grad_query_low = asker_side_derivative_total.reshape(rows_here, block_len, -1).astype(
        jnp.bfloat16
    )
    grad_key_low = grad_key_sum.astype(jnp.bfloat16)
    grad_value_low = grad_value_sum.astype(jnp.bfloat16)
    grad_query_proj = weight_grad(normed_low, grad_query_low)
    grad_key_proj = weight_grad(normed_low, grad_key_low)
    grad_value_proj = weight_grad(normed_low, grad_value_low)
    grad_normed_one = (
        project_back(grad_query_low, query_weight)
        + project_back(grad_key_low, key_weight)
        + project_back(grad_value_low, value_weight)
    )
    _, norm_one_back = jax.vjp(rms_norm, inputs, gain_one)
    grad_inputs_norm, grad_gain_one = norm_one_back(grad_normed_one)
    grad_inputs = grad_hidden + grad_inputs_norm
    summed = lax.psum(
        (
            grad_gain_one,
            grad_query_proj,
            grad_key_proj,
            grad_value_proj,
            grad_out_proj,
            grad_bias,
            grad_gain_two,
            grad_gate,
            grad_up,
            grad_down,
        ),
        ("rows", "seq"),
    )
    return (
        output,
        grad_inputs,
        summed[0],
        summed[1],
        summed[2],
        summed[3],
        summed[4],
        summed[5],
        summed[6],
        summed[7],
        summed[8],
        summed[9],
    )


def solution(mesh):
    in_specs = (
        P("rows", "seq", None),
        P(),
        P(),
        P(),
        P(),
        P(),
        P(),
        P(),
        P(),
        P(),
        P(),
        P("rows", None),
        P("rows", "seq", None),
    )
    out_specs = (
        P("rows", "seq", None),
        P("rows", "seq", None),
        P(),
        P(),
        P(),
        P(),
        P(),
        P(),
        P(),
        P(),
        P(),
        P(),
    )
    return jax.shard_map(shards, mesh=mesh, in_specs=in_specs, out_specs=out_specs, check_vma=False)
```

profile of v0, /device:TPU:0, one launch (start us, length us, event | category | flops | bytes accessed | tf_op | source)
XLA Modules:
  0.0 527.8 jit_solution(10151658925964556263)
XLA Ops:
  9.1 2.1 convolution_convert_fusion.4
  11.3 2.1 convolution_convert_fusion.2
  14.4 1.4 convolution_convert_fusion.3
  17.4 2.5 convolution_convert_fusion
  19.9 19.9 %all-gather.5.cloned.1.call-done = bf16[2048,384]{1,0:T(8,128)(2,1)} async-done(((bf16[256,384]{1,0:T(8,128)(2,1)}), bf16[2048,384]{1,0:T(8,128)(2,1)}) %all-gather.5.cloned.1.call-update) | async-done | bytes 1572880 | tf_op jit(solution)/shard_map/all_gather | solution.py:169
  39.8 2.6 copy.63
  42.4 25.6 %all-gather.7.cloned.1.call-done = bf16[2048,384]{1,0:T(8,128)(2,1)} async-done(((bf16[256,384]{1,0:T(8,128)(2,1)}), bf16[2048,384]{1,0:T(8,128)(2,1)}) %all-gather.7.cloned.1.call-update) | async-done | bytes 1572880 | tf_op jit(solution)/shard_map/all_gather | solution.py:170
  68.0 2.6 copy.64
  70.6 77.9 %while.38 = (s32[]{:T(128)}, f32[1,6,256]{2,1,0:T(8,128)S(1)}, f32[1,6,256]{2,1,0:T(8,128)S(1)}, f32[1,6,256,64]{2,3,1,0:T(8,128)S(1)}, s32[1,256]{1,0:T(1,128)S...) while((s32[]{:T(128)}, f32[1,6,256]{2,1,0:T(8,128)S(1)}, ...), condition=%wide.region_6.7_spmd.clone, body=%wide.region_3.6_spmd.clone.sunk | while | flops 268216064 | bytes 39368312 | solution.py:96
  71.5 4.5 fusion.200
  76.1 4.9 copy.82
  82.3 4.2 fusion.201
  86.5 2.5 fusion.203
  91.0 4.5 fusion.200
  95.5 4.9 copy.82
  101.7 4.2 fusion.201
  106.0 2.5 fusion.203
  110.5 4.5 fusion.200
  115.0 4.9 copy.82
  121.2 4.2 fusion.201
  125.5 2.5 fusion.203
  130.0 4.5 fusion.200
  134.5 4.9 copy.82
  140.7 4.2 fusion.201
  144.9 2.5 fusion.203
  148.5 1.5 multiply_reduce_fusion
  150.7 1.9 fusion.87
  155.5 2.0 broadcast_in_dim.141
  157.5 2.0 broadcast_in_dim.141.clone
  159.6 66.0 %while.39 = (s32[]{:T(128)}, f32[1,256,6,64]{1,3,2,0:T(8,128)S(1)}, f32[32,6]{0,1:T(8,128)S(1)}, f32[1,2048,384]{1,2,0:T(8,128)}, f32[1,2048,384]{1,2,0:T(8,128)...) while((s32[]{:T(128)}, f32[1,256,6,64]{1,3,2,0:T(8,128)S(1)}, ...), condition=%wide.region_11.12_spmd.clone, body=%wide.region_10.11_spmd.clone.sunk | while | flops 625017984 | bytes 59665596 | solution.py:96
  161.6 2.5 fusion.217
  164.3 1.7 fusion.218
  166.0 1.3 constant_dynamic-slice_fusion.15
  168.8 3.1 fusion.221
  173.1 3.0 fusion.224
  178.1 2.5 fusion.217
  180.8 1.7 fusion.218
  182.5 1.3 constant_dynamic-slice_fusion.15
  185.4 3.1 fusion.221
  189.7 2.9 fusion.224
  194.6 2.5 fusion.217
  197.3 1.7 fusion.218
  199.0 1.3 constant_dynamic-slice_fusion.15
  201.9 3.1 fusion.221
  206.2 2.9 fusion.224
  211.0 2.5 fusion.217
  213.8 1.7 fusion.218
  215.5 1.3 constant_dynamic-slice_fusion.15
  218.3 3.1 fusion.221
  222.6 3.0 fusion.224
  225.6 3.4 convert_element_type.526
  229.1 3.4 convert_element_type.527
  235.4 1.8 fusion.133
  237.1 1.8 fusion.114
  239.0 2.0 fusion.119
  241.0 26.6 %reduce-scatter.3.cloned.1.call-done = bf16[1,256,384]{1,2,0:T(8,128)(2,1)} async-done(((bf16[1,2048,384]{1,2,0:T(8,128)(2,1)}), bf16[1,256,384]{1,2,0:T(8,128)(2,1)}) %reduce-scatter.3.cloned.1.call-update) | async-done | bytes 196624 | tf_op jit(solution)/shard_map/reduce_scatter | solution.py:271
  267.6 2.3 fusion.109
  269.8 39.4 %reduce-scatter.5.cloned.1.call-done = bf16[1,256,384]{1,2,0:T(8,128)(2,1)} async-done(((bf16[1,2048,384]{1,2,0:T(8,128)(2,1)}), bf16[1,256,384]{1,2,0:T(8,128)(2,1)}) %reduce-scatter.5.cloned.1.call-update) | async-done | bytes 196624 | tf_op jit(solution)/shard_map/reduce_scatter | solution.py:274
  309.2 2.3 fusion.106
  312.4 1.4 fusion.132
  315.9 41.5 %all-reduce = (f32[512]{0:T(512)}, f32[32,6]{0,1:T(8,128)}, f32[512]{0:T(512)}) all-reduce(f32[512]{0:T(512)S(1)} %get-tuple-element.622, f32[32,6]{0,1:T(8,128)S(1)} %get-tuple-element.451, f32[512]{0:T(512)S(1)} %get-tuple-element.620), channel_id=1, replica_groups=mesh['rows'=4,'seq'=8] {'rows','seq'}, use_global_device_ids=true, to_apply=%region_16.17 | all-reduce | flops 1216 | bytes 9728 | tf_op jit(solution)/shard_map/psum | solution.py:294
  358.4 152.8 %all-reduce.4.cloned.1.call-done = (f32[512,384]{1,0:T(8,128)}, f32[512,384]{1,0:T(8,128)}, f32[512,384]{1,0:T(8,128)}, f32[384,512]{1,0:T(8,128)}, f32[512,1024...) async-done(((f32[512,384]{1,0:T(8,128)}, f32[512,384]{1,0:T(8,128)}, f32[512,384]{1,0:T(8,128)}, f32[384,512]{1,0:T(8,128)}, f32[512,1024]{1,0:T(8,128)}, ...) | async-done | bytes 9437200 | tf_op jit(solution)/shard_map/psum | solution.py:294
  511.2 2.2 copy.121
  513.4 2.1 copy.122
  (230 shorter events, 52.7 us)
Async XLA Ops:
  7.2 143.5 %copy-start = (bf16[512,1024]{1,0:T(8,128)(2,1)S(1)}, bf16[512,1024]{1,0:T(8,128)(2,1)}, u32[]{:S(2)}) copy-start(bf16[512,1024]{1,0:T(8,128)(2,1)} %param.25) | copy-start | bytes 3145732
  7.2 8.8 %copy-start.40 = (bf16[512]{0:T(512)(128)(2,1)S(1)}, bf16[512]{0:T(512)(128)(2,1)}, u32[]{:S(2)}) copy-start(bf16[512]{0:T(512)(128)(2,1)} %param.24) | copy-start | bytes 3076
  7.2 10.2 %copy-start.14 = (bf16[1,256,512]{2,1,0:T(8,128)(2,1)S(1)}, bf16[1,256,512]{2,1,0:T(8,128)(2,1)}, u32[]{:S(2)}) copy-start(bf16[1,256,512]{2,1,0:T(8,128)(2,1)} %param.29) | copy-start | bytes 786436
  7.2 32.6 %all-gather.5.cloned.1.call-start = ((), (), s32[]{:S(2)}) async-start(), calls=%async_computation.4 | async-start | bytes 1769472 | tf_op jit(solution)/shard_map/all_gather | solution.py:169
  11.3 56.7 %all-gather.7.cloned.1.call-start = ((), (), s32[]{:S(2)}) async-start(), calls=%async_computation.5 | async-start | bytes 1769472 | tf_op jit(solution)/shard_map/all_gather | solution.py:170
  13.4 254.2 %reduce-scatter.3.cloned.1.call-start = ((), (), s32[]{:S(2)}) async-start(), calls=%async_computation.2 | async-start | bytes 1769472 | tf_op jit(solution)/shard_map/reduce_scatter | solution.py:271
  39.8 30.8 %copy-start.39 = (bf16[32,6]{0,1:T(8,128)(2,1)S(1)}, bf16[32,6]{0,1:T(8,128)(2,1)}, u32[]{:S(2)}) copy-start(bf16[32,6]{0,1:T(8,128)(2,1)} %param.23) | copy-start | bytes 1156
  70.6 78.0 %copy-start.5 = (bf16[1,256,512]{2,1,0:T(8,128)(2,1)S(1)}, bf16[1,256,512]{2,1,0:T(8,128)(2,1)}, u32[]{:S(2)}) copy-start(bf16[1,256,512]{2,1,0:T(8,128)(2,1)} %param.17) | copy-start | bytes 786436
  86.5 2.8 copy-start.2
  106.0 2.8 copy-start.2
  125.5 2.8 copy-start.2
  144.9 2.8 copy-start.2
  148.5 1.8 copy-start.32
  148.5 2.2 copy-start.16
  148.5 4.1 copy-start.25
  150.1 4.6 copy-start.9
  150.2 2.4 copy-start.11
  152.7 0.8 copy-start.23
  152.7 2.0 copy-start.30
  153.9 1.0 copy-start.29
  154.9 4.6 copy-start.7
  166.0 1.8 copy-start.3
  168.8 3.1 copy-start.4
  182.5 1.8 copy-start.3
  185.3 3.1 copy-start.4
  199.0 1.8 copy-start.3
  201.8 3.1 copy-start.4
  215.5 1.8 copy-start.3
  218.3 3.1 copy-start.4
  229.0 80.2 %reduce-scatter.5.cloned.1.call-start = ((), (), s32[]{:S(2)}) async-start(), calls=%async_computation.3 | async-start | bytes 1769472 | tf_op jit(solution)/shard_map/reduce_scatter | solution.py:274
  229.0 3.8 copy-start.6
  229.0 5.1 copy-start.8
  229.1 5.1 copy-start.26
  232.5 2.9 copy-start.12
  232.5 2.9 copy-start.24
  232.5 4.6 copy-start.15
  232.5 4.6 copy-start.21
  232.5 278.7 %all-reduce.4.cloned.1.call-start = ((), (), s32[]{:S(2)}) async-start(), calls=%async_computation.6 | async-start | bytes 18874368 | tf_op jit(solution)/shard_map/psum | solution.py:294
  232.8 6.2 %copy-start.27 = (bf16[1,256,6,64]{1,3,2,0:T(8,128)(2,1)}, bf16[1,256,6,64]{1,3,2,0:T(8,128)(2,1)S(1)}, u32[]{:S(2)}) copy-start(bf16[1,256,6,64]{1,3,2,0:T(8,128)(2,1)S(1)} %convert_element_type.524) | copy-start | bytes 589828
  235.3 3.6 copy-start.17
  235.3 3.6 copy-start.31
  311.5 0.9 copy-start.28
  311.5 2.4 copy-start.10
  311.5 2.4 copy-start.13
  311.5 2.4 copy-start.22
  312.4 2.6 copy-start.35
  312.4 2.6 copy-start.37
  312.4 3.0 copy-start.36
  312.4 3.0 copy-start.38
  511.2 4.3 copy-start.34
  511.2 5.2 copy-start.33
  511.2 6.0 %copy-start.20 = (f32[512,1024]{1,0:T(8,128)S(1)}, f32[512,1024]{1,0:T(8,128)}, u32[]{:S(2)}) copy-start(f32[512,1024]{1,0:T(8,128)} %get-tuple-element.986) | copy-start | bytes 6291460
  516.4 2.2 copy-start.19
  517.3 2.7 copy-start.18
  518.6 2.7 copy-start.1
Sparse Core Ops, SparseCore 0:
  11.4 28.3 all-gather.4
  42.3 25.6 all-gather.6
  229.1 38.4 reduce-scatter.2
  270.7 38.4 reduce-scatter.4
  316.6 194.5 all-reduce.3
where the time goes:
time: 529 us; the launch traced here: 528 us
  waiting for transfers between devices  264 us (50%)
  matrix products  106 us (20%)
  local copies, waits for them, and re-layouts  58.7 us (11%)
  other arithmetic  42.1 us (8%)
  blocking collectives  41.5 us (8%)
  between operations  14.3 us (3%)
    psum x1, waiting for transfers between devices, shards(): lax.psum((grad_gain_one, grad_query_proj, grad_key_proj, grad_value_proj,...  153 us
    psum x1, blocking collectives, shards(): lax.psum((grad_gain_one, grad_query_proj, grad_key_proj, grad_value_proj,...  41.5 us
    reduce_scatter x1, waiting for transfers between devices, shards(): lax.psum_scatter(backward_result[3].astype(jnp.bfloat16), 'seq', scatter_...  39.4 us
    dot_general x8, matrix products, bias_pieces(): jnp.einsum('xpt,xn->npt', distance_class_onehot, bucket_bias_table, prefe...  28.4 us
    reduce_scatter x1, waiting for transfers between devices, shards(): lax.psum_scatter(backward_result[2].astype(jnp.bfloat16), 'seq', scatter_...  26.6 us
    all_gather x1, waiting for transfers between devices, shards(): lax.all_gather(value_low, 'seq', axis=1, tiled=True)  25.6 us
    dot_general x8, matrix products, masked_scores(): jnp.einsum('rqhd,rkhd->rhqk', heads_of_query, key_heads, preferred_elemen...  23.9 us
    all_gather x1, waiting for transfers between devices, shards(): lax.all_gather(key_low, 'seq', axis=1, tiled=True)  19.9 us
  transfers between devices with their start and end apart: 5, of which 5 were waited for; matrix products, arithmetic and copies ran while one was open for 6% of the time, Pallas kernels for 0%

commit v1 on v0

v1 whole, which is shorter than its diff:
```python
from functools import partial

import jax
import jax.numpy as jnp
from jax import lax
from jax.experimental import pallas as pl
from jax.experimental.pallas import tpu as pltpu
from jax.sharding import PartitionSpec as P

EPS = 1e-6
BIG = -(2.0**30)
LEFT, RIGHT, ONES = 17, 18, 19
SMALL = 16
VMEM = 56 * 1024 * 1024

f32, bf16, i32 = jnp.float32, jnp.bfloat16, jnp.int32


def thresholds(buckets, max_distance):
    half = buckets // 2
    exact = half // 2
    steps = half - exact
    out = list(range(1, exact))
    for j in range(steps):
        target = exact ** (steps - j) * max_distance**j
        m = exact
        while m**steps < target:
            m += 1
        out.append(m)
    return out


def bucket_of(offset, buckets):
    distance = jnp.abs(offset)
    bucket = (offset > 0).astype(i32) * (buckets // 2)
    for t in thresholds(buckets, 128):
        bucket = bucket + (distance >= t).astype(i32)
    return bucket


def nn(a, b):
    return lax.dot_general(a, b, (((1,), (0,)), ((), ())), preferred_element_type=f32)


def nt(a, b):
    return lax.dot_general(a, b, (((1,), (1,)), ((), ())), preferred_element_type=f32)


def tn(a, b):
    return lax.dot_general(a, b, (((0,), (0,)), ((), ())), preferred_element_type=f32)


def iota(shape, dim):
    return lax.broadcasted_iota(i32, shape, dim)


def rms(values, gain):
    scale = lax.rsqrt(jnp.mean(values * values, axis=-1, keepdims=True) + EPS)
    return values * scale * gain


def attention_kernel(n, ids, lens, table, gain, *refs):
    x = refs[:n]
    wq, wkv, n1, kv, e, p, o, q, s, bias, qe = refs[n:]
    step = pl.program_id(0)
    me = ids[0]
    t = x[0].shape[0]
    buckets = table.shape[0]

    @pl.when(step == 0)
    def _():
        lane = iota((1, 128), 1)
        low = jnp.full((1, 128), 2**30, i32)
        high = jnp.full((1, 128), -1, i32)
        low = jnp.where(lane == 0, -1, low)
        total = 0
        for k in range(lens.shape[0]):
            total = total + lens[k]
            high = jnp.where(lane == k, total, high)
            low = jnp.where(lane == k + 1, total, low)
        high = jnp.where(lane == lens.shape[0], 2**30, high)
        row = iota((t, 128), 0)
        lanes = iota((t, 128), 1)
        for j in range(n):
            n1[j] = rms(x[j][...].astype(f32), gain[...]).astype(bf16)
            pos = row + (me ^ j) * t
            away = (me ^ j) - me
            flag = jnp.where(away <= -2, LEFT, jnp.where(away >= 2, RIGHT, ONES))
            here = ((pos >= low) & (pos < high)) | (lanes == flag) | (lanes == ONES)
            e[j] = here.astype(f32).astype(bf16)
        other = (e[0][...].astype(f32) - 1.0) * -BIG
        qe[...] = jnp.where(lanes < LEFT, other, 0.0)

    q2 = nn(n1[0], wq[...]).astype(bf16)
    q[...] = q2
    for j in range(n):
        kv2 = nn(n1[j], wkv[...]).astype(bf16)
        kv[0, j] = kv2[:, :128]
        kv[1, j] = kv2[:, 128:]
    lanes = iota((t, 128), 1)
    for hh in range(2):
        h = 2 * step + hh
        far_left = table[buckets // 2 - 1, h]
        far_right = table[buckets - 1, h]
        ext = jnp.where(lanes == LEFT, far_left, jnp.where(lanes == RIGHT, far_right, qe[...]))
        qa = jnp.concatenate([q2[:, hh * 128 : hh * 128 + 128], ext.astype(bf16)], axis=1)
        for j in range(n):
            s[j] = nt(qa, jnp.concatenate([kv[hh, j], e[j]], axis=1))
        u = iota((1, 4 * t), 1)
        bucket = bucket_of(jnp.where(u < 3 * t, u - t, u - 5 * t), buckets)
        line = jnp.zeros((1, 4 * t), f32)
        for b in range(buckets):
            line = jnp.where(bucket == b, table[b, h], line)
        band = pltpu.roll(jnp.broadcast_to(line, (t, 4 * t)), 0, 1, stride=1, stride_axis=0)
        for r in range(3):
            bias[r] = band[:, r * t : (r + 1) * t]
        bias[3] = jnp.zeros((t, t), f32)
        for r in (-1, 0, 1):
            there = me + r
            inside = (there >= 0) & (there < n)
            slot = jnp.where(inside, me ^ there, 0)
            s[slot] = s[slot] + bias[jnp.where(inside, r + 1, 3)]
        top = jnp.maximum(s[0][:, :128], s[0][:, 128:])
        for j in range(1, n):
            top = jnp.maximum(top, jnp.maximum(s[j][:, :128], s[j][:, 128:]))
        top = jnp.max(top, axis=1, keepdims=True)
        acc = jnp.zeros((t, 256), f32)
        for j in range(n):
            raised = jnp.exp(s[j] - top).astype(bf16)
            p[hh, j] = raised
            acc = acc + nn(raised, jnp.concatenate([kv[hh, j], e[j]], axis=1))
        inverse = 1.0 / acc[:, 128 + ONES : 129 + ONES]
        o[:, hh * 128 : hh * 128 + 128] = jnp.where(lanes < 64, inverse, acc[:, :128] * inverse)


def attention_forward(ids, lens, table, gain, blocks, wq, wkv):
    n = len(blocks)
    t, d = blocks[0].shape
    heads = wq.shape[1] // 128
    smem = pl.BlockSpec(memory_space=pltpu.SMEM)
    const = lambda *shape: pl.BlockSpec(shape, lambda i: (0,) * len(shape), pipeline_mode=pl.Buffered(1))
    keep = lambda *shape: pl.BlockSpec(shape, lambda i: (0,) * len(shape))
    pair = lambda rows: pl.BlockSpec((rows, 256), lambda i: (0, i))
    by_head = lambda *shape: pl.BlockSpec((2, n, *shape), lambda i: (i, 0, 0, 0))
    shape = jax.ShapeDtypeStruct
    return pl.pallas_call(
        partial(attention_kernel, n),
        grid=(heads // 2,),
        in_specs=[smem, smem, smem, const(1, d)] + [const(t, d)] * n + [pair(d), pair(d)],
        out_specs=[keep(n, t, d), by_head(t, 128), keep(n, t, 128), by_head(t, t), pair(t), pair(t)],
        out_shape=[
            shape((n, t, d), bf16),
            shape((heads, n, t, 128), bf16),
            shape((n, t, 128), bf16),
            shape((heads, n, t, t), bf16),
            shape((t, heads * 128), f32),
            shape((t, heads * 128), bf16),
        ],
        scratch_shapes=[
            pltpu.VMEM((n, t, t), f32),
            pltpu.VMEM((4, t, t), f32),
            pltpu.VMEM((t, 128), f32),
        ],
        compiler_params=pltpu.CompilerParams(vmem_limit_bytes=VMEM),
        name="attention_forward",
    )(ids, lens, table, gain, *blocks, wq, wkv)


def feed_forward_kernel(ids, lens, gain, x, o, wo, wg, wu, wd, cot, out, dh, dop, delta, gwo, keep, send, gn, grads):
    t, d = x.shape
    ff = wg.shape[1]
    heads = o.shape[1] // 128
    mixed = o[...].astype(bf16)
    h1 = x[...].astype(f32) + nn(mixed, wo[...])
    g2 = gain[...]
    s2 = lax.rsqrt(jnp.mean(h1 * h1, axis=-1, keepdims=True) + EPS)
    hat = h1 * s2
    n2 = (hat * g2).astype(bf16)
    gate = nn(n2, wg[...])
    up = nn(n2, wu[...])
    c0 = 0.7978845608028654
    square = gate * gate
    th = jnp.tanh(c0 * gate * (1.0 + 0.044715 * square))
    half = 0.5 * (1.0 + th)
    act = gate * half
    dact = half + 0.5 * gate * (1.0 - th * th) * (c0 * (1.0 + 3 * 0.044715 * square))
    u = (act * up).astype(bf16)
    out[...] = (h1 + nn(u, wd[...])).astype(bf16)
    total = lens[0]
    for k in range(1, lens.shape[0]):
        total = total + lens[k]
    pos = ids[0] * t + iota((t, 1), 0)
    g = cot[...].astype(f32) * (pos < total).astype(f32)
    gb = g.astype(bf16)
    down = tn(u, gb).astype(bf16)
    grads[2 * d : 3 * d, :d] = down[:d]
    grads[2 * d : 3 * d, d:] = down[d:]
    du = nt(gb, wd[...]).astype(bf16).astype(f32)
    dgate = (du * up * dact).astype(bf16)
    dup = (du * act).astype(bf16)
    grads[0:d] = tn(n2, dgate).astype(bf16)
    grads[d : 2 * d] = tn(n2, dup).astype(bf16)
    rows = keep.shape[0]
    core = ids[0] % 2
    keep[...] = grads[pl.ds(pl.multiple_of(core * rows, 16), rows)]
    send[...] = grads[pl.ds(pl.multiple_of((1 - core) * rows, 16), rows)]
    dn2 = nt(dgate, wg[...]) + nt(dup, wu[...])
    gn[...] = jnp.sum(dn2 * hat, axis=0, keepdims=True)
    scaled = dn2 * g2
    dh1 = g + s2 * (scaled - hat * jnp.mean(hat * scaled, axis=-1, keepdims=True))
    dh[...] = dh1
    dhb = dh1.astype(bf16)
    full = tn(mixed, dhb)
    dmix = nt(dhb, wo[...]).astype(bf16).astype(f32)
    lanes = iota((t, 128), 1)
    deltas = jnp.zeros((t, 128), f32)
    for h in range(heads):
        gwo[h * 64 : h * 64 + 64] = full[h * 128 + 64 : h * 128 + 128].astype(bf16)
        inverse = o[:, h * 128 : h * 128 + 1]
        dm = dmix[:, h * 128 : h * 128 + 128] * inverse
        deltas = jnp.where(lanes == h, jnp.sum(dm * o[:, h * 128 : h * 128 + 128], axis=1, keepdims=True), deltas)
        dop[:, h * 128 : h * 128 + 128] = dm.astype(bf16)
    delta[...] = deltas


def feed_forward(ids, lens, gain, x, o, wo, wg, wu, wd, cot):
    t, d = x.shape
    ff = wg.shape[1]
    smem = pl.BlockSpec(memory_space=pltpu.SMEM)
    vmem = pl.BlockSpec(memory_space=pltpu.VMEM)
    shape = jax.ShapeDtypeStruct
    half = 3 * d // 2
    return pl.pallas_call(
        feed_forward_kernel,
        in_specs=[smem, smem] + [vmem] * 8,
        out_specs=[vmem] * 8,
        out_shape=[
            shape((t, d), bf16),
            shape((t, d), f32),
            shape((t, o.shape[1]), bf16),
            shape((t, 128), f32),
            shape((o.shape[1] // 2, d), bf16),
            shape((half, ff), bf16),
            shape((half, ff), bf16),
            shape((1, d), f32),
        ],
        scratch_shapes=[pltpu.VMEM((3 * d, ff), bf16)],
        compiler_params=pltpu.CompilerParams(vmem_limit_bytes=VMEM),
        name="feed_forward",
    )(ids, lens, gain, x, o, wo, wg, wu, wd, cot)


def attention_back_kernel(
    n, buckets, ids, gain, p, kv, e, n1, q, do, delta, wq, wkv, wqt, wkvt, gwo, gn,
    even, odd, dn1q, keep, send, ds, dkv, dq, grads, sums, line,
):
    h = pl.program_id(0)
    heads = pl.num_programs(0)
    me = ids[0]
    t = q.shape[0]
    width = gwo.shape[0]
    lanes = iota((t, 128), 1)
    lhs = jnp.concatenate([q[...].T, do[...].T], axis=1)
    shift = jnp.sum(jnp.where(lanes == h, delta[...], 0.0), axis=1, keepdims=True)
    acc = jnp.zeros((t, 256), f32)
    weight = jnp.zeros((128, n1.shape[2]), f32)
    for j in range(n):
        probs = p[0, j]
        keys = kv[0, j]
        d_score = (probs.astype(f32) * (nt(do[...], keys) - shift)).astype(bf16)
        ds[j] = d_score
        acc = acc + nn(d_score, jnp.concatenate([keys, e[j]], axis=1))
        both = nn(lhs, jnp.concatenate([d_score, probs], axis=0)).astype(bf16)
        dkv[j, pl.ds(pl.multiple_of(h * 128, 128), 128)] = both
        weight = weight + nn(both, n1[j])
    dqb = acc[:, :128].astype(bf16)
    dq[h] = dqb
    from_q = nn(dqb.T, n1[0])[:64]
    at = pl.multiple_of(h * 64, 64)
    grads[pl.ds(at, 64)] = from_q.astype(bf16)
    grads[pl.ds(pl.multiple_of(width + h * 64, 64), 64)] = weight[:64].astype(bf16)
    grads[pl.ds(pl.multiple_of(2 * width + h * 64, 64), 64)] = weight[64:].astype(bf16)
    gains = jnp.sum(from_q * wqt[...].astype(f32), axis=0, keepdims=True)
    gains = gains + jnp.sum(weight * wkvt[...].astype(f32), axis=0, keepdims=True)

    @pl.when(h == 0)
    def _():
        sums[...] = jnp.zeros_like(sums)
        line[...] = jnp.zeros_like(line)

    sums[0:1] = sums[0:1] + gains
    back = (iota((t, t), 0) + iota((t, t), 1) == t - 1).astype(f32).astype(bf16)
    parts = []
    for r in (-1, 0, 1):
        there = me + r
        inside = (there >= 0) & (there < n)
        slot = jnp.where(inside, me ^ there, 0)
        parts.append(nn(back, ds[slot]) * inside.astype(f32))
    parts.append(jnp.zeros((t, t), f32))
    band = pltpu.roll(jnp.concatenate(parts, axis=1), 0, 1, stride=1, stride_axis=0)
    line[...] = line[...] + jnp.where(iota(line.shape, 0) == h, jnp.sum(band, axis=0, keepdims=True), 0.0)
    ends = jnp.sum(acc[:, 128:], axis=0, keepdims=True)
    lane = iota((1, 128), 1)
    left = jnp.sum(jnp.where(lane == LEFT, ends, 0.0), axis=1, keepdims=True)
    right = jnp.sum(jnp.where(lane == RIGHT, ends, 0.0), axis=1, keepdims=True)
    far = jnp.where(lane == buckets // 2 - 1, left, jnp.where(lane == buckets - 1, right, 0.0))
    sums[:, :128] = sums[:, :128] + jnp.where(iota((SMALL, 128), 0) == 2 + h, far, 0.0)

    @pl.when(h == heads - 1)
    def _():
        for j in range(0, n, 2):
            even[j // 2] = nn(wkv[...], dkv[j]).astype(bf16)
            odd[j // 2] = nn(wkv[...], dkv[j + 1]).astype(bf16)
        total = jnp.zeros((t, n1.shape[2]), f32)
        for k in range(dq.shape[0]):
            total = total + nt(dq[k], wq[:, k * 128 : k * 128 + 128])
        dn1q[...] = total
        u = iota((4 * t, 128), 0)
        pick = (bucket_of(u - (2 * t - 1), buckets) == iota((4 * t, 128), 1)).astype(f32)
        near = lax.dot_general(line[...], pick, (((1,), (0,)), ((), ())), precision=lax.Precision.HIGHEST,
                               preferred_element_type=f32)
        sums[2:8, :128] = sums[2:8, :128] + near[:6]
        sums[0:1] = sums[0:1] / gain[...]
        sums[1:2] = gn[...]
        small = sums[...].astype(bf16)
        grads[pl.ds(3 * width, width)] = gwo[...]
        rows = 2 * width
        core = me % 2
        keep[:rows] = grads[pl.ds(pl.multiple_of(core * rows, 16), rows)]
        send[:rows] = grads[pl.ds(pl.multiple_of((1 - core) * rows, 16), rows)]
        keep[rows:] = small
        send[rows:] = small


def attention_back(ids, gain, buckets, p, kv, e, n1, q, do, delta, wq, wkv, wqt, wkvt, gwo, gn):
    heads, n, t, _ = p.shape
    d = n1.shape[2]
    smem = pl.BlockSpec(memory_space=pltpu.SMEM)
    const = lambda *shape: pl.BlockSpec(shape, lambda i: (0,) * len(shape), pipeline_mode=pl.Buffered(1))
    keep = lambda *shape: pl.BlockSpec(shape, lambda i: (0,) * len(shape))
    by_head = lambda *shape: pl.BlockSpec((1, n, *shape), lambda i: (i, 0, 0, 0))
    column = pl.BlockSpec((t, 128), lambda i: (0, i))
    shape = jax.ShapeDtypeStruct
    half = 2 * gwo.shape[0] + SMALL
    return pl.pallas_call(
        partial(attention_back_kernel, n, buckets),
        grid=(heads,),
        in_specs=[
            smem, const(1, d), by_head(t, t), by_head(t, 128), const(n, t, 128), const(n, t, d),
            column, column, const(t, 128), const(*wq.shape), const(*wkv.shape),
            pl.BlockSpec((64, d), lambda i: (i, 0)), pl.BlockSpec((128, d), lambda i: (i, 0)),
            const(*gwo.shape), const(1, d),
        ],
        out_specs=[keep(n // 2, d, t), keep(n // 2, d, t), keep(t, d), keep(half, d), keep(half, d)],
        out_shape=[
            shape((n // 2, d, t), bf16),
            shape((n // 2, d, t), bf16),
            shape((t, d), f32),
            shape((half, d), bf16),
            shape((half, d), bf16),
        ],
        scratch_shapes=[
            pltpu.VMEM((n, t, t), bf16),
            pltpu.VMEM((n, heads * 128, t), bf16),
            pltpu.VMEM((heads, t, 128), bf16),
            pltpu.VMEM((4 * gwo.shape[0], d), bf16),
            pltpu.VMEM((SMALL, d), f32),
            pltpu.VMEM((8, 4 * t), f32),
        ],
        compiler_params=pltpu.CompilerParams(vmem_limit_bytes=VMEM),
        name="attention_back",
    )(ids, gain, p, kv, e, n1, q, do, delta, wq, wkv, wqt, wkvt, gwo, gn)


def whole_call(kernel, name, out_shape, *args, scratch=()):
    smem = pl.BlockSpec(memory_space=pltpu.SMEM)
    vmem = pl.BlockSpec(memory_space=pltpu.VMEM)
    return pl.pallas_call(
        kernel,
        in_specs=[smem] + [vmem] * (len(args) - 1),
        out_specs=jax.tree.map(lambda _: vmem, out_shape),
        out_shape=out_shape,
        scratch_shapes=list(scratch),
        compiler_params=pltpu.CompilerParams(vmem_limit_bytes=VMEM),
        name=name,
    )(*args)


def split_kernel(which, count, extra, ids, *refs):
    inputs, outs = refs[:-count], refs[-count:]
    rows = (inputs[0].shape[0] - extra) // count
    own = ids[which]
    for j in range(count):
        at = pl.ds(pl.multiple_of((own ^ j) * rows, 16), rows)
        total = inputs[0][at].astype(f32)
        for ref in inputs[1:]:
            total = total + ref[at].astype(f32)
        outs[j][:rows] = total.astype(bf16)
    if extra:
        at = pl.ds(rows * count, extra)
        total = inputs[0][at].astype(f32)
        for ref in inputs[1:]:
            total = total + ref[at].astype(f32)
        for j in range(count):
            outs[j][rows:] = total.astype(bf16)


def add_and_split(which, count, extra, ids, *arrays):
    rows = (arrays[0].shape[0] - extra) // count + extra
    out = jax.ShapeDtypeStruct((rows, arrays[0].shape[1]), bf16)
    return whole_call(partial(split_kernel, which, count, extra), "add_parts", [out] * count, ids, *arrays)


def swap(array, axis, j):
    size = lax.axis_size(axis)
    return lax.ppermute(array, axis, [(i, i ^ j) for i in range(size)])


def reduce_halves(ids, keep, send, extra):
    chips, rows = lax.axis_size("seq") // 2, lax.axis_size("rows")
    recv = swap(send, "seq", 1)
    size = keep.shape[0] - extra
    if size % (16 * chips * rows):
        both = add_and_split(0, 1, extra, ids * 0, keep, recv)[0].astype(f32)
        placed = jnp.zeros((2 * size, keep.shape[1]), f32)
        placed = lax.dynamic_update_slice_in_dim(placed, both[:size], ids[1] * size, 0)
        full, tail = lax.psum((placed, both[size:] * 0.5), ("rows", "seq"))
        mine = lax.dynamic_slice_in_dim(full, ids[1] * size, size, 0)
        other = lax.dynamic_slice_in_dim(full, (1 - ids[1]) * size, size, 0)
        return mine.astype(bf16), other.astype(bf16), tail.astype(bf16)
    parts = add_and_split(2, chips, extra, ids, keep, recv)
    parts = [parts[0]] + [swap(parts[j], "seq", 2 * j) for j in range(1, chips)]
    parts = add_and_split(3, rows, extra, ids, *parts)
    parts = [parts[0]] + [swap(parts[j], "rows", j) for j in range(1, rows)]
    done = add_and_split(3, 1, extra, ids * 0, *parts)[0]
    least = size // (chips * rows)
    chunk = done[:least]
    line = jnp.concatenate([chunk] + [swap(chunk, "rows", j) for j in range(1, rows)], axis=0)
    half = jnp.concatenate([line] + [swap(line, "seq", 2 * j) for j in range(1, chips)], axis=0)
    return half, swap(half, "seq", 1), done[least:]


def place_halves(ids, mine, other, full, chips, rows):
    size = mine.shape[0]
    least = size // (chips * rows)
    for c, ref in ((ids[1], mine), (1 - ids[1], other)):
        if chips * rows == 1:
            full[pl.ds(pl.multiple_of(c * size, 16), size)] = ref[...]
            continue
        for a in range(chips):
            for b in range(rows):
                at = c * size + ((ids[2] ^ a) * rows + (ids[3] ^ b)) * least
                full[pl.ds(pl.multiple_of(at, 16), least)] = ref[pl.ds((a * rows + b) * least, least)]


def unpack_ffn_kernel(chips, rows, ids, mine, other, gate, up, down, full):
    place_halves(ids, mine, other, full, chips, rows)
    d = gate.shape[0]
    gate[...] = full[:d].astype(f32)
    up[...] = full[d : 2 * d].astype(f32)
    down[:d] = full[2 * d :, :d].astype(f32)
    down[d:] = full[2 * d :, d:].astype(f32)


def unpack_attention_kernel(chips, rows, heads, ids, mine, other, tail, gq, gk, gv, go, g1, g2, gb, full):
    place_halves(ids, mine, other, full, chips, rows)
    w = gq.shape[1]
    for k, ref in enumerate((gq, gk, gv)):
        ref[...] = full[k * w : (k + 1) * w].astype(f32).T
    go[...] = full[3 * w :].astype(f32)
    small = tail[...].astype(f32)
    g1[...] = small[0:1]
    g2[...] = small[1:2]
    gb[...] = small[0:8, :128].T[: gb.shape[0], 2 : 2 + heads]


def input_grad_kernel(ids, *refs):
    *parts, dn1q, x, dh, gain, out = refs
    total = parts[0][...].astype(f32)
    for ref in parts[1:]:
        total = total + ref[...].astype(f32)
    dn1 = total.T + dn1q[...]
    value = x[...].astype(f32)
    s1 = lax.rsqrt(jnp.mean(value * value, axis=-1, keepdims=True) + EPS)
    hat = value * s1
    scaled = dn1 * gain[...]
    out[...] = dh[...] + s1 * (scaled - hat * jnp.mean(hat * scaled, axis=-1, keepdims=True))


def slots_kernel(count, ids, mine, other, *outs):
    for j in range(count):
        outs[j][...] = (mine[j].astype(f32) + other[j].astype(f32)).astype(bf16)


def shards(
    tokens, norm_attn, query_weight, key_weight, value_weight, out_weight, bucket_bias_table, norm_ffn,
    gate_weight, expansion_matrix, down_weight, lengths, cotangent,
):
    _, t, d = tokens.shape
    n = lax.axis_size("seq")
    buckets, heads = bucket_bias_table.shape
    width = query_weight.shape[1]
    dk = width // heads
    seq = lax.axis_index("seq")
    ids = jnp.stack([seq, seq % 2, seq // 2, lax.axis_index("rows")]).astype(i32)
    x = tokens.reshape(t, d)
    cot = cotangent.reshape(t, d)
    lens = lengths.reshape(-1)

    blocks = [None] * n
    blocks[0] = x
    for j in range(n - 2, 0, -2):
        blocks[j] = swap(x, "seq", j)
    for j in range(0, n, 2):
        blocks[j + 1] = swap(blocks[j], "seq", 1)

    by_head = lambda w: w.reshape(d, heads, dk)
    wq = jnp.pad(by_head(query_weight), ((0, 0), (0, 0), (0, 128 - dk))).reshape(d, heads * 128)
    wkv = jnp.concatenate([by_head(key_weight), by_head(value_weight)], axis=2).reshape(d, heads * 128)
    wo = jnp.pad(out_weight.reshape(heads, dk, d), ((0, 0), (128 - dk, 0), (0, 0))).reshape(heads * 128, d)
    table = bucket_bias_table.astype(f32)
    gain1 = norm_attn.astype(f32).reshape(1, d)
    gain2 = norm_ffn.astype(f32).reshape(1, d)

    n1, kv, e, p, o, q = attention_forward(ids, lens, table, gain1, blocks, wq, wkv)
    output, dh, do, delta, gwo, keep, send, gn = feed_forward(
        ids, lens, gain2, x, o, wo, gate_weight, expansion_matrix, down_weight, cot
    )
    ffn = reduce_halves(ids, keep, send, 0)
    even, odd, dn1q, keep, send = attention_back(
        ids, gain1, buckets, p, kv, e, n1, q, do, delta, wq, wkv, query_weight.T, wkv.T, gwo, gn
    )
    mine, other, tail = reduce_halves(ids, keep, send, SMALL)
    recv = swap(odd, "seq", 1)
    half = n // 2
    parts = whole_call(partial(slots_kernel, half), "add_slots",
                       [jax.ShapeDtypeStruct((d, t), bf16)] * half, ids, even, recv)
    parts = [parts[0]] + [swap(parts[j], "seq", 2 * j) for j in range(1, half)]
    grad_tokens = whole_call(input_grad_kernel, "input_grad", jax.ShapeDtypeStruct((t, d), f32),
                             ids, *parts, dn1q, x, dh, gain1)

    rows = lax.axis_size("rows")
    chips = n // 2
    if keep.shape[0] - SMALL and (keep.shape[0] - SMALL) % (16 * chips * rows):
        chips = rows = 1
    ff = gate_weight.shape[1]
    shape = jax.ShapeDtypeStruct
    gate, up, down = whole_call(
        partial(unpack_ffn_kernel, chips, rows), "unpack_ffn",
        [shape((d, ff), f32), shape((d, ff), f32), shape((ff, d), f32)],
        ids, ffn[0], ffn[1], scratch=[pltpu.VMEM((3 * d, ff), bf16)],
    )
    gq, gk, gv, go, g1, g2, gb = whole_call(
        partial(unpack_attention_kernel, chips, rows, heads), "unpack_attention",
        [shape((d, width), f32)] * 3 + [shape((width, d), f32)] + [shape((1, d), f32)] * 2
        + [shape((buckets, heads), f32)],
        ids, mine, other, tail, scratch=[pltpu.VMEM((4 * width, d), bf16)],
    )
    return (
        output.reshape(tokens.shape), grad_tokens.reshape(tokens.shape), g1.reshape(d), gq, gk, gv, go, gb,
        g2.reshape(d), gate, up, down,
    )


def solution(mesh):
    split = P("rows", "seq", None)
    in_specs = (split,) + (P(),) * 10 + (P("rows", None), split)
    out_specs = (split, split) + (P(),) * 10
    return jax.shard_map(shards, mesh=mesh, in_specs=in_specs, out_specs=out_specs, check_vma=False)
```

time: 529 us -> 232 us (0.44)
  waiting for transfers between devices: 264 us -> 86 us
  matrix products: 106 us -> 0 us
  Pallas kernels: 0 us -> 78.3 us
  blocking collectives: 41.5 us -> 0 us
  starting transfers between devices: 0.43 us -> 41.1 us
  local copies, waits for them, and re-layouts: 58.7 us -> 20.6 us
  other arithmetic: 42.1 us -> 4.18 us
  between operations: 14.3 us -> 1.08 us
    psum x1 -> x0, waiting for transfers between devices: 153 us -> none  [shards(): lax.psum((grad_gain_one, grad_query_proj, grad_key_proj, grad_value_proj,...]
    dot_general x61 -> x0, matrix products: 106 us -> none  [the longest x8 28.4 us: bias_pieces(): jnp.einsum('xpt,xn->npt', distance_class_onehot, bucket_bias_table, prefe...]
    ppermute x0 -> x39, waiting for transfers between devices: none -> 86 us  [swap(): return lax.ppermute(array, axis, [(i, i ^ j) for i in range(size)])]
    pallas_call x0 -> x13, Pallas kernels: none -> 78.3 us  [the longest x1 28.8 us: attention_back(): pl.pallas_call(partial(attention_back_kernel, n, buckets), grid=(heads,),...]
    reduce_scatter x2 -> x0, waiting for transfers between devices: 66 us -> none  [the longest x1 39.4 us: shards(): lax.psum_scatter(backward_result[3].astype(jnp.bfloat16), 'seq', scatter_...]
    all_gather x2 -> x0, waiting for transfers between devices: 45.5 us -> none  [the longest x1 25.6 us: shards(): lax.all_gather(value_low, 'seq', axis=1, tiled=True)]
    psum x1 -> x0, blocking collectives: 41.5 us -> none  [shards(): lax.psum((grad_gain_one, grad_query_proj, grad_key_proj, grad_value_proj,...]
    ppermute x0 -> x39, starting transfers between devices: none -> 41.1 us  [swap(): return lax.ppermute(array, axis, [(i, i ^ j) for i in range(size)])]
  transfers between devices with their start and end apart: 5 -> 39, of which waited for: 5 -> 15; matrix products, arithmetic and copies ran while one was open for 6% -> 7% of each run, Pallas kernels for 0% -> 22%
where the time goes in v1:
time: 232 us; the launch traced here: 231 us
  waiting for transfers between devices  86 us (37%)
  Pallas kernels  78.3 us (34%)
  starting transfers between devices  41.1 us (18%)
  local copies, waits for them, and re-layouts  20.6 us (9%)
  other arithmetic  4.18 us (2%)
    ppermute x39, waiting for transfers between devices, swap(): return lax.ppermute(array, axis, [(i, i ^ j) for i in range(size)])  86 us
    ppermute x39, starting transfers between devices, swap(): return lax.ppermute(array, axis, [(i, i ^ j) for i in range(size)])  41.1 us
    pallas_call x1, Pallas kernels, attention_back(): pl.pallas_call(partial(attention_back_kernel, n, buckets), grid=(heads,),...  28.8 us
    pallas_call x10, Pallas kernels, whole_call(): pl.pallas_call(kernel, in_specs=[smem] + [vmem] * (len(args) - 1), out_sp...  27.1 us
    pallas_call x1, Pallas kernels, attention_forward(): pl.pallas_call(partial(attention_kernel, n), grid=(heads // 2,), in_specs...  14.5 us
    unnamed x89, local copies, waits for them, and re-layouts  13.2 us
    pallas_call x1, Pallas kernels, feed_forward(): pl.pallas_call(feed_forward_kernel, in_specs=[smem, smem] + [vmem] * 8, o...  7.94 us
  transfers between devices with their start and end apart: 39, of which 15 were waited for; matrix products, arithmetic and copies ran while one was open for 7% of the time, Pallas kernels for 22%

profile of v1, /device:TPU:0, one launch (start us, length us, event | category | flops | bytes accessed | tf_op | source)
XLA Modules:
  0.0 231.3 jit_solution(8829572008876547472)
XLA Ops:
  0.6 3.0 %collective-permute-start.1 = (bf16[256,512]{1,0:T(8,128)(2,1)}, bf16[256,512]{1,0:T(8,128)(2,1)S(1)}, u32[]{:S(2)}, u32[]{:S(2)}) collective-permute-start(bf16[256,512]{1,0:T(8,128)(2,1)} %bitcast.29), channel_id=1, source_target_pairs={{0,2},{1,3},{2,0},{3,1},{4,6},{5,7},{6,4},{7,5},{8,10},{9,11},{10,... | collective-permute-start | bytes 786440 | tf_op jit(solution)/shard_map/ppermute | solution.py:416
  3.6 1.5 collective-permute-start.3
  5.2 5.8 %collective-permute-done.1.refs_2_ = bf16[256,512]{1,0:T(8,128)(2,1)S(1)} collective-permute-done((bf16[256,512]{1,0:T(8,128)(2,1)}, bf16[256,512]{1,0:T(8,128)(2,1)S(1)}, u32[]{:S(2)}, u32[]{:S(2)}) %collective-permute-start.1) | collective-permute-done | bytes 262176 | tf_op jit(solution)/shard_map/ppermute | solution.py:416
  11.0 6.2 %collective-permute-done.3.refs_4_ = bf16[256,512]{1,0:T(8,128)(2,1)S(1)} collective-permute-done((bf16[256,512]{1,0:T(8,128)(2,1)}, bf16[256,512]{1,0:T(8,128)(2,1)S(1)}, u32[]{:S(2)}, u32[]{:S(2)}) %collective-permute-start.3) | collective-permute-done | bytes 262176 | tf_op jit(solution)/shard_map/ppermute | solution.py:416
  17.8 1.3 reshape.94
  19.0 1.4 copy.45.table
  20.4 1.3 reshape.96
  21.6 1.2 copy.42
  22.9 1.2 copy.46.refs_8_.wq
  24.6 1.2 copy.47.refs_9_.wkv
  25.8 0.9 pad.9
  28.3 14.5 %attention_forward.1 = (bf16[8,256,512]{2,1,0:T(8,128)(2,1)}, bf16[6,8,256,128]{3,2,1,0:T(8,128)(2,1)}, bf16[8,256,128]{2,1,0:T(8,128)(2,1)}, bf16[6,8,256,256]{...) custom-call(s32[4]{0:T(128)} %pad_add_fusion.ids, s32[16]{0:T(128)} %bitcast.45, ...), custom_call_target="tpu_custom_call" | custom-call | tf_op jit(solution)/shard_map/attention_forward/pallas_call | solution.py:146
  42.8 7.9 %feed_forward.1 = (bf16[256,512]{1,0:T(8,128)(2,1)}, f32[256,512]{1,0:T(8,128)}, bf16[256,768]{1,0:T(8,128)(2,1)}, f32[256,128]{1,0:T(8,128)}, bf16[384,512]{1,0...) custom-call(s32[4]{0:T(128)} %pad_add_fusion.ids, s32[16]{0:T(128)} %bitcast.46, ...), custom_call_target="tpu_custom_call" | custom-call | tf_op jit(solution)/shard_map/feed_forward/pallas_call | solution.py:233
  50.9 28.8 %attention_back.1 = (bf16[4,512,256]{2,1,0:T(8,128)(2,1)}, bf16[4,512,256]{2,1,0:T(8,128)(2,1)}, f32[256,512]{1,0:T(8,128)}, bf16[784,512]{1,0:T(8,128)(2,1)}, bf16[784,512]{1,0:T(8,128)(2,1)}) custom-call(s32[4]{0:T(128)} %pad_add_fusion.ids, f32[1,512]{1,0:T(1,128)} %bitcast.42, bf16[6,8,256,256]{3,2,1,0:T(8,128)(2,1)} %get-tuple-element.63.p, ...), custom_call_target="tpu_custom_call" | custom-call | tf_op jit(solution)/shard_map/attention_back/pallas_call | solution.py:345
  80.1 2.1 collective-permute-done.11.refs_1_
  83.2 2.4 %add_parts.6 = (bf16[208,512]{1,0:T(8,128)(2,1)}, bf16[208,512]{1,0:T(8,128)(2,1)}, bf16[208,512]{1,0:T(8,128)(2,1)}, bf16[208,512]{1,0:T(8,128)(2,1)}) custom-call(s32[4]{0:T(128)} %pad_add_fusion.ids, bf16[784,512]{1,0:T(8,128)(2,1)} %get-tuple-element.80.refs_0_, bf16[784,512]{1,0:T(8,128)(2,1)} %copy-done.7), custom_call_target="tpu_custom_call" | custom-call | tf_op jit(solution)/shard_map/add_parts/pallas_call | solution.py:378
  85.6 1.1 collective-permute-start.12
  86.7 1.1 copy-done.4
  87.8 3.4 %add_parts.9 = (bf16[192,1024]{1,0:T(8,128)(2,1)}, bf16[192,1024]{1,0:T(8,128)(2,1)}, bf16[192,1024]{1,0:T(8,128)(2,1)}, bf16[192,1024]{1,0:T(8,128)(2,1)}) custom-call(s32[4]{0:T(128)} %pad_add_fusion.ids, bf16[768,1024]{1,0:T(8,128)(2,1)} %get-tuple-element.97.refs_0_, bf16[768,1024]{1,0:T(8,128)(2,1)} %copy-done.4), custom_call_target="tpu_custom_call" | custom-call | tf_op jit(solution)/shard_map/add_parts/pallas_call | solution.py:378
  91.2 1.0 collective-permute-start.26
  92.1 1.5 collective-permute-start.27
  93.7 1.0 collective-permute-start.28
  94.7 1.0 collective-permute-start.13
  95.7 1.5 collective-permute-start.14
  97.2 23.6 %collective-permute-done.13.refs_2_ = bf16[208,512]{1,0:T(8,128)(2,1)S(1)} collective-permute-done((bf16[208,512]{1,0:T(8,128)(2,1)S(1)}, bf16[208,512]{1,0:T(8,128)(2,1)S(1)}, u32[]{:S(2)}, u32[]{:S(2)}) %collective-permute-start.13) | collective-permute-done | bytes 213024 | tf_op jit(solution)/shard_map/ppermute | solution.py:416
  121.5 2.0 add_parts.7
  123.5 1.6 collective-permute-start.15
  126.1 2.2 add_parts.10
  128.8 2.6 %collective-permute-start.30 = (bf16[48,1024]{1,0:T(8,128)(2,1)}, bf16[48,1024]{1,0:T(8,128)(2,1)S(1)}, u32[]{:S(2)}, u32[]{:S(2)}) collective-permute-start(bf16[48,1024]{1,0:T(8,128)(2,1)} %get-tuple-element.105), channel_id=1, source_target_pairs={{0,16},{8,24},{16,0},{24,8},{1,17},{9,25},{17,1},{25,9},{2,18},{10... | collective-permute-start | bytes 294920 | tf_op jit(solution)/shard_map/ppermute | solution.py:416
  131.4 1.3 collective-permute-start.31
  132.8 1.7 collective-permute-start.16
  134.5 1.0 collective-permute-start.17
  135.4 9.8 %collective-permute-done.16.refs_2_ = bf16[64,512]{1,0:T(8,128)(2,1)S(1)} collective-permute-done((bf16[64,512]{1,0:T(8,128)(2,1)S(1)}, bf16[64,512]{1,0:T(8,128)(2,1)S(1)}, u32[]{:S(2)}, u32[]{:S(2)}) %collective-permute-start.16) | collective-permute-done | bytes 65568 | tf_op jit(solution)/shard_map/ppermute | solution.py:416
  145.8 1.6 add_parts.8
  148.1 1.7 add_parts.11
  149.9 1.2 collective-permute-start.32
  151.1 1.9 collective-permute-start.33
  153.0 1.2 collective-permute-start.34
  155.4 1.1 collective-permute-done.32
  156.5 5.2 %collective-permute-done.33 = bf16[48,1024]{1,0:T(8,128)(2,1)S(1)} collective-permute-done((bf16[48,1024]{1,0:T(8,128)(2,1)}, bf16[48,1024]{1,0:T(8,128)(2,1)S(1)}, u32[]{:S(2)}, u32[]{:S(2)}) %collective-permute-start.33) | collective-permute-done | bytes 98336 | tf_op jit(solution)/shard_map/ppermute | solution.py:416
  164.2 1.5 collective-permute-start.36
  165.7 1.4 collective-permute-start.37
  167.1 7.6 %collective-permute-done.35 = bf16[192,1024]{1,0:T(8,128)(2,1)S(1)} collective-permute-done((bf16[192,1024]{1,0:T(8,128)(2,1)S(1)}, bf16[192,1024]{1,0:T(8,128)(2,1)S(1)}, u32[]{:S(2)}, u32[]{:S(2)}) %collective-permute-start.35) | collective-permute-done | bytes 393248 | tf_op jit(solution)/shard_map/ppermute | solution.py:416
  174.8 2.5 %collective-permute-start.19 = (bf16[48,512]{1,0:T(8,128)(2,1)S(1)}, bf16[48,512]{1,0:T(8,128)(2,1)S(1)}, u32[]{:S(2)}, u32[]{:S(2)}) collective-permute-start(bf16[48,512]{1,0:T(8,128)(2,1)S(1)} %get-tuple-element.146), channel_id=1, source_target_pairs={{0,16},{8,24},{16,0},{24,8},{1,17},{9,25},{17,1},{25,9},{2,18},{10... | collective-permute-start | bytes 147464 | tf_op jit(solution)/shard_map/ppermute | solution.py:416
  177.3 4.1 %collective-permute-done.36 = bf16[192,1024]{1,0:T(8,128)(2,1)S(1)} collective-permute-done((bf16[192,1024]{1,0:T(8,128)(2,1)S(1)}, bf16[192,1024]{1,0:T(8,128)(2,1)S(1)}, u32[]{:S(2)}, u32[]{:S(2)}) %collective-permute-start.36) | collective-permute-done | bytes 393248 | tf_op jit(solution)/shard_map/ppermute | solution.py:416
  181.5 1.6 collective-permute-start.20
  183.3 4.2 %collective-permute-done.20 = bf16[48,512]{1,0:T(8,128)(2,1)S(1)} collective-permute-done((bf16[48,512]{1,0:T(8,128)(2,1)S(1)}, bf16[48,512]{1,0:T(8,128)(2,1)S(1)}, u32[]{:S(2)}, u32[]{:S(2)}) %collective-permute-start.20) | collective-permute-done | bytes 49184 | tf_op jit(solution)/shard_map/ppermute | solution.py:416
  187.5 1.5 collective-permute-start.21
  189.0 1.5 collective-permute-start.22
  191.0 2.2 collective-permute-done.21
  193.2 2.6 %collective-permute-done.22 = bf16[192,512]{1,0:T(8,128)(2,1)S(1)} collective-permute-done((bf16[192,512]{1,0:T(8,128)(2,1)S(1)}, bf16[192,512]{1,0:T(8,128)(2,1)S(1)}, u32[]{:S(2)}, u32[]{:S(2)}) %collective-permute-start.22) | collective-permute-done | bytes 196640 | tf_op jit(solution)/shard_map/ppermute | solution.py:416
  195.9 1.2 collective-permute-done.23
  197.2 1.1 copy-done.5
  198.4 2.6 %add_slots.1 = (bf16[512,256]{1,0:T(8,128)(2,1)}, bf16[512,256]{1,0:T(8,128)(2,1)}, bf16[512,256]{1,0:T(8,128)(2,1)}, bf16[512,256]{1,0:T(8,128)(2,1)}) custom-call(s32[4]{0:T(128)} %pad_add_fusion.ids, bf16[4,512,256]{2,1,0:T(8,128)(2,1)} %get-tuple-element.72.mine, bf16[4,512,256]{2,1,0:T(8,128)(2,1)} %copy-done.5), custom_call_target="tpu_custom_call" | custom-call | tf_op jit(solution)/shard_map/add_slots/pallas_call | solution.py:378
  201.6 1.1 collective-permute-start.9
  202.7 1.7 collective-permute-start.10
  204.4 1.3 slice.9.tail
  205.7 4.5 %collective-permute-done.8.refs_1_ = bf16[512,256]{1,0:T(8,128)(2,1)S(1)} collective-permute-done((bf16[512,256]{1,0:T(8,128)(2,1)}, bf16[512,256]{1,0:T(8,128)(2,1)S(1)}, u32[]{:S(2)}, u32[]{:S(2)}) %collective-permute-start.8) | collective-permute-done | bytes 262176 | tf_op jit(solution)/shard_map/ppermute | solution.py:416
  210.3 5.6 %collective-permute-done.10.refs_3_ = bf16[512,256]{1,0:T(8,128)(2,1)S(1)} collective-permute-done((bf16[512,256]{1,0:T(8,128)(2,1)}, bf16[512,256]{1,0:T(8,128)(2,1)S(1)}, u32[]{:S(2)}, u32[]{:S(2)}) %collective-permute-start.10) | collective-permute-done | bytes 262176 | tf_op jit(solution)/shard_map/ppermute | solution.py:416
  216.7 2.8 %input_grad.1 = f32[256,512]{1,0:T(8,128)} custom-call(s32[4]{0:T(128)} %pad_add_fusion.ids, bf16[512,256]{1,0:T(8,128)(2,1)} %get-tuple-element.74.refs_0_, bf16[512,256]{1,0:T(8,128)(2,1)} %copy-done.21, bf16[512,256]{1,0:T(8,128)(2,1)} %copy-done.22, bf16[512,256]{1,0:T(8,128)(2,1)} %copy-done.23, f32[256,512]{1,0:T(8,128)} %get-tuple-element.78.refs_4_, ...), custom_call_target="tpu_custom_call" | custom-call | tf_op jit(solution)/shard_map/input_grad/pallas_call | solution.py:378
  220.4 3.4 %unpack_attention.1 = (f32[512,384]{1,0:T(8,128)}, f32[512,384]{1,0:T(8,128)}, f32[512,384]{1,0:T(8,128)}, f32[384,512]{1,0:T(8,128)}, f32[1,512]{1,0:T(1,128)}, /*index=5*/f32[1,512]{1,0:T(1,128)}, f32[32,6]{1,0:T(8,128)}) custom-call(s32[4]{0:T(128)} %pad_add_fusion.ids, bf16[768,512]{1,0:T(8,128)(2,1)} %copy-done.6, bf16[768,512]{1,0:T(8,128)(2,1)} %copy-done.8, ...), custom_call_target="tpu_custom_call" | custom-call | tf_op jit(solution)/shard_map/unpack_attention/pallas_call | solution.py:378
  223.8 1.4 copy.51
  225.2 1.1 copy-done.3
  226.3 4.9 %unpack_ffn.1 = (f32[512,1024]{1,0:T(8,128)}, f32[512,1024]{1,0:T(8,128)}, f32[1024,512]{1,0:T(8,128)}) custom-call(s32[4]{0:T(128)} %pad_add_fusion.ids, bf16[768,1024]{1,0:T(8,128)(2,1)} %copy-done.2, bf16[768,1024]{1,0:T(8,128)(2,1)} %copy-done.3), custom_call_target="tpu_custom_call" | custom-call | tf_op jit(solution)/shard_map/unpack_ffn/pallas_call | solution.py:378
  (132 shorter events, 14.3 us)
Async XLA Ops:
  0.6 10.4 %collective-permute-start.1 = (bf16[256,512]{1,0:T(8,128)(2,1)}, bf16[256,512]{1,0:T(8,128)(2,1)S(1)}, u32[]{:S(2)}, u32[]{:S(2)}) collective-permute-start(bf16[256,512]{1,0:T(8,128)(2,1)} %bitcast.29), channel_id=1, source_target_pairs={{0,2},{1,3},{2,0},{3,1},{4,6},{5,7},{6,4},{7,5},{8,10},{9,11},{10,... | collective-permute-start | bytes 786440 | tf_op jit(solution)/shard_map/ppermute | solution.py:416
  3.6 13.6 %collective-permute-start.3 = (bf16[256,512]{1,0:T(8,128)(2,1)}, bf16[256,512]{1,0:T(8,128)(2,1)S(1)}, u32[]{:S(2)}, u32[]{:S(2)}) collective-permute-start(bf16[256,512]{1,0:T(8,128)(2,1)} %bitcast.30), channel_id=1, source_target_pairs={{0,4},{1,5},{2,6},{3,7},{4,0},{5,1},{6,2},{7,3},{8,12},{9,13},{10,... | collective-permute-start | bytes 786440 | tf_op jit(solution)/shard_map/ppermute | solution.py:416
  5.2 12.1 %collective-permute-start.5 = (bf16[256,512]{1,0:T(8,128)(2,1)}, bf16[256,512]{1,0:T(8,128)(2,1)S(1)}, u32[]{:S(2)}, u32[]{:S(2)}) collective-permute-start(bf16[256,512]{1,0:T(8,128)(2,1)} %bitcast.31), channel_id=1, source_target_pairs={{0,6},{1,7},{2,4},{3,5},{4,2},{5,3},{6,0},{7,1},{8,14},{9,15},{10,... | collective-permute-start | bytes 786440 | tf_op jit(solution)/shard_map/ppermute | solution.py:416
  5.2 22.2 %collective-permute-start = (bf16[256,512]{1,0:T(8,128)(2,1)}, bf16[256,512]{1,0:T(8,128)(2,1)S(1)}, u32[]{:S(2)}, u32[]{:S(2)}) collective-permute-start(bf16[256,512]{1,0:T(8,128)(2,1)} %bitcast.32), channel_id=1, source_target_pairs={{0,1},{1,0},{2,3},{3,2},{4,5},{5,4},{6,7},{7,6},{8,9},{9,8},{10,11... | collective-permute-start | bytes 786440 | tf_op jit(solution)/shard_map/ppermute | solution.py:416
  11.0 13.1 %copy-start.15 = (bf16[256,512]{1,0:T(8,128)(2,1)}, bf16[256,512]{1,0:T(8,128)(2,1)S(1)}, u32[]{:S(2)}) copy-start(bf16[256,512]{1,0:T(8,128)(2,1)S(1)} %collective-permute-done.1.refs_2_) | copy-start | bytes 786436
  11.0 16.4 %collective-permute-start.2 = (bf16[256,512]{1,0:T(8,128)(2,1)S(1)}, bf16[256,512]{1,0:T(8,128)(2,1)S(1)}, u32[]{:S(2)}, u32[]{:S(2)}) collective-permute-start(bf16[256,512]{1,0:T(8,128)(2,1)S(1)} %collective-permute-done.1.refs_2_), channel_id=1, source_target_pairs={{0,1},{1,0},{2,3},{3,2},{4,5},{5,4},{6,7},{7,6},{8,9},{9,8},{10,11... | collective-permute-start | bytes 786440 | tf_op jit(solution)/shard_map/ppermute | solution.py:416
  17.2 6.8 %copy-start.16 = (bf16[256,512]{1,0:T(8,128)(2,1)}, bf16[256,512]{1,0:T(8,128)(2,1)S(1)}, u32[]{:S(2)}) copy-start(bf16[256,512]{1,0:T(8,128)(2,1)S(1)} %collective-permute-done.3.refs_4_) | copy-start | bytes 786436
  17.2 10.2 %collective-permute-start.4 = (bf16[256,512]{1,0:T(8,128)(2,1)S(1)}, bf16[256,512]{1,0:T(8,128)(2,1)S(1)}, u32[]{:S(2)}, u32[]{:S(2)}) collective-permute-start(bf16[256,512]{1,0:T(8,128)(2,1)S(1)} %collective-permute-done.3.refs_4_), channel_id=1, source_target_pairs={{0,1},{1,0},{2,3},{3,2},{4,5},{5,4},{6,7},{7,6},{8,9},{9,8},{10,11... | collective-permute-start | bytes 786440 | tf_op jit(solution)/shard_map/ppermute | solution.py:416
  17.3 6.8 %copy-start.17 = (bf16[256,512]{1,0:T(8,128)(2,1)}, bf16[256,512]{1,0:T(8,128)(2,1)S(1)}, u32[]{:S(2)}) copy-start(bf16[256,512]{1,0:T(8,128)(2,1)S(1)} %collective-permute-done.5.refs_6_) | copy-start | bytes 786436
  17.3 10.2 %collective-permute-start.6 = (bf16[256,512]{1,0:T(8,128)(2,1)S(1)}, bf16[256,512]{1,0:T(8,128)(2,1)}, u32[]{:S(2)}, u32[]{:S(2)}) collective-permute-start(bf16[256,512]{1,0:T(8,128)(2,1)S(1)} %collective-permute-done.5.refs_6_), channel_id=1, source_target_pairs={{0,1},{1,0},{2,3},{3,2},{4,5},{5,4},{6,7},{7,6},{8,9},{9,8},{10,11... | collective-permute-start | bytes 786440 | tf_op jit(solution)/shard_map/ppermute | solution.py:416
  22.8 1.5 copy-start.1
  22.8 1.3 copy-start.9
  22.8 1.5 copy-start.10
  24.5 1.3 copy-start.11
  24.6 18.2 %copy-start = (bf16[512,6,128]{0,2,1:T(8,128)(2,1)}, bf16[512,6,128]{0,2,1:T(8,128)(2,1)S(1)}, u32[]{:S(2)}) copy-start(bf16[512,6,128]{0,2,1:T(8,128)(2,1)S(1)} %pad_maximum_fusion) | copy-start | bytes 2359300
  50.7 36.0 %collective-permute-start.25 = (bf16[768,1024]{1,0:T(8,128)(2,1)}, bf16[768,1024]{1,0:T(8,128)(2,1)S(1)}, u32[]{:S(2)}, u32[]{:S(2)}) collective-permute-start(bf16[768,1024]{1,0:T(8,128)(2,1)} %get-tuple-element.98), channel_id=1, source_target_pairs={{0,1},{1,0},{2,3},{3,2},{4,5},{5,4},{6,7},{7,6},{8,9},{9,8},{10,11... | collective-permute-start | bytes 4718600 | tf_op jit(solution)/shard_map/ppermute | solution.py:416
  79.7 2.6 %collective-permute-start.11 = (bf16[784,512]{1,0:T(8,128)(2,1)}, bf16[784,512]{1,0:T(8,128)(2,1)S(1)}, u32[]{:S(2)}, u32[]{:S(2)}) collective-permute-start(bf16[784,512]{1,0:T(8,128)(2,1)} %get-tuple-element.81), channel_id=1, source_target_pairs={{0,1},{1,0},{2,3},{3,2},{4,5},{5,4},{6,7},{7,6},{8,9},{9,8},{10,11... | collective-permute-start | bytes 2408456 | tf_op jit(solution)/shard_map/ppermute | solution.py:416
  82.3 0.9 copy-start.7
  85.6 10.1 %collective-permute-start.12 = (bf16[208,512]{1,0:T(8,128)(2,1)}, bf16[208,512]{1,0:T(8,128)(2,1)S(1)}, u32[]{:S(2)}, u32[]{:S(2)}) collective-permute-start(bf16[208,512]{1,0:T(8,128)(2,1)} %get-tuple-element.83), channel_id=1, source_target_pairs={{0,2},{1,3},{2,0},{3,1},{4,6},{5,7},{6,4},{7,5},{8,10},{9,11},{10,... | collective-permute-start | bytes 638984 | tf_op jit(solution)/shard_map/ppermute | solution.py:416
  86.7 1.1 copy-start.4
  87.8 6.9 %copy-start.34 = (bf16[208,512]{1,0:T(8,128)(2,1)S(1)}, bf16[208,512]{1,0:T(8,128)(2,1)}, u32[]{:S(2)}) copy-start(bf16[208,512]{1,0:T(8,128)(2,1)} %get-tuple-element.84) | copy-start | bytes 638980
  87.8 7.9 %copy-start.33 = (bf16[208,512]{1,0:T(8,128)(2,1)S(1)}, bf16[208,512]{1,0:T(8,128)(2,1)}, u32[]{:S(2)}) copy-start(bf16[208,512]{1,0:T(8,128)(2,1)} %get-tuple-element.85) | copy-start | bytes 638980
  91.2 33.9 %collective-permute-start.26 = (bf16[192,1024]{1,0:T(8,128)(2,1)}, bf16[192,1024]{1,0:T(8,128)(2,1)S(1)}, u32[]{:S(2)}, u32[]{:S(2)}) collective-permute-start(bf16[192,1024]{1,0:T(8,128)(2,1)} %get-tuple-element.100), channel_id=1, source_target_pairs={{0,2},{1,3},{2,0},{3,1},{4,6},{5,7},{6,4},{7,5},{8,10},{9,11},{10,... | collective-permute-start | bytes 1179656 | tf_op jit(solution)/shard_map/ppermute | solution.py:416
  92.1 33.0 %collective-permute-start.27 = (bf16[192,1024]{1,0:T(8,128)(2,1)}, bf16[192,1024]{1,0:T(8,128)(2,1)S(1)}, u32[]{:S(2)}, u32[]{:S(2)}) collective-permute-start(bf16[192,1024]{1,0:T(8,128)(2,1)} %get-tuple-element.101), channel_id=1, source_target_pairs={{0,4},{1,5},{2,6},{3,7},{4,0},{5,1},{6,2},{7,3},{8,12},{9,13},{10,... | collective-permute-start | bytes 1179656 | tf_op jit(solution)/shard_map/ppermute | solution.py:416
  93.7 31.5 %collective-permute-start.28 = (bf16[192,1024]{1,0:T(8,128)(2,1)}, bf16[192,1024]{1,0:T(8,128)(2,1)S(1)}, u32[]{:S(2)}, u32[]{:S(2)}) collective-permute-start(bf16[192,1024]{1,0:T(8,128)(2,1)} %get-tuple-element.102), channel_id=1, source_target_pairs={{0,6},{1,7},{2,4},{3,5},{4,2},{5,3},{6,0},{7,1},{8,14},{9,15},{10,... | collective-permute-start | bytes 1179656 | tf_op jit(solution)/shard_map/ppermute | solution.py:416
  94.7 26.0 %collective-permute-start.13 = (bf16[208,512]{1,0:T(8,128)(2,1)S(1)}, bf16[208,512]{1,0:T(8,128)(2,1)S(1)}, u32[]{:S(2)}, u32[]{:S(2)}) collective-permute-start(bf16[208,512]{1,0:T(8,128)(2,1)S(1)} %copy-done.34), channel_id=1, source_target_pairs={{0,4},{1,5},{2,6},{3,7},{4,0},{5,1},{6,2},{7,3},{8,12},{9,13},{10,... | collective-permute-start | bytes 638984 | tf_op jit(solution)/shard_map/ppermute | solution.py:416
  95.7 25.1 %copy-start.24 = (bf16[208,512]{1,0:T(8,128)(2,1)}, bf16[208,512]{1,0:T(8,128)(2,1)S(1)}, u32[]{:S(2)}) copy-start(bf16[208,512]{1,0:T(8,128)(2,1)S(1)} %collective-permute-done.12.refs_1_) | copy-start | bytes 638980
  95.7 25.1 %collective-permute-start.14 = (bf16[208,512]{1,0:T(8,128)(2,1)S(1)}, bf16[208,512]{1,0:T(8,128)(2,1)S(1)}, u32[]{:S(2)}, u32[]{:S(2)}) collective-permute-start(bf16[208,512]{1,0:T(8,128)(2,1)S(1)} %copy-done.33), channel_id=1, source_target_pairs={{0,6},{1,7},{2,4},{3,5},{4,2},{5,3},{6,0},{7,1},{8,14},{9,15},{10,... | collective-permute-start | bytes 638984 | tf_op jit(solution)/shard_map/ppermute | solution.py:416
  123.5 9.3 %copy-start.36 = (bf16[64,512]{1,0:T(8,128)(2,1)S(1)}, bf16[64,512]{1,0:T(8,128)(2,1)}, u32[]{:S(2)}) copy-start(bf16[64,512]{1,0:T(8,128)(2,1)} %get-tuple-element.88) | copy-start | bytes 196612
  123.5 11.0 %copy-start.35 = (bf16[64,512]{1,0:T(8,128)(2,1)S(1)}, bf16[64,512]{1,0:T(8,128)(2,1)}, u32[]{:S(2)}) copy-start(bf16[64,512]{1,0:T(8,128)(2,1)} %get-tuple-element.89) | copy-start | bytes 196612
  123.5 11.0 %collective-permute-start.15 = (bf16[64,512]{1,0:T(8,128)(2,1)}, bf16[64,512]{1,0:T(8,128)(2,1)S(1)}, u32[]{:S(2)}, u32[]{:S(2)}) collective-permute-start(bf16[64,512]{1,0:T(8,128)(2,1)} %get-tuple-element.87), channel_id=1, source_target_pairs={{0,8},{8,0},{16,24},{24,16},{1,9},{9,1},{17,25},{25,17},{2,10},{10... | collective-permute-start | bytes 196616 | tf_op jit(solution)/shard_map/ppermute | solution.py:416
  125.1 0.9 copy-start.13
  125.2 1.0 copy-start.14
  128.4 19.1 %collective-permute-start.29 = (bf16[48,1024]{1,0:T(8,128)(2,1)}, bf16[48,1024]{1,0:T(8,128)(2,1)S(1)}, u32[]{:S(2)}, u32[]{:S(2)}) collective-permute-start(bf16[48,1024]{1,0:T(8,128)(2,1)} %get-tuple-element.104), channel_id=1, source_target_pairs={{0,8},{8,0},{16,24},{24,16},{1,9},{9,1},{17,25},{25,17},{2,10},{10... | collective-permute-start | bytes 294920 | tf_op jit(solution)/shard_map/ppermute | solution.py:416
  128.8 18.6 %collective-permute-start.30 = (bf16[48,1024]{1,0:T(8,128)(2,1)}, bf16[48,1024]{1,0:T(8,128)(2,1)S(1)}, u32[]{:S(2)}, u32[]{:S(2)}) collective-permute-start(bf16[48,1024]{1,0:T(8,128)(2,1)} %get-tuple-element.105), channel_id=1, source_target_pairs={{0,16},{8,24},{16,0},{24,8},{1,17},{9,25},{17,1},{25,9},{2,18},{10... | collective-permute-start | bytes 294920 | tf_op jit(solution)/shard_map/ppermute | solution.py:416
  131.4 16.1 %collective-permute-start.31 = (bf16[48,1024]{1,0:T(8,128)(2,1)}, bf16[48,1024]{1,0:T(8,128)(2,1)S(1)}, u32[]{:S(2)}, u32[]{:S(2)}) collective-permute-start(bf16[48,1024]{1,0:T(8,128)(2,1)} %get-tuple-element.106), channel_id=1, source_target_pairs={{0,24},{8,16},{16,8},{24,0},{1,25},{9,17},{17,9},{25,1},{2,26},{10... | collective-permute-start | bytes 294920 | tf_op jit(solution)/shard_map/ppermute | solution.py:416
  132.8 12.4 %collective-permute-start.16 = (bf16[64,512]{1,0:T(8,128)(2,1)S(1)}, bf16[64,512]{1,0:T(8,128)(2,1)S(1)}, u32[]{:S(2)}, u32[]{:S(2)}) collective-permute-start(bf16[64,512]{1,0:T(8,128)(2,1)S(1)} %copy-done.36), channel_id=1, source_target_pairs={{0,16},{8,24},{16,0},{24,8},{1,17},{9,25},{17,1},{25,9},{2,18},{10... | collective-permute-start | bytes 196616 | tf_op jit(solution)/shard_map/ppermute | solution.py:416
  134.4 11.3 %copy-start.30 = (bf16[64,512]{1,0:T(8,128)(2,1)}, bf16[64,512]{1,0:T(8,128)(2,1)S(1)}, u32[]{:S(2)}) copy-start(bf16[64,512]{1,0:T(8,128)(2,1)S(1)} %collective-permute-done.15.refs_1_) | copy-start | bytes 196612
  134.5 10.7 %collective-permute-start.17 = (bf16[64,512]{1,0:T(8,128)(2,1)S(1)}, bf16[64,512]{1,0:T(8,128)(2,1)S(1)}, u32[]{:S(2)}, u32[]{:S(2)}) collective-permute-start(bf16[64,512]{1,0:T(8,128)(2,1)S(1)} %copy-done.35), channel_id=1, source_target_pairs={{0,24},{8,16},{16,8},{24,0},{1,25},{9,17},{17,9},{25,1},{2,26},{10... | collective-permute-start | bytes 196616 | tf_op jit(solution)/shard_map/ppermute | solution.py:416
  145.2 52.0 %collective-permute-start.7 = (bf16[4,512,256]{2,1,0:T(8,128)(2,1)}, bf16[4,512,256]{2,1,0:T(8,128)(2,1)S(1)}, u32[]{:S(2)}, u32[]{:S(2)}) collective-permute-start(bf16[4,512,256]{2,1,0:T(8,128)(2,1)} %get-tuple-element.73), channel_id=1, source_target_pairs={{0,1},{1,0},{2,3},{3,2},{4,5},{5,4},{6,7},{7,6},{8,9},{9,8},{10,11... | collective-permute-start | bytes 3145736 | tf_op jit(solution)/shard_map/ppermute | solution.py:416
  149.9 6.6 %collective-permute-start.32 = (bf16[48,1024]{1,0:T(8,128)(2,1)}, bf16[48,1024]{1,0:T(8,128)(2,1)S(1)}, u32[]{:S(2)}, u32[]{:S(2)}) collective-permute-start(bf16[48,1024]{1,0:T(8,128)(2,1)} %add_parts.11), channel_id=1, source_target_pairs={{0,8},{8,0},{16,24},{24,16},{1,9},{9,1},{17,25},{25,17},{2,10},{10... | collective-permute-start | bytes 294920 | tf_op jit(solution)/shard_map/ppermute | solution.py:416
  151.1 10.6 %collective-permute-start.33 = (bf16[48,1024]{1,0:T(8,128)(2,1)}, bf16[48,1024]{1,0:T(8,128)(2,1)S(1)}, u32[]{:S(2)}, u32[]{:S(2)}) collective-permute-start(bf16[48,1024]{1,0:T(8,128)(2,1)} %add_parts.11), channel_id=1, source_target_pairs={{0,16},{8,24},{16,0},{24,8},{1,17},{9,25},{17,1},{25,9},{2,18},{10... | collective-permute-start | bytes 294920 | tf_op jit(solution)/shard_map/ppermute | solution.py:416
  153.0 8.7 %collective-permute-start.34 = (bf16[48,1024]{1,0:T(8,128)(2,1)}, bf16[48,1024]{1,0:T(8,128)(2,1)S(1)}, u32[]{:S(2)}, u32[]{:S(2)}) collective-permute-start(bf16[48,1024]{1,0:T(8,128)(2,1)} %add_parts.11), channel_id=1, source_target_pairs={{0,24},{8,16},{16,8},{24,0},{1,25},{9,17},{17,9},{25,1},{2,26},{10... | collective-permute-start | bytes 294920 | tf_op jit(solution)/shard_map/ppermute | solution.py:416
  155.1 28.2 %collective-permute-start.18 = (bf16[48,512]{1,0:T(8,128)(2,1)S(1)}, bf16[48,512]{1,0:T(8,128)(2,1)S(1)}, u32[]{:S(2)}, u32[]{:S(2)}) collective-permute-start(bf16[48,512]{1,0:T(8,128)(2,1)S(1)} %get-tuple-element.146), channel_id=1, source_target_pairs={{0,8},{8,0},{16,24},{24,16},{1,9},{9,1},{17,25},{25,17},{2,10},{10... | collective-permute-start | bytes 147464 | tf_op jit(solution)/shard_map/ppermute | solution.py:416
  162.6 12.1 %collective-permute-start.35 = (bf16[192,1024]{1,0:T(8,128)(2,1)S(1)}, bf16[192,1024]{1,0:T(8,128)(2,1)S(1)}, u32[]{:S(2)}, u32[]{:S(2)}) collective-permute-start(bf16[192,1024]{1,0:T(8,128)(2,1)S(1)} %pad_maximum_fusion.1), channel_id=1, source_target_pairs={{0,2},{1,3},{2,0},{3,1},{4,6},{5,7},{6,4},{7,5},{8,10},{9,11},{10,... | collective-permute-start | bytes 1179656 | tf_op jit(solution)/shard_map/ppermute | solution.py:416
  164.2 17.3 %collective-permute-start.36 = (bf16[192,1024]{1,0:T(8,128)(2,1)S(1)}, bf16[192,1024]{1,0:T(8,128)(2,1)S(1)}, u32[]{:S(2)}, u32[]{:S(2)}) collective-permute-start(bf16[192,1024]{1,0:T(8,128)(2,1)S(1)} %pad_maximum_fusion.1), channel_id=1, source_target_pairs={{0,4},{1,5},{2,6},{3,7},{4,0},{5,1},{6,2},{7,3},{8,12},{9,13},{10,... | collective-permute-start | bytes 1179656 | tf_op jit(solution)/shard_map/ppermute | solution.py:416
  165.7 17.5 %collective-permute-start.37 = (bf16[192,1024]{1,0:T(8,128)(2,1)S(1)}, bf16[192,1024]{1,0:T(8,128)(2,1)S(1)}, u32[]{:S(2)}, u32[]{:S(2)}) collective-permute-start(bf16[192,1024]{1,0:T(8,128)(2,1)S(1)} %pad_maximum_fusion.1), channel_id=1, source_target_pairs={{0,6},{1,7},{2,4},{3,5},{4,2},{5,3},{6,0},{7,1},{8,14},{9,15},{10,... | collective-permute-start | bytes 1179656 | tf_op jit(solution)/shard_map/ppermute | solution.py:416
  174.8 8.5 %collective-permute-start.19 = (bf16[48,512]{1,0:T(8,128)(2,1)S(1)}, bf16[48,512]{1,0:T(8,128)(2,1)S(1)}, u32[]{:S(2)}, u32[]{:S(2)}) collective-permute-start(bf16[48,512]{1,0:T(8,128)(2,1)S(1)} %get-tuple-element.146), channel_id=1, source_target_pairs={{0,16},{8,24},{16,0},{24,8},{1,17},{9,25},{17,1},{25,9},{2,18},{10... | collective-permute-start | bytes 147464 | tf_op jit(solution)/shard_map/ppermute | solution.py:416
  181.5 6.0 %collective-permute-start.20 = (bf16[48,512]{1,0:T(8,128)(2,1)S(1)}, bf16[48,512]{1,0:T(8,128)(2,1)S(1)}, u32[]{:S(2)}, u32[]{:S(2)}) collective-permute-start(bf16[48,512]{1,0:T(8,128)(2,1)S(1)} %get-tuple-element.146), channel_id=1, source_target_pairs={{0,24},{8,16},{16,8},{24,0},{1,25},{9,17},{17,9},{25,1},{2,26},{10... | collective-permute-start | bytes 147464 | tf_op jit(solution)/shard_map/ppermute | solution.py:416
  183.2 17.8 %copy-start.2 = (bf16[768,1024]{1,0:T(8,128)(2,1)}, bf16[768,1024]{1,0:T(8,128)(2,1)S(1)}, u32[]{:S(2)}) copy-start(bf16[768,1024]{1,0:T(8,128)(2,1)S(1)} %constant_dynamic-update-slice_fusion.7.mine) | copy-start | bytes 4718596
  183.2 42.0 %collective-permute-start.38 = (bf16[768,1024]{1,0:T(8,128)(2,1)S(1)}, bf16[768,1024]{1,0:T(8,128)(2,1)S(1)}, u32[]{:S(2)}, u32[]{:S(2)}) collective-permute-start(bf16[768,1024]{1,0:T(8,128)(2,1)S(1)} %constant_dynamic-update-slice_fusion.7.mine), channel_id=1, source_target_pairs={{0,1},{1,0},{2,3},{3,2},{4,5},{5,4},{6,7},{7,6},{8,9},{9,8},{10,11... | collective-permute-start | bytes 4718600 | tf_op jit(solution)/shard_map/ppermute | solution.py:416
  187.5 5.7 %collective-permute-start.21 = (bf16[192,512]{1,0:T(8,128)(2,1)S(1)}, bf16[192,512]{1,0:T(8,128)(2,1)S(1)}, u32[]{:S(2)}, u32[]{:S(2)}) collective-permute-start(bf16[192,512]{1,0:T(8,128)(2,1)S(1)} %pad_maximum_fusion.2), channel_id=1, source_target_pairs={{0,2},{1,3},{2,0},{3,1},{4,6},{5,7},{6,4},{7,5},{8,10},{9,11},{10,... | collective-permute-start | bytes 589832 | tf_op jit(solution)/shard_map/ppermute | solution.py:416
  189.0 6.8 %collective-permute-start.22 = (bf16[192,512]{1,0:T(8,128)(2,1)S(1)}, bf16[192,512]{1,0:T(8,128)(2,1)S(1)}, u32[]{:S(2)}, u32[]{:S(2)}) collective-permute-start(bf16[192,512]{1,0:T(8,128)(2,1)S(1)} %pad_maximum_fusion.2), channel_id=1, source_target_pairs={{0,4},{1,5},{2,6},{3,7},{4,0},{5,1},{6,2},{7,3},{8,12},{9,13},{10,... | collective-permute-start | bytes 589832 | tf_op jit(solution)/shard_map/ppermute | solution.py:416
  190.5 6.6 %collective-permute-start.23 = (bf16[192,512]{1,0:T(8,128)(2,1)S(1)}, bf16[192,512]{1,0:T(8,128)(2,1)S(1)}, u32[]{:S(2)}, u32[]{:S(2)}) collective-permute-start(bf16[192,512]{1,0:T(8,128)(2,1)S(1)} %pad_maximum_fusion.2), channel_id=1, source_target_pairs={{0,6},{1,7},{2,4},{3,5},{4,2},{5,3},{6,0},{7,1},{8,14},{9,15},{10,... | collective-permute-start | bytes 589832 | tf_op jit(solution)/shard_map/ppermute | solution.py:416
  197.1 22.4 %copy-start.6 = (bf16[768,512]{1,0:T(8,128)(2,1)}, bf16[768,512]{1,0:T(8,128)(2,1)S(1)}, u32[]{:S(2)}) copy-start(bf16[768,512]{1,0:T(8,128)(2,1)S(1)} %constant_dynamic-update-slice_fusion.mine) | copy-start | bytes 2359300
  197.1 22.4 %collective-permute-start.24 = (bf16[768,512]{1,0:T(8,128)(2,1)S(1)}, bf16[768,512]{1,0:T(8,128)(2,1)S(1)}, u32[]{:S(2)}, u32[]{:S(2)}) collective-permute-start(bf16[768,512]{1,0:T(8,128)(2,1)S(1)} %constant_dynamic-update-slice_fusion.mine), channel_id=1, source_target_pairs={{0,1},{1,0},{2,3},{3,2},{4,5},{5,4},{6,7},{7,6},{8,9},{9,8},{10,11... | collective-permute-start | bytes 2359304 | tf_op jit(solution)/shard_map/ppermute | solution.py:416
  197.2 1.1 copy-start.5
  200.9 9.3 %collective-permute-start.8 = (bf16[512,256]{1,0:T(8,128)(2,1)}, bf16[512,256]{1,0:T(8,128)(2,1)S(1)}, u32[]{:S(2)}, u32[]{:S(2)}) collective-permute-start(bf16[512,256]{1,0:T(8,128)(2,1)} %get-tuple-element.75), channel_id=1, source_target_pairs={{0,2},{1,3},{2,0},{3,1},{4,6},{5,7},{6,4},{7,5},{8,10},{9,11},{10,... | collective-permute-start | bytes 786440 | tf_op jit(solution)/shard_map/ppermute | solution.py:416
  201.6 8.7 %collective-permute-start.9 = (bf16[512,256]{1,0:T(8,128)(2,1)}, bf16[512,256]{1,0:T(8,128)(2,1)S(1)}, u32[]{:S(2)}, u32[]{:S(2)}) collective-permute-start(bf16[512,256]{1,0:T(8,128)(2,1)} %get-tuple-element.76), channel_id=1, source_target_pairs={{0,4},{1,5},{2,6},{3,7},{4,0},{5,1},{6,2},{7,3},{8,12},{9,13},{10,... | collective-permute-start | bytes 786440 | tf_op jit(solution)/shard_map/ppermute | solution.py:416
  202.7 13.3 %collective-permute-start.10 = (bf16[512,256]{1,0:T(8,128)(2,1)}, bf16[512,256]{1,0:T(8,128)(2,1)S(1)}, u32[]{:S(2)}, u32[]{:S(2)}) collective-permute-start(bf16[512,256]{1,0:T(8,128)(2,1)} %get-tuple-element.77), channel_id=1, source_target_pairs={{0,6},{1,7},{2,4},{3,5},{4,2},{5,3},{6,0},{7,1},{8,14},{9,15},{10,... | collective-permute-start | bytes 786440 | tf_op jit(solution)/shard_map/ppermute | solution.py:416
  210.3 5.7 %copy-start.21 = (bf16[512,256]{1,0:T(8,128)(2,1)}, bf16[512,256]{1,0:T(8,128)(2,1)S(1)}, u32[]{:S(2)}) copy-start(bf16[512,256]{1,0:T(8,128)(2,1)S(1)} %collective-permute-done.8.refs_1_) | copy-start | bytes 786436
  210.3 5.7 %copy-start.22 = (bf16[512,256]{1,0:T(8,128)(2,1)}, bf16[512,256]{1,0:T(8,128)(2,1)S(1)}, u32[]{:S(2)}) copy-start(bf16[512,256]{1,0:T(8,128)(2,1)S(1)} %collective-permute-done.9.refs_2_) | copy-start | bytes 786436
  219.5 0.9 copy-start.8
  225.2 1.1 copy-start.3
  (12 other events, 8.5 us)

commit v2 on v1

v2 whole, which is shorter than its diff:
```python
from functools import partial

import jax
import jax.numpy as jnp
from jax import lax
from jax.experimental import pallas as pl
from jax.experimental.pallas import tpu as pltpu
from jax.sharding import PartitionSpec as P

EPS = 1e-6
BIG = -(2.0**30)
LEFT, RIGHT, ONES = 17, 18, 19
SMALL = 16
VMEM = 24 * 1024 * 1024
MUCH = 56 * 1024 * 1024

f32, bf16, i32 = jnp.float32, jnp.bfloat16, jnp.int32


def thresholds(buckets, max_distance):
    half = buckets // 2
    exact = half // 2
    steps = half - exact
    out = list(range(1, exact))
    for j in range(steps):
        target = exact ** (steps - j) * max_distance**j
        m = exact
        while m**steps < target:
            m += 1
        out.append(m)
    return out


def bucket_of(offset, buckets):
    distance = jnp.abs(offset)
    bucket = (offset > 0).astype(i32) * (buckets // 2)
    for t in thresholds(buckets, 128):
        bucket = bucket + (distance >= t).astype(i32)
    return bucket


def nn(a, b):
    return lax.dot_general(a, b, (((1,), (0,)), ((), ())), preferred_element_type=f32)


def nt(a, b):
    return lax.dot_general(a, b, (((1,), (1,)), ((), ())), preferred_element_type=f32)


def tn(a, b):
    return lax.dot_general(a, b, (((0,), (0,)), ((), ())), preferred_element_type=f32)


def iota(shape, dim):
    return lax.broadcasted_iota(i32, shape, dim)


def rms(values, gain):
    scale = lax.rsqrt(jnp.mean(values * values, axis=-1, keepdims=True) + EPS)
    return values * scale * gain


def call(kernel, name, us, out_shape, smem_args, args, scratch=(), much=False):
    smem = pl.BlockSpec(memory_space=pltpu.SMEM)
    vmem = pl.BlockSpec(memory_space=pltpu.VMEM)
    return pl.pallas_call(
        kernel,
        in_specs=[smem] * len(smem_args) + [vmem] * len(args),
        out_specs=jax.tree.map(lambda _: vmem, out_shape),
        out_shape=out_shape,
        scratch_shapes=list(scratch),
        compiler_params=pltpu.CompilerParams(vmem_limit_bytes=MUCH if much else VMEM),
        cost_estimate=pl.CostEstimate(flops=int(us * 1e9), bytes_accessed=int(us * 2e6), transcendentals=0),
        name=name,
    )(*smem_args, *args)


def shape(*dims, dtype=bf16):
    return jax.ShapeDtypeStruct(dims, dtype)


def low_half(t):
    return iota((t, 128), 1) < 64


def turn(pair):
    return pltpu.roll(pair, 64, 1)


def prepare_kernel(ids, lens, x, gain, table, wq, wk, wv, q, ext, bands, wt, line):
    t = x.shape[0]
    buckets, heads = table.shape
    n1 = rms(x[...].astype(f32), gain[...].astype(f32)).astype(bf16)
    q[...] = nn(n1, wq[...]).astype(bf16)
    low, high = segment_bounds(lens)
    lanes = iota((t, 128), 1)
    pos = iota((t, 128), 0) + ids[0] * t
    other = jnp.where((pos >= low) & (pos < high), 0.0, BIG)
    ext[...] = jnp.where(lanes < LEFT, other, 0.0)
    u = iota((buckets, 4 * t), 1)
    bucket = bucket_of(jnp.where(u < 3 * t, u - t, u - 5 * t), buckets)
    pick = (bucket == iota((buckets, 4 * t), 0)).astype(f32).astype(bf16)
    line[...] = jnp.zeros_like(line)
    line[:heads] = tn(table[...], pick)
    for h in range(heads):
        band = pltpu.roll(jnp.broadcast_to(line[h : h + 1], (t, 4 * t)), 0, 1, stride=1, stride_axis=0)
        for r in range(3):
            bands[h, r] = band[:, r * t : (r + 1) * t].astype(bf16)
        bands[h, 3] = jnp.zeros((t, t), bf16)
    w = wq.shape[1]
    for k, ref in enumerate((wq, wk, wv)):
        wt[k * w : (k + 1) * w] = ref[...].astype(f32).T.astype(bf16)


def prepare(ids, lens, x, gain, table, wq, wk, wv):
    t, d = x.shape
    heads, w = table.shape[1], wq.shape[1]
    return call(
        prepare_kernel, "prepare", 4,
        [shape(t, w), shape(t, 128, dtype=f32), shape(heads, 4, t, t), shape(3 * w, d), shape(8, 4 * t, dtype=f32)],
        (ids, lens), (x, gain, table, wq, wk, wv),
    )


def segment_bounds(lens):
    lane = iota((1, 128), 1)
    low = jnp.where(lane == 0, -1, 2**30)
    high = jnp.full((1, 128), -1, i32)
    total = 0
    for k in range(lens.shape[0]):
        total = total + lens[k]
        high = jnp.where(lane == k, total, high)
        low = jnp.where(lane == k + 1, total, low)
    return low, jnp.where(lane == lens.shape[0], 2**30, high)


def attend_kernel(n, first, count, ids, lens, *refs):
    x = refs[:count]
    gain, wk, wv, q, ext, bands, line, n1, e, acc, stat = refs[count : count + 11]
    pairs = q.shape[1] // 128
    kv, p = refs[count + 11 : count + 11 + pairs], refs[count + 11 + pairs : -1]
    s = refs[-1]
    me = ids[0]
    t = x[0].shape[0]
    low, high = segment_bounds(lens)
    row = iota((t, 128), 0)
    lanes = iota((t, 128), 1)
    for i in range(count):
        at = slice(i * t, (i + 1) * t)
        n1[at] = rms(x[i][...].astype(f32), gain[...].astype(f32)).astype(bf16)
        block = me ^ (first + i)
        pos = row + block * t
        away = block - me
        flag = jnp.where(away <= -2, LEFT, jnp.where(away >= 2, RIGHT, ONES))
        here = ((pos >= low) & (pos < high)) | (lanes == flag) | (lanes == ONES)
        e[at] = here.astype(f32).astype(bf16)
    upper = iota((count * t, 128), 1) >= 64
    stats = jnp.zeros((t, 128), f32)
    for g in range(pairs):
        at = slice(g * 128, g * 128 + 128)
        both = nn(n1[...], jnp.concatenate([wk[:, at], wv[:, at]], axis=1))
        keys, values = both[:, :128], turn(both[:, 128:])
        kv[g][0] = jnp.where(upper, values, keys).astype(bf16)
        kv[g][1] = jnp.where(upper, keys, values).astype(bf16)
        q2 = q[:, at].astype(f32)
        sums = []
        for k in range(2):
            h = 2 * g + k
            lane_ext = jnp.where(lanes == LEFT, line[h : h + 1, 0:1],
                                 jnp.where(lanes == RIGHT, line[h : h + 1, 3 * t - 1 : 3 * t], ext[...]))
            qh = jnp.where(low_half(t) == (k == 0), q2, 0.0)
            qa = jnp.concatenate([qh, lane_ext], axis=1).astype(bf16)
            right = jnp.concatenate([kv[g][k], e[...]], axis=1)
            s[...] = nt(qa, right)
            for r in (-1, 0, 1):
                there = me + r
                slot = (me ^ there) - first
                inside = (there >= 0) & (there < n) & (slot >= 0) & (slot < count)
                if r == 0 and first > 0:
                    continue
                where = pl.ds(pl.multiple_of(jnp.where(inside, slot, 0) * t, t), t)
                s[:, where] = s[:, where] + bands[h, jnp.where(inside, r + 1, 3)].astype(f32)
            top = s[:, :128]
            for i in range(1, count * t // 128):
                top = jnp.maximum(top, s[:, i * 128 : (i + 1) * 128])
            top = jnp.max(top, axis=1, keepdims=True)
            raised = jnp.exp(s[...] - top).astype(bf16)
            p[g][k] = raised
            out = nn(raised, right)
            sums.append(out[:, :128])
            stats = jnp.where(lanes == h, top, stats)
            stats = jnp.where(lanes == 8 + h, out[:, 128 + ONES : 129 + ONES], stats)
        acc[:, at] = turn(jnp.where(low_half(t), sums[1], sums[0]))
    stat[...] = stats


def attend(n, first, ids, lens, blocks, gain, wk, wv, q, ext, bands, line):
    count = len(blocks)
    t, d = blocks[0].shape
    pairs = wk.shape[1] // 128
    c = count * t
    out = call(
        partial(attend_kernel, n, first, count), "attend", 2 * count,
        [shape(c, d), shape(c, 128), shape(t, wk.shape[1], dtype=f32), shape(t, 128, dtype=f32)]
        + [shape(2, c, 128)] * pairs + [shape(2, t, c)] * pairs,
        (ids, lens), (*blocks, gain, wk, wv, q, ext, bands, line), scratch=[pltpu.VMEM((t, c), f32)], much=n > 8,
    )
    return dict(n1=out[0], e=out[1], acc=out[2], stat=out[3], kv=out[4 : 4 + pairs], p=out[4 + pairs :])


def feed_forward_kernel(phases, ids, lens, gain, x, wo, wg, wu, wd, cot, *refs):
    accs, stats = refs[:phases], refs[phases : 2 * phases]
    out, dh, do, scale, gwo, keep, send, gn, o, grads = refs[2 * phases :]
    t, d = x.shape
    pairs = wo.shape[0] // 128
    lanes = iota((t, 128), 1)
    scales = jnp.zeros((t, 128), f32)
    for g in range(pairs):
        at = slice(g * 128, g * 128 + 128)
        factors = []
        for h in (2 * g, 2 * g + 1):
            tops = [ref[:, h : h + 1] for ref in stats]
            top = tops[0]
            for other in tops[1:]:
                top = jnp.maximum(top, other)
            weights = [jnp.exp(v - top) for v in tops]
            total = weights[0] * stats[0][:, 8 + h : 9 + h]
            for w, ref in zip(weights[1:], stats[1:], strict=True):
                total = total + w * ref[:, 8 + h : 9 + h]
            weights = [w / total for w in weights]
            for i, w in enumerate(weights):
                scales = jnp.where(lanes == 8 * i + h, w, scales)
            factors.append(weights)
        value = jnp.zeros((t, 128), f32)
        for i in range(phases):
            value = value + accs[i][:, at] * jnp.where(lanes < 64, factors[0][i], factors[1][i])
        o[:, at] = value
    mixed = o[...].astype(bf16)
    h1 = x[...].astype(f32) + nn(mixed, wo[...])
    g2 = gain[...].astype(f32)
    s2 = lax.rsqrt(jnp.mean(h1 * h1, axis=-1, keepdims=True) + EPS)
    hat = h1 * s2
    n2 = (hat * g2).astype(bf16)
    gate = nn(n2, wg[...])
    up = nn(n2, wu[...])
    c0 = 0.7978845608028654
    square = gate * gate
    th = jnp.tanh(c0 * gate * (1.0 + 0.044715 * square))
    half = 0.5 * (1.0 + th)
    act = gate * half
    dact = half + 0.5 * gate * (1.0 - th * th) * (c0 * (1.0 + 3 * 0.044715 * square))
    u = (act * up).astype(bf16)
    out[...] = (h1 + nn(u, wd[...])).astype(bf16)
    total = lens[0]
    for k in range(1, lens.shape[0]):
        total = total + lens[k]
    pos = ids[0] * t + iota((t, 1), 0)
    g = cot[...].astype(f32) * (pos < total).astype(f32)
    gb = g.astype(bf16)
    down = tn(u, gb).astype(bf16)
    grads[2 * d : 3 * d, :d] = down[:d]
    grads[2 * d : 3 * d, d:] = down[d:]
    du = nt(gb, wd[...]).astype(bf16).astype(f32)
    dgate = (du * up * dact).astype(bf16)
    dup = (du * act).astype(bf16)
    grads[0:d] = tn(n2, dgate).astype(bf16)
    grads[d : 2 * d] = tn(n2, dup).astype(bf16)
    rows = keep.shape[0]
    core = ids[1]
    keep[...] = grads[pl.ds(pl.multiple_of(core * rows, 16), rows)]
    send[...] = grads[pl.ds(pl.multiple_of((1 - core) * rows, 16), rows)]
    dn2 = nt(dgate, wg[...]) + nt(dup, wu[...])
    gn[...] = jnp.sum(dn2 * hat, axis=0, keepdims=True)
    scaled = dn2 * g2
    dh1 = g + s2 * (scaled - hat * jnp.mean(hat * scaled, axis=-1, keepdims=True))
    dh[...] = dh1
    dhb = dh1.astype(bf16)
    gwo[...] = tn(mixed, dhb).astype(bf16)
    dmix = nt(dhb, wo[...]).astype(bf16)
    do[...] = dmix
    product = dmix.astype(f32) * o[...]
    for h in range(2 * pairs):
        part = product[:, h // 2 * 128 : h // 2 * 128 + 128]
        delta = jnp.sum(jnp.where(low_half(t) == (h % 2 == 0), part, 0.0), axis=1, keepdims=True)
        scales = jnp.where(lanes == 64 + h, delta, scales)
    scale[...] = scales


def feed_forward(ids, lens, gain, x, wo, wg, wu, wd, cot, parts):
    t, d = x.shape
    ff, w = wg.shape[1], wo.shape[0]
    half = 3 * d // 2
    return call(
        partial(feed_forward_kernel, len(parts)), "feed_forward", 8,
        [shape(t, d), shape(t, d, dtype=f32), shape(t, w), shape(t, 128, dtype=f32), shape(w, d),
         shape(half, ff), shape(half, ff), shape(1, d, dtype=f32)],
        (ids, lens), (gain, x, wo, wg, wu, wd, cot, *[v["acc"] for v in parts], *[v["stat"] for v in parts]),
        scratch=[pltpu.VMEM((t, w), f32), pltpu.VMEM((3 * d, ff), bf16)],
    )


def attend_back_kernel(n, g, counts, ids, q, do, scale, *refs):
    phases = len(counts)
    p, kv, e = (refs[k * phases : (k + 1) * phases] for k in range(3))
    dk, dv = (refs[k * phases : (k + 1) * phases] for k in (3, 4))
    dq, line, ds, stack = refs[5 * phases :]
    me = ids[0]
    t = q.shape[0]
    lower = low_half(t)
    at = slice(g * 128, g * 128 + 128)
    q2 = q[:, at].astype(f32)
    do2 = turn(do[:, at].astype(f32))
    back = (iota((t, t), 0) + iota((t, t), 1) == t - 1).astype(f32).astype(bf16)
    lane = iota((1, 128), 1)
    line[...] = jnp.zeros_like(line)
    sums = []
    for k in range(2):
        h = 2 * g + k
        qh = jnp.where(lower == (k == 0), q2, 0.0)
        doh = jnp.where(lower == (k == 1), do2, 0.0)
        acc = jnp.zeros((t, 256), f32)
        start = 0
        for i, count in enumerate(counts):
            c = count * t
            cols = slice(start, start + c)
            factor = scale[:, 8 * i + h : 8 * i + h + 1]
            scaled = doh * factor
            low = scaled.astype(bf16)
            keys = kv[i][k]
            probs = p[i][k]
            d_score = (probs.astype(f32) * (nt(low, keys) - scale[:, 64 + h : 65 + h] * factor)).astype(bf16)
            ds[:, cols] = d_score
            stack[:t, :c] = d_score
            stack[t:, :c] = probs
            acc = acc + nn(d_score, jnp.concatenate([keys, e[i][...]], axis=1))
            lhs = jnp.concatenate([qh.T, scaled.T], axis=1).astype(bf16)
            both = nn(lhs, stack[:, :c]).astype(bf16)
            mine, other = (both[:64], both[64:]) if k == 0 else (both[64:], both[:64])
            dk[i][k * 64 : k * 64 + 64] = mine
            dv[i][k * 64 : k * 64 + 64] = other
            start += c
        sums.append(acc[:, :128])
        parts = []
        for r in (-1, 0, 1):
            there = me + r
            inside = (there >= 0) & (there < n)
            slot = jnp.where(inside, me ^ there, 0)
            block = ds[:, pl.ds(pl.multiple_of(slot * t, t), t)]
            parts.append(nn(back, block) * inside.astype(f32))
        parts.append(jnp.zeros((t, t), f32))
        band = pltpu.roll(jnp.concatenate(parts, axis=1), 0, 1, stride=1, stride_axis=0)
        line[k : k + 1, : 4 * t] = jnp.sum(band, axis=0, keepdims=True)
        ends = jnp.sum(acc[:, 128:], axis=0, keepdims=True)
        line[k : k + 1, 4 * t :] = jnp.where((lane == LEFT) | (lane == RIGHT), ends, 0.0)
    dq[...] = jnp.where(lower, sums[0], sums[1]).astype(bf16)


def attend_back(n, g, ids, q, do, scale, parts):
    t = q.shape[0]
    widths = [v["e"].shape[0] for v in parts]
    s = sum(widths)
    phases = len(parts)
    out = call(
        partial(attend_back_kernel, n, g, [w // t for w in widths]), "attend_back", 4,
        [shape(128, w) for w in widths] * 2 + [shape(t, 128), shape(8, 4 * t + 128, dtype=f32)],
        (ids,), (q, do, scale, *[v["p"][g] for v in parts], *[v["kv"][g] for v in parts], *[v["e"] for v in parts]),
        scratch=[pltpu.VMEM((t, s), bf16), pltpu.VMEM((2 * t, max(widths)), bf16)], much=n > 8,
    )
    return dict(dk=out[:phases], dv=out[phases : 2 * phases], dq=out[-2], line=out[-1])


def gather_back_kernel(n, buckets, counts, pairs, ids, gain, gn, gwo, wq, wk, wv, wt, *refs):
    phases = len(counts)
    n1 = refs[:phases]
    dk = [refs[phases + 2 * i * pairs :][:pairs] for i in range(phases)]
    dv = [refs[phases + (2 * i + 1) * pairs :][:pairs] for i in range(phases)]
    refs = refs[phases + 2 * phases * pairs :]
    dq, lines = refs[:pairs], refs[pairs : 2 * pairs]
    even, odd, dn1q, keep, send, grads, sums, diagonal = refs[2 * pairs :]
    d, w = wq.shape
    t = dn1q.shape[0]
    weights = jnp.concatenate([wk[...], wv[...]], axis=1)
    total = jnp.zeros((2 * w, d), f32)
    slot = 0
    for i, count in enumerate(counts):
        both = jnp.concatenate([ref[...] for ref in (*dk[i], *dv[i])], axis=0)
        total = total + nn(both, n1[i][...])
        back = nn(weights, both).astype(bf16)
        for _ in range(count):
            ref = odd if slot % 2 else even
            ref[slot // 2] = back[:, (slot * t - sum(counts[:i]) * t) :][:, :t]
            slot += 1
    dq_all = jnp.concatenate([ref[...] for ref in dq], axis=1)
    from_q = tn(dq_all, n1[0][:t])
    dn1q[...] = nt(dq_all, wq[...])
    grads[:w] = from_q.astype(bf16)
    grads[w : 3 * w] = total.astype(bf16)
    grads[3 * w :] = gwo[...]
    gains = jnp.sum(from_q * wt[:w].astype(f32), axis=0, keepdims=True)
    gains = gains + jnp.sum(total * wt[w:].astype(f32), axis=0, keepdims=True)
    sums[...] = jnp.zeros_like(sums)
    sums[0:1] = gains / gain[...].astype(f32)
    sums[1:2] = gn[...]
    diagonal[...] = jnp.zeros_like(diagonal)
    for g in range(pairs):
        diagonal[2 * g : 2 * g + 2] = lines[g][:2]
    width = diagonal.shape[1]
    u = iota((width, 128), 0)
    bucket = bucket_of(u - (2 * t - 1), buckets)
    bucket = jnp.where(u == 4 * t + LEFT, buckets // 2 - 1, jnp.where(u == 4 * t + RIGHT, buckets - 1, bucket))
    pick = (bucket == iota((width, 128), 1)).astype(f32)
    sums[8:16, :128] = lax.dot_general(diagonal[...], pick, (((1,), (0,)), ((), ())),
                                       precision=lax.Precision.HIGHEST, preferred_element_type=f32)
    small = sums[...].astype(bf16)
    rows = 2 * w
    keep[:rows] = grads[pl.ds(pl.multiple_of(ids[1] * rows, 16), rows)]
    send[:rows] = grads[pl.ds(pl.multiple_of((1 - ids[1]) * rows, 16), rows)]
    keep[rows:] = small
    send[rows:] = small


def gather_back(n, buckets, ids, gain, gn, gwo, wq, wk, wv, wt, parts, backs):
    d, w = wq.shape
    t = backs[0]["dq"].shape[0]
    pairs = w // 128
    counts = [v["e"].shape[0] // t for v in parts]
    pieces = []
    for i in range(len(parts)):
        pieces += [v["dk"][i] for v in backs] + [v["dv"][i] for v in backs]
    half = 2 * w + SMALL
    return call(
        partial(gather_back_kernel, n, buckets, counts, pairs), "gather_back", 6,
        [shape(n // 2, d, t), shape(n // 2, d, t), shape(t, d, dtype=f32), shape(half, d), shape(half, d)],
        (ids,), (gain, gn, gwo, wq, wk, wv, wt, *[v["n1"] for v in parts], *pieces, *[v["dq"] for v in backs],
                 *[v["line"] for v in backs]),
        scratch=[pltpu.VMEM((4 * w, d), bf16), pltpu.VMEM((SMALL, d), f32), pltpu.VMEM((8, 4 * t + 128), f32)], much=n > 8,
    )


def split_kernel(which, count, extra, ids, *refs):
    inputs, outs = refs[:-count], refs[-count:]
    rows = (inputs[0].shape[0] - extra) // count
    own = ids[which]
    for j in range(count):
        at = pl.ds(pl.multiple_of((own ^ j) * rows, 16), rows)
        total = inputs[0][at].astype(f32)
        for ref in inputs[1:]:
            total = total + ref[at].astype(f32)
        outs[j][:rows] = total.astype(bf16)
    if extra:
        at = pl.ds(rows * count, extra)
        total = inputs[0][at].astype(f32)
        for ref in inputs[1:]:
            total = total + ref[at].astype(f32)
        for j in range(count):
            outs[j][rows:] = total.astype(bf16)


def add_and_split(which, count, extra, ids, *arrays):
    rows = (arrays[0].shape[0] - extra) // count + extra
    out = shape(rows, arrays[0].shape[1])
    return call(partial(split_kernel, which, count, extra), "add_parts", 1, [out] * count, (ids,), arrays)


def swap(array, axis, j):
    size = lax.axis_size(axis)
    return lax.ppermute(array, axis, [(i, i ^ j) for i in range(size)])


def reduce_start(ids, keep, send, extra):
    chips, rows = lax.axis_size("seq") // 2, lax.axis_size("rows")
    recv = swap(send, "seq", 1)
    if (keep.shape[0] - extra) % (64 * chips) or rows != 4:
        return add_and_split(0, 1, extra, ids * 0, keep, recv)
    return add_and_split(2, chips, extra, ids, keep, recv)


def reduce_finish(ids, parts, extra):
    chips, rows = lax.axis_size("seq") // 2, lax.axis_size("rows")
    if len(parts) == 1:
        both = parts[0].astype(f32)
        size = both.shape[0] - extra
        placed = jnp.zeros((2 * size, both.shape[1]), f32)
        placed = lax.dynamic_update_slice_in_dim(placed, both[:size], ids[1] * size, 0)
        full, tail = lax.psum((placed, both[size:] * 0.5), ("rows", "seq"))
        mine = lax.dynamic_slice_in_dim(full, ids[1] * size, size, 0)
        other = lax.dynamic_slice_in_dim(full, (1 - ids[1]) * size, size, 0)
        return [mine.astype(bf16)], [other.astype(bf16)], tail.astype(bf16)
    parts = [parts[0]] + [swap(parts[j], "seq", 2 * j) for j in range(1, chips)]
    near = ids[3:4] % 2
    mine, other = add_and_split(0, 2, extra, near, *parts)
    mine = add_and_split(0, 1, extra, near * 0, mine, swap(other, "rows", 1))[0]
    mine = add_and_split(0, 1, extra, near * 0, mine, swap(mine, "rows", 2))[0]
    size = mine.shape[0] - extra
    line = jnp.concatenate([mine[:size], swap(mine[:size], "rows", 1)], axis=0)
    own = [line] + [swap(line, "seq", 2 * j) for j in range(1, chips)]
    return own, [swap(v, "seq", 1) for v in own], mine[size:]


def place_halves(ids, mine, other, full):
    size = full.shape[0] // 2
    if len(mine) == 1:
        full[pl.ds(pl.multiple_of(ids[1] * size, 16), size)] = mine[0][...]
        full[pl.ds(pl.multiple_of((1 - ids[1]) * size, 16), size)] = other[0][...]
        return
    piece = size // len(mine)
    for c, refs in ((ids[1], mine), (1 - ids[1], other)):
        for a, ref in enumerate(refs):
            at = c * size + (ids[2] ^ a) * piece
            for b in range(2):
                where = at + ((ids[3] % 2) ^ b) * (piece // 2)
                full[pl.ds(pl.multiple_of(where, 16), piece // 2)] = ref[b * (piece // 2) : (b + 1) * (piece // 2)]


def unpack_ffn_kernel(pieces, ids, *refs):
    gate, up, down, full = refs[2 * pieces :]
    place_halves(ids, refs[:pieces], refs[pieces : 2 * pieces], full)
    d = gate.shape[0]
    gate[...] = full[:d].astype(f32)
    up[...] = full[d : 2 * d].astype(f32)
    down[:d] = full[2 * d :, :d].astype(f32)
    down[d:] = full[2 * d :, d:].astype(f32)


def unpack_attention_kernel(pieces, heads, ids, tail, *refs):
    gq, gk, gv, go, g1, g2, gb, full = refs[2 * pieces :]
    place_halves(ids, refs[:pieces], refs[pieces : 2 * pieces], full)
    w = gq.shape[1]
    for k, ref in enumerate((gq, gk, gv)):
        ref[...] = full[k * w : (k + 1) * w].astype(f32).T
    go[...] = full[3 * w :].astype(f32)
    small = tail[...].astype(f32)
    g1[...] = small[0:1]
    g2[...] = small[1:2]
    gb[...] = small[8:16, :128].T[: gb.shape[0], :heads]


def input_grad_kernel(ids, *refs):
    *parts, dn1q, x, dh, gain, out = refs
    total = parts[0][...].astype(f32)
    for ref in parts[1:]:
        total = total + ref[...].astype(f32)
    dn1 = total.T + dn1q[...]
    value = x[...].astype(f32)
    s1 = lax.rsqrt(jnp.mean(value * value, axis=-1, keepdims=True) + EPS)
    hat = value * s1
    scaled = dn1 * gain[...].astype(f32)
    out[...] = dh[...] + s1 * (scaled - hat * jnp.mean(hat * scaled, axis=-1, keepdims=True))


def slots_kernel(count, ids, mine, other, *outs):
    for j in range(count):
        outs[j][...] = (mine[j].astype(f32) + other[j].astype(f32)).astype(bf16)


def shards(
    tokens, norm_attn, query_weight, key_weight, value_weight, out_weight, bucket_bias_table, norm_ffn,
    gate_weight, expansion_matrix, down_weight, lengths, cotangent,
):
    _, t, d = tokens.shape
    n = lax.axis_size("seq")
    buckets, heads = bucket_bias_table.shape
    width = query_weight.shape[1]
    ff = gate_weight.shape[1]
    seq = lax.axis_index("seq")
    ids = jnp.stack([seq, seq % 2, seq // 2, lax.axis_index("rows")]).astype(i32)
    x = tokens.reshape(t, d)
    cot = cotangent.reshape(t, d)
    lens = lengths.reshape(-1)
    gain1 = norm_attn.reshape(1, d)
    gain2 = norm_ffn.reshape(1, d)

    blocks = [None] * n
    blocks[0] = x
    for j in range(n - 2, 0, -2):
        blocks[j] = swap(x, "seq", j)
    for j in range(0, n, 2):
        blocks[j + 1] = swap(blocks[j], "seq", 1)

    q, ext, bands, wt, line = prepare(ids, lens, x, gain1, bucket_bias_table, query_weight, key_weight, value_weight)
    cuts = [0, 2, 6, 8] if n == 8 else [0, 2, *range(8, n, 8), n]
    parts = [
        attend(n, a, ids, lens, blocks[a:b], gain1, key_weight, value_weight, q, ext, bands, line)
        for a, b in zip(cuts[:-1], cuts[1:], strict=True)
    ]
    output, dh, do, scale, gwo, keep, send, gn = feed_forward(
        ids, lens, gain2, x, out_weight, gate_weight, expansion_matrix, down_weight, cot, parts
    )
    ffn = reduce_start(ids, keep, send, 0)
    backs = [attend_back(n, 0, ids, q, do, scale, parts)]
    (*ffn, do, scale) = lax.optimization_barrier((*ffn, do, scale))
    backs += [attend_back(n, g, ids, q, do, scale, parts) for g in range(1, width // 128)]
    even, odd, dn1q, keep, send = gather_back(
        n, buckets, ids, gain1, gn, gwo, query_weight, key_weight, value_weight, wt, parts, backs
    )
    attention = reduce_start(ids, keep, send, SMALL)
    recv = swap(odd, "seq", 1)
    half = n // 2
    slots = call(partial(slots_kernel, half), "add_slots", 1, [shape(d, t)] * half, (ids,), (even, recv))
    slots = [slots[0]] + [swap(slots[j], "seq", 2 * j) for j in range(1, half)]
    grad_tokens = call(input_grad_kernel, "input_grad", 2, shape(t, d, dtype=f32), (ids,),
                       (*slots, dn1q, x, dh, gain1))

    mine, other, _ = reduce_finish(ids, ffn, 0)
    gate, up, down = call(
        partial(unpack_ffn_kernel, len(mine)), "unpack_ffn", 4,
        [shape(d, ff, dtype=f32), shape(d, ff, dtype=f32), shape(ff, d, dtype=f32)],
        (ids,), (*mine, *other), scratch=[pltpu.VMEM((3 * d, ff), bf16)],
    )
    mine, other, tail = reduce_finish(ids, attention, SMALL)
    gq, gk, gv, go, g1, g2, gb = call(
        partial(unpack_attention_kernel, len(mine), heads), "unpack_attention", 3,
        [shape(d, width, dtype=f32)] * 3 + [shape(width, d, dtype=f32)] + [shape(1, d, dtype=f32)] * 2
        + [shape(buckets, heads, dtype=f32)],
        (ids,), (tail, *mine, *other), scratch=[pltpu.VMEM((4 * width, d), bf16)],
    )
    return (
        output.reshape(tokens.shape), grad_tokens.reshape(tokens.shape), g1.reshape(d), gq, gk, gv, go, gb,
        g2.reshape(d), gate, up, down,
    )


def solution(mesh):
    split = P("rows", "seq", None)
    in_specs = (split,) + (P(),) * 10 + (P("rows", None), split)
    out_specs = (split, split) + (P(),) * 10
    return jax.shard_map(shards, mesh=mesh, in_specs=in_specs, out_specs=out_specs, check_vma=False)
```

time: 232 us -> 146 us (0.63)
  waiting for transfers between devices: 86 us -> 54.2 us
  Pallas kernels: 78.3 us -> 48.2 us
  local copies, waits for them, and re-layouts: 20.6 us -> 7.46 us
  starting transfers between devices: 41.1 us -> 34.8 us
  other arithmetic: 4.18 us -> 0.12 us
    ppermute x39, waiting for transfers between devices: 86 us -> 54.2 us  [swap(): return lax.ppermute(array, axis, [(i, i ^ j) for i in range(size)])]
    pallas_call x13 -> x21, Pallas kernels: 78.3 us -> 48.2 us  [call(): pl.pallas_call(kernel, in_specs=[smem] * len(smem_args) + [vmem] * len(ar...]
    unnamed x89 -> x30, local copies, waits for them, and re-layouts: 13.2 us -> 6.08 us
    ppermute x39, starting transfers between devices: 41.1 us -> 34.8 us  [swap(): return lax.ppermute(array, axis, [(i, i ^ j) for i in range(size)])]
    reshape x2 -> x0, other arithmetic: 2.51 us -> none  [the longest x1 1.26 us: shards(): gain2 = norm_ffn.astype(f32).reshape(1, d)]
  transfers between devices with their start and end apart: 39 -> 39, of which waited for: 15 -> 16; matrix products, arithmetic and copies ran while one was open for 7% -> 2% of each run, Pallas kernels for 22% -> 13%
where the time goes in v2:
time: 146 us
  waiting for transfers between devices  54.2 us (37%)
  Pallas kernels  48.2 us (33%)
  starting transfers between devices  34.8 us (24%)
  local copies, waits for them, and re-layouts  7.46 us (5%)
    ppermute x39, waiting for transfers between devices, swap(): return lax.ppermute(array, axis, [(i, i ^ j) for i in range(size)])  54.2 us
    pallas_call x21, Pallas kernels, call(): pl.pallas_call(kernel, in_specs=[smem] * len(smem_args) + [vmem] * len(ar...  48.2 us
    ppermute x39, starting transfers between devices, swap(): return lax.ppermute(array, axis, [(i, i ^ j) for i in range(size)])  34.8 us
    unnamed x30, local copies, waits for them, and re-layouts  6.08 us
  transfers between devices with their start and end apart: 39, of which 16 were waited for; matrix products, arithmetic and copies ran while one was open for 2% of the time, Pallas kernels for 13%

profile of v2, /device:TPU:0, one launch (start us, length us, event | category | flops | bytes accessed | tf_op | source)
XLA Modules:
  0.0 145.7 jit_solution(2595926090822716574)
XLA Ops:
  0.6 4.0 %collective-permute-start.5 = (bf16[256,512]{1,0:T(8,128)(2,1)}, bf16[256,512]{1,0:T(8,128)(2,1)S(1)}, u32[]{:S(2)}, u32[]{:S(2)}) collective-permute-start(bf16[256,512]{1,0:T(8,128)(2,1)} %bitcast.12), channel_id=1, source_target_pairs={{0,6},{1,7},{2,4},{3,5},{4,2},{5,3},{6,0},{7,1},{8,14},{9,15},{10,... | collective-permute-start | bytes 786440 | tf_op jit(solution)/shard_map/ppermute | solution.py:467
  4.6 0.5 collective-permute-start.3
  5.3 0.7 reshape.57.gain.refs_2_.refs_4_.refs_7_
  5.9 0.7 reshape.54.gain
  6.6 0.8 copy.25.table
  7.5 1.0 copy-done.4
  8.5 1.0 copy-done.6
  9.5 1.0 copy-done.8
  10.5 0.9 copy-done.11
  11.4 0.7 copy-done.13
  12.1 1.8 %prepare.1 = (bf16[256,384]{1,0:T(8,128)(2,1)S(1)}, f32[256,128]{1,0:T(8,128)S(1)}, bf16[6,4,256,256]{3,2,1,0:T(8,128)(2,1)S(1)}, bf16[1152,512]{1,0:T(8,128)(2,1)S(1)}, f32[8,1024]{1,0:T(8,128)S(1)}) custom-call(s32[4]{0:T(128)S(1)} %pad_add_fusion.ids, s32[16]{0:T(128)S(1)} %bitcast.20, bf16[256,512]{1,0:T(8,128)(2,1)S(1)} %bitcast.16, ...), custom_call_target="tpu_custom_call" | custom-call | flops 4000000000 | bytes 8000000 | tf_op jit(solution)/shard_map/prepare/pallas_call | solution.py:66
  13.9 0.6 collective-permute-start.6
  14.5 2.3 %collective-permute-done.3.refs_2_ = bf16[256,512]{1,0:T(8,128)(2,1)S(1)} collective-permute-done((bf16[256,512]{1,0:T(8,128)(2,1)}, bf16[256,512]{1,0:T(8,128)(2,1)S(1)}, u32[]{:S(2)}, u32[]{:S(2)}) %collective-permute-start.3) | collective-permute-done | bytes 262176 | tf_op jit(solution)/shard_map/ppermute | solution.py:467
  17.3 4.1 %attend.3 = (bf16[512,512]{1,0:T(8,128)(2,1)S(1)}, bf16[512,128]{1,0:T(8,128)(2,1)S(1)}, f32[256,384]{1,0:T(8,128)S(1)}, f32[256,128]{1,0:T(8,128)S(1)}, bf16[2,...) custom-call(s32[4]{0:T(128)S(1)} %pad_add_fusion.ids, ...), custom_call_target="tpu_custom_call" | custom-call | flops 4000000000 | bytes 8000000 | tf_op jit(solution)/shard_map/attend/pallas_call | solution.py:66
  21.4 4.0 %attend.5 = (bf16[512,512]{1,0:T(8,128)(2,1)S(1)}, bf16[512,128]{1,0:T(8,128)(2,1)S(1)}, f32[256,384]{1,0:T(8,128)S(1)}, f32[256,128]{1,0:T(8,128)S(1)}, bf16[2,...) custom-call(s32[4]{0:T(128)S(1)} %pad_add_fusion.ids, ...), custom_call_target="tpu_custom_call" | custom-call | flops 4000000000 | bytes 8000000 | tf_op jit(solution)/shard_map/attend/pallas_call | solution.py:66
  25.5 6.1 %attend.4 = (bf16[1024,512]{1,0:T(8,128)(2,1)S(1)}, bf16[1024,128]{1,0:T(8,128)(2,1)S(1)}, f32[256,384]{1,0:T(8,128)S(1)}, f32[256,128]{1,0:T(8,128)S(1)}, bf16[...) custom-call(s32[4]{0:T(128)S(1)} %pad_add_fusion.ids, ...), custom_call_target="tpu_custom_call" | custom-call | flops 8000000000 | bytes 16000000 | tf_op jit(solution)/shard_map/attend/pallas_call | solution.py:66
  31.6 6.2 %feed_forward.1 = (bf16[256,512]{1,0:T(8,128)(2,1)}, f32[256,512]{1,0:T(8,128)S(1)}, bf16[256,384]{1,0:T(8,128)(2,1)S(1)}, f32[256,128]{1,0:T(8,128)S(1)}, bf16[...) custom-call(s32[4]{0:T(128)S(1)} %pad_add_fusion.ids, ...), custom_call_target="tpu_custom_call" | custom-call | flops 8000000000 | bytes 16000000 | tf_op jit(solution)/shard_map/feed_forward/pallas_call | solution.py:66
  38.1 3.4 %attend_back.3 = (bf16[128,512]{1,0:T(8,128)(2,1)S(1)}, bf16[128,1024]{1,0:T(8,128)(2,1)S(1)}, bf16[128,512]{1,0:T(8,128)(2,1)S(1)}, bf16[128,512]{1,0:T(8,128)(...) custom-call(s32[4]{0:T(128)S(1)} %pad_add_fusion.ids, ...), custom_call_target="tpu_custom_call" | custom-call | flops 4000000000 | bytes 8000000 | tf_op jit(solution)/shard_map/attend_back/pallas_call | solution.py:66
  41.6 0.9 add_parts.8
  42.5 3.4 %attend_back.5 = (bf16[128,512]{1,0:T(8,128)(2,1)S(1)}, bf16[128,1024]{1,0:T(8,128)(2,1)S(1)}, bf16[128,512]{1,0:T(8,128)(2,1)S(1)}, bf16[128,512]{1,0:T(8,128)(...) custom-call(s32[4]{0:T(128)S(1)} %pad_add_fusion.ids, ...), custom_call_target="tpu_custom_call" | custom-call | flops 4000000000 | bytes 8000000 | tf_op jit(solution)/shard_map/attend_back/pallas_call | solution.py:66
  45.9 3.7 %attend_back.4 = (bf16[128,512]{1,0:T(8,128)(2,1)S(1)}, bf16[128,1024]{1,0:T(8,128)(2,1)S(1)}, bf16[128,512]{1,0:T(8,128)(2,1)S(1)}, bf16[128,512]{1,0:T(8,128)(...) custom-call(s32[4]{0:T(128)S(1)} %pad_add_fusion.ids, ...), custom_call_target="tpu_custom_call" | custom-call | flops 4000000000 | bytes 8000000 | tf_op jit(solution)/shard_map/attend_back/pallas_call | solution.py:66
  49.6 4.7 %gather_back.1 = (bf16[4,512,256]{2,1,0:T(8,128)(2,1)S(1)}, bf16[4,512,256]{2,1,0:T(8,128)(2,1)S(1)}, f32[256,512]{1,0:T(8,128)S(1)}, bf16[784,512]{1,0:T(8,128)(2,1)S(1)}, bf16[784,512]{1,0:T(8,128)(2,1)S(1)}) custom-call(s32[4]{0:T(128)S(1)} %pad_add_fusion.ids, bf16[1,512]{1,0:T(2,128)(2,1)S(1)} %reshape.57.gain.refs_2_.refs_4_.refs_7_, ...), custom_call_target="tpu_custom_call" | custom-call | flops 6000000000 | bytes 12000000 | tf_op jit(solution)/shard_map/gather_back/pallas_call | solution.py:66
  54.5 1.7 %collective-permute-start.26 = (bf16[192,1024]{1,0:T(8,128)(2,1)S(1)}, bf16[192,1024]{1,0:T(8,128)(2,1)S(1)}, u32[]{:S(2)}, u32[]{:S(2)}) collective-permute-start(bf16[192,1024]{1,0:T(8,128)(2,1)S(1)} %get-tuple-element.212), channel_id=1, source_target_pairs={{0,2},{1,3},{2,0},{3,1},{4,6},{5,7},{6,4},{7,5},{8,10},{9,11},{10,... | collective-permute-start | bytes 1179656 | tf_op jit(solution)/shard_map/ppermute | solution.py:467
  56.2 0.7 collective-permute-start.27
  56.9 1.1 collective-permute-start.28
  58.0 8.4 %collective-permute-done.26.refs_1_ = bf16[192,1024]{1,0:T(8,128)(2,1)S(1)} collective-permute-done((bf16[192,1024]{1,0:T(8,128)(2,1)S(1)}, bf16[192,1024]{1,0:T(8,128)(2,1)S(1)}, u32[]{:S(2)}, u32[]{:S(2)}) %collective-permute-start.26) | collective-permute-done | bytes 393248 | tf_op jit(solution)/shard_map/ppermute | solution.py:467
  66.5 9.0 %collective-permute-done.27.refs_2_ = bf16[192,1024]{1,0:T(8,128)(2,1)S(1)} collective-permute-done((bf16[192,1024]{1,0:T(8,128)(2,1)S(1)}, bf16[192,1024]{1,0:T(8,128)(2,1)S(1)}, u32[]{:S(2)}, u32[]{:S(2)}) %collective-permute-start.27) | collective-permute-done | bytes 393248 | tf_op jit(solution)/shard_map/ppermute | solution.py:467
  75.7 1.7 %collective-permute-start.29 = (bf16[96,1024]{1,0:T(8,128)(2,1)S(1)}, bf16[96,1024]{1,0:T(8,128)(2,1)S(1)}, u32[]{:S(2)}, u32[]{:S(2)}) collective-permute-start(bf16[96,1024]{1,0:T(8,128)(2,1)S(1)} %get-tuple-element.216), channel_id=1, source_target_pairs={{0,8},{8,0},{16,24},{24,16},{1,9},{9,1},{17,25},{25,17},{2,10},{10... | collective-permute-start | bytes 589832 | tf_op jit(solution)/shard_map/ppermute | solution.py:467
  77.3 0.7 add_parts.9
  78.1 0.6 collective-permute-start.13
  78.6 1.5 %collective-permute-start.14 = (bf16[208,512]{1,0:T(8,128)(2,1)S(1)}, bf16[208,512]{1,0:T(8,128)(2,1)S(1)}, u32[]{:S(2)}, u32[]{:S(2)}) collective-permute-start(bf16[208,512]{1,0:T(8,128)(2,1)S(1)} %get-tuple-element.200), channel_id=1, source_target_pairs={{0,4},{1,5},{2,6},{3,7},{4,0},{5,1},{6,2},{7,3},{8,12},{9,13},{10,... | collective-permute-start | bytes 638984 | tf_op jit(solution)/shard_map/ppermute | solution.py:467
  80.1 1.5 %collective-permute-start.15 = (bf16[208,512]{1,0:T(8,128)(2,1)S(1)}, bf16[208,512]{1,0:T(8,128)(2,1)S(1)}, u32[]{:S(2)}, u32[]{:S(2)}) collective-permute-start(bf16[208,512]{1,0:T(8,128)(2,1)S(1)} %get-tuple-element.201), channel_id=1, source_target_pairs={{0,6},{1,7},{2,4},{3,5},{4,2},{5,3},{6,0},{7,1},{8,14},{9,15},{10,... | collective-permute-start | bytes 638984 | tf_op jit(solution)/shard_map/ppermute | solution.py:467
  81.7 2.6 %collective-permute-start.30 = (bf16[96,1024]{1,0:T(8,128)(2,1)S(1)}, bf16[96,1024]{1,0:T(8,128)(2,1)S(1)}, u32[]{:S(2)}, u32[]{:S(2)}) collective-permute-start(bf16[96,1024]{1,0:T(8,128)(2,1)S(1)} %add_parts.14.refs_0_), channel_id=1, source_target_pairs={{0,16},{8,24},{16,0},{24,8},{1,17},{9,25},{17,1},{25,9},{2,18},{10... | collective-permute-start | bytes 589832 | tf_op jit(solution)/shard_map/ppermute | solution.py:467
  84.3 1.9 %collective-permute-done.13.refs_1_ = bf16[208,512]{1,0:T(8,128)(2,1)S(1)} collective-permute-done((bf16[208,512]{1,0:T(8,128)(2,1)S(1)}, bf16[208,512]{1,0:T(8,128)(2,1)S(1)}, u32[]{:S(2)}, u32[]{:S(2)}) %collective-permute-start.13) | collective-permute-done | bytes 213024 | tf_op jit(solution)/shard_map/ppermute | solution.py:467
  86.2 2.7 %collective-permute-done.14.refs_2_ = bf16[208,512]{1,0:T(8,128)(2,1)S(1)} collective-permute-done((bf16[208,512]{1,0:T(8,128)(2,1)S(1)}, bf16[208,512]{1,0:T(8,128)(2,1)S(1)}, u32[]{:S(2)}, u32[]{:S(2)}) %collective-permute-start.14) | collective-permute-done | bytes 213024 | tf_op jit(solution)/shard_map/ppermute | solution.py:467
  89.1 0.5 collective-permute-start.16
  89.6 2.1 %collective-permute-done.30.refs_1_ = bf16[96,1024]{1,0:T(8,128)(2,1)S(1)} collective-permute-done((bf16[96,1024]{1,0:T(8,128)(2,1)S(1)}, bf16[96,1024]{1,0:T(8,128)(2,1)S(1)}, u32[]{:S(2)}, u32[]{:S(2)}) %collective-permute-start.30) | collective-permute-done | bytes 196640 | tf_op jit(solution)/shard_map/ppermute | solution.py:467
  91.7 0.7 collective-permute-start.31
  92.4 2.3 %collective-permute-done.16.refs_1_ = bf16[112,512]{1,0:T(8,128)(2,1)S(1)} collective-permute-done((bf16[112,512]{1,0:T(8,128)(2,1)S(1)}, bf16[112,512]{1,0:T(8,128)(2,1)S(1)}, u32[]{:S(2)}, u32[]{:S(2)}) %collective-permute-start.16) | collective-permute-done | bytes 114720 | tf_op jit(solution)/shard_map/ppermute | solution.py:467
  94.7 2.8 %collective-permute-start.17 = (bf16[112,512]{1,0:T(8,128)(2,1)S(1)}, bf16[112,512]{1,0:T(8,128)(2,1)S(1)}, u32[]{:S(2)}, u32[]{:S(2)}) collective-permute-start(bf16[112,512]{1,0:T(8,128)(2,1)S(1)} %add_parts.11.refs_0_), channel_id=1, source_target_pairs={{0,16},{8,24},{16,0},{24,8},{1,17},{9,25},{17,1},{25,9},{2,18},{10... | collective-permute-start | bytes 344072 | tf_op jit(solution)/shard_map/ppermute | solution.py:467
  97.5 0.8 add_slots.1
  98.3 1.6 %collective-permute-start.9 = (bf16[512,256]{1,0:T(8,128)(2,1)S(1)}, bf16[512,256]{1,0:T(8,128)(2,1)S(1)}, u32[]{:S(2)}, u32[]{:S(2)}) collective-permute-start(bf16[512,256]{1,0:T(8,128)(2,1)S(1)} %get-tuple-element.191), channel_id=1, source_target_pairs={{0,2},{1,3},{2,0},{3,1},{4,6},{5,7},{6,4},{7,5},{8,10},{9,11},{10,... | collective-permute-start | bytes 786440 | tf_op jit(solution)/shard_map/ppermute | solution.py:467
  99.8 0.5 collective-permute-start.10
  100.3 1.5 %collective-permute-start.11 = (bf16[512,256]{1,0:T(8,128)(2,1)S(1)}, bf16[512,256]{1,0:T(8,128)(2,1)S(1)}, u32[]{:S(2)}, u32[]{:S(2)}) collective-permute-start(bf16[512,256]{1,0:T(8,128)(2,1)S(1)} %get-tuple-element.193), channel_id=1, source_target_pairs={{0,6},{1,7},{2,4},{3,5},{4,2},{5,3},{6,0},{7,1},{8,14},{9,15},{10,... | collective-permute-start | bytes 786440 | tf_op jit(solution)/shard_map/ppermute | solution.py:467
  101.8 1.1 collective-permute-done.17.refs_1_
  103.0 0.4 collective-permute-start.18
  103.4 1.6 %collective-permute-start.34 = (bf16[192,1024]{1,0:T(8,128)(2,1)S(1)}, bf16[192,1024]{1,0:T(8,128)(2,1)S(1)}, u32[]{:S(2)}, u32[]{:S(2)}) collective-permute-start(bf16[192,1024]{1,0:T(8,128)(2,1)S(1)} %pad_maximum_fusion.refs_0_), channel_id=1, source_target_pairs={{0,6},{1,7},{2,4},{3,5},{4,2},{5,3},{6,0},{7,1},{8,14},{9,15},{10,... | collective-permute-start | bytes 1179656 | tf_op jit(solution)/shard_map/ppermute | solution.py:467
  105.1 2.5 %collective-permute-done.9.refs_1_ = bf16[512,256]{1,0:T(8,128)(2,1)S(1)} collective-permute-done((bf16[512,256]{1,0:T(8,128)(2,1)S(1)}, bf16[512,256]{1,0:T(8,128)(2,1)S(1)}, u32[]{:S(2)}, u32[]{:S(2)}) %collective-permute-start.9) | collective-permute-done | bytes 262176 | tf_op jit(solution)/shard_map/ppermute | solution.py:467
  107.6 1.2 collective-permute-start.33
  108.8 0.8 collective-permute-start.32
  109.6 8.3 %collective-permute-done.10.refs_2_ = bf16[512,256]{1,0:T(8,128)(2,1)S(1)} collective-permute-done((bf16[512,256]{1,0:T(8,128)(2,1)S(1)}, bf16[512,256]{1,0:T(8,128)(2,1)S(1)}, u32[]{:S(2)}, u32[]{:S(2)}) %collective-permute-start.10) | collective-permute-done | bytes 262176 | tf_op jit(solution)/shard_map/ppermute | solution.py:467
  117.9 1.7 %collective-permute-start.21 = (bf16[192,512]{1,0:T(8,128)(2,1)S(1)}, bf16[192,512]{1,0:T(8,128)(2,1)S(1)}, u32[]{:S(2)}, u32[]{:S(2)}) collective-permute-start(bf16[192,512]{1,0:T(8,128)(2,1)S(1)} %pad_maximum_fusion.1.refs_0_), channel_id=1, source_target_pairs={{0,6},{1,7},{2,4},{3,5},{4,2},{5,3},{6,0},{7,1},{8,14},{9,15},{10,... | collective-permute-start | bytes 589832 | tf_op jit(solution)/shard_map/ppermute | solution.py:467
  119.6 2.3 %collective-permute-start.20 = (bf16[192,512]{1,0:T(8,128)(2,1)S(1)}, bf16[192,512]{1,0:T(8,128)(2,1)S(1)}, u32[]{:S(2)}, u32[]{:S(2)}) collective-permute-start(bf16[192,512]{1,0:T(8,128)(2,1)S(1)} %pad_maximum_fusion.1.refs_0_), channel_id=1, source_target_pairs={{0,4},{1,5},{2,6},{3,7},{4,0},{5,1},{6,2},{7,3},{8,12},{9,13},{10,... | collective-permute-start | bytes 589832 | tf_op jit(solution)/shard_map/ppermute | solution.py:467
  121.9 0.4 collective-permute-done.34.refs_3_
  122.3 0.8 collective-permute-start.19
  123.1 8.9 %collective-permute-done.33.refs_2_ = bf16[192,1024]{1,0:T(8,128)(2,1)S(1)} collective-permute-done((bf16[192,1024]{1,0:T(8,128)(2,1)S(1)}, bf16[192,1024]{1,0:T(8,128)(2,1)S(1)}, u32[]{:S(2)}, u32[]{:S(2)}) %collective-permute-start.33) | collective-permute-done | bytes 393248 | tf_op jit(solution)/shard_map/ppermute | solution.py:467
  132.0 1.1 collective-permute-done.21.refs_3_
  133.2 2.4 %collective-permute-done.20.refs_2_ = bf16[192,512]{1,0:T(8,128)(2,1)S(1)} collective-permute-done((bf16[192,512]{1,0:T(8,128)(2,1)S(1)}, bf16[192,512]{1,0:T(8,128)(2,1)S(1)}, u32[]{:S(2)}, u32[]{:S(2)}) %collective-permute-start.20) | collective-permute-done | bytes 196640 | tf_op jit(solution)/shard_map/ppermute | solution.py:467
  135.6 0.5 collective-permute-start.23
  136.2 0.4 collective-permute-start.38
  137.1 1.8 %input_grad.1 = f32[256,512]{1,0:T(8,128)} custom-call(s32[4]{0:T(128)S(1)} %pad_add_fusion.ids, bf16[512,256]{1,0:T(8,128)(2,1)S(1)} %get-tuple-element.190.refs_0_, bf16[512,256]{1,0:T(8,128)(2,1)S(1)} %collective-permute-done.9.refs_1_, bf16[512,256]{1,0:T(8,128)(2,1)S(1)} %collective-permute-done.10.refs_2_, ...), custom_call_target="tpu_custom_call" | custom-call | flops 2000000000 | bytes 4000000 | tf_op jit(solution)/shard_map/input_grad/pallas_call | solution.py:66
  138.9 2.5 %unpack_attention.1 = (f32[512,384]{1,0:T(8,128)}, f32[512,384]{1,0:T(8,128)}, f32[512,384]{1,0:T(8,128)}, f32[384,512]{1,0:T(8,128)}, f32[1,512]{1,0:T(1,128)}, /*index=5*/f32[1,512]{1,0:T(1,128)}, f32[32,6]{1,0:T(8,128)S(1)}) custom-call(s32[4]{0:T(128)S(1)} %pad_add_fusion.ids, bf16[16,512]{1,0:T(8,128)(2,1)S(1)} %slice.9.tail, ...), custom_call_target="tpu_custom_call" | custom-call | flops 3000000000 | bytes 6000000 | tf_op jit(solution)/shard_map/unpack_attention/pallas_call | solution.py:66
  141.4 0.7 copy.26
  142.1 3.6 %unpack_ffn.1 = (f32[512,1024]{1,0:T(8,128)}, f32[512,1024]{1,0:T(8,128)}, f32[1024,512]{1,0:T(8,128)}) custom-call(s32[4]{0:T(128)S(1)} %pad_add_fusion.ids, bf16[192,1024]{1,0:T(8,128)(2,1)S(1)} %pad_maximum_fusion.refs_0_, bf16[192,1024]{1,0:T(8,128)(2,1)S(1)} %collective-permute-done.32.refs_1_, bf16[192,1024]{1,0:T(8,128)(2,1)S(1)} %collective-permute-done.33.refs_2_, ...), custom_call_target="tpu_custom_call" | custom-call | flops 4000000000 | bytes 8000000 | tf_op jit(solution)/shard_map/unpack_ffn/pallas_call | solution.py:66
  (72 shorter events, 2.5 us)
Async XLA Ops:
  0.6 13.2 %collective-permute-start.5 = (bf16[256,512]{1,0:T(8,128)(2,1)}, bf16[256,512]{1,0:T(8,128)(2,1)S(1)}, u32[]{:S(2)}, u32[]{:S(2)}) collective-permute-start(bf16[256,512]{1,0:T(8,128)(2,1)} %bitcast.12), channel_id=1, source_target_pairs={{0,6},{1,7},{2,4},{3,5},{4,2},{5,3},{6,0},{7,1},{8,14},{9,15},{10,... | collective-permute-start | bytes 786440 | tf_op jit(solution)/shard_map/ppermute | solution.py:467
  4.6 12.1 %collective-permute-start.3 = (bf16[256,512]{1,0:T(8,128)(2,1)}, bf16[256,512]{1,0:T(8,128)(2,1)S(1)}, u32[]{:S(2)}, u32[]{:S(2)}) collective-permute-start(bf16[256,512]{1,0:T(8,128)(2,1)} %bitcast.13), channel_id=1, source_target_pairs={{0,4},{1,5},{2,6},{3,7},{4,0},{5,1},{6,2},{7,3},{8,12},{9,13},{10,... | collective-permute-start | bytes 786440 | tf_op jit(solution)/shard_map/ppermute | solution.py:467
  5.1 11.9 %collective-permute-start.1 = (bf16[256,512]{1,0:T(8,128)(2,1)}, bf16[256,512]{1,0:T(8,128)(2,1)S(1)}, u32[]{:S(2)}, u32[]{:S(2)}) collective-permute-start(bf16[256,512]{1,0:T(8,128)(2,1)} %bitcast.14), channel_id=1, source_target_pairs={{0,2},{1,3},{2,0},{3,1},{4,6},{5,7},{6,4},{7,5},{8,10},{9,11},{10,... | collective-permute-start | bytes 786440 | tf_op jit(solution)/shard_map/ppermute | solution.py:467
  5.2 12.0 %collective-permute-start = (bf16[256,512]{1,0:T(8,128)(2,1)}, bf16[256,512]{1,0:T(8,128)(2,1)S(1)}, u32[]{:S(2)}, u32[]{:S(2)}) collective-permute-start(bf16[256,512]{1,0:T(8,128)(2,1)} %bitcast.15), channel_id=1, source_target_pairs={{0,1},{1,0},{2,3},{3,2},{4,5},{5,4},{6,7},{7,6},{8,9},{9,8},{10,11... | collective-permute-start | bytes 786440 | tf_op jit(solution)/shard_map/ppermute | solution.py:467
  7.5 1.0 copy-start.4
  8.5 1.0 copy-start.6
  9.5 1.0 copy-start.8
  10.5 0.9 copy-start.11
  11.4 0.7 copy-start.13
  12.1 5.2 %copy-start.5 = (bf16[512,384]{1,0:T(8,128)(2,1)S(1)}, bf16[512,384]{1,0:T(8,128)(2,1)}, u32[]{:S(2)}) copy-start(bf16[512,384]{1,0:T(8,128)(2,1)} %wk.3) | copy-start | bytes 1179652
  12.1 5.2 %copy-start.7 = (bf16[512,384]{1,0:T(8,128)(2,1)S(1)}, bf16[512,384]{1,0:T(8,128)(2,1)}, u32[]{:S(2)}) copy-start(bf16[512,384]{1,0:T(8,128)(2,1)} %wv.3) | copy-start | bytes 1179652
  13.9 7.5 %collective-permute-start.6 = (bf16[256,512]{1,0:T(8,128)(2,1)S(1)}, bf16[256,512]{1,0:T(8,128)(2,1)S(1)}, u32[]{:S(2)}, u32[]{:S(2)}) collective-permute-start(bf16[256,512]{1,0:T(8,128)(2,1)S(1)} %collective-permute-done.5.refs_0_), channel_id=1, source_target_pairs={{0,1},{1,0},{2,3},{3,2},{4,5},{5,4},{6,7},{7,6},{8,9},{9,8},{10,11... | collective-permute-start | bytes 786440 | tf_op jit(solution)/shard_map/ppermute | solution.py:467
  16.7 8.7 %collective-permute-start.4 = (bf16[256,512]{1,0:T(8,128)(2,1)S(1)}, bf16[256,512]{1,0:T(8,128)(2,1)S(1)}, u32[]{:S(2)}, u32[]{:S(2)}) collective-permute-start(bf16[256,512]{1,0:T(8,128)(2,1)S(1)} %collective-permute-done.3.refs_2_), channel_id=1, source_target_pairs={{0,1},{1,0},{2,3},{3,2},{4,5},{5,4},{6,7},{7,6},{8,9},{9,8},{10,11... | collective-permute-start | bytes 786440 | tf_op jit(solution)/shard_map/ppermute | solution.py:467
  17.0 8.4 %collective-permute-start.2 = (bf16[256,512]{1,0:T(8,128)(2,1)S(1)}, bf16[256,512]{1,0:T(8,128)(2,1)S(1)}, u32[]{:S(2)}, u32[]{:S(2)}) collective-permute-start(bf16[256,512]{1,0:T(8,128)(2,1)S(1)} %collective-permute-done.1.refs_0_), channel_id=1, source_target_pairs={{0,1},{1,0},{2,3},{3,2},{4,5},{5,4},{6,7},{7,6},{8,9},{9,8},{10,11... | collective-permute-start | bytes 786440 | tf_op jit(solution)/shard_map/ppermute | solution.py:467
  25.4 6.2 %copy-start = (bf16[512,1024]{1,0:T(8,128)(2,1)S(1)}, bf16[512,1024]{1,0:T(8,128)(2,1)}, u32[]{:S(2)}) copy-start(bf16[512,1024]{1,0:T(8,128)(2,1)} %wg.1) | copy-start | bytes 3145732
  25.4 6.2 %copy-start.1 = (bf16[512,1024]{1,0:T(8,128)(2,1)S(1)}, bf16[512,1024]{1,0:T(8,128)(2,1)}, u32[]{:S(2)}) copy-start(bf16[512,1024]{1,0:T(8,128)(2,1)} %wu.1) | copy-start | bytes 3145732
  25.4 6.2 %copy-start.2 = (bf16[1024,512]{1,0:T(8,128)(2,1)S(1)}, bf16[1024,512]{1,0:T(8,128)(2,1)}, u32[]{:S(2)}) copy-start(bf16[1024,512]{1,0:T(8,128)(2,1)} %wd.1) | copy-start | bytes 3145732
  25.4 6.2 %copy-start.3 = (bf16[384,512]{1,0:T(8,128)(2,1)S(1)}, bf16[384,512]{1,0:T(8,128)(2,1)}, u32[]{:S(2)}) copy-start(bf16[384,512]{1,0:T(8,128)(2,1)} %wo.1) | copy-start | bytes 1179652
  25.4 6.2 %copy-start.10 = (bf16[1,256,512]{2,1,0:T(8,128)(2,1)S(1)}, bf16[1,256,512]{2,1,0:T(8,128)(2,1)}, u32[]{:S(2)}) copy-start(bf16[1,256,512]{2,1,0:T(8,128)(2,1)} %param.25) | copy-start | bytes 786436
  37.9 3.7 %collective-permute-start.7 = (bf16[768,1024]{1,0:T(8,128)(2,1)S(1)}, bf16[768,1024]{1,0:T(8,128)(2,1)S(1)}, u32[]{:S(2)}, u32[]{:S(2)}) collective-permute-start(bf16[768,1024]{1,0:T(8,128)(2,1)S(1)} %get-tuple-element.146), channel_id=1, source_target_pairs={{0,1},{1,0},{2,3},{3,2},{4,5},{5,4},{6,7},{7,6},{8,9},{9,8},{10,11... | collective-permute-start | bytes 4718600 | tf_op jit(solution)/shard_map/ppermute | solution.py:467
  45.9 3.7 %copy-start.9 = (bf16[512,384]{1,0:T(8,128)(2,1)S(1)}, bf16[512,384]{1,0:T(8,128)(2,1)}, u32[]{:S(2)}) copy-start(bf16[512,384]{1,0:T(8,128)(2,1)} %wq.3) | copy-start | bytes 1179652
  54.3 23.0 %collective-permute-start.12 = (bf16[784,512]{1,0:T(8,128)(2,1)S(1)}, bf16[784,512]{1,0:T(8,128)(2,1)S(1)}, u32[]{:S(2)}, u32[]{:S(2)}) collective-permute-start(bf16[784,512]{1,0:T(8,128)(2,1)S(1)} %get-tuple-element.197), channel_id=1, source_target_pairs={{0,1},{1,0},{2,3},{3,2},{4,5},{5,4},{6,7},{7,6},{8,9},{9,8},{10,11... | collective-permute-start | bytes 2408456 | tf_op jit(solution)/shard_map/ppermute | solution.py:467
  54.5 11.9 %collective-permute-start.26 = (bf16[192,1024]{1,0:T(8,128)(2,1)S(1)}, bf16[192,1024]{1,0:T(8,128)(2,1)S(1)}, u32[]{:S(2)}, u32[]{:S(2)}) collective-permute-start(bf16[192,1024]{1,0:T(8,128)(2,1)S(1)} %get-tuple-element.212), channel_id=1, source_target_pairs={{0,2},{1,3},{2,0},{3,1},{4,6},{5,7},{6,4},{7,5},{8,10},{9,11},{10,... | collective-permute-start | bytes 1179656 | tf_op jit(solution)/shard_map/ppermute | solution.py:467
  56.2 19.3 %collective-permute-start.27 = (bf16[192,1024]{1,0:T(8,128)(2,1)S(1)}, bf16[192,1024]{1,0:T(8,128)(2,1)S(1)}, u32[]{:S(2)}, u32[]{:S(2)}) collective-permute-start(bf16[192,1024]{1,0:T(8,128)(2,1)S(1)} %get-tuple-element.213), channel_id=1, source_target_pairs={{0,4},{1,5},{2,6},{3,7},{4,0},{5,1},{6,2},{7,3},{8,12},{9,13},{10,... | collective-permute-start | bytes 1179656 | tf_op jit(solution)/shard_map/ppermute | solution.py:467
  56.9 18.6 %collective-permute-start.28 = (bf16[192,1024]{1,0:T(8,128)(2,1)S(1)}, bf16[192,1024]{1,0:T(8,128)(2,1)S(1)}, u32[]{:S(2)}, u32[]{:S(2)}) collective-permute-start(bf16[192,1024]{1,0:T(8,128)(2,1)S(1)} %get-tuple-element.214), channel_id=1, source_target_pairs={{0,6},{1,7},{2,4},{3,5},{4,2},{5,3},{6,0},{7,1},{8,14},{9,15},{10,... | collective-permute-start | bytes 1179656 | tf_op jit(solution)/shard_map/ppermute | solution.py:467
  58.0 39.5 %collective-permute-start.8 = (bf16[4,512,256]{2,1,0:T(8,128)(2,1)S(1)}, bf16[4,512,256]{2,1,0:T(8,128)(2,1)S(1)}, u32[]{:S(2)}, u32[]{:S(2)}) collective-permute-start(bf16[4,512,256]{2,1,0:T(8,128)(2,1)S(1)} %get-tuple-element.189), channel_id=1, source_target_pairs={{0,1},{1,0},{2,3},{3,2},{4,5},{5,4},{6,7},{7,6},{8,9},{9,8},{10,11... | collective-permute-start | bytes 3145736 | tf_op jit(solution)/shard_map/ppermute | solution.py:467
  75.7 6.0 %collective-permute-start.29 = (bf16[96,1024]{1,0:T(8,128)(2,1)S(1)}, bf16[96,1024]{1,0:T(8,128)(2,1)S(1)}, u32[]{:S(2)}, u32[]{:S(2)}) collective-permute-start(bf16[96,1024]{1,0:T(8,128)(2,1)S(1)} %get-tuple-element.216), channel_id=1, source_target_pairs={{0,8},{8,0},{16,24},{24,16},{1,9},{9,1},{17,25},{25,17},{2,10},{10... | collective-permute-start | bytes 589832 | tf_op jit(solution)/shard_map/ppermute | solution.py:467
  78.1 8.2 %collective-permute-start.13 = (bf16[208,512]{1,0:T(8,128)(2,1)S(1)}, bf16[208,512]{1,0:T(8,128)(2,1)S(1)}, u32[]{:S(2)}, u32[]{:S(2)}) collective-permute-start(bf16[208,512]{1,0:T(8,128)(2,1)S(1)} %get-tuple-element.199), channel_id=1, source_target_pairs={{0,2},{1,3},{2,0},{3,1},{4,6},{5,7},{6,4},{7,5},{8,10},{9,11},{10,... | collective-permute-start | bytes 638984 | tf_op jit(solution)/shard_map/ppermute | solution.py:467
  78.6 10.3 %collective-permute-start.14 = (bf16[208,512]{1,0:T(8,128)(2,1)S(1)}, bf16[208,512]{1,0:T(8,128)(2,1)S(1)}, u32[]{:S(2)}, u32[]{:S(2)}) collective-permute-start(bf16[208,512]{1,0:T(8,128)(2,1)S(1)} %get-tuple-element.200), channel_id=1, source_target_pairs={{0,4},{1,5},{2,6},{3,7},{4,0},{5,1},{6,2},{7,3},{8,12},{9,13},{10,... | collective-permute-start | bytes 638984 | tf_op jit(solution)/shard_map/ppermute | solution.py:467
  80.1 8.8 %collective-permute-start.15 = (bf16[208,512]{1,0:T(8,128)(2,1)S(1)}, bf16[208,512]{1,0:T(8,128)(2,1)S(1)}, u32[]{:S(2)}, u32[]{:S(2)}) collective-permute-start(bf16[208,512]{1,0:T(8,128)(2,1)S(1)} %get-tuple-element.201), channel_id=1, source_target_pairs={{0,6},{1,7},{2,4},{3,5},{4,2},{5,3},{6,0},{7,1},{8,14},{9,15},{10,... | collective-permute-start | bytes 638984 | tf_op jit(solution)/shard_map/ppermute | solution.py:467
  81.7 10.0 %collective-permute-start.30 = (bf16[96,1024]{1,0:T(8,128)(2,1)S(1)}, bf16[96,1024]{1,0:T(8,128)(2,1)S(1)}, u32[]{:S(2)}, u32[]{:S(2)}) collective-permute-start(bf16[96,1024]{1,0:T(8,128)(2,1)S(1)} %add_parts.14.refs_0_), channel_id=1, source_target_pairs={{0,16},{8,24},{16,0},{24,8},{1,17},{9,25},{17,1},{25,9},{2,18},{10... | collective-permute-start | bytes 589832 | tf_op jit(solution)/shard_map/ppermute | solution.py:467
  89.1 5.6 %collective-permute-start.16 = (bf16[112,512]{1,0:T(8,128)(2,1)S(1)}, bf16[112,512]{1,0:T(8,128)(2,1)S(1)}, u32[]{:S(2)}, u32[]{:S(2)}) collective-permute-start(bf16[112,512]{1,0:T(8,128)(2,1)S(1)} %get-tuple-element.203), channel_id=1, source_target_pairs={{0,8},{8,0},{16,24},{24,16},{1,9},{9,1},{17,25},{25,17},{2,10},{10... | collective-permute-start | bytes 344072 | tf_op jit(solution)/shard_map/ppermute | solution.py:467
  91.7 11.7 %collective-permute-start.31 = (bf16[96,1024]{1,0:T(8,128)(2,1)S(1)}, bf16[96,1024]{1,0:T(8,128)(2,1)S(1)}, u32[]{:S(2)}, u32[]{:S(2)}) collective-permute-start(bf16[96,1024]{1,0:T(8,128)(2,1)S(1)} %add_parts.15), channel_id=1, source_target_pairs={{0,8},{8,0},{16,24},{24,16},{1,9},{9,1},{17,25},{25,17},{2,10},{10... | collective-permute-start | bytes 589832 | tf_op jit(solution)/shard_map/ppermute | solution.py:467
  94.7 8.2 %collective-permute-start.17 = (bf16[112,512]{1,0:T(8,128)(2,1)S(1)}, bf16[112,512]{1,0:T(8,128)(2,1)S(1)}, u32[]{:S(2)}, u32[]{:S(2)}) collective-permute-start(bf16[112,512]{1,0:T(8,128)(2,1)S(1)} %add_parts.11.refs_0_), channel_id=1, source_target_pairs={{0,16},{8,24},{16,0},{24,8},{1,17},{9,25},{17,1},{25,9},{2,18},{10... | collective-permute-start | bytes 344072 | tf_op jit(solution)/shard_map/ppermute | solution.py:467
  98.3 9.3 %collective-permute-start.9 = (bf16[512,256]{1,0:T(8,128)(2,1)S(1)}, bf16[512,256]{1,0:T(8,128)(2,1)S(1)}, u32[]{:S(2)}, u32[]{:S(2)}) collective-permute-start(bf16[512,256]{1,0:T(8,128)(2,1)S(1)} %get-tuple-element.191), channel_id=1, source_target_pairs={{0,2},{1,3},{2,0},{3,1},{4,6},{5,7},{6,4},{7,5},{8,10},{9,11},{10,... | collective-permute-start | bytes 786440 | tf_op jit(solution)/shard_map/ppermute | solution.py:467
  99.8 18.1 %collective-permute-start.10 = (bf16[512,256]{1,0:T(8,128)(2,1)S(1)}, bf16[512,256]{1,0:T(8,128)(2,1)S(1)}, u32[]{:S(2)}, u32[]{:S(2)}) collective-permute-start(bf16[512,256]{1,0:T(8,128)(2,1)S(1)} %get-tuple-element.192), channel_id=1, source_target_pairs={{0,4},{1,5},{2,6},{3,7},{4,0},{5,1},{6,2},{7,3},{8,12},{9,13},{10,... | collective-permute-start | bytes 786440 | tf_op jit(solution)/shard_map/ppermute | solution.py:467
  100.3 36.8 %copy-start.12 = (bf16[1,256,512]{2,1,0:T(8,128)(2,1)S(1)}, bf16[1,256,512]{2,1,0:T(8,128)(2,1)}, u32[]{:S(2)}) copy-start(bf16[1,256,512]{2,1,0:T(8,128)(2,1)} %param.13) | copy-start | bytes 786436
  100.3 19.3 %collective-permute-start.11 = (bf16[512,256]{1,0:T(8,128)(2,1)S(1)}, bf16[512,256]{1,0:T(8,128)(2,1)S(1)}, u32[]{:S(2)}, u32[]{:S(2)}) collective-permute-start(bf16[512,256]{1,0:T(8,128)(2,1)S(1)} %get-tuple-element.193), channel_id=1, source_target_pairs={{0,6},{1,7},{2,4},{3,5},{4,2},{5,3},{6,0},{7,1},{8,14},{9,15},{10,... | collective-permute-start | bytes 786440 | tf_op jit(solution)/shard_map/ppermute | solution.py:467
  103.0 5.8 %collective-permute-start.18 = (bf16[96,512]{1,0:T(8,128)(2,1)S(1)}, bf16[96,512]{1,0:T(8,128)(2,1)S(1)}, u32[]{:S(2)}, u32[]{:S(2)}) collective-permute-start(bf16[96,512]{1,0:T(8,128)(2,1)S(1)} %slice.10), channel_id=1, source_target_pairs={{0,8},{8,0},{16,24},{24,16},{1,9},{9,1},{17,25},{25,17},{2,10},{10... | collective-permute-start | bytes 294920 | tf_op jit(solution)/shard_map/ppermute | solution.py:467
  103.4 18.8 %collective-permute-start.34 = (bf16[192,1024]{1,0:T(8,128)(2,1)S(1)}, bf16[192,1024]{1,0:T(8,128)(2,1)S(1)}, u32[]{:S(2)}, u32[]{:S(2)}) collective-permute-start(bf16[192,1024]{1,0:T(8,128)(2,1)S(1)} %pad_maximum_fusion.refs_0_), channel_id=1, source_target_pairs={{0,6},{1,7},{2,4},{3,5},{4,2},{5,3},{6,0},{7,1},{8,14},{9,15},{10,... | collective-permute-start | bytes 1179656 | tf_op jit(solution)/shard_map/ppermute | solution.py:467
  107.6 24.4 %collective-permute-start.33 = (bf16[192,1024]{1,0:T(8,128)(2,1)S(1)}, bf16[192,1024]{1,0:T(8,128)(2,1)S(1)}, u32[]{:S(2)}, u32[]{:S(2)}) collective-permute-start(bf16[192,1024]{1,0:T(8,128)(2,1)S(1)} %pad_maximum_fusion.refs_0_), channel_id=1, source_target_pairs={{0,4},{1,5},{2,6},{3,7},{4,0},{5,1},{6,2},{7,3},{8,12},{9,13},{10,... | collective-permute-start | bytes 1179656 | tf_op jit(solution)/shard_map/ppermute | solution.py:467
  108.8 27.3 %collective-permute-start.32 = (bf16[192,1024]{1,0:T(8,128)(2,1)S(1)}, bf16[192,1024]{1,0:T(8,128)(2,1)S(1)}, u32[]{:S(2)}, u32[]{:S(2)}) collective-permute-start(bf16[192,1024]{1,0:T(8,128)(2,1)S(1)} %pad_maximum_fusion.refs_0_), channel_id=1, source_target_pairs={{0,2},{1,3},{2,0},{3,1},{4,6},{5,7},{6,4},{7,5},{8,10},{9,11},{10,... | collective-permute-start | bytes 1179656 | tf_op jit(solution)/shard_map/ppermute | solution.py:467
  117.9 15.2 %collective-permute-start.21 = (bf16[192,512]{1,0:T(8,128)(2,1)S(1)}, bf16[192,512]{1,0:T(8,128)(2,1)S(1)}, u32[]{:S(2)}, u32[]{:S(2)}) collective-permute-start(bf16[192,512]{1,0:T(8,128)(2,1)S(1)} %pad_maximum_fusion.1.refs_0_), channel_id=1, source_target_pairs={{0,6},{1,7},{2,4},{3,5},{4,2},{5,3},{6,0},{7,1},{8,14},{9,15},{10,... | collective-permute-start | bytes 589832 | tf_op jit(solution)/shard_map/ppermute | solution.py:467
  119.6 15.9 %collective-permute-start.20 = (bf16[192,512]{1,0:T(8,128)(2,1)S(1)}, bf16[192,512]{1,0:T(8,128)(2,1)S(1)}, u32[]{:S(2)}, u32[]{:S(2)}) collective-permute-start(bf16[192,512]{1,0:T(8,128)(2,1)S(1)} %pad_maximum_fusion.1.refs_0_), channel_id=1, source_target_pairs={{0,4},{1,5},{2,6},{3,7},{4,0},{5,1},{6,2},{7,3},{8,12},{9,13},{10,... | collective-permute-start | bytes 589832 | tf_op jit(solution)/shard_map/ppermute | solution.py:467
  122.3 13.3 %collective-permute-start.19 = (bf16[192,512]{1,0:T(8,128)(2,1)S(1)}, bf16[192,512]{1,0:T(8,128)(2,1)S(1)}, u32[]{:S(2)}, u32[]{:S(2)}) collective-permute-start(bf16[192,512]{1,0:T(8,128)(2,1)S(1)} %pad_maximum_fusion.1.refs_0_), channel_id=1, source_target_pairs={{0,2},{1,3},{2,0},{3,1},{4,6},{5,7},{6,4},{7,5},{8,10},{9,11},{10,... | collective-permute-start | bytes 589832 | tf_op jit(solution)/shard_map/ppermute | solution.py:467
  132.0 4.1 %collective-permute-start.22 = (bf16[192,512]{1,0:T(8,128)(2,1)S(1)}, bf16[192,512]{1,0:T(8,128)(2,1)S(1)}, u32[]{:S(2)}, u32[]{:S(2)}) collective-permute-start(bf16[192,512]{1,0:T(8,128)(2,1)S(1)} %pad_maximum_fusion.1.refs_0_), channel_id=1, source_target_pairs={{0,1},{1,0},{2,3},{3,2},{4,5},{5,4},{6,7},{7,6},{8,9},{9,8},{10,11... | collective-permute-start | bytes 589832 | tf_op jit(solution)/shard_map/ppermute | solution.py:467
  133.2 3.4 %collective-permute-start.25 = (bf16[192,512]{1,0:T(8,128)(2,1)S(1)}, bf16[192,512]{1,0:T(8,128)(2,1)S(1)}, u32[]{:S(2)}, u32[]{:S(2)}) collective-permute-start(bf16[192,512]{1,0:T(8,128)(2,1)S(1)} %collective-permute-done.21.refs_3_), channel_id=1, source_target_pairs={{0,1},{1,0},{2,3},{3,2},{4,5},{5,4},{6,7},{7,6},{8,9},{9,8},{10,11... | collective-permute-start | bytes 589832 | tf_op jit(solution)/shard_map/ppermute | solution.py:467
  135.5 1.4 collective-permute-start.24
  135.6 3.4 %collective-permute-start.23 = (bf16[192,512]{1,0:T(8,128)(2,1)S(1)}, bf16[192,512]{1,0:T(8,128)(2,1)S(1)}, u32[]{:S(2)}, u32[]{:S(2)}) collective-permute-start(bf16[192,512]{1,0:T(8,128)(2,1)S(1)} %collective-permute-done.19.refs_1_), channel_id=1, source_target_pairs={{0,1},{1,0},{2,3},{3,2},{4,5},{5,4},{6,7},{7,6},{8,9},{9,8},{10,11... | collective-permute-start | bytes 589832 | tf_op jit(solution)/shard_map/ppermute | solution.py:467
  136.1 6.0 %collective-permute-start.35 = (bf16[192,1024]{1,0:T(8,128)(2,1)S(1)}, bf16[192,1024]{1,0:T(8,128)(2,1)S(1)}, u32[]{:S(2)}, u32[]{:S(2)}) collective-permute-start(bf16[192,1024]{1,0:T(8,128)(2,1)S(1)} %pad_maximum_fusion.refs_0_), channel_id=1, source_target_pairs={{0,1},{1,0},{2,3},{3,2},{4,5},{5,4},{6,7},{7,6},{8,9},{9,8},{10,11... | collective-permute-start | bytes 1179656 | tf_op jit(solution)/shard_map/ppermute | solution.py:467
  136.2 6.0 %collective-permute-start.38 = (bf16[192,1024]{1,0:T(8,128)(2,1)S(1)}, bf16[192,1024]{1,0:T(8,128)(2,1)S(1)}, u32[]{:S(2)}, u32[]{:S(2)}) collective-permute-start(bf16[192,1024]{1,0:T(8,128)(2,1)S(1)} %collective-permute-done.34.refs_3_), channel_id=1, source_target_pairs={{0,1},{1,0},{2,3},{3,2},{4,5},{5,4},{6,7},{7,6},{8,9},{9,8},{10,11... | collective-permute-start | bytes 1179656 | tf_op jit(solution)/shard_map/ppermute | solution.py:467
  136.6 5.5 %collective-permute-start.37 = (bf16[192,1024]{1,0:T(8,128)(2,1)S(1)}, bf16[192,1024]{1,0:T(8,128)(2,1)S(1)}, u32[]{:S(2)}, u32[]{:S(2)}) collective-permute-start(bf16[192,1024]{1,0:T(8,128)(2,1)S(1)} %collective-permute-done.33.refs_2_), channel_id=1, source_target_pairs={{0,1},{1,0},{2,3},{3,2},{4,5},{5,4},{6,7},{7,6},{8,9},{9,8},{10,11... | collective-permute-start | bytes 1179656 | tf_op jit(solution)/shard_map/ppermute | solution.py:467
  137.0 5.1 %collective-permute-start.36 = (bf16[192,1024]{1,0:T(8,128)(2,1)S(1)}, bf16[192,1024]{1,0:T(8,128)(2,1)S(1)}, u32[]{:S(2)}, u32[]{:S(2)}) collective-permute-start(bf16[192,1024]{1,0:T(8,128)(2,1)S(1)} %collective-permute-done.32.refs_1_), channel_id=1, source_target_pairs={{0,1},{1,0},{2,3},{3,2},{4,5},{5,4},{6,7},{7,6},{8,9},{9,8},{10,11... | collective-permute-start | bytes 1179656 | tf_op jit(solution)/shard_map/ppermute | solution.py:467

commit v3 on v2

v3 whole, which is shorter than its diff:
```python
from functools import partial

import jax
import jax.numpy as jnp
from jax import lax
from jax.experimental import pallas as pl
from jax.experimental.pallas import tpu as pltpu
from jax.sharding import PartitionSpec as P

EPS = 1e-6
BIG = -(2.0**30)
LEFT, RIGHT, ONES = 17, 18, 19
FFN_CHUNKS = 1
SMALL = 16
VMEM = 24 * 1024 * 1024
MUCH = 56 * 1024 * 1024

f32, bf16, i32 = jnp.float32, jnp.bfloat16, jnp.int32


def thresholds(buckets, max_distance):
    half = buckets // 2
    exact = half // 2
    steps = half - exact
    out = list(range(1, exact))
    for j in range(steps):
        target = exact ** (steps - j) * max_distance**j
        m = exact
        while m**steps < target:
            m += 1
        out.append(m)
    return out


def bucket_of(offset, buckets):
    distance = jnp.abs(offset)
    bucket = (offset > 0).astype(i32) * (buckets // 2)
    for t in thresholds(buckets, 128):
        bucket = bucket + (distance >= t).astype(i32)
    return bucket


def nn(a, b):
    return lax.dot_general(a, b, (((1,), (0,)), ((), ())), preferred_element_type=f32)


def nt(a, b):
    return lax.dot_general(a, b, (((1,), (1,)), ((), ())), preferred_element_type=f32)


def tn(a, b):
    return lax.dot_general(a, b, (((0,), (0,)), ((), ())), preferred_element_type=f32)


def iota(shape, dim):
    return lax.broadcasted_iota(i32, shape, dim)


def rms(values, gain):
    scale = lax.rsqrt(jnp.mean(values * values, axis=-1, keepdims=True) + EPS)
    return values * scale * gain


def call(kernel, name, us, out_shape, smem_args, args, scratch=(), much=False, anywhere=0):
    smem = pl.BlockSpec(memory_space=pltpu.SMEM)
    vmem = pl.BlockSpec(memory_space=pltpu.VMEM)
    return pl.pallas_call(
        kernel,
        in_specs=[smem] * len(smem_args) + [vmem] * (len(args) - anywhere) + [pl.BlockSpec(memory_space=pltpu.HBM)] * anywhere,
        out_specs=jax.tree.map(lambda _: vmem, out_shape),
        out_shape=out_shape,
        scratch_shapes=list(scratch),
        compiler_params=pltpu.CompilerParams(vmem_limit_bytes=MUCH if much else VMEM),
        cost_estimate=pl.CostEstimate(flops=int(us * 1e6), bytes_accessed=int(us * 2e3), transcendentals=0),
        name=name,
    )(*smem_args, *args)


def shape(*dims, dtype=bf16):
    return jax.ShapeDtypeStruct(dims, dtype)


def low_half(t):
    return iota((t, 128), 1) < 64


def turn(pair):
    return pltpu.roll(pair, 64, 1)


def prepare_kernel(ids, lens, gain, table, x, wq, wk, wv, q, ext, bands, wt, line, x_here, wq_here, wk_here, wv_here, sems):
    pairs = ((x, x_here), (wq, wq_here), (wk, wk_here), (wv, wv_here))
    copies = [pltpu.make_async_copy(a, b, sems.at[i]) for i, (a, b) in enumerate(pairs)]
    for copy in copies:
        copy.start()
    t = x.shape[0]
    heads, buckets = table.shape
    low, high = segment_bounds(lens)
    lanes = iota((t, 128), 1)
    pos = iota((t, 128), 0) + ids[0] * t
    other = jnp.where((pos >= low) & (pos < high), 0.0, BIG)
    ext[...] = jnp.where(lanes < LEFT, other, 0.0)
    u = iota((buckets, 4 * t), 1)
    bucket = bucket_of(jnp.where(u < 3 * t, u - t, u - 5 * t), buckets)
    pick = (bucket == iota((buckets, 4 * t), 0)).astype(f32).astype(bf16)
    line[...] = jnp.zeros_like(line)
    line[:heads] = nn(table[...], pick)
    for h in range(heads):
        band = pltpu.roll(jnp.broadcast_to(line[h : h + 1], (t, 4 * t)), 0, 1, stride=1, stride_axis=0)
        for r in range(3):
            bands[h, r] = band[:, r * t : (r + 1) * t].astype(bf16)
        bands[h, 3] = jnp.zeros((t, t), bf16)
    for copy in copies:
        copy.wait()
    n1 = rms(x_here[...].astype(f32), gain[...].astype(f32)).astype(bf16)
    q[...] = nn(n1, wq_here[...]).astype(bf16)
    w = wq.shape[1]
    for k, ref in enumerate((wq_here, wk_here, wv_here)):
        wt[k * w : (k + 1) * w] = ref[...].astype(f32).T.astype(bf16)


def prepare(ids, lens, x, gain, table, wq, wk, wv):
    t, d = x.shape
    heads, w = table.shape[0], wq.shape[1]
    return call(
        prepare_kernel, "prepare", 4,
        [shape(t, w), shape(t, 128, dtype=f32), shape(heads, 4, t, t), shape(3 * w, d), shape(8, 4 * t, dtype=f32),
         shape(t, d), shape(d, w), shape(d, w), shape(d, w)],
        (ids, lens), (gain, table, x, wq, wk, wv), anywhere=4, scratch=[pltpu.SemaphoreType.DMA((4,))],
    )


def segment_bounds(lens):
    lane = iota((1, 128), 1)
    low = jnp.where(lane == 0, -1, 2**30)
    high = jnp.full((1, 128), -1, i32)
    total = 0
    for k in range(lens.shape[0]):
        total = total + lens[k]
        high = jnp.where(lane == k, total, high)
        low = jnp.where(lane == k + 1, total, low)
    return low, jnp.where(lane == lens.shape[0], 2**30, high)


def attend_kernel(n, first, count, ids, lens, *refs):
    x = refs[:count]
    gain, wk, wv, q, ext, bands, line, n1, e, acc, stat = refs[count : count + 11]
    pairs = q.shape[1] // 128
    kv, p = refs[count + 11 : count + 11 + pairs], refs[count + 11 + pairs : -1]
    s = refs[-1]
    me = ids[0]
    t = x[0].shape[0]
    low, high = segment_bounds(lens)
    row = iota((t, 128), 0)
    lanes = iota((t, 128), 1)
    for i in range(count):
        at = slice(i * t, (i + 1) * t)
        n1[at] = rms(x[i][...].astype(f32), gain[...].astype(f32)).astype(bf16)
        block = me ^ (first + i)
        pos = row + block * t
        away = block - me
        flag = jnp.where(away <= -2, LEFT, jnp.where(away >= 2, RIGHT, ONES))
        here = ((pos >= low) & (pos < high)) | (lanes == flag) | (lanes == ONES)
        e[at] = here.astype(f32).astype(bf16)
    upper = iota((t, 128), 1) >= 64
    near = [i for i in range(count) if (first + i) & (first + i + 1) == 0]

    def project(g, i):
        rows, at = slice(i * t, (i + 1) * t), slice(g * 128, g * 128 + 128)
        both = nn(n1[rows], jnp.concatenate([wk[:, at], wv[:, at]], axis=1))
        keys, values = both[:, :128], turn(both[:, 128:])
        kv[g][0, rows] = jnp.where(upper, values, keys).astype(bf16)
        kv[g][1, rows] = jnp.where(upper, keys, values).astype(bf16)

    def query(h):
        lane_ext = jnp.where(lanes == LEFT, line[h : h + 1, 0:1],
                             jnp.where(lanes == RIGHT, line[h : h + 1, 3 * t - 1 : 3 * t], ext[...]))
        q2 = q[:, h // 2 * 128 : h // 2 * 128 + 128].astype(f32)
        return jnp.concatenate([jnp.where(upper == (h % 2 == 1), q2, 0.0), lane_ext], axis=1).astype(bf16)

    def keys_of(h, i):
        rows = slice(i * t, (i + 1) * t)
        return jnp.concatenate([kv[h // 2][h % 2, rows], e[rows]], axis=1)

    def score(h, i, qa, top):
        block = nt(qa, keys_of(h, i))
        if i in near:
            away = (me ^ (first + i)) - me
            block = block + bands[h, jnp.where(jnp.abs(away) <= 1, away + 1, 3)].astype(f32)
        s[h % 2, :, i * t : (i + 1) * t] = block
        here = block[:, :128]
        for c in range(1, t // 128):
            here = jnp.maximum(here, block[:, c * 128 : (c + 1) * 128])
        return here if top is None else jnp.maximum(top, here)

    def mix(h, i, top, out):
        raised = jnp.exp(s[h % 2, :, i * t : (i + 1) * t] - top).astype(bf16)
        p[h // 2][h % 2, :, i * t : (i + 1) * t] = raised
        more = nn(raised, keys_of(h, i))
        return more if out is None else out + more

    for i in range(count):
        project(0, i)
    stats = jnp.zeros((t, 128), f32)
    last = None
    sums = []
    for h in range(2 * pairs + 1):
        qa = query(h) if h < 2 * pairs else None
        top = out = None
        for i in range(count):
            if h < 2 * pairs:
                top = score(h, i, qa, top)
            if h > 0:
                out = mix(h - 1, i, last, out)
            if h % 2 == 1 and h // 2 + 1 < pairs:
                project(h // 2 + 1, i)
        if h > 0:
            stats = jnp.where(lanes == h - 1, last, stats)
            stats = jnp.where(lanes == 7 + h, out[:, 128 + ONES : 129 + ONES], stats)
            sums.append(out[:, :128])
        if h < 2 * pairs:
            last = jnp.max(top, axis=1, keepdims=True)
    for g in range(pairs):
        acc[:, g * 128 : g * 128 + 128] = turn(jnp.where(upper, sums[2 * g], sums[2 * g + 1]))
    stat[...] = stats


def attend(n, first, ids, lens, blocks, gain, wk, wv, q, ext, bands, line):
    count = len(blocks)
    t, d = blocks[0].shape
    pairs = wk.shape[1] // 128
    c = count * t
    out = call(
        partial(attend_kernel, n, first, count), "attend", 2 * count,
        [shape(c, d), shape(c, 128), shape(t, wk.shape[1], dtype=f32), shape(t, 128, dtype=f32)]
        + [shape(2, c, 128)] * pairs + [shape(2, t, c)] * pairs,
        (ids, lens), (*blocks, gain, wk, wv, q, ext, bands, line), scratch=[pltpu.VMEM((2, t, c), f32)], much=n > 8,
    )
    return dict(n1=out[0], e=out[1], acc=out[2], stat=out[3], kv=out[4 : 4 + pairs], p=out[4 + pairs :])


def feed_forward_kernel(phases, ids, lens, gain, x, wo, wg, wu, wd, cot, *refs):
    accs, stats = refs[:phases], refs[phases : 2 * phases]
    out, dh, do, scale, gwo, keep, send, gn, grads, mixed_all, n2_all, u_all, gb_all, dg_all, du_all, dh_all = refs[2 * phases :]
    t, d = x.shape
    pairs = wo.shape[0] // 128
    chunk = t // FFN_CHUNKS
    lanes = iota((chunk, 128), 1)
    g2 = gain[...].astype(f32)
    last = lens[0]
    for k in range(1, lens.shape[0]):
        last = last + lens[k]
    work = [dict(rows=slice(c * chunk, (c + 1) * chunk)) for c in range(FFN_CHUNKS)]

    def weigh(v):
        rows = v["rows"]
        tops = [ref[rows] for ref in stats]
        top = tops[0]
        for other in tops[1:]:
            top = jnp.maximum(top, other)
        weights = [jnp.exp(a - top) for a in tops]
        total = jnp.where(lanes < 2 * pairs, 0.0, 1.0)
        for w, ref in zip(weights, stats, strict=True):
            total = total + w * pltpu.roll(ref[rows], 120, 1)
        weights = [jnp.where(lanes < 2 * pairs, w / total, 0.0) for w in weights]
        v["scales"] = weights[0]
        for i, w in enumerate(weights[1:], 1):
            v["scales"] = v["scales"] + pltpu.roll(w, 8 * i, 1)
        v["o"] = []
        for g in range(pairs):
            at = slice(g * 128, g * 128 + 128)
            value = jnp.zeros((chunk, 128), f32)
            for i, w in enumerate(weights):
                value = value + accs[i][rows, at] * jnp.where(lanes < 64, w[:, 2 * g : 2 * g + 1], w[:, 2 * g + 1 : 2 * g + 2])
            v["o"].append(value)
            mixed_all[rows, at] = value.astype(bf16)
        pos = ids[0] * t + rows.start + iota((chunk, 1), 0)
        v["g"] = cot[rows].astype(f32) * (pos < last).astype(f32)
        gb_all[rows] = v["g"].astype(bf16)

    def norm(v):
        rows = v["rows"]
        v["h1"] = x[rows].astype(f32) + nn(mixed_all[rows], wo[...])
        v["s2"] = lax.rsqrt(jnp.mean(v["h1"] * v["h1"], axis=-1, keepdims=True) + EPS)
        v["hat"] = v["h1"] * v["s2"]
        n2_all[rows] = (v["hat"] * g2).astype(bf16)

    def project(v):
        rows = v["rows"]
        v["gate"], v["up"] = nn(n2_all[rows], wg[...]), nn(n2_all[rows], wu[...])
        v["du"] = nt(gb_all[rows], wd[...]).astype(bf16).astype(f32)

    def activate(v):
        rows, gate, up = v["rows"], v["gate"], v["up"]
        c0 = 0.7978845608028654
        square = gate * gate
        th = jnp.tanh(c0 * gate * (1.0 + 0.044715 * square))
        half = 0.5 * (1.0 + th)
        act = gate * half
        dact = half + 0.5 * gate * (1.0 - th * th) * (c0 * (1.0 + 3 * 0.044715 * square))
        u_all[rows] = (act * up).astype(bf16)
        dg_all[rows] = (v["du"] * up * dact).astype(bf16)
        du_all[rows] = (v["du"] * act).astype(bf16)

    def down(v):
        rows = v["rows"]
        out[rows] = (v["h1"] + nn(u_all[rows], wd[...])).astype(bf16)
        v["dn2"] = nt(dg_all[rows], wg[...]) + nt(du_all[rows], wu[...])

    def norm_back(v):
        rows, dn2, hat, s2 = v["rows"], v["dn2"], v["hat"], v["s2"]
        v["gn"] = jnp.sum(dn2 * hat, axis=0, keepdims=True)
        scaled = dn2 * g2
        dh1 = v["g"] + s2 * (scaled - hat * jnp.mean(hat * scaled, axis=-1, keepdims=True))
        dh[rows] = dh1
        dh_all[rows] = dh1.astype(bf16)

    def mix_back(v):
        rows = v["rows"]
        dmix = nt(dh_all[rows], wo[...]).astype(bf16)
        do[rows] = dmix
        scales = v["scales"]
        for h in range(2 * pairs):
            at = slice(h // 2 * 128, h // 2 * 128 + 128)
            product = dmix[:, at].astype(f32) * v["o"][h // 2]
            own = jnp.where((lanes < 64) == (h % 2 == 0), product, 0.0)
            scales = jnp.where(lanes == 64 + h, jnp.sum(own, axis=1, keepdims=True), scales)
        scale[rows] = scales

    def weights_kernel():
        low = tn(u_all[...], gb_all[...]).astype(bf16)
        grads[2 * d : 3 * d, :d] = low[:d]
        grads[2 * d : 3 * d, d:] = low[d:]
        grads[0:d] = tn(n2_all[...], dg_all[...]).astype(bf16)
        grads[d : 2 * d] = tn(n2_all[...], du_all[...]).astype(bf16)

    stages = [weigh, norm, project, activate, down, norm_back, mix_back]
    for step in range(len(stages) + FFN_CHUNKS - 1):
        for c, v in enumerate(work):
            if 0 <= step - c < len(stages):
                stages[step - c](v)
        if step == 3 + FFN_CHUNKS - 1:
            weights_kernel()
    gn[...] = sum(v["gn"] for v in work)
    gwo[...] = tn(mixed_all[...], dh_all[...]).astype(bf16)
    rows = keep.shape[0]
    keep[...] = grads[pl.ds(pl.multiple_of(ids[1] * rows, 16), rows)]
    send[...] = grads[pl.ds(pl.multiple_of((1 - ids[1]) * rows, 16), rows)]


def feed_forward(ids, lens, gain, x, wo, wg, wu, wd, cot, parts):
    t, d = x.shape
    ff, w = wg.shape[1], wo.shape[0]
    half = 3 * d // 2
    return call(
        partial(feed_forward_kernel, len(parts)), "feed_forward", 8,
        [shape(t, d), shape(t, d, dtype=f32), shape(t, w), shape(t, 128, dtype=f32), shape(w, d),
         shape(half, ff), shape(half, ff), shape(1, d, dtype=f32)],
        (ids, lens), (gain, x, wo, wg, wu, wd, cot, *[v["acc"] for v in parts], *[v["stat"] for v in parts]),
        scratch=[pltpu.VMEM((3 * d, ff), bf16)]
        + [pltpu.VMEM((t, k), bf16) for k in (w, d, ff, d, ff, ff, d)],
    )


def attend_back_kernel(n, pairs, counts, ids, q, do, scale, *refs):
    phases, size = len(counts), len(pairs)
    p = [refs[i * size : (i + 1) * size] for i in range(phases)]
    refs = refs[phases * size :]
    kv = [refs[i * size : (i + 1) * size] for i in range(phases)]
    e, refs = refs[phases * size : phases * size + phases], refs[phases * size + phases :]
    dk, dv, refs = refs[:size], refs[size : 2 * size], refs[2 * size :]
    dq, line, ds = refs
    me = ids[0]
    t = q.shape[0]
    lower = low_half(t)
    back = (iota((t, t), 0) + iota((t, t), 1) == t - 1).astype(f32).astype(bf16)
    lane = iota((1, 128), 1)
    line[...] = jnp.zeros_like(line)
    slots = [(i, j) for i, count in enumerate(counts) for j in range(count)]

    def operands(k):
        h = 2 * pairs[k // 2] + k % 2
        at = slice(h // 2 * 128, h // 2 * 128 + 128)
        qt = jnp.where(lower == (k % 2 == 0), q[:, at].astype(f32), 0.0).T
        doh = jnp.where(lower == (k % 2 == 1), turn(do[:, at].astype(f32)), 0.0)
        out = []
        for i in range(phases):
            factor = scale[:, 8 * i + h : 8 * i + h + 1]
            scaled = doh * factor
            shift = scale[:, 64 + h : 65 + h] * factor
            out.append((scaled.astype(bf16), shift, jnp.concatenate([qt, scaled.T], axis=1).astype(bf16)))
        return out

    def start(k, s, ops):
        i, j = slots[s]
        return nt(ops[i][0], kv[i][k // 2][k % 2, j * t : (j + 1) * t])

    def finish(k, s, ops, d_prob, acc):
        i, j = slots[s]
        rows = slice(j * t, (j + 1) * t)
        probs = p[i][k // 2][k % 2, :, rows]
        d_score = (probs.astype(f32) * (d_prob - ops[i][1])).astype(bf16)
        ds[k % 2, :, s * t : (s + 1) * t] = d_score
        more = nn(d_score, jnp.concatenate([kv[i][k // 2][k % 2, rows], e[i][rows]], axis=1))
        both = nn(ops[i][2], jnp.concatenate([d_score, probs], axis=0)).astype(bf16)
        mine, other = (both[:64], both[64:]) if k % 2 == 0 else (both[64:], both[:64])
        dk[k // 2][k % 2 * 64 : k % 2 * 64 + 64, s * t : (s + 1) * t] = mine
        dv[k // 2][k % 2 * 64 : k % 2 * 64 + 64, s * t : (s + 1) * t] = other
        return more if acc is None else acc + more

    def bias(k, acc):
        parts = []
        for r in (-1, 0, 1):
            there = me + r
            inside = (there >= 0) & (there < n)
            slot = jnp.where(inside, me ^ there, 0)
            block = ds[k % 2, :, pl.ds(pl.multiple_of(slot * t, t), t)]
            parts.append(nn(back, block) * inside.astype(f32))
        parts.append(jnp.zeros((t, t), f32))
        band = pltpu.roll(jnp.concatenate(parts, axis=1), 0, 1, stride=1, stride_axis=0)
        line[k : k + 1, : 4 * t] = jnp.sum(band, axis=0, keepdims=True)
        ends = jnp.sum(acc[:, 128:], axis=0, keepdims=True)
        line[k : k + 1, 4 * t :] = jnp.where((lane == LEFT) | (lane == RIGHT), ends, 0.0)

    tasks = [(k, s) for k in range(2 * size) for s in range(len(slots))]
    ops = [operands(0)]
    d_prob = start(0, 0, ops[0])
    accs = [None] * (2 * size)
    for index, (k, s) in enumerate(tasks):
        if s == 0 and k + 1 < 2 * size:
            ops.append(operands(k + 1))
        later = None
        if index + 1 < len(tasks):
            k2, s2 = tasks[index + 1]
            later = start(k2, s2, ops[k2])
        accs[k] = finish(k, s, ops[k], d_prob, accs[k])
        d_prob = later
        if s == len(slots) - 1:
            bias(k, accs[k])
    for g in range(size):
        dq[:, g * 128 : g * 128 + 128] = jnp.where(lower, accs[2 * g][:, :128], accs[2 * g + 1][:, :128]).astype(bf16)


def attend_back(n, pairs, ids, q, do, scale, parts):
    t = q.shape[0]
    widths = [v["e"].shape[0] for v in parts]
    s = sum(widths)
    size = len(pairs)
    out = call(
        partial(attend_back_kernel, n, pairs, [w // t for w in widths]), "attend_back", 4 * size,
        [shape(128, s)] * (2 * size) + [shape(t, 128 * size), shape(8, 4 * t + 128, dtype=f32)],
        (ids,), (q, do, scale, *[v["p"][g] for v in parts for g in pairs],
                 *[v["kv"][g] for v in parts for g in pairs], *[v["e"] for v in parts]),
        scratch=[pltpu.VMEM((2, t, s), bf16)], much=n > 8,
    )
    return dict(dk=out[:size], dv=out[size : 2 * size], dq=out[-2], line=out[-1], pairs=size)


def gather_back_kernel(n, buckets, counts, pairs, ids, gain, gn, gwo, wq, wk, wv, wt, *refs):
    phases = len(counts)
    n1, refs = refs[:phases], refs[phases:]
    total_pairs = sum(pairs)
    dkv, refs = refs[: 2 * total_pairs], refs[2 * total_pairs :]
    dq, lines = refs[: len(pairs)], refs[len(pairs) : 2 * len(pairs)]
    even, odd, dn1q, keep, send, grads, sums, diagonal = refs[2 * len(pairs) :]
    d, w = wq.shape
    t = dn1q.shape[0]
    weights = jnp.concatenate([wk[...], wv[...]], axis=1)
    total = jnp.zeros((2 * w, d), f32)
    slot = 0
    for i, count in enumerate(counts):
        begin = sum(counts[:i]) * t
        both = jnp.concatenate([ref[:, begin : begin + count * t] for ref in dkv], axis=0)
        total = total + nn(both, n1[i][...])
        back = nn(weights, both).astype(bf16)
        for _ in range(count):
            ref = odd if slot % 2 else even
            ref[slot // 2] = back[:, slot * t - begin : slot * t - begin + t]
            slot += 1
    dq_all = jnp.concatenate([ref[...] for ref in dq], axis=1)
    from_q = tn(dq_all, n1[0][:t])
    dn1q[...] = nt(dq_all, wq[...])
    grads[:w] = from_q.astype(bf16)
    grads[w : 3 * w] = total.astype(bf16)
    grads[3 * w :] = gwo[...]
    gains = jnp.sum(from_q * wt[:w].astype(f32), axis=0, keepdims=True)
    gains = gains + jnp.sum(total * wt[w:].astype(f32), axis=0, keepdims=True)
    sums[...] = jnp.zeros_like(sums)
    sums[0:1] = gains / gain[...].astype(f32)
    sums[1:2] = gn[...]
    diagonal[...] = jnp.zeros_like(diagonal)
    begin = 0
    for ref, count in zip(lines, pairs, strict=True):
        diagonal[begin : begin + 2 * count] = ref[: 2 * count]
        begin += 2 * count
    width = diagonal.shape[1]
    u = iota((width, 128), 0)
    bucket = bucket_of(u - (2 * t - 1), buckets)
    bucket = jnp.where(u == 4 * t + LEFT, buckets // 2 - 1, jnp.where(u == 4 * t + RIGHT, buckets - 1, bucket))
    pick = (bucket == iota((width, 128), 1)).astype(f32)
    sums[8:16, :128] = lax.dot_general(diagonal[...], pick, (((1,), (0,)), ((), ())),
                                       precision=lax.Precision.HIGHEST, preferred_element_type=f32)
    small = sums[...].astype(bf16)
    rows = 2 * w
    keep[:rows] = grads[pl.ds(pl.multiple_of(ids[1] * rows, 16), rows)]
    send[:rows] = grads[pl.ds(pl.multiple_of((1 - ids[1]) * rows, 16), rows)]
    keep[rows:] = small
    send[rows:] = small


def gather_back(n, buckets, ids, gain, gn, gwo, wq, wk, wv, wt, parts, backs):
    d, w = wq.shape
    t = backs[0]["dq"].shape[0]
    pairs = [v["pairs"] for v in backs]
    counts = [v["e"].shape[0] // t for v in parts]
    pieces = [ref for v in backs for ref in v["dk"]] + [ref for v in backs for ref in v["dv"]]
    half = 2 * w + SMALL
    return call(
        partial(gather_back_kernel, n, buckets, counts, pairs), "gather_back", 6,
        [shape(n // 2, d, t), shape(n // 2, d, t), shape(t, d, dtype=f32), shape(half, d), shape(half, d)],
        (ids,), (gain, gn, gwo, wq, wk, wv, wt, *[v["n1"] for v in parts], *pieces, *[v["dq"] for v in backs],
                 *[v["line"] for v in backs]),
        scratch=[pltpu.VMEM((4 * w, d), bf16), pltpu.VMEM((SMALL, d), f32), pltpu.VMEM((8, 4 * t + 128), f32)], much=n > 8,
    )


def split_kernel(which, count, extra, ids, *refs):
    inputs, outs = refs[:-count], refs[-count:]
    rows = (inputs[0].shape[0] - extra) // count
    own = ids[which]
    for j in range(count):
        at = pl.ds(pl.multiple_of((own ^ j) * rows, 16), rows)
        total = inputs[0][at].astype(f32)
        for ref in inputs[1:]:
            total = total + ref[at].astype(f32)
        outs[j][:rows] = total.astype(bf16)
    if extra:
        at = pl.ds(rows * count, extra)
        total = inputs[0][at].astype(f32)
        for ref in inputs[1:]:
            total = total + ref[at].astype(f32)
        for j in range(count):
            outs[j][rows:] = total.astype(bf16)


def add_and_split(which, count, extra, ids, *arrays):
    rows = (arrays[0].shape[0] - extra) // count + extra
    out = shape(rows, arrays[0].shape[1])
    return call(partial(split_kernel, which, count, extra), "add_parts", 1, [out] * count, (ids,), arrays)


def by_chip_kernel(ids, keep, recv, *outs):
    rows = keep.shape[0] // 4
    for half, own in ((0, ids[2] % 2), (1, ids[2] // 2)):
        for j in range(2):
            at = pl.ds(pl.multiple_of((2 * half + (own ^ j)) * rows, 16), rows)
            outs[2 * half + j][...] = (keep[at].astype(f32) + recv[at].astype(f32)).astype(bf16)


def by_next_chip_kernel(ids, keep_x, recv_x, keep_y, recv_y, *outs):
    rows = keep_x.shape[0] // 2
    for half, own, a, b in ((0, ids[2] // 2, keep_x, recv_x), (1, ids[2] % 2, keep_y, recv_y)):
        for j in range(2):
            at = pl.ds(pl.multiple_of((own ^ j) * rows, 16), rows)
            outs[2 * half + j][...] = (a[at].astype(f32) + b[at].astype(f32)).astype(bf16)


def by_row_kernel(ids, keep_x, recv_x, keep_y, recv_y, mine, other):
    first = keep_x[...].astype(f32) + recv_x[...].astype(f32)
    second = keep_y[...].astype(f32) + recv_y[...].astype(f32)
    even = ids[3] % 2 == 0
    mine[...] = jnp.where(even, first, second).astype(bf16)
    other[...] = jnp.where(even, second, first).astype(bf16)


def pick_kernel(ids, mine, other, first, second):
    even = ids[3] % 2 == 0
    a, b = mine[...].astype(f32), other[...].astype(f32)
    first[...] = jnp.where(even, a, b).astype(bf16)
    second[...] = jnp.where(even, b, a).astype(bf16)


def join_kernel(ids, a, b, c, d, first, second):
    rows = a.shape[0]
    first[:rows], first[rows:] = a[...], b[...]
    second[:rows], second[rows:] = c[...], d[...]


def swap(array, axis, j):
    size = lax.axis_size(axis)
    return lax.ppermute(array, axis, [(i, i ^ j) for i in range(size)])


def order(first, *values):
    first, values = lax.optimization_barrier((first, values))
    return values if len(values) > 1 else values[0]


def sum_all(ids, keep, recv, extra):
    both = add_and_split(0, 1, extra, ids * 0, keep, recv)[0].astype(f32)
    size = both.shape[0] - extra
    placed = jnp.zeros((2 * size, both.shape[1]), f32)
    placed = lax.dynamic_update_slice_in_dim(placed, both[:size], ids[1] * size, 0)
    full, tail = lax.psum((placed, both[size:] * 0.5), ("rows", "seq"))
    mine = lax.dynamic_slice_in_dim(full, ids[1] * size, size, 0)
    other = lax.dynamic_slice_in_dim(full, (1 - ids[1]) * size, size, 0)
    return [mine.astype(bf16)], [other.astype(bf16)], tail.astype(bf16)


def to_chips(parts):
    return [parts[0]] + [swap(parts[j], "seq", 2 * j) for j in range(1, len(parts))]


def place_halves(ids, mine, other, full):
    size = full.shape[0] // 2
    if len(mine) == 1:
        full[pl.ds(pl.multiple_of(ids[1] * size, 16), size)] = mine[0][...]
        full[pl.ds(pl.multiple_of((1 - ids[1]) * size, 16), size)] = other[0][...]
        return
    piece = size // len(mine)
    for c, refs in ((ids[1], mine), (1 - ids[1], other)):
        for a, ref in enumerate(refs):
            at = c * size + (ids[2] ^ a) * piece
            for b in range(2):
                where = at + ((ids[3] % 2) ^ b) * (piece // 2)
                full[pl.ds(pl.multiple_of(where, 16), piece // 2)] = ref[b * (piece // 2) : (b + 1) * (piece // 2)]


def unpack_ffn_kernel(pieces, ids, *refs):
    gate, up, down, full = refs[2 * pieces :]
    size = full.shape[0] // 2
    x, y = ids[2] % 2, ids[2] // 2
    for c, parts in ((ids[1], refs[:pieces]), (1 - ids[1], refs[pieces : 2 * pieces])):
        if pieces == 1:
            full[pl.ds(pl.multiple_of(c * size, 16), size)] = parts[0][...]
            continue
        rows = size // 8
        for half, first, second in ((0, x, y), (1, y, x)):
            for a in range(2):
                for b in range(2):
                    where = c * size + (4 * half + 2 * (first ^ a) + (second ^ b)) * rows
                    piece = parts[2 * half + a][b * rows : (b + 1) * rows]
                    full[pl.ds(pl.multiple_of(where, 16), rows)] = piece
    d = gate.shape[0]
    gate[...] = full[:d].astype(f32)
    up[...] = full[d : 2 * d].astype(f32)
    down[:d] = full[2 * d :, :d].astype(f32)
    down[d:] = full[2 * d :, d:].astype(f32)


def unpack_attention_kernel(pieces, ids, *refs):
    gq, gk, gv, go, full = refs[2 * pieces :]
    place_halves(ids, refs[:pieces], refs[pieces : 2 * pieces], full)
    w = gq.shape[1]
    for k, ref in enumerate((gq, gk, gv)):
        ref[...] = full[k * w : (k + 1) * w].astype(f32).T
    go[...] = full[3 * w :].astype(f32)


def unpack_small_kernel(ids, tail, g1, g2, gb):
    small = tail[...].astype(f32)
    g1[...] = small[0:1]
    g2[...] = small[1:2]
    gb[...] = small[8 : 8 + gb.shape[0], : gb.shape[1]]


def input_grad_kernel(ids, *refs):
    *parts, dn1q, x, dh, gain, out = refs
    total = parts[0][...].astype(f32)
    for ref in parts[1:]:
        total = total + ref[...].astype(f32)
    dn1 = total.T + dn1q[...]
    value = x[...].astype(f32)
    s1 = lax.rsqrt(jnp.mean(value * value, axis=-1, keepdims=True) + EPS)
    hat = value * s1
    scaled = dn1 * gain[...].astype(f32)
    out[...] = dh[...] + s1 * (scaled - hat * jnp.mean(hat * scaled, axis=-1, keepdims=True))


def slots_kernel(count, ids, mine, other, *outs):
    for j in range(count):
        outs[j][...] = (mine[j].astype(f32) + other[j].astype(f32)).astype(bf16)


def shards(
    tokens, norm_attn, query_weight, key_weight, value_weight, out_weight, bucket_bias_table, norm_ffn,
    gate_weight, expansion_matrix, down_weight, lengths, cotangent,
):
    _, t, d = tokens.shape
    n = lax.axis_size("seq")
    buckets, heads = bucket_bias_table.shape
    width = query_weight.shape[1]
    ff = gate_weight.shape[1]
    seq = lax.axis_index("seq")
    ids = jnp.stack([seq, seq % 2, seq // 2, lax.axis_index("rows")]).astype(i32)
    x = tokens.reshape(t, d)
    cot = cotangent.reshape(t, d)
    lens = lengths.reshape(-1)
    gain1 = norm_attn.reshape(1, d)
    gain2 = norm_ffn.reshape(1, d)

    blocks = [None] * n
    blocks[0], blocks[1] = x, swap(x, "seq", 1)
    for j in range(2, n, 2):
        blocks[j] = swap(x, "seq", j)
    q, ext, bands, wt, line, x, wq, wk, wv = prepare(
        ids, lens, x, gain1, bucket_bias_table.T, query_weight, key_weight, value_weight
    )
    blocks[0] = x
    cuts = [0, 2, *range(8, n, 8), n]

    def phase(a, b):
        return attend(n, a, ids, lens, blocks[a:b], gain1, wk, wv, q, ext, bands, line)

    parts = [phase(0, 2)]
    for j in range(2, n, 2):
        blocks[j] = order(parts[0]["acc"], blocks[j])
        blocks[j + 1] = swap(blocks[j], "seq", 1)
    parts += [phase(a, b) for a, b in zip(cuts[1:-1], cuts[2:], strict=True)]
    output, dh, do, scale, gwo, keep, send, gn = feed_forward(
        ids, lens, gain2, x, out_weight, gate_weight, expansion_matrix, down_weight, cot, parts
    )
    half = n // 2
    pairs = width // 128
    whole = n != 8 or lax.axis_size("rows") != 4
    zero, near = ids * 0, ids[3:4] % 2

    def unpack_ffn(mine, other):
        return call(
            partial(unpack_ffn_kernel, len(mine)), "unpack_ffn", 4,
            [shape(d, ff, dtype=f32), shape(d, ff, dtype=f32), shape(ff, d, dtype=f32)],
            (ids,), (*mine, *other), scratch=[pltpu.VMEM((3 * d, ff), bf16)],
        )

    def unpack_attention(mine, other):
        return call(
            partial(unpack_attention_kernel, len(mine)), "unpack_attention", 3,
            [shape(d, width, dtype=f32)] * 3 + [shape(width, d, dtype=f32)],
            (ids,), (*mine, *other), scratch=[pltpu.VMEM((4 * width, d), bf16)],
        )

    def unpack_small(tail):
        return call(unpack_small_kernel, "unpack_small", 1,
                    [shape(1, d, dtype=f32)] * 2 + [shape(heads, buckets, dtype=f32)], (ids,), (tail,))

    def input_grad(slots):
        return call(input_grad_kernel, "input_grad", 2, shape(t, d, dtype=f32), (ids,), (*slots, dn1q, x, dh, gain1))

    def add_slots(recv):
        return call(partial(slots_kernel, half), "add_slots", 1, [shape(d, t)] * half, (ids,), (even, recv))

    f_core = swap(send, "seq", 1)
    backs = [attend_back(n, [0], ids, q, do, scale, parts)]
    f_keep = keep
    part = lambda rows: shape(f_keep.shape[0] // rows, ff)
    if not whole:
        f_core = order(backs[0]["dq"], f_core)
        f_x, f_x2, f_y, f_y2 = call(by_chip_kernel, "add_parts", 1, [part(4)] * 4, (ids,), (keep, f_core))
        do = order(f_x, do)
        f_x2, f_y2 = swap(f_x2, "seq", 2), swap(f_y2, "seq", 4)
    backs.append(attend_back(n, list(range(1, pairs)), ids, q, do, scale, parts))
    even, odd, dn1q, keep, send = gather_back(
        n, buckets, ids, gain1, gn, gwo, wq, wk, wv, wt, parts, backs
    )
    if not whole:
        send, odd = order((f_x2, f_y2), send, odd)
    a_core, d_core = swap(send, "seq", 1), swap(odd, "seq", 1)
    if whole:
        mine, other, _ = sum_all(ids, f_keep, f_core, 0)
        gate, up, down = unpack_ffn(mine, other)
        grad_tokens = input_grad(to_chips(add_slots(d_core)))
        mine, other, tail = sum_all(ids, keep, a_core, SMALL)
        gq, gk, gv, go = unpack_attention(mine, other)
        g1, g2, gb = unpack_small(tail)
    else:
        f_x, f_x2, f_y, f_y2 = call(
            by_next_chip_kernel, "add_parts", 1, [part(8)] * 4, (ids,), (f_x, f_x2, f_y, f_y2)
        )
        f_x2, f_y2 = swap(f_x2, "seq", 4), swap(f_y2, "seq", 2)
        a_core = order(f_x, a_core)
        a_parts = to_chips(add_and_split(2, half, SMALL, ids, keep, a_core))
        f_x2, f_y2 = order(a_parts[0], f_x2, f_y2)
        f_mine, f_other = call(by_row_kernel, "add_parts", 1, [part(8)] * 2, (ids,), (f_x, f_x2, f_y, f_y2))
        f_other = swap(f_other, "rows", 1)
        d_core = order(f_mine, d_core)
        d_parts = add_slots(d_core)
        f_other = order(d_parts, f_other)
        f_mine = add_and_split(0, 1, 0, zero, f_mine, f_other)[0]
        f_other = swap(f_mine, "rows", 2)
        d_parts = to_chips(order(f_mine, d_parts))
        a_parts = order(f_mine, a_parts)
        a_mine, a_other = add_and_split(0, 2, SMALL, near, *a_parts)
        a_other = swap(a_other, "rows", 1)
        f_other = order(a_mine, f_other)
        f_mine = add_and_split(0, 1, 0, zero, f_mine, f_other)[0]
        f_other = swap(f_mine, "rows", 1)
        a_other = order(f_mine, a_other)
        a_mine = add_and_split(0, 1, SMALL, zero, a_mine, a_other)[0]
        a_other = swap(a_mine, "rows", 2)
        f_other = order(a_mine, f_other)
        f_x, f_y = call(pick_kernel, "pick", 1, [part(8)] * 2, (ids,), (f_mine, f_other))
        f_x2, f_y2 = swap(f_x, "seq", 4), swap(f_y, "seq", 2)
        a_other = order(f_x, a_other)
        a_mine = add_and_split(0, 1, SMALL, zero, a_mine, a_other)[0]
        size = a_mine.shape[0] - SMALL
        a_other = swap(a_mine[:size], "rows", 1)
        d_parts = order(a_mine, d_parts)
        a_other = order(d_parts, a_other)
        a_line = jnp.concatenate([a_mine[:size], a_other], axis=0)
        a_own = [a_line] + [swap(a_line, "seq", 2 * j) for j in range(1, half)]
        grad_tokens = input_grad(order(a_line, d_parts))
        f_x2, f_y2, grad_tokens = order(grad_tokens, f_x2, f_y2, grad_tokens)
        f_x, f_y = call(join_kernel, "join", 1, [part(4)] * 2, (ids,), (f_x, f_x2, f_y, f_y2))
        f_own = [f_x, swap(f_x, "seq", 2), f_y, swap(f_y, "seq", 4)]
        g1, g2, gb = unpack_small(order(f_x, a_mine[size:]))
        a_own, g1 = order(g1, a_own, g1)
        f_own = order(a_own, f_own)
        gate, up, down = unpack_ffn(f_own, [swap(v, "seq", 1) for v in f_own])
        gq, gk, gv, go = unpack_attention(a_own, [swap(v, "seq", 1) for v in a_own])
    return (
        output.reshape(tokens.shape), grad_tokens.reshape(tokens.shape), g1.reshape(d), gq, gk, gv, go, gb.T,
        g2.reshape(d), gate, up, down,
    )


def solution(mesh):
    split = P("rows", "seq", None)
    in_specs = (split,) + (P(),) * 10 + (P("rows", None), split)
    out_specs = (split, split) + (P(),) * 10
    return jax.shard_map(shards, mesh=mesh, in_specs=in_specs, out_specs=out_specs, check_vma=False)
```

time: 146 us -> 124 us (0.85)
  waiting for transfers between devices: 54.2 us -> 35.3 us
    ppermute x39 -> x41, waiting for transfers between devices: 54.2 us -> 35.3 us  [swap(): return lax.ppermute(array, axis, [(i, i ^ j) for i in range(size)])]
    ppermute x39 -> x41, starting transfers between devices: 34.8 us -> 33.5 us  [swap(): return lax.ppermute(array, axis, [(i, i ^ j) for i in range(size)])]
    unnamed x30 -> x26, local copies, waits for them, and re-layouts: 6.08 us -> 5.31 us
    pallas_call x21 -> x23, Pallas kernels: 48.2 us -> 48 us  [call(): pl.pallas_call(kernel, in_specs=[smem] * len(smem_args) + [vmem] * (len(a...]
  transfers between devices with their start and end apart: 39 -> 41, of which waited for: 16 -> 20; matrix products, arithmetic and copies ran while one was open for 2% -> 1% of each run, Pallas kernels for 13% -> 25%
where the time goes in v3:
time: 124 us
  Pallas kernels  48 us (39%)
  waiting for transfers between devices  35.3 us (28%)
  starting transfers between devices  33.5 us (27%)
  local copies, waits for them, and re-layouts  6.01 us (5%)
    pallas_call x23, Pallas kernels, call(): pl.pallas_call(kernel, in_specs=[smem] * len(smem_args) + [vmem] * (len(a...  48 us
    ppermute x41, waiting for transfers between devices, swap(): return lax.ppermute(array, axis, [(i, i ^ j) for i in range(size)])  35.3 us
    ppermute x41, starting transfers between devices, swap(): return lax.ppermute(array, axis, [(i, i ^ j) for i in range(size)])  33.5 us
    unnamed x26, local copies, waits for them, and re-layouts  5.31 us
  transfers between devices with their start and end apart: 41, of which 20 were waited for; matrix products, arithmetic and copies ran while one was open for 1% of the time, Pallas kernels for 25%

profile of v3, /device:TPU:0, one launch (start us, length us, event | category | flops | bytes accessed | tf_op | source)
XLA Modules:
  0.0 123.9 jit_solution(8912313038011820152)
XLA Ops:
  1.2 2.6 %collective-permute-start.1 = (bf16[256,512]{1,0:T(8,128)(2,1)}, bf16[256,512]{1,0:T(8,128)(2,1)S(1)}, u32[]{:S(2)}, u32[]{:S(2)}) collective-permute-start(bf16[256,512]{1,0:T(8,128)(2,1)} %bitcast.14), channel_id=1, source_target_pairs={{0,2},{1,3},{2,0},{3,1},{4,6},{5,7},{6,4},{7,5},{8,10},{9,11},{10,... | collective-permute-start | bytes 786440 | tf_op jit(solution)/shard_map/ppermute | solution.py:591
  3.7 1.5 %collective-permute-start.3 = (bf16[256,512]{1,0:T(8,128)(2,1)}, bf16[256,512]{1,0:T(8,128)(2,1)S(1)}, u32[]{:S(2)}, u32[]{:S(2)}) collective-permute-start(bf16[256,512]{1,0:T(8,128)(2,1)} %bitcast.15), channel_id=1, source_target_pairs={{0,4},{1,5},{2,6},{3,7},{4,0},{5,1},{6,2},{7,3},{8,12},{9,13},{10,... | collective-permute-start | bytes 786440 | tf_op jit(solution)/shard_map/ppermute | solution.py:591
  5.3 0.7 reshape.55.gain.refs_2_.refs_6_.refs_7_
  6.0 1.0 copy-done.3
  7.0 1.0 copy-done.4
  8.0 1.0 copy-done.5
  9.0 0.9 copy-done.7
  10.0 0.7 copy-done.9
  10.6 0.7 copy-done.11
  11.3 2.3 %prepare.1 = (bf16[256,384]{1,0:T(8,128)(2,1)S(1)}, f32[256,128]{1,0:T(8,128)S(1)}, bf16[6,4,256,256]{3,2,1,0:T(8,128)(2,1)S(1)}, bf16[1152,512]{1,0:T(8,128)(2,...) custom-call(s32[4]{0:T(128)S(1)} %pad_add_fusion.ids, ...), custom_call_target="tpu_custom_call" | custom-call | flops 4000000 | bytes 8000 | tf_op jit(solution)/shard_map/prepare/pallas_call | solution.py:67
  13.7 3.3 %attend.2 = (bf16[512,512]{1,0:T(8,128)(2,1)S(1)}, bf16[512,128]{1,0:T(8,128)(2,1)S(1)}, f32[256,384]{1,0:T(8,128)S(1)}, f32[256,128]{1,0:T(8,128)S(1)}, bf16[2,...) custom-call(s32[4]{0:T(128)S(1)} %pad_add_fusion.ids, ...), custom_call_target="tpu_custom_call" | custom-call | flops 4000000 | bytes 8000 | tf_op jit(solution)/shard_map/attend/pallas_call | solution.py:67
  17.1 0.9 collective-permute-done.3.refs_2_
  18.6 0.9 collective-permute-done.4.refs_3_
  19.8 6.2 %attend.3 = (bf16[1536,512]{1,0:T(8,128)(2,1)S(1)}, bf16[1536,128]{1,0:T(8,128)(2,1)S(1)}, f32[256,384]{1,0:T(8,128)S(1)}, f32[256,128]{1,0:T(8,128)S(1)}, bf16[...) custom-call(s32[4]{0:T(128)S(1)} %pad_add_fusion.ids, ...), custom_call_target="tpu_custom_call" | custom-call | flops 12000000 | bytes 24000 | tf_op jit(solution)/shard_map/attend/pallas_call | solution.py:67
  26.1 5.9 %feed_forward.1 = (bf16[256,512]{1,0:T(8,128)(2,1)}, f32[256,512]{1,0:T(8,128)S(1)}, bf16[256,384]{1,0:T(8,128)(2,1)S(1)}, f32[256,128]{1,0:T(8,128)S(1)}, bf16[...) custom-call(s32[4]{0:T(128)S(1)} %pad_add_fusion.ids, ...), custom_call_target="tpu_custom_call" | custom-call | flops 8000000 | bytes 16000 | tf_op jit(solution)/shard_map/feed_forward/pallas_call | solution.py:67
  32.1 3.3 %attend_back.2 = (bf16[128,2048]{1,0:T(8,128)(2,1)S(1)}, bf16[128,2048]{1,0:T(8,128)(2,1)S(1)}, bf16[256,128]{1,0:T(8,128)(2,1)S(1)}, f32[8,1152]{1,0:T(8,128)S(1)}) custom-call(s32[4]{0:T(128)S(1)} %pad_add_fusion.ids, bf16[256,384]{1,0:T(8,128)(2,1)S(1)} %get-tuple-element.147.refs_5_.refs_9_.q, bf16[256,384]{1,0:T(8,128)(2,1)S(1)} %get-tuple-element.183.do, ...), custom_call_target="tpu_custom_call" | custom-call | flops 4000000 | bytes 8000 | tf_op jit(solution)/shard_map/attend_back/pallas_call | solution.py:67
  35.4 0.9 add_parts.9
  36.3 1.5 %collective-permute-start.8 = (bf16[192,1024]{1,0:T(8,128)(2,1)S(1)}, bf16[192,1024]{1,0:T(8,128)(2,1)S(1)}, u32[]{:S(2)}, u32[]{:S(2)}) collective-permute-start(bf16[192,1024]{1,0:T(8,128)(2,1)S(1)} %get-tuple-element.172), channel_id=1, source_target_pairs={{0,2},{1,3},{2,0},{3,1},{4,6},{5,7},{6,4},{7,5},{8,10},{9,11},{10,... | collective-permute-start | bytes 1179656 | tf_op jit(solution)/shard_map/ppermute | solution.py:591
  37.8 1.5 %collective-permute-start.9 = (bf16[192,1024]{1,0:T(8,128)(2,1)S(1)}, bf16[192,1024]{1,0:T(8,128)(2,1)S(1)}, u32[]{:S(2)}, u32[]{:S(2)}) collective-permute-start(bf16[192,1024]{1,0:T(8,128)(2,1)S(1)} %get-tuple-element.174), channel_id=1, source_target_pairs={{0,4},{1,5},{2,6},{3,7},{4,0},{5,1},{6,2},{7,3},{8,12},{9,13},{10,... | collective-permute-start | bytes 1179656 | tf_op jit(solution)/shard_map/ppermute | solution.py:591
  39.4 5.7 %attend_back.3 = (bf16[128,2048]{1,0:T(8,128)(2,1)S(1)}, bf16[128,2048]{1,0:T(8,128)(2,1)S(1)}, bf16[128,2048]{1,0:T(8,128)(2,1)S(1)}, bf16[128,2048]{1,0:T(8,12...) custom-call(s32[4]{0:T(128)S(1)} %pad_add_fusion.ids, ...), custom_call_target="tpu_custom_call" | custom-call | flops 8000000 | bytes 16000 | tf_op jit(solution)/shard_map/attend_back/pallas_call | solution.py:67
  45.0 4.7 %gather_back.1 = (bf16[4,512,256]{2,1,0:T(8,128)(2,1)S(1)}, bf16[4,512,256]{2,1,0:T(8,128)(2,1)S(1)}, f32[256,512]{1,0:T(8,128)S(1)}, bf16[784,512]{1,0:T(8,128)(2,1)S(1)}, bf16[784,512]{1,0:T(8,128)(2,1)S(1)}) custom-call(s32[4]{0:T(128)S(1)} %pad_add_fusion.ids, bf16[1,512]{1,0:T(2,128)(2,1)S(1)} %reshape.55.gain.refs_2_.refs_6_.refs_7_, ...), custom_call_target="tpu_custom_call" | custom-call | flops 6000000 | bytes 12000 | tf_op jit(solution)/shard_map/gather_back/pallas_call | solution.py:67
  50.2 1.0 add_parts.10
  51.2 0.8 collective-permute-start.11
  52.0 0.6 collective-permute-start.12
  52.6 1.0 collective-permute-done.10.refs_1_
  53.5 0.7 add_parts.11
  54.3 3.9 %collective-permute-done.11.recv_x = bf16[96,1024]{1,0:T(8,128)(2,1)S(1)} collective-permute-done((bf16[96,1024]{1,0:T(8,128)(2,1)S(1)}, bf16[96,1024]{1,0:T(8,128)(2,1)S(1)}, u32[]{:S(2)}, u32[]{:S(2)}) %collective-permute-start.11) | collective-permute-done | bytes 196640 | tf_op jit(solution)/shard_map/ppermute | solution.py:591
  58.5 0.7 add_parts.12
  59.2 1.6 %collective-permute-start.14 = (bf16[96,1024]{1,0:T(8,128)(2,1)S(1)}, bf16[96,1024]{1,0:T(8,128)(2,1)S(1)}, u32[]{:S(2)}, u32[]{:S(2)}) collective-permute-start(bf16[96,1024]{1,0:T(8,128)(2,1)S(1)} %get-tuple-element.219), channel_id=1, source_target_pairs={{0,8},{8,0},{16,24},{24,16},{1,9},{9,1},{17,25},{25,17},{2,10},{10... | collective-permute-start | bytes 589832 | tf_op jit(solution)/shard_map/ppermute | solution.py:591
  60.8 0.6 collective-permute-start.15
  61.4 1.4 %collective-permute-start.16 = (bf16[208,512]{1,0:T(8,128)(2,1)S(1)}, bf16[208,512]{1,0:T(8,128)(2,1)S(1)}, u32[]{:S(2)}, u32[]{:S(2)}) collective-permute-start(bf16[208,512]{1,0:T(8,128)(2,1)S(1)} %get-tuple-element.222), channel_id=1, source_target_pairs={{0,4},{1,5},{2,6},{3,7},{4,0},{5,1},{6,2},{7,3},{8,12},{9,13},{10,... | collective-permute-start | bytes 638984 | tf_op jit(solution)/shard_map/ppermute | solution.py:591
  62.8 1.5 %collective-permute-start.17 = (bf16[208,512]{1,0:T(8,128)(2,1)S(1)}, bf16[208,512]{1,0:T(8,128)(2,1)S(1)}, u32[]{:S(2)}, u32[]{:S(2)}) collective-permute-start(bf16[208,512]{1,0:T(8,128)(2,1)S(1)} %get-tuple-element.223), channel_id=1, source_target_pairs={{0,6},{1,7},{2,4},{3,5},{4,2},{5,3},{6,0},{7,1},{8,14},{9,15},{10,... | collective-permute-start | bytes 638984 | tf_op jit(solution)/shard_map/ppermute | solution.py:591
  64.3 0.8 add_slots.1
  65.1 0.6 add_parts.13.refs_0_
  65.7 2.7 %collective-permute-start.18 = (bf16[96,1024]{1,0:T(8,128)(2,1)S(1)}, bf16[96,1024]{1,0:T(8,128)(2,1)S(1)}, u32[]{:S(2)}, u32[]{:S(2)}) collective-permute-start(bf16[96,1024]{1,0:T(8,128)(2,1)S(1)} %add_parts.13.refs_0_), channel_id=1, source_target_pairs={{0,16},{8,24},{16,0},{24,8},{1,17},{9,25},{17,1},{25,9},{2,18},{10... | collective-permute-start | bytes 589832 | tf_op jit(solution)/shard_map/ppermute | solution.py:591
  68.4 0.6 collective-permute-start.24
  69.5 4.9 %collective-permute-done.17.refs_3_ = bf16[208,512]{1,0:T(8,128)(2,1)S(1)} collective-permute-done((bf16[208,512]{1,0:T(8,128)(2,1)S(1)}, bf16[208,512]{1,0:T(8,128)(2,1)S(1)}, u32[]{:S(2)}, u32[]{:S(2)}) %collective-permute-start.17) | collective-permute-done | bytes 213024 | tf_op jit(solution)/shard_map/ppermute | solution.py:591
  74.6 1.0 collective-permute-done.18.refs_1_
  75.6 0.6 add_parts.15.mine
  76.2 1.1 collective-permute-start.20
  77.3 0.8 collective-permute-start.25
  78.1 1.1 collective-permute-start.26
  79.2 1.3 %collective-permute-done.19.refs_1_ = bf16[112,512]{1,0:T(8,128)(2,1)S(1)} collective-permute-done((bf16[112,512]{1,0:T(8,128)(2,1)S(1)}, bf16[112,512]{1,0:T(8,128)(2,1)S(1)}, u32[]{:S(2)}, u32[]{:S(2)}) %collective-permute-start.19) | collective-permute-done | bytes 114720 | tf_op jit(solution)/shard_map/ppermute | solution.py:591
  80.5 0.6 add_parts.16.refs_0_
  81.1 2.7 %collective-permute-start.23 = (bf16[112,512]{1,0:T(8,128)(2,1)S(1)}, bf16[112,512]{1,0:T(8,128)(2,1)S(1)}, u32[]{:S(2)}, u32[]{:S(2)}) collective-permute-start(bf16[112,512]{1,0:T(8,128)(2,1)S(1)} %add_parts.16.refs_0_), channel_id=1, source_target_pairs={{0,16},{8,24},{16,0},{24,8},{1,17},{9,25},{17,1},{25,9},{2,18},{10... | collective-permute-start | bytes 344072 | tf_op jit(solution)/shard_map/ppermute | solution.py:591
  83.8 0.6 collective-permute-done.20.other
  84.4 0.6 pick.1
  85.0 3.1 %collective-permute-done.23.refs_1_ = bf16[112,512]{1,0:T(8,128)(2,1)S(1)} collective-permute-done((bf16[112,512]{1,0:T(8,128)(2,1)S(1)}, bf16[112,512]{1,0:T(8,128)(2,1)S(1)}, u32[]{:S(2)}, u32[]{:S(2)}) %collective-permute-start.23) | collective-permute-done | bytes 114720 | tf_op jit(solution)/shard_map/ppermute | solution.py:591
  88.2 0.6 add_parts.17
  88.8 1.1 collective-permute-start.21
  89.9 0.8 collective-permute-start.22
  90.7 2.7 %collective-permute-done.27 = bf16[96,512]{1,0:T(8,128)(2,1)S(1)} collective-permute-done((bf16[96,512]{1,0:T(8,128)(2,1)S(1)}, bf16[96,512]{1,0:T(8,128)(2,1)S(1)}, u32[]{:S(2)}, u32[]{:S(2)}) %collective-permute-start.27) | collective-permute-done | bytes 98336 | tf_op jit(solution)/shard_map/ppermute | solution.py:591
  93.5 1.8 %input_grad.1 = f32[256,512]{1,0:T(8,128)} custom-call(s32[4]{0:T(128)S(1)} %pad_add_fusion.ids, bf16[512,256]{1,0:T(8,128)(2,1)S(1)} %get-tuple-element.245.refs_0_, bf16[512,256]{1,0:T(8,128)(2,1)S(1)} %collective-permute-done.24.refs_1_, bf16[512,256]{1,0:T(8,128)(2,1)S(1)} %collective-permute-done.25.refs_2_, ...), custom_call_target="tpu_custom_call" | custom-call | flops 2000000 | bytes 4000 | tf_op jit(solution)/shard_map/input_grad/pallas_call | solution.py:67
  95.6 0.6 join.1
  96.2 0.9 collective-permute-start.35
  97.0 0.9 collective-permute-start.36
  98.0 1.8 %collective-permute-start.28 = (bf16[192,512]{1,0:T(8,128)(2,1)S(1)}, bf16[192,512]{1,0:T(8,128)(2,1)S(1)}, u32[]{:S(2)}, u32[]{:S(2)}) collective-permute-start(bf16[192,512]{1,0:T(8,128)(2,1)S(1)} %pad_maximum_fusion.refs_0_), channel_id=1, source_target_pairs={{0,2},{1,3},{2,0},{3,1},{4,6},{5,7},{6,4},{7,5},{8,10},{9,11},{10,... | collective-permute-start | bytes 589832 | tf_op jit(solution)/shard_map/ppermute | solution.py:591
  100.3 1.2 collective-permute-start.30
  101.5 1.1 unpack_small.1
  102.6 8.2 %collective-permute-done.28.refs_1_ = bf16[192,512]{1,0:T(8,128)(2,1)S(1)} collective-permute-done((bf16[192,512]{1,0:T(8,128)(2,1)S(1)}, bf16[192,512]{1,0:T(8,128)(2,1)S(1)}, u32[]{:S(2)}, u32[]{:S(2)}) %collective-permute-start.28) | collective-permute-done | bytes 196640 | tf_op jit(solution)/shard_map/ppermute | solution.py:591
  110.8 2.4 %collective-permute-done.29.refs_2_ = bf16[192,512]{1,0:T(8,128)(2,1)S(1)} collective-permute-done((bf16[192,512]{1,0:T(8,128)(2,1)S(1)}, bf16[192,512]{1,0:T(8,128)(2,1)S(1)}, u32[]{:S(2)}, u32[]{:S(2)}) %collective-permute-start.29) | collective-permute-done | bytes 196640 | tf_op jit(solution)/shard_map/ppermute | solution.py:591
  115.4 2.3 %collective-permute-done.34.refs_7_ = bf16[192,512]{1,0:T(8,128)(2,1)S(1)} collective-permute-done((bf16[192,512]{1,0:T(8,128)(2,1)S(1)}, bf16[192,512]{1,0:T(8,128)(2,1)S(1)}, u32[]{:S(2)}, u32[]{:S(2)}) %collective-permute-start.34) | collective-permute-done | bytes 196640 | tf_op jit(solution)/shard_map/ppermute | solution.py:591
  117.7 2.5 %unpack_attention.1 = (f32[512,384]{1,0:T(8,128)}, f32[512,384]{1,0:T(8,128)}, f32[512,384]{1,0:T(8,128)}, f32[384,512]{1,0:T(8,128)}) custom-call(s32[4]{0:T(128)S(1)} %pad_add_fusion.ids, bf16[192,512]{1,0:T(8,128)(2,1)S(1)} %pad_maximum_fusion.refs_0_, bf16[192,512]{1,0:T(8,128)(2,1)S(1)} %collective-permute-done.28.refs_1_, ...), custom_call_target="tpu_custom_call" | custom-call | flops 3000000 | bytes 6000 | tf_op jit(solution)/shard_map/unpack_attention/pallas_call | solution.py:67
  120.3 3.6 %unpack_ffn.1 = (f32[512,1024]{1,0:T(8,128)}, f32[512,1024]{1,0:T(8,128)}, f32[1024,512]{1,0:T(8,128)}) custom-call(s32[4]{0:T(128)S(1)} %pad_add_fusion.ids, bf16[192,1024]{1,0:T(8,128)(2,1)S(1)} %get-tuple-element.269.refs_0_, bf16[192,1024]{1,0:T(8,128)(2,1)S(1)} %collective-permute-done.35.refs_1_, bf16[192,1024]{1,0:T(8,128)(2,1)S(1)} %get-tuple-element.271.refs_2_, ...), custom_call_target="tpu_custom_call" | custom-call | flops 4000000 | bytes 8000 | tf_op jit(solution)/shard_map/unpack_ffn/pallas_call | solution.py:67
  (74 shorter events, 6.6 us)
Async XLA Ops:
  0.6 13.0 %collective-permute-start = (bf16[256,512]{1,0:T(8,128)(2,1)}, bf16[256,512]{1,0:T(8,128)(2,1)S(1)}, u32[]{:S(2)}, u32[]{:S(2)}) collective-permute-start(bf16[256,512]{1,0:T(8,128)(2,1)} %bitcast.13), channel_id=1, source_target_pairs={{0,1},{1,0},{2,3},{3,2},{4,5},{5,4},{6,7},{7,6},{8,9},{9,8},{10,11... | collective-permute-start | bytes 786440 | tf_op jit(solution)/shard_map/ppermute | solution.py:591
  1.2 15.8 %collective-permute-start.1 = (bf16[256,512]{1,0:T(8,128)(2,1)}, bf16[256,512]{1,0:T(8,128)(2,1)S(1)}, u32[]{:S(2)}, u32[]{:S(2)}) collective-permute-start(bf16[256,512]{1,0:T(8,128)(2,1)} %bitcast.14), channel_id=1, source_target_pairs={{0,2},{1,3},{2,0},{3,1},{4,6},{5,7},{6,4},{7,5},{8,10},{9,11},{10,... | collective-permute-start | bytes 786440 | tf_op jit(solution)/shard_map/ppermute | solution.py:591
  3.7 14.2 %collective-permute-start.3 = (bf16[256,512]{1,0:T(8,128)(2,1)}, bf16[256,512]{1,0:T(8,128)(2,1)S(1)}, u32[]{:S(2)}, u32[]{:S(2)}) collective-permute-start(bf16[256,512]{1,0:T(8,128)(2,1)} %bitcast.15), channel_id=1, source_target_pairs={{0,4},{1,5},{2,6},{3,7},{4,0},{5,1},{6,2},{7,3},{8,12},{9,13},{10,... | collective-permute-start | bytes 786440 | tf_op jit(solution)/shard_map/ppermute | solution.py:591
  5.2 12.7 %collective-permute-start.5 = (bf16[256,512]{1,0:T(8,128)(2,1)}, bf16[256,512]{1,0:T(8,128)(2,1)S(1)}, u32[]{:S(2)}, u32[]{:S(2)}) collective-permute-start(bf16[256,512]{1,0:T(8,128)(2,1)} %bitcast.16), channel_id=1, source_target_pairs={{0,6},{1,7},{2,4},{3,5},{4,2},{5,3},{6,0},{7,1},{8,14},{9,15},{10,... | collective-permute-start | bytes 786440 | tf_op jit(solution)/shard_map/ppermute | solution.py:591
  6.0 1.0 copy-start.3
  7.0 1.0 copy-start.4
  8.0 1.0 copy-start.5
  9.0 0.9 copy-start.7
  10.0 0.7 copy-start.9
  10.6 0.7 copy-start.11
  13.7 4.8 %copy-start.12 = (bf16[512]{0:T(512)(128)(2,1)S(1)}, bf16[512]{0:T(512)(128)(2,1)}, u32[]{:S(2)}) copy-start(bf16[512]{0:T(512)(128)(2,1)} %param.20) | copy-start | bytes 3076
  13.7 6.2 %copy-start.10 = (s32[1,16]{1,0:T(1,128)S(1)}, s32[1,16]{1,0:T(1,128)}, u32[]{:S(2)}) copy-start(s32[1,16]{1,0:T(1,128)} %param.24) | copy-start | bytes 196
  17.0 1.6 %collective-permute-start.2 = (bf16[256,512]{1,0:T(8,128)(2,1)S(1)}, bf16[256,512]{1,0:T(8,128)(2,1)S(1)}, u32[]{:S(2)}, u32[]{:S(2)}) collective-permute-start(bf16[256,512]{1,0:T(8,128)(2,1)S(1)} %collective-permute-done.1.refs_0_), channel_id=1, source_target_pairs={{0,1},{1,0},{2,3},{3,2},{4,5},{5,4},{6,7},{7,6},{8,9},{9,8},{10,11... | collective-permute-start | bytes 786440 | tf_op jit(solution)/shard_map/ppermute | solution.py:591
  17.9 1.5 %collective-permute-start.4 = (bf16[256,512]{1,0:T(8,128)(2,1)S(1)}, bf16[256,512]{1,0:T(8,128)(2,1)S(1)}, u32[]{:S(2)}, u32[]{:S(2)}) collective-permute-start(bf16[256,512]{1,0:T(8,128)(2,1)S(1)} %collective-permute-done.3.refs_2_), channel_id=1, source_target_pairs={{0,1},{1,0},{2,3},{3,2},{4,5},{5,4},{6,7},{7,6},{8,9},{9,8},{10,11... | collective-permute-start | bytes 786440 | tf_op jit(solution)/shard_map/ppermute | solution.py:591
  17.9 1.9 %collective-permute-start.6 = (bf16[256,512]{1,0:T(8,128)(2,1)S(1)}, bf16[256,512]{1,0:T(8,128)(2,1)S(1)}, u32[]{:S(2)}, u32[]{:S(2)}) collective-permute-start(bf16[256,512]{1,0:T(8,128)(2,1)S(1)} %collective-permute-done.5.refs_4_), channel_id=1, source_target_pairs={{0,1},{1,0},{2,3},{3,2},{4,5},{5,4},{6,7},{7,6},{8,9},{9,8},{10,11... | collective-permute-start | bytes 786440 | tf_op jit(solution)/shard_map/ppermute | solution.py:591
  18.5 7.6 %copy-start = (bf16[512,1024]{1,0:T(8,128)(2,1)S(1)}, bf16[512,1024]{1,0:T(8,128)(2,1)}, u32[]{:S(2)}) copy-start(bf16[512,1024]{1,0:T(8,128)(2,1)} %wg.1) | copy-start | bytes 3145732
  18.5 7.6 %copy-start.1 = (bf16[512,1024]{1,0:T(8,128)(2,1)S(1)}, bf16[512,1024]{1,0:T(8,128)(2,1)}, u32[]{:S(2)}) copy-start(bf16[512,1024]{1,0:T(8,128)(2,1)} %wu.1) | copy-start | bytes 3145732
  18.5 7.6 %copy-start.2 = (bf16[1024,512]{1,0:T(8,128)(2,1)S(1)}, bf16[1024,512]{1,0:T(8,128)(2,1)}, u32[]{:S(2)}) copy-start(bf16[1024,512]{1,0:T(8,128)(2,1)} %wd.1) | copy-start | bytes 3145732
  18.5 7.6 %copy-start.6 = (bf16[384,512]{1,0:T(8,128)(2,1)S(1)}, bf16[384,512]{1,0:T(8,128)(2,1)}, u32[]{:S(2)}) copy-start(bf16[384,512]{1,0:T(8,128)(2,1)} %wo.1) | copy-start | bytes 1179652
  18.5 7.6 %copy-start.8 = (bf16[1,256,512]{2,1,0:T(8,128)(2,1)S(1)}, bf16[1,256,512]{2,1,0:T(8,128)(2,1)}, u32[]{:S(2)}) copy-start(bf16[1,256,512]{2,1,0:T(8,128)(2,1)} %param.25) | copy-start | bytes 786436
  31.9 3.5 %collective-permute-start.7 = (bf16[768,1024]{1,0:T(8,128)(2,1)S(1)}, bf16[768,1024]{1,0:T(8,128)(2,1)S(1)}, u32[]{:S(2)}, u32[]{:S(2)}) collective-permute-start(bf16[768,1024]{1,0:T(8,128)(2,1)S(1)} %get-tuple-element.169), channel_id=1, source_target_pairs={{0,1},{1,0},{2,3},{3,2},{4,5},{5,4},{6,7},{7,6},{8,9},{9,8},{10,11... | collective-permute-start | bytes 4718600 | tf_op jit(solution)/shard_map/ppermute | solution.py:591
  36.3 13.4 %collective-permute-start.8 = (bf16[192,1024]{1,0:T(8,128)(2,1)S(1)}, bf16[192,1024]{1,0:T(8,128)(2,1)S(1)}, u32[]{:S(2)}, u32[]{:S(2)}) collective-permute-start(bf16[192,1024]{1,0:T(8,128)(2,1)S(1)} %get-tuple-element.172), channel_id=1, source_target_pairs={{0,2},{1,3},{2,0},{3,1},{4,6},{5,7},{6,4},{7,5},{8,10},{9,11},{10,... | collective-permute-start | bytes 1179656 | tf_op jit(solution)/shard_map/ppermute | solution.py:591
  37.8 11.8 %collective-permute-start.9 = (bf16[192,1024]{1,0:T(8,128)(2,1)S(1)}, bf16[192,1024]{1,0:T(8,128)(2,1)S(1)}, u32[]{:S(2)}, u32[]{:S(2)}) collective-permute-start(bf16[192,1024]{1,0:T(8,128)(2,1)S(1)} %get-tuple-element.174), channel_id=1, source_target_pairs={{0,4},{1,5},{2,6},{3,7},{4,0},{5,1},{6,2},{7,3},{8,12},{9,13},{10,... | collective-permute-start | bytes 1179656 | tf_op jit(solution)/shard_map/ppermute | solution.py:591
  49.7 14.6 %collective-permute-start.13 = (bf16[4,512,256]{2,1,0:T(8,128)(2,1)S(1)}, bf16[4,512,256]{2,1,0:T(8,128)(2,1)S(1)}, u32[]{:S(2)}, u32[]{:S(2)}) collective-permute-start(bf16[4,512,256]{2,1,0:T(8,128)(2,1)S(1)} %get-tuple-element.213), channel_id=1, source_target_pairs={{0,1},{1,0},{2,3},{3,2},{4,5},{5,4},{6,7},{7,6},{8,9},{9,8},{10,11... | collective-permute-start | bytes 3145736 | tf_op jit(solution)/shard_map/ppermute | solution.py:591
  49.7 3.8 %collective-permute-start.10 = (bf16[784,512]{1,0:T(8,128)(2,1)S(1)}, bf16[784,512]{1,0:T(8,128)(2,1)S(1)}, u32[]{:S(2)}, u32[]{:S(2)}) collective-permute-start(bf16[784,512]{1,0:T(8,128)(2,1)S(1)} %get-tuple-element.203), channel_id=1, source_target_pairs={{0,1},{1,0},{2,3},{3,2},{4,5},{5,4},{6,7},{7,6},{8,9},{9,8},{10,11... | collective-permute-start | bytes 2408456 | tf_op jit(solution)/shard_map/ppermute | solution.py:591
  51.2 7.0 %collective-permute-start.11 = (bf16[96,1024]{1,0:T(8,128)(2,1)S(1)}, bf16[96,1024]{1,0:T(8,128)(2,1)S(1)}, u32[]{:S(2)}, u32[]{:S(2)}) collective-permute-start(bf16[96,1024]{1,0:T(8,128)(2,1)S(1)} %get-tuple-element.206), channel_id=1, source_target_pairs={{0,4},{1,5},{2,6},{3,7},{4,0},{5,1},{6,2},{7,3},{8,12},{9,13},{10,... | collective-permute-start | bytes 589832 | tf_op jit(solution)/shard_map/ppermute | solution.py:591
  52.0 6.5 %collective-permute-start.12 = (bf16[96,1024]{1,0:T(8,128)(2,1)S(1)}, bf16[96,1024]{1,0:T(8,128)(2,1)S(1)}, u32[]{:S(2)}, u32[]{:S(2)}) collective-permute-start(bf16[96,1024]{1,0:T(8,128)(2,1)S(1)} %get-tuple-element.207), channel_id=1, source_target_pairs={{0,2},{1,3},{2,0},{3,1},{4,6},{5,7},{6,4},{7,5},{8,10},{9,11},{10,... | collective-permute-start | bytes 589832 | tf_op jit(solution)/shard_map/ppermute | solution.py:591
  59.2 5.9 %collective-permute-start.14 = (bf16[96,1024]{1,0:T(8,128)(2,1)S(1)}, bf16[96,1024]{1,0:T(8,128)(2,1)S(1)}, u32[]{:S(2)}, u32[]{:S(2)}) collective-permute-start(bf16[96,1024]{1,0:T(8,128)(2,1)S(1)} %get-tuple-element.219), channel_id=1, source_target_pairs={{0,8},{8,0},{16,24},{24,16},{1,9},{9,1},{17,25},{25,17},{2,10},{10... | collective-permute-start | bytes 589832 | tf_op jit(solution)/shard_map/ppermute | solution.py:591
  60.8 8.2 %collective-permute-start.15 = (bf16[208,512]{1,0:T(8,128)(2,1)S(1)}, bf16[208,512]{1,0:T(8,128)(2,1)S(1)}, u32[]{:S(2)}, u32[]{:S(2)}) collective-permute-start(bf16[208,512]{1,0:T(8,128)(2,1)S(1)} %get-tuple-element.221), channel_id=1, source_target_pairs={{0,2},{1,3},{2,0},{3,1},{4,6},{5,7},{6,4},{7,5},{8,10},{9,11},{10,... | collective-permute-start | bytes 638984 | tf_op jit(solution)/shard_map/ppermute | solution.py:591
  61.4 8.1 %collective-permute-start.16 = (bf16[208,512]{1,0:T(8,128)(2,1)S(1)}, bf16[208,512]{1,0:T(8,128)(2,1)S(1)}, u32[]{:S(2)}, u32[]{:S(2)}) collective-permute-start(bf16[208,512]{1,0:T(8,128)(2,1)S(1)} %get-tuple-element.222), channel_id=1, source_target_pairs={{0,4},{1,5},{2,6},{3,7},{4,0},{5,1},{6,2},{7,3},{8,12},{9,13},{10,... | collective-permute-start | bytes 638984 | tf_op jit(solution)/shard_map/ppermute | solution.py:591
  62.8 11.6 %collective-permute-start.17 = (bf16[208,512]{1,0:T(8,128)(2,1)S(1)}, bf16[208,512]{1,0:T(8,128)(2,1)S(1)}, u32[]{:S(2)}, u32[]{:S(2)}) collective-permute-start(bf16[208,512]{1,0:T(8,128)(2,1)S(1)} %get-tuple-element.223), channel_id=1, source_target_pairs={{0,6},{1,7},{2,4},{3,5},{4,2},{5,3},{6,0},{7,1},{8,14},{9,15},{10,... | collective-permute-start | bytes 638984 | tf_op jit(solution)/shard_map/ppermute | solution.py:591
  65.7 9.9 %collective-permute-start.18 = (bf16[96,1024]{1,0:T(8,128)(2,1)S(1)}, bf16[96,1024]{1,0:T(8,128)(2,1)S(1)}, u32[]{:S(2)}, u32[]{:S(2)}) collective-permute-start(bf16[96,1024]{1,0:T(8,128)(2,1)S(1)} %add_parts.13.refs_0_), channel_id=1, source_target_pairs={{0,16},{8,24},{16,0},{24,8},{1,17},{9,25},{17,1},{25,9},{2,18},{10... | collective-permute-start | bytes 589832 | tf_op jit(solution)/shard_map/ppermute | solution.py:591
  68.4 21.5 %collective-permute-start.24 = (bf16[512,256]{1,0:T(8,128)(2,1)S(1)}, bf16[512,256]{1,0:T(8,128)(2,1)S(1)}, u32[]{:S(2)}, u32[]{:S(2)}) collective-permute-start(bf16[512,256]{1,0:T(8,128)(2,1)S(1)} %get-tuple-element.237), channel_id=1, source_target_pairs={{0,2},{1,3},{2,0},{3,1},{4,6},{5,7},{6,4},{7,5},{8,10},{9,11},{10,... | collective-permute-start | bytes 786440 | tf_op jit(solution)/shard_map/ppermute | solution.py:591
  74.5 6.0 %collective-permute-start.19 = (bf16[112,512]{1,0:T(8,128)(2,1)S(1)}, bf16[112,512]{1,0:T(8,128)(2,1)S(1)}, u32[]{:S(2)}, u32[]{:S(2)}) collective-permute-start(bf16[112,512]{1,0:T(8,128)(2,1)S(1)} %get-tuple-element.230), channel_id=1, source_target_pairs={{0,8},{8,0},{16,24},{24,16},{1,9},{9,1},{17,25},{25,17},{2,10},{10... | collective-permute-start | bytes 344072 | tf_op jit(solution)/shard_map/ppermute | solution.py:591
  76.2 8.2 %collective-permute-start.20 = (bf16[96,1024]{1,0:T(8,128)(2,1)S(1)}, bf16[96,1024]{1,0:T(8,128)(2,1)S(1)}, u32[]{:S(2)}, u32[]{:S(2)}) collective-permute-start(bf16[96,1024]{1,0:T(8,128)(2,1)S(1)} %add_parts.15.mine), channel_id=1, source_target_pairs={{0,8},{8,0},{16,24},{24,16},{1,9},{9,1},{17,25},{25,17},{2,10},{10... | collective-permute-start | bytes 589832 | tf_op jit(solution)/shard_map/ppermute | solution.py:591
  77.3 13.4 %collective-permute-start.25 = (bf16[512,256]{1,0:T(8,128)(2,1)S(1)}, bf16[512,256]{1,0:T(8,128)(2,1)S(1)}, u32[]{:S(2)}, u32[]{:S(2)}) collective-permute-start(bf16[512,256]{1,0:T(8,128)(2,1)S(1)} %get-tuple-element.238), channel_id=1, source_target_pairs={{0,4},{1,5},{2,6},{3,7},{4,0},{5,1},{6,2},{7,3},{8,12},{9,13},{10,... | collective-permute-start | bytes 786440 | tf_op jit(solution)/shard_map/ppermute | solution.py:591
  78.1 12.6 %collective-permute-start.26 = (bf16[512,256]{1,0:T(8,128)(2,1)S(1)}, bf16[512,256]{1,0:T(8,128)(2,1)S(1)}, u32[]{:S(2)}, u32[]{:S(2)}) collective-permute-start(bf16[512,256]{1,0:T(8,128)(2,1)S(1)} %get-tuple-element.239), channel_id=1, source_target_pairs={{0,6},{1,7},{2,4},{3,5},{4,2},{5,3},{6,0},{7,1},{8,14},{9,15},{10,... | collective-permute-start | bytes 786440 | tf_op jit(solution)/shard_map/ppermute | solution.py:591
  81.1 7.1 %collective-permute-start.23 = (bf16[112,512]{1,0:T(8,128)(2,1)S(1)}, bf16[112,512]{1,0:T(8,128)(2,1)S(1)}, u32[]{:S(2)}, u32[]{:S(2)}) collective-permute-start(bf16[112,512]{1,0:T(8,128)(2,1)S(1)} %add_parts.16.refs_0_), channel_id=1, source_target_pairs={{0,16},{8,24},{16,0},{24,8},{1,17},{9,25},{17,1},{25,9},{2,18},{10... | collective-permute-start | bytes 344072 | tf_op jit(solution)/shard_map/ppermute | solution.py:591
  88.8 4.7 %collective-permute-start.27 = (bf16[96,512]{1,0:T(8,128)(2,1)S(1)}, bf16[96,512]{1,0:T(8,128)(2,1)S(1)}, u32[]{:S(2)}, u32[]{:S(2)}) collective-permute-start(bf16[96,512]{1,0:T(8,128)(2,1)S(1)} %slice.9), channel_id=1, source_target_pairs={{0,8},{8,0},{16,24},{24,16},{1,9},{9,1},{17,25},{25,17},{2,10},{10... | collective-permute-start | bytes 294920 | tf_op jit(solution)/shard_map/ppermute | solution.py:591
  88.8 6.4 %collective-permute-start.21 = (bf16[96,1024]{1,0:T(8,128)(2,1)S(1)}, bf16[96,1024]{1,0:T(8,128)(2,1)S(1)}, u32[]{:S(2)}, u32[]{:S(2)}) collective-permute-start(bf16[96,1024]{1,0:T(8,128)(2,1)S(1)} %get-tuple-element.233.a), channel_id=1, source_target_pairs={{0,4},{1,5},{2,6},{3,7},{4,0},{5,1},{6,2},{7,3},{8,12},{9,13},{10,... | collective-permute-start | bytes 589832 | tf_op jit(solution)/shard_map/ppermute | solution.py:591
  89.9 5.7 %collective-permute-start.22 = (bf16[96,1024]{1,0:T(8,128)(2,1)S(1)}, bf16[96,1024]{1,0:T(8,128)(2,1)S(1)}, u32[]{:S(2)}, u32[]{:S(2)}) collective-permute-start(bf16[96,1024]{1,0:T(8,128)(2,1)S(1)} %get-tuple-element.234.c), channel_id=1, source_target_pairs={{0,2},{1,3},{2,0},{3,1},{4,6},{5,7},{6,4},{7,5},{8,10},{9,11},{10,... | collective-permute-start | bytes 589832 | tf_op jit(solution)/shard_map/ppermute | solution.py:591
  96.2 17.6 %collective-permute-start.35 = (bf16[192,1024]{1,0:T(8,128)(2,1)S(1)}, bf16[192,1024]{1,0:T(8,128)(2,1)S(1)}, u32[]{:S(2)}, u32[]{:S(2)}) collective-permute-start(bf16[192,1024]{1,0:T(8,128)(2,1)S(1)} %get-tuple-element.269.refs_0_), channel_id=1, source_target_pairs={{0,2},{1,3},{2,0},{3,1},{4,6},{5,7},{6,4},{7,5},{8,10},{9,11},{10,... | collective-permute-start | bytes 1179656 | tf_op jit(solution)/shard_map/ppermute | solution.py:591
  97.0 16.7 %collective-permute-start.36 = (bf16[192,1024]{1,0:T(8,128)(2,1)S(1)}, bf16[192,1024]{1,0:T(8,128)(2,1)S(1)}, u32[]{:S(2)}, u32[]{:S(2)}) collective-permute-start(bf16[192,1024]{1,0:T(8,128)(2,1)S(1)} %get-tuple-element.271.refs_2_), channel_id=1, source_target_pairs={{0,4},{1,5},{2,6},{3,7},{4,0},{5,1},{6,2},{7,3},{8,12},{9,13},{10,... | collective-permute-start | bytes 1179656 | tf_op jit(solution)/shard_map/ppermute | solution.py:591
  98.0 12.8 %collective-permute-start.28 = (bf16[192,512]{1,0:T(8,128)(2,1)S(1)}, bf16[192,512]{1,0:T(8,128)(2,1)S(1)}, u32[]{:S(2)}, u32[]{:S(2)}) collective-permute-start(bf16[192,512]{1,0:T(8,128)(2,1)S(1)} %pad_maximum_fusion.refs_0_), channel_id=1, source_target_pairs={{0,2},{1,3},{2,0},{3,1},{4,6},{5,7},{6,4},{7,5},{8,10},{9,11},{10,... | collective-permute-start | bytes 589832 | tf_op jit(solution)/shard_map/ppermute | solution.py:591
  99.8 13.4 %collective-permute-start.29 = (bf16[192,512]{1,0:T(8,128)(2,1)S(1)}, bf16[192,512]{1,0:T(8,128)(2,1)S(1)}, u32[]{:S(2)}, u32[]{:S(2)}) collective-permute-start(bf16[192,512]{1,0:T(8,128)(2,1)S(1)} %pad_maximum_fusion.refs_0_), channel_id=1, source_target_pairs={{0,4},{1,5},{2,6},{3,7},{4,0},{5,1},{6,2},{7,3},{8,12},{9,13},{10,... | collective-permute-start | bytes 589832 | tf_op jit(solution)/shard_map/ppermute | solution.py:591
  100.3 12.9 %collective-permute-start.30 = (bf16[192,512]{1,0:T(8,128)(2,1)S(1)}, bf16[192,512]{1,0:T(8,128)(2,1)S(1)}, u32[]{:S(2)}, u32[]{:S(2)}) collective-permute-start(bf16[192,512]{1,0:T(8,128)(2,1)S(1)} %pad_maximum_fusion.refs_0_), channel_id=1, source_target_pairs={{0,6},{1,7},{2,4},{3,5},{4,2},{5,3},{6,0},{7,1},{8,14},{9,15},{10,... | collective-permute-start | bytes 589832 | tf_op jit(solution)/shard_map/ppermute | solution.py:591
  113.2 1.4 %collective-permute-start.31 = (bf16[192,512]{1,0:T(8,128)(2,1)S(1)}, bf16[192,512]{1,0:T(8,128)(2,1)S(1)}, u32[]{:S(2)}, u32[]{:S(2)}) collective-permute-start(bf16[192,512]{1,0:T(8,128)(2,1)S(1)} %pad_maximum_fusion.refs_0_), channel_id=1, source_target_pairs={{0,1},{1,0},{2,3},{3,2},{4,5},{5,4},{6,7},{7,6},{8,9},{9,8},{10,11... | collective-permute-start | bytes 589832 | tf_op jit(solution)/shard_map/ppermute | solution.py:591
  113.2 1.7 %collective-permute-start.32 = (bf16[192,512]{1,0:T(8,128)(2,1)S(1)}, bf16[192,512]{1,0:T(8,128)(2,1)S(1)}, u32[]{:S(2)}, u32[]{:S(2)}) collective-permute-start(bf16[192,512]{1,0:T(8,128)(2,1)S(1)} %collective-permute-done.28.refs_1_), channel_id=1, source_target_pairs={{0,1},{1,0},{2,3},{3,2},{4,5},{5,4},{6,7},{7,6},{8,9},{9,8},{10,11... | collective-permute-start | bytes 589832 | tf_op jit(solution)/shard_map/ppermute | solution.py:591
  113.7 1.5 %collective-permute-start.33 = (bf16[192,512]{1,0:T(8,128)(2,1)S(1)}, bf16[192,512]{1,0:T(8,128)(2,1)S(1)}, u32[]{:S(2)}, u32[]{:S(2)}) collective-permute-start(bf16[192,512]{1,0:T(8,128)(2,1)S(1)} %collective-permute-done.29.refs_2_), channel_id=1, source_target_pairs={{0,1},{1,0},{2,3},{3,2},{4,5},{5,4},{6,7},{7,6},{8,9},{9,8},{10,11... | collective-permute-start | bytes 589832 | tf_op jit(solution)/shard_map/ppermute | solution.py:591
  113.7 6.5 %collective-permute-start.37 = (bf16[192,1024]{1,0:T(8,128)(2,1)S(1)}, bf16[192,1024]{1,0:T(8,128)(2,1)S(1)}, u32[]{:S(2)}, u32[]{:S(2)}) collective-permute-start(bf16[192,1024]{1,0:T(8,128)(2,1)S(1)} %get-tuple-element.269.refs_0_), channel_id=1, source_target_pairs={{0,1},{1,0},{2,3},{3,2},{4,5},{5,4},{6,7},{7,6},{8,9},{9,8},{10,11... | collective-permute-start | bytes 1179656 | tf_op jit(solution)/shard_map/ppermute | solution.py:591
  114.2 6.0 %collective-permute-start.38 = (bf16[192,1024]{1,0:T(8,128)(2,1)S(1)}, bf16[192,1024]{1,0:T(8,128)(2,1)S(1)}, u32[]{:S(2)}, u32[]{:S(2)}) collective-permute-start(bf16[192,1024]{1,0:T(8,128)(2,1)S(1)} %collective-permute-done.35.refs_1_), channel_id=1, source_target_pairs={{0,1},{1,0},{2,3},{3,2},{4,5},{5,4},{6,7},{7,6},{8,9},{9,8},{10,11... | collective-permute-start | bytes 1179656 | tf_op jit(solution)/shard_map/ppermute | solution.py:591
  114.7 5.6 %collective-permute-start.39 = (bf16[192,1024]{1,0:T(8,128)(2,1)S(1)}, bf16[192,1024]{1,0:T(8,128)(2,1)S(1)}, u32[]{:S(2)}, u32[]{:S(2)}) collective-permute-start(bf16[192,1024]{1,0:T(8,128)(2,1)S(1)} %get-tuple-element.271.refs_2_), channel_id=1, source_target_pairs={{0,1},{1,0},{2,3},{3,2},{4,5},{5,4},{6,7},{7,6},{8,9},{9,8},{10,11... | collective-permute-start | bytes 1179656 | tf_op jit(solution)/shard_map/ppermute | solution.py:591
  114.9 5.3 %collective-permute-start.40 = (bf16[192,1024]{1,0:T(8,128)(2,1)S(1)}, bf16[192,1024]{1,0:T(8,128)(2,1)S(1)}, u32[]{:S(2)}, u32[]{:S(2)}) collective-permute-start(bf16[192,1024]{1,0:T(8,128)(2,1)S(1)} %collective-permute-done.36.refs_3_), channel_id=1, source_target_pairs={{0,1},{1,0},{2,3},{3,2},{4,5},{5,4},{6,7},{7,6},{8,9},{9,8},{10,11... | collective-permute-start | bytes 1179656 | tf_op jit(solution)/shard_map/ppermute | solution.py:591
  115.2 2.5 %collective-permute-start.34 = (bf16[192,512]{1,0:T(8,128)(2,1)S(1)}, bf16[192,512]{1,0:T(8,128)(2,1)S(1)}, u32[]{:S(2)}, u32[]{:S(2)}) collective-permute-start(bf16[192,512]{1,0:T(8,128)(2,1)S(1)} %collective-permute-done.30.refs_3_), channel_id=1, source_target_pairs={{0,1},{1,0},{2,3},{3,2},{4,5},{5,4},{6,7},{7,6},{8,9},{9,8},{10,11... | collective-permute-start | bytes 589832 | tf_op jit(solution)/shard_map/ppermute | solution.py:591

commit v4 on v3

--- a/solution.py
+++ b/solution.py
@@ -10,7 +10,11 @@
 EPS = 1e-6
 BIG = -(2.0**30)
 LEFT, RIGHT, ONES = 17, 18, 19
+PIECE = 32
 FFN_CHUNKS = 1
+STEPS = """
+    a_chips f_rows f_z0 a_rows d_slots f_z1 f_pick a_z0 d:3 d_out a_z1 f_join a_stack f_near small a_swap f_swap last
+"""
 SMALL = 16
 VMEM = 24 * 1024 * 1024
 MUCH = 56 * 1024 * 1024
@@ -329,10 +333,13 @@
 
     def weights_kernel():
         low = tn(u_all[...], gb_all[...]).astype(bf16)
-        grads[2 * d : 3 * d, :d] = low[:d]
-        grads[2 * d : 3 * d, d:] = low[d:]
-        grads[0:d] = tn(n2_all[...], dg_all[...]).astype(bf16)
-        grads[d : 2 * d] = tn(n2_all[...], du_all[...]).astype(bf16)
+        for k, value in enumerate((tn(n2_all[...], dg_all[...]).astype(bf16), tn(n2_all[...], du_all[...]).astype(bf16))):
+            for i in range(d // PIECE):
+                grads[(3 * i + k) * PIECE : (3 * i + k + 1) * PIECE] = value[i * PIECE : (i + 1) * PIECE]
+        for i in range(d // PIECE):
+            at = slice((3 * i + 2) * PIECE, (3 * i + 3) * PIECE)
+            grads[at, :d] = low[i * PIECE : (i + 1) * PIECE]
+            grads[at, d:] = low[d + i * PIECE : d + (i + 1) * PIECE]
 
     stages = [weigh, norm, project, activate, down, norm_back, mix_back]
     for step in range(len(stages) + FFN_CHUNKS - 1):
@@ -524,6 +531,35 @@
     )
 
 
+def rest_back_kernel(n, buckets, pairs, counts, sizes, ids, *refs):
+    first, second, outs, inner = (refs[a:b] for a, b in zip(sizes[:-1], sizes[1:], strict=True))
+    size = len(pairs)
+    dkv, (dq, line), ds = inner[: 2 * size], inner[2 * size : 2 * size + 2], inner[2 * size + 2]
+    attend_back_kernel(n, pairs, counts, ids, *first, *dkv, dq, line, ds)
+    head, (dk0, dv0, dq0, line0) = second[: 7 + len(counts)], second[7 + len(counts) :]
+    gather_back_kernel(n, buckets, counts, [1, size], ids, *head, dk0, *dkv[:size], dv0, *dkv[size:], dq0, dq, line0, line,
+                       *outs, *inner[2 * size + 3 :])
+
+
+def rest_back(n, buckets, pairs, ids, q, do, scale, gain, gn, gwo, wq, wk, wv, wt, parts, back):
+    d, w = wq.shape
+    t = q.shape[0]
+    widths = [v["e"].shape[0] for v in parts]
+    s, size, half = sum(widths), len(pairs), 2 * w + SMALL
+    first = (q, do, scale, *[v["p"][g] for v in parts for g in pairs], *[v["kv"][g] for v in parts for g in pairs],
+             *[v["e"] for v in parts])
+    second = (gain, gn, gwo, wq, wk, wv, wt, *[v["n1"] for v in parts], back["dk"][0], back["dv"][0], back["dq"], back["line"])
+    cuts = [0, len(first), len(first) + len(second), len(first) + len(second) + 5]
+    inner = [pltpu.VMEM((128, s), bf16)] * (2 * size) + [pltpu.VMEM((t, 128 * size), bf16), pltpu.VMEM((8, 4 * t + 128), f32),
+             pltpu.VMEM((2, t, s), bf16), pltpu.VMEM((4 * w, d), bf16), pltpu.VMEM((SMALL, d), f32),
+             pltpu.VMEM((8, 4 * t + 128), f32)]
+    return call(
+        partial(rest_back_kernel, n, buckets, pairs, [v // t for v in widths], [*cuts, cuts[-1] + len(inner)]), "rest_back", 10,
+        [shape(n // 2, d, t), shape(n // 2, d, t), shape(t, d, dtype=f32), shape(half, d), shape(half, d)],
+        (ids,), (*first, *second), scratch=inner,
+    )
+
+
 def split_kernel(which, count, extra, ids, *refs):
     inputs, outs = refs[:-count], refs[-count:]
     rows = (inputs[0].shape[0] - extra) // count
@@ -580,6 +616,13 @@
     second[...] = jnp.where(even, b, a).astype(bf16)
 
 
+def stack_kernel(ids, *refs):
+    *parts, out = refs
+    rows = parts[0].shape[0]
+    for i, ref in enumerate(parts):
+        out[i * rows : (i + 1) * rows] = ref[...]
+
+
 def join_kernel(ids, a, b, c, d, first, second):
     rows = a.shape[0]
     first[:rows], first[rows:] = a[...], b[...]
@@ -626,26 +669,75 @@
                 full[pl.ds(pl.multiple_of(where, 16), piece // 2)] = ref[b * (piece // 2) : (b + 1) * (piece // 2)]
 
 
-def unpack_ffn_kernel(pieces, ids, *refs):
-    gate, up, down, full = refs[2 * pieces :]
-    size = full.shape[0] // 2
+def send_out(copies, source, target, sem):
+    copies.append(pltpu.make_async_copy(source, target, sem))
+    copies[-1].start()
+
+
+def write_ffn(far, ids, parts, gate, up, down, full, sems):
+    d = gate.shape[0]
     x, y = ids[2] % 2, ids[2] // 2
-    for c, parts in ((ids[1], refs[:pieces]), (1 - ids[1], refs[pieces : 2 * pieces])):
-        if pieces == 1:
-            full[pl.ds(pl.multiple_of(c * size, 16), size)] = parts[0][...]
-            continue
-        rows = size // 8
+    rows = 3 * PIECE
+    copies = []
+    for c, pair in ((ids[1], parts[:2]), (1 - ids[1], parts[2:])):
         for half, first, second in ((0, x, y), (1, y, x)):
-            for a in range(2):
-                for b in range(2):
-                    where = c * size + (4 * half + 2 * (first ^ a) + (second ^ b)) * rows
-                    piece = parts[2 * half + a][b * rows : (b + 1) * rows]
-                    full[pl.ds(pl.multiple_of(where, 16), rows)] = piece
-    d = gate.shape[0]
-    gate[...] = full[:d].astype(f32)
-    up[...] = full[d : 2 * d].astype(f32)
-    down[:d] = full[2 * d :, :d].astype(f32)
-    down[d:] = full[2 * d :, d:].astype(f32)
+            for b in range(2):
+                k = len(copies) // 4
+                piece = 8 * c + 4 * half + 2 * (first ^ far) + (second ^ b)
+                full[k] = pair[half][b * rows : (b + 1) * rows].astype(f32)
+                at = pl.multiple_of(piece * PIECE, PIECE)
+                send_out(copies, full.at[k, :PIECE], gate.at[pl.ds(at, PIECE)], sems.at[4 * k])
+                send_out(copies, full.at[k, PIECE : 2 * PIECE], up.at[pl.ds(at, PIECE)], sems.at[4 * k + 1])
+                send_out(copies, full.at[k, 2 * PIECE :, :d], down.at[pl.ds(at, PIECE)], sems.at[4 * k + 2])
+                send_out(copies, full.at[k, 2 * PIECE :, d:], down.at[pl.ds(d + at, PIECE)], sems.at[4 * k + 3])
+    return copies
+
+
+def unpack_near_kernel(ids, *refs):
+    for copy in write_ffn(0, ids, refs[:4], *refs[4:]):
+        copy.wait()
+
+
+def unpack_far_kernel(pieces, ids, *refs):
+    parts, stacks = refs[:4], refs[4:8]
+    gate, up, down, *attention, full, sems, both, wide, tall, sem2 = refs[8 + 3 :]
+    copies = write_ffn(1, ids, parts, gate, up, down, full, sems)
+    size = both.shape[0] // 2
+    rows = stacks[0].shape[0] // pieces
+    for k, stack in enumerate(stacks):
+        for a in range(pieces):
+            where = (ids[1] ^ (k // 2)) * size + ((ids[2] ^ a) * 2 + ((ids[3] % 2) ^ (k % 2))) * rows
+            both[pl.ds(pl.multiple_of(where, 16), rows)] = stack[a * rows : (a + 1) * rows]
+    w = wide.shape[2]
+    tall[...] = both[3 * w :].astype(f32)
+    send_out(copies, tall, attention[3], sem2.at[3])
+    for k in range(3):
+        wide[k] = both[k * w : (k + 1) * w].astype(f32).T
+        send_out(copies, wide.at[k], attention[k], sem2.at[k])
+    for copy in copies:
+        copy.wait()
+
+
+def unpack(kernel, ids, vmem_args, filled, out_shape, scratch):
+    vmem, hbm = pl.BlockSpec(memory_space=pltpu.VMEM), pl.BlockSpec(memory_space=pl.ANY)
+    return pl.pallas_call(
+        kernel,
+        in_specs=[pl.BlockSpec(memory_space=pltpu.SMEM)] + [vmem] * len(vmem_args) + [hbm] * len(filled),
+        out_specs=[hbm] * len(out_shape),
+        out_shape=out_shape,
+        scratch_shapes=scratch,
+        input_output_aliases={1 + len(vmem_args) + i: i for i in range(len(filled))},
+        compiler_params=pltpu.CompilerParams(vmem_limit_bytes=VMEM),
+        cost_estimate=pl.CostEstimate(flops=1000, bytes_accessed=1000, transcendentals=0),
+        name="unpack",
+    )(ids, *vmem_args, *filled)
+
+
+def unpack_ffn_halves(ids, mine, other, d, ff):
+    full = jnp.where(ids[1] == 0, jnp.concatenate([mine, other]), jnp.concatenate([other, mine])).astype(f32)
+    full = full.reshape(d // PIECE, 3, PIECE, ff)
+    low = full[:, 2].reshape(d, ff)
+    return full[:, 0].reshape(d, ff), full[:, 1].reshape(d, ff), jnp.concatenate([low[:, :d], low[:, d:]])
 
 
 def unpack_attention_kernel(pieces, ids, *refs):
@@ -725,13 +817,6 @@
     whole = n != 8 or lax.axis_size("rows") != 4
     zero, near = ids * 0, ids[3:4] % 2
 
-    def unpack_ffn(mine, other):
-        return call(
-            partial(unpack_ffn_kernel, len(mine)), "unpack_ffn", 4,
-            [shape(d, ff, dtype=f32), shape(d, ff, dtype=f32), shape(ff, d, dtype=f32)],
-            (ids,), (*mine, *other), scratch=[pltpu.VMEM((3 * d, ff), bf16)],
-        )
-
     def unpack_attention(mine, other):
         return call(
             partial(unpack_attention_kernel, len(mine)), "unpack_attention", 3,
@@ -750,73 +835,140 @@
         return call(partial(slots_kernel, half), "add_slots", 1, [shape(d, t)] * half, (ids,), (even, recv))
 
     f_core = swap(send, "seq", 1)
-    backs = [attend_back(n, [0], ids, q, do, scale, parts)]
+    back = attend_back(n, [0], ids, q, do, scale, parts)
     f_keep = keep
-    part = lambda rows: shape(f_keep.shape[0] // rows, ff)
-    if not whole:
-        f_core = order(backs[0]["dq"], f_core)
-        f_x, f_x2, f_y, f_y2 = call(by_chip_kernel, "add_parts", 1, [part(4)] * 4, (ids,), (keep, f_core))
-        do = order(f_x, do)
-        f_x2, f_y2 = swap(f_x2, "seq", 2), swap(f_y2, "seq", 4)
-    backs.append(attend_back(n, list(range(1, pairs)), ids, q, do, scale, parts))
-    even, odd, dn1q, keep, send = gather_back(
-        n, buckets, ids, gain1, gn, gwo, wq, wk, wv, wt, parts, backs
-    )
-    if not whole:
-        send, odd = order((f_x2, f_y2), send, odd)
-    a_core, d_core = swap(send, "seq", 1), swap(odd, "seq", 1)
     if whole:
+        backs = [back, attend_back(n, list(range(1, pairs)), ids, q, do, scale, parts)]
+        even, odd, dn1q, keep, send = gather_back(n, buckets, ids, gain1, gn, gwo, wq, wk, wv, wt, parts, backs)
+        a_core, d_core = swap(send, "seq", 1), swap(odd, "seq", 1)
         mine, other, _ = sum_all(ids, f_keep, f_core, 0)
-        gate, up, down = unpack_ffn(mine, other)
+        gate, up, down = unpack_ffn_halves(ids, mine[0], other[0], d, ff)
         grad_tokens = input_grad(to_chips(add_slots(d_core)))
         mine, other, tail = sum_all(ids, keep, a_core, SMALL)
         gq, gk, gv, go = unpack_attention(mine, other)
         g1, g2, gb = unpack_small(tail)
     else:
+        part = lambda rows: shape(f_keep.shape[0] // rows, ff)
+        f_core = order(back["dq"], f_core)
+        f_x, f_x2, f_y, f_y2 = call(by_chip_kernel, "add_parts", 1, [part(4)] * 4, (ids,), (keep, f_core))
+        do = order(f_x, do)
+        f_x2, f_y2 = swap(f_x2, "seq", 2), swap(f_y2, "seq", 4)
+        even, odd, dn1q, keep, send = rest_back(
+            n, buckets, list(range(1, pairs)), ids, q, do, scale, gain1, gn, gwo, wq, wk, wv, wt, parts, back
+        )
+        send, odd = order((f_x2, f_y2), send, odd)
+        live = dict(a=swap(send, "seq", 1), d=swap(odd, "seq", 1))
         f_x, f_x2, f_y, f_y2 = call(
             by_next_chip_kernel, "add_parts", 1, [part(8)] * 4, (ids,), (f_x, f_x2, f_y, f_y2)
         )
-        f_x2, f_y2 = swap(f_x2, "seq", 4), swap(f_y2, "seq", 2)
-        a_core = order(f_x, a_core)
-        a_parts = to_chips(add_and_split(2, half, SMALL, ids, keep, a_core))
-        f_x2, f_y2 = order(a_parts[0], f_x2, f_y2)
-        f_mine, f_other = call(by_row_kernel, "add_parts", 1, [part(8)] * 2, (ids,), (f_x, f_x2, f_y, f_y2))
-        f_other = swap(f_other, "rows", 1)
-        d_core = order(f_mine, d_core)
-        d_parts = add_slots(d_core)
-        f_other = order(d_parts, f_other)
-        f_mine = add_and_split(0, 1, 0, zero, f_mine, f_other)[0]
-        f_other = swap(f_mine, "rows", 2)
-        d_parts = to_chips(order(f_mine, d_parts))
-        a_parts = order(f_mine, a_parts)
-        a_mine, a_other = add_and_split(0, 2, SMALL, near, *a_parts)
-        a_other = swap(a_other, "rows", 1)
-        f_other = order(a_mine, f_other)
-        f_mine = add_and_split(0, 1, 0, zero, f_mine, f_other)[0]
-        f_other = swap(f_mine, "rows", 1)
-        a_other = order(f_mine, a_other)
-        a_mine = add_and_split(0, 1, SMALL, zero, a_mine, a_other)[0]
-        a_other = swap(a_mine, "rows", 2)
-        f_other = order(a_mine, f_other)
-        f_x, f_y = call(pick_kernel, "pick", 1, [part(8)] * 2, (ids,), (f_mine, f_other))
-        f_x2, f_y2 = swap(f_x, "seq", 4), swap(f_y, "seq", 2)
-        a_other = order(f_x, a_other)
-        a_mine = add_and_split(0, 1, SMALL, zero, a_mine, a_other)[0]
-        size = a_mine.shape[0] - SMALL
-        a_other = swap(a_mine[:size], "rows", 1)
-        d_parts = order(a_mine, d_parts)
-        a_other = order(d_parts, a_other)
-        a_line = jnp.concatenate([a_mine[:size], a_other], axis=0)
-        a_own = [a_line] + [swap(a_line, "seq", 2 * j) for j in range(1, half)]
-        grad_tokens = input_grad(order(a_line, d_parts))
-        f_x2, f_y2, grad_tokens = order(grad_tokens, f_x2, f_y2, grad_tokens)
-        f_x, f_y = call(join_kernel, "join", 1, [part(4)] * 2, (ids,), (f_x, f_x2, f_y, f_y2))
-        f_own = [f_x, swap(f_x, "seq", 2), f_y, swap(f_y, "seq", 4)]
-        g1, g2, gb = unpack_small(order(f_x, a_mine[size:]))
-        a_own, g1 = order(g1, a_own, g1)
-        f_own = order(a_own, f_own)
-        gate, up, down = unpack_ffn(f_own, [swap(v, "seq", 1) for v in f_own])
-        gq, gk, gv, go = unpack_attention(a_own, [swap(v, "seq", 1) for v in a_own])
+        live["f"] = [swap(f_x2, "seq", 4), swap(f_y2, "seq", 2)]
+        size = (keep.shape[0] - SMALL) // 8
+        ffn_out = [shape(d, ff, dtype=f32), shape(d, ff, dtype=f32), shape(ff, d, dtype=f32)]
+        ffn_scratch = [pltpu.VMEM((8, 3 * PIECE, ff), f32), pltpu.SemaphoreType.DMA((32,))]
+        kept = dict(f=(f_x, f_y))
+
+        def f_rows():
+            (f_x, f_y), (f_x2, f_y2) = kept["f"], live["f"]
+            mine, other = call(by_row_kernel, "add_parts", 1, [part(8)] * 2, (ids,), (f_x, f_x2, f_y, f_y2))
+            kept["f"], live["f"] = mine, swap(other, "rows", 1)
+            return mine
+
+        def f_add(j):
+            mine = add_and_split(0, 1, 0, zero, kept["f"], live["f"])[0]
+            kept["f"], live["f"] = mine, swap(mine, "rows", j)
+            return mine
+
+        def f_pick():
+            x, y = call(pick_kernel, "pick", 1, [part(8)] * 2, (ids,), (kept["f"], live["f"]))
+            kept["f"], live["f"] = (x, y), [swap(x, "seq", 4), swap(y, "seq", 2)]
+            return x
+
+        def f_join():
+            (x, y), (x2, y2) = kept["f"], live["f"]
+            x, y = call(join_kernel, "join", 1, [part(4)] * 2, (ids,), (x, x2, y, y2))
+            kept["f"], live["f"] = (x, y), [swap(x, "seq", 2), swap(y, "seq", 4)]
+            live["near"] = [swap(v, "seq", 1) for v in (x, y)]
+            return x
+
+        def f_near():
+            kept["near"] = unpack(unpack_near_kernel, ids, (*kept["f"], *live["near"]), (), ffn_out, ffn_scratch)
+            return kept["near"][0]
+
+        def f_swap():
+            live["far"] = [swap(v, "seq", 1) for v in live["f"]]
+            return None
+
+        def a_chips():
+            kept["a"] = add_and_split(2, half, SMALL, ids, keep, live["a"])
+            live["a"] = to_chips(kept["a"])
+            return kept["a"][0]
+
+        def a_rows():
+            kept["a"], other = add_and_split(0, 2, SMALL, near, *live["a"])
+            live["a"] = swap(other, "rows", 1)
+            return kept["a"]
+
+        def a_add(j):
+            kept["a"] = add_and_split(0, 1, SMALL, zero, kept["a"], live["a"])[0]
+            live["a"] = swap(kept["a"], "rows", 2) if j == 2 else to_chips([kept["a"][:size]] * half)
+            return kept["a"]
+
+        def a_stack():
+            kept["stack"] = call(stack_kernel, "stack", 1, shape(half * size, d), (ids,), live["a"])
+            live["a"] = swap(kept["stack"], "rows", 1)
+            live["anear"] = swap(kept["stack"], "seq", 1)
+            return kept["stack"]
+
+        def a_swap():
+            live["afar"] = swap(live["a"], "seq", 1)
+            return None
+
+        def last():
+            kept["out"] = unpack(
+                partial(unpack_far_kernel, half), ids,
+                (*live["f"], *live["far"], kept["stack"], live["a"], live["anear"], live["afar"]), kept["near"],
+                ffn_out + [shape(d, width, dtype=f32)] * 3 + [shape(width, d, dtype=f32)],
+                [*ffn_scratch, pltpu.VMEM((4 * width, d), bf16), pltpu.VMEM((3, d, width), f32),
+                 pltpu.VMEM((width, d), f32), pltpu.SemaphoreType.DMA((4,))],
+            )
+            return kept["out"][0]
+
+        def d_slots():
+            kept["d"] = add_slots(live["d"])
+            live["d"] = to_chips(kept["d"])
+            return kept["d"][0]
+
+        def d_out():
+            kept["tokens"] = input_grad(live["d"])
+            return kept["tokens"]
+
+        def small():
+            kept["small"] = unpack_small(kept["a"][size:])
+            return kept["small"][0]
+
+        steps = dict(
+            f_rows=(f_rows, "f"), f_z0=(partial(f_add, 2), "f"), f_z1=(partial(f_add, 1), "f"), f_pick=(f_pick, "f"),
+            f_join=(f_join, "f"), f_near=(f_near, "near"), f_swap=(f_swap, "f"), last=(last, "far"),
+            a_chips=(a_chips, "a"), a_rows=(a_rows, "a"), a_z0=(partial(a_add, 2), "a"), a_z1=(partial(a_add, 1), "a"),
+            a_stack=(a_stack, "a"), a_swap=(a_swap, "a"),
+            d_slots=(d_slots, "d"), d_out=(d_out, "d"), small=(small, None),
+        )
+        token = f_x
+        for name in STEPS.split():
+            if ":" in name:
+                stream, j = name.split(":")
+                live[stream][int(j)] = token = order(token, live[stream][int(j)])
+                continue
+            step, stream = steps[name]
+            if stream is not None:
+                live[stream] = order(token, live[stream])
+            elif name == "small":
+                kept["a"] = order(token, kept["a"])
+            done = step()
+            token = live[stream] if done is None else done
+        gate, up, down, gq, gk, gv, go = kept["out"]
+        g1, g2, gb = kept["small"]
+        grad_tokens = kept["tokens"]
     return (
         output.reshape(tokens.shape), grad_tokens.reshape(tokens.shape), g1.reshape(d), gq, gk, gv, go, gb.T,
         g2.reshape(d), gate, up, down,

time: 124 us -> 117 us (0.944)
  waiting for transfers between devices: 35.3 us -> 26 us
  starting transfers between devices: 33.5 us -> 36.3 us
    ppermute x41 -> x39, waiting for transfers between devices: 35.3 us -> 26 us  [swap(): return lax.ppermute(array, axis, [(i, i ^ j) for i in range(size)])]
    pallas_call x23 -> x21, Pallas kernels: 48 us -> 41.2 us  [call(): pl.pallas_call(kernel, in_specs=[smem] * len(smem_args) + [vmem] * (len(a...]
    pallas_call x0 -> x2, Pallas kernels: none -> 6.27 us  [unpack(): pl.pallas_call(kernel, in_specs=[pl.BlockSpec(memory_space=pltpu.SMEM)] +...]
    ppermute x41 -> x39, starting transfers between devices: 33.5 us -> 36.3 us  [swap(): return lax.ppermute(array, axis, [(i, i ^ j) for i in range(size)])]
  transfers between devices with their start and end apart: 41 -> 39, of which waited for: 20 -> 24; matrix products, arithmetic and copies ran while one was open for 1% -> 1% of each run, Pallas kernels for 25% -> 26%
where the time goes in v4:
time: 117 us
  Pallas kernels  47.4 us (41%)
  starting transfers between devices  36.3 us (31%)
  waiting for transfers between devices  26 us (22%)
  local copies, waits for them, and re-layouts  6.01 us (5%)
    pallas_call x21, Pallas kernels, call(): pl.pallas_call(kernel, in_specs=[smem] * len(smem_args) + [vmem] * (len(a...  41.2 us
    ppermute x39, starting transfers between devices, swap(): return lax.ppermute(array, axis, [(i, i ^ j) for i in range(size)])  36.3 us
    ppermute x39, waiting for transfers between devices, swap(): return lax.ppermute(array, axis, [(i, i ^ j) for i in range(size)])  26 us
    pallas_call x2, Pallas kernels, unpack(): pl.pallas_call(kernel, in_specs=[pl.BlockSpec(memory_space=pltpu.SMEM)] +...  6.27 us
    unnamed x26, local copies, waits for them, and re-layouts  5.31 us
  transfers between devices with their start and end apart: 39, of which 24 were waited for; matrix products, arithmetic and copies ran while one was open for 1% of the time, Pallas kernels for 26%

profile of v4, /device:TPU:0, one launch (start us, length us, event | category | flops | bytes accessed | tf_op | source)
XLA Modules:
  0.0 117.0 jit_solution(8512462934795525642)
XLA Ops:
  1.2 2.6 %collective-permute-start.1 = (bf16[256,512]{1,0:T(8,128)(2,1)}, bf16[256,512]{1,0:T(8,128)(2,1)S(1)}, u32[]{:S(2)}, u32[]{:S(2)}) collective-permute-start(bf16[256,512]{1,0:T(8,128)(2,1)} %bitcast.14), channel_id=1, source_target_pairs={{0,2},{1,3},{2,0},{3,1},{4,6},{5,7},{6,4},{7,5},{8,10},{9,11},{10,... | collective-permute-start | bytes 786440 | tf_op jit(solution)/shard_map/ppermute | solution.py:634
  3.7 1.5 %collective-permute-start.3 = (bf16[256,512]{1,0:T(8,128)(2,1)}, bf16[256,512]{1,0:T(8,128)(2,1)S(1)}, u32[]{:S(2)}, u32[]{:S(2)}) collective-permute-start(bf16[256,512]{1,0:T(8,128)(2,1)} %bitcast.15), channel_id=1, source_target_pairs={{0,4},{1,5},{2,6},{3,7},{4,0},{5,1},{6,2},{7,3},{8,12},{9,13},{10,... | collective-permute-start | bytes 786440 | tf_op jit(solution)/shard_map/ppermute | solution.py:634
  5.3 0.7 reshape.55.gain.refs_2_.refs_6_.refs_13_.refs_7_
  6.0 1.0 copy-done.3
  7.0 1.0 copy-done.4
  8.0 1.0 copy-done.5
  9.0 0.9 copy-done.7
  10.0 0.7 copy-done.9
  10.6 0.7 copy-done.11
  11.3 2.3 %prepare.1 = (bf16[256,384]{1,0:T(8,128)(2,1)S(1)}, f32[256,128]{1,0:T(8,128)S(1)}, bf16[6,4,256,256]{3,2,1,0:T(8,128)(2,1)S(1)}, bf16[1152,512]{1,0:T(8,128)(2,...) custom-call(s32[4]{0:T(128)S(1)} %pad_add_fusion.ids, ...), custom_call_target="tpu_custom_call" | custom-call | flops 4000000 | bytes 8000 | tf_op jit(solution)/shard_map/prepare/pallas_call | solution.py:71
  13.7 3.2 %attend.2 = (bf16[512,512]{1,0:T(8,128)(2,1)S(1)}, bf16[512,128]{1,0:T(8,128)(2,1)S(1)}, f32[256,384]{1,0:T(8,128)S(1)}, f32[256,128]{1,0:T(8,128)S(1)}, bf16[2,...) custom-call(s32[4]{0:T(128)S(1)} %pad_add_fusion.ids, ...), custom_call_target="tpu_custom_call" | custom-call | flops 4000000 | bytes 8000 | tf_op jit(solution)/shard_map/attend/pallas_call | solution.py:71
  17.0 0.9 collective-permute-done.3.refs_2_
  18.6 0.9 collective-permute-done.4.refs_3_
  19.8 6.1 %attend.3 = (bf16[1536,512]{1,0:T(8,128)(2,1)S(1)}, bf16[1536,128]{1,0:T(8,128)(2,1)S(1)}, f32[256,384]{1,0:T(8,128)S(1)}, f32[256,128]{1,0:T(8,128)S(1)}, bf16[...) custom-call(s32[4]{0:T(128)S(1)} %pad_add_fusion.ids, ...), custom_call_target="tpu_custom_call" | custom-call | flops 12000000 | bytes 24000 | tf_op jit(solution)/shard_map/attend/pallas_call | solution.py:71
  26.0 5.8 %feed_forward.1 = (bf16[256,512]{1,0:T(8,128)(2,1)}, f32[256,512]{1,0:T(8,128)S(1)}, bf16[256,384]{1,0:T(8,128)(2,1)S(1)}, f32[256,128]{1,0:T(8,128)S(1)}, bf16[...) custom-call(s32[4]{0:T(128)S(1)} %pad_add_fusion.ids, ...), custom_call_target="tpu_custom_call" | custom-call | flops 8000000 | bytes 16000 | tf_op jit(solution)/shard_map/feed_forward/pallas_call | solution.py:71
  32.0 3.3 %attend_back.1 = (bf16[128,2048]{1,0:T(8,128)(2,1)S(1)}, bf16[128,2048]{1,0:T(8,128)(2,1)S(1)}, bf16[256,128]{1,0:T(8,128)(2,1)S(1)}, f32[8,1152]{1,0:T(8,128)S(1)}) custom-call(s32[4]{0:T(128)S(1)} %pad_add_fusion.ids, bf16[256,384]{1,0:T(8,128)(2,1)S(1)} %get-tuple-element.137.refs_5_.refs_9_.q.refs_0_, ...), custom_call_target="tpu_custom_call" | custom-call | flops 4000000 | bytes 8000 | tf_op jit(solution)/shard_map/attend_back/pallas_call | solution.py:71
  35.3 0.9 add_parts.9
  36.3 1.5 %collective-permute-start.8 = (bf16[192,1024]{1,0:T(8,128)(2,1)S(1)}, bf16[192,1024]{1,0:T(8,128)(2,1)S(1)}, u32[]{:S(2)}, u32[]{:S(2)}) collective-permute-start(bf16[192,1024]{1,0:T(8,128)(2,1)S(1)} %get-tuple-element.181), channel_id=1, source_target_pairs={{0,2},{1,3},{2,0},{3,1},{4,6},{5,7},{6,4},{7,5},{8,10},{9,11},{10,... | collective-permute-start | bytes 1179656 | tf_op jit(solution)/shard_map/ppermute | solution.py:634
  37.7 1.5 %collective-permute-start.9 = (bf16[192,1024]{1,0:T(8,128)(2,1)S(1)}, bf16[192,1024]{1,0:T(8,128)(2,1)S(1)}, u32[]{:S(2)}, u32[]{:S(2)}) collective-permute-start(bf16[192,1024]{1,0:T(8,128)(2,1)S(1)} %get-tuple-element.183), channel_id=1, source_target_pairs={{0,4},{1,5},{2,6},{3,7},{4,0},{5,1},{6,2},{7,3},{8,12},{9,13},{10,... | collective-permute-start | bytes 1179656 | tf_op jit(solution)/shard_map/ppermute | solution.py:634
  39.3 9.3 %rest_back.1 = (bf16[4,512,256]{2,1,0:T(8,128)(2,1)S(1)}, bf16[4,512,256]{2,1,0:T(8,128)(2,1)S(1)}, f32[256,512]{1,0:T(8,128)S(1)}, bf16[784,512]{1,0:T(8,128)(2,1)S(1)}, bf16[784,512]{1,0:T(8,128)(2,1)S(1)}) custom-call(s32[4]{0:T(128)S(1)} %pad_add_fusion.ids, bf16[256,384]{1,0:T(8,128)(2,1)S(1)} %get-tuple-element.137.refs_5_.refs_9_.q.refs_0_, ...), custom_call_target="tpu_custom_call" | custom-call | flops 10000000 | bytes 20000 | tf_op jit(solution)/shard_map/rest_back/pallas_call | solution.py:71
  49.4 0.7 add_parts.10
  50.1 1.6 %collective-permute-start.11 = (bf16[96,1024]{1,0:T(8,128)(2,1)S(1)}, bf16[96,1024]{1,0:T(8,128)(2,1)S(1)}, u32[]{:S(2)}, u32[]{:S(2)}) collective-permute-start(bf16[96,1024]{1,0:T(8,128)(2,1)S(1)} %get-tuple-element.191), channel_id=1, source_target_pairs={{0,4},{1,5},{2,6},{3,7},{4,0},{5,1},{6,2},{7,3},{8,12},{9,13},{10,... | collective-permute-start | bytes 589832 | tf_op jit(solution)/shard_map/ppermute | solution.py:634
  51.7 0.6 collective-permute-start.12
  52.3 0.7 add_parts.11
  53.0 3.9 %collective-permute-done.11.recv_x = bf16[96,1024]{1,0:T(8,128)(2,1)S(1)} collective-permute-done((bf16[96,1024]{1,0:T(8,128)(2,1)S(1)}, bf16[96,1024]{1,0:T(8,128)(2,1)S(1)}, u32[]{:S(2)}, u32[]{:S(2)}) %collective-permute-start.11) | collective-permute-done | bytes 196640 | tf_op jit(solution)/shard_map/ppermute | solution.py:634
  57.0 1.2 %collective-permute-done.12.recv_y = bf16[96,1024]{1,0:T(8,128)(2,1)S(1)} collective-permute-done((bf16[96,1024]{1,0:T(8,128)(2,1)S(1)}, bf16[96,1024]{1,0:T(8,128)(2,1)S(1)}, u32[]{:S(2)}, u32[]{:S(2)}) %collective-permute-start.12) | collective-permute-done | bytes 196640 | tf_op jit(solution)/shard_map/ppermute | solution.py:634
  58.2 0.7 add_parts.12
  58.9 1.6 %collective-permute-start.13 = (bf16[96,1024]{1,0:T(8,128)(2,1)S(1)}, bf16[96,1024]{1,0:T(8,128)(2,1)S(1)}, u32[]{:S(2)}, u32[]{:S(2)}) collective-permute-start(bf16[96,1024]{1,0:T(8,128)(2,1)S(1)} %get-tuple-element.197), channel_id=1, source_target_pairs={{0,8},{8,0},{16,24},{24,16},{1,9},{9,1},{17,25},{25,17},{2,10},{10... | collective-permute-start | bytes 589832 | tf_op jit(solution)/shard_map/ppermute | solution.py:634
  60.5 0.6 collective-permute-start.14
  61.1 0.6 collective-permute-start.15
  61.7 2.3 %collective-permute-start.16 = (bf16[208,512]{1,0:T(8,128)(2,1)S(1)}, bf16[208,512]{1,0:T(8,128)(2,1)S(1)}, u32[]{:S(2)}, u32[]{:S(2)}) collective-permute-start(bf16[208,512]{1,0:T(8,128)(2,1)S(1)} %get-tuple-element.201), channel_id=1, source_target_pairs={{0,6},{1,7},{2,4},{3,5},{4,2},{5,3},{6,0},{7,1},{8,14},{9,15},{10,... | collective-permute-start | bytes 638984 | tf_op jit(solution)/shard_map/ppermute | solution.py:634
  64.0 0.6 collective-permute-done.13.refs_1_
  64.6 0.6 add_parts.13.refs_0_
  65.2 2.7 %collective-permute-start.20 = (bf16[96,1024]{1,0:T(8,128)(2,1)S(1)}, bf16[96,1024]{1,0:T(8,128)(2,1)S(1)}, u32[]{:S(2)}, u32[]{:S(2)}) collective-permute-start(bf16[96,1024]{1,0:T(8,128)(2,1)S(1)} %add_parts.13.refs_0_), channel_id=1, source_target_pairs={{0,16},{8,24},{16,0},{24,8},{1,17},{9,25},{17,1},{25,9},{2,18},{10... | collective-permute-start | bytes 589832 | tf_op jit(solution)/shard_map/ppermute | solution.py:634
  67.9 0.6 collective-permute-done.14.refs_1_
  68.5 2.6 %collective-permute-done.15.refs_2_ = bf16[208,512]{1,0:T(8,128)(2,1)S(1)} collective-permute-done((bf16[208,512]{1,0:T(8,128)(2,1)S(1)}, bf16[208,512]{1,0:T(8,128)(2,1)S(1)}, u32[]{:S(2)}, u32[]{:S(2)}) %collective-permute-start.15) | collective-permute-done | bytes 213024 | tf_op jit(solution)/shard_map/ppermute | solution.py:634
  71.3 0.8 add_slots.1
  72.1 1.5 %collective-permute-start.23 = (bf16[512,256]{1,0:T(8,128)(2,1)S(1)}, bf16[512,256]{1,0:T(8,128)(2,1)S(1)}, u32[]{:S(2)}, u32[]{:S(2)}) collective-permute-start(bf16[512,256]{1,0:T(8,128)(2,1)S(1)} %get-tuple-element.217), channel_id=1, source_target_pairs={{0,6},{1,7},{2,4},{3,5},{4,2},{5,3},{6,0},{7,1},{8,14},{9,15},{10,... | collective-permute-start | bytes 786440 | tf_op jit(solution)/shard_map/ppermute | solution.py:634
  73.6 1.3 %collective-permute-done.20.refs_1_ = bf16[96,1024]{1,0:T(8,128)(2,1)S(1)} collective-permute-done((bf16[96,1024]{1,0:T(8,128)(2,1)S(1)}, bf16[96,1024]{1,0:T(8,128)(2,1)S(1)}, u32[]{:S(2)}, u32[]{:S(2)}) %collective-permute-start.20) | collective-permute-done | bytes 196640 | tf_op jit(solution)/shard_map/ppermute | solution.py:634
  74.9 0.6 add_parts.15.mine
  75.5 0.7 collective-permute-start.21
  76.2 0.6 collective-permute-start.18
  76.8 0.7 collective-permute-start.19
  77.5 1.3 %collective-permute-start.22 = (bf16[112,512]{1,0:T(8,128)(2,1)S(1)}, bf16[112,512]{1,0:T(8,128)(2,1)S(1)}, u32[]{:S(2)}, u32[]{:S(2)}) collective-permute-start(bf16[112,512]{1,0:T(8,128)(2,1)S(1)} %get-tuple-element.215), channel_id=1, source_target_pairs={{0,8},{8,0},{16,24},{24,16},{1,9},{9,1},{17,25},{25,17},{2,10},{10... | collective-permute-start | bytes 344072 | tf_op jit(solution)/shard_map/ppermute | solution.py:634
  78.9 3.6 %collective-permute-done.21.other = bf16[96,1024]{1,0:T(8,128)(2,1)S(1)} collective-permute-done((bf16[96,1024]{1,0:T(8,128)(2,1)S(1)}, bf16[96,1024]{1,0:T(8,128)(2,1)S(1)}, u32[]{:S(2)}, u32[]{:S(2)}) %collective-permute-start.21) | collective-permute-done | bytes 196640 | tf_op jit(solution)/shard_map/ppermute | solution.py:634
  82.4 0.6 pick.1
  84.2 2.3 %collective-permute-start.24 = (bf16[112,512]{1,0:T(8,128)(2,1)S(1)}, bf16[112,512]{1,0:T(8,128)(2,1)S(1)}, u32[]{:S(2)}, u32[]{:S(2)}) collective-permute-start(bf16[112,512]{1,0:T(8,128)(2,1)S(1)} %add_parts.16.refs_0_), channel_id=1, source_target_pairs={{0,16},{8,24},{16,0},{24,8},{1,17},{9,25},{17,1},{25,9},{2,18},{10... | collective-permute-start | bytes 344072 | tf_op jit(solution)/shard_map/ppermute | solution.py:634
  86.5 1.2 %collective-permute-start.25 = (bf16[96,1024]{1,0:T(8,128)(2,1)S(1)}, bf16[96,1024]{1,0:T(8,128)(2,1)S(1)}, u32[]{:S(2)}, u32[]{:S(2)}) collective-permute-start(bf16[96,1024]{1,0:T(8,128)(2,1)S(1)} %get-tuple-element.214.a), channel_id=1, source_target_pairs={{0,4},{1,5},{2,6},{3,7},{4,0},{5,1},{6,2},{7,3},{8,12},{9,13},{10,... | collective-permute-start | bytes 589832 | tf_op jit(solution)/shard_map/ppermute | solution.py:634
  87.7 1.4 %collective-permute-start.26 = (bf16[96,1024]{1,0:T(8,128)(2,1)S(1)}, bf16[96,1024]{1,0:T(8,128)(2,1)S(1)}, u32[]{:S(2)}, u32[]{:S(2)}) collective-permute-start(bf16[96,1024]{1,0:T(8,128)(2,1)S(1)} %get-tuple-element.226.c), channel_id=1, source_target_pairs={{0,2},{1,3},{2,0},{3,1},{4,6},{5,7},{6,4},{7,5},{8,10},{9,11},{10,... | collective-permute-start | bytes 589832 | tf_op jit(solution)/shard_map/ppermute | solution.py:634
  89.1 1.8 %input_grad.1 = f32[256,512]{1,0:T(8,128)} custom-call(s32[4]{0:T(128)S(1)} %pad_add_fusion.ids, bf16[512,256]{1,0:T(8,128)(2,1)S(1)} %get-tuple-element.219.refs_0_, bf16[512,256]{1,0:T(8,128)(2,1)S(1)} %collective-permute-done.18.refs_1_, bf16[512,256]{1,0:T(8,128)(2,1)S(1)} %collective-permute-done.19.refs_2_, ...), custom_call_target="tpu_custom_call" | custom-call | flops 2000000 | bytes 4000 | tf_op jit(solution)/shard_map/input_grad/pallas_call | solution.py:71
  91.8 0.7 collective-permute-start.27
  92.5 1.2 %collective-permute-start.28 = (bf16[96,512]{1,0:T(8,128)(2,1)S(1)}, bf16[96,512]{1,0:T(8,128)(2,1)S(1)}, u32[]{:S(2)}, u32[]{:S(2)}) collective-permute-start(bf16[96,512]{1,0:T(8,128)(2,1)S(1)} %slice.8.refs_0_), channel_id=1, source_target_pairs={{0,4},{1,5},{2,6},{3,7},{4,0},{5,1},{6,2},{7,3},{8,12},{9,13},{10,... | collective-permute-start | bytes 294920 | tf_op jit(solution)/shard_map/ppermute | solution.py:634
  93.7 1.6 %collective-permute-start.29 = (bf16[96,512]{1,0:T(8,128)(2,1)S(1)}, bf16[96,512]{1,0:T(8,128)(2,1)S(1)}, u32[]{:S(2)}, u32[]{:S(2)}) collective-permute-start(bf16[96,512]{1,0:T(8,128)(2,1)S(1)} %slice.8.refs_0_), channel_id=1, source_target_pairs={{0,6},{1,7},{2,4},{3,5},{4,2},{5,3},{6,0},{7,1},{8,14},{9,15},{10,... | collective-permute-start | bytes 294920 | tf_op jit(solution)/shard_map/ppermute | solution.py:634
  95.5 0.6 join.1
  97.1 2.1 %collective-permute-done.29.refs_3_ = bf16[96,512]{1,0:T(8,128)(2,1)S(1)} collective-permute-done((bf16[96,512]{1,0:T(8,128)(2,1)S(1)}, bf16[96,512]{1,0:T(8,128)(2,1)S(1)}, u32[]{:S(2)}, u32[]{:S(2)}) %collective-permute-start.29) | collective-permute-done | bytes 98336 | tf_op jit(solution)/shard_map/ppermute | solution.py:634
  99.8 1.1 collective-permute-start.32
  100.9 0.6 collective-permute-start.33
  101.5 0.9 collective-permute-start.34
  102.4 2.5 %unpack.2 = (f32[512,1024]{1,0:T(8,128)}, f32[512,1024]{1,0:T(8,128)}, f32[1024,512]{1,0:T(8,128)}) custom-call(s32[4]{0:T(128)S(1)} %pad_add_fusion.ids, bf16[192,1024]{1,0:T(8,128)(2,1)S(1)} %get-tuple-element.229.refs_0_, bf16[192,1024]{1,0:T(8,128)(2,1)S(1)} %get-tuple-element.230.refs_1_, bf16[192,1024]{1,0:T(8,128)(2,1)S(1)} %collective-permute-done.30.refs_2_, ...), custom_call_target="tpu_custom_call" | custom-call | flops 1000 | bytes 1000 | tf_op jit(solution)/shard_map/unpack/pallas_call | solution.py:723
  104.9 1.1 unpack_small.1
  106.1 2.3 %collective-permute-done.32.refs_5_ = bf16[384,512]{1,0:T(8,128)(2,1)S(1)} collective-permute-done((bf16[384,512]{1,0:T(8,128)(2,1)S(1)}, bf16[384,512]{1,0:T(8,128)(2,1)S(1)}, u32[]{:S(2)}, u32[]{:S(2)}) %collective-permute-start.32) | collective-permute-done | bytes 393248 | tf_op jit(solution)/shard_map/ppermute | solution.py:634
  108.9 0.7 collective-permute-done.34.refs_1_
  110.6 0.7 collective-permute-done.35.refs_2_
  113.0 3.8 %unpack.3 = (f32[512,1024]{1,0:T(8,128)}, f32[512,1024]{1,0:T(8,128)}, f32[1024,512]{1,0:T(8,128)}, f32[512,384]{1,0:T(8,128)}, f32[512,384]{1,0:T(8,128)}, /*index=5*/f32[512,384]{1,0:T(8,128)}, f32[384,512]{1,0:T(8,128)}) custom-call(s32[4]{0:T(128)S(1)} %pad_add_fusion.ids, ...), custom_call_target="tpu_custom_call", output_to_operand_aliasing={{0}: (9, {}), {1}: (10, {}), {2}: (11, {})} | custom-call | flops 1000 | bytes 1000 | tf_op jit(solution)/shard_map/unpack/pallas_call | solution.py:723
  (69 shorter events, 9.7 us)
Async XLA Ops:
  0.6 13.0 %collective-permute-start = (bf16[256,512]{1,0:T(8,128)(2,1)}, bf16[256,512]{1,0:T(8,128)(2,1)S(1)}, u32[]{:S(2)}, u32[]{:S(2)}) collective-permute-start(bf16[256,512]{1,0:T(8,128)(2,1)} %bitcast.13), channel_id=1, source_target_pairs={{0,1},{1,0},{2,3},{3,2},{4,5},{5,4},{6,7},{7,6},{8,9},{9,8},{10,11... | collective-permute-start | bytes 786440 | tf_op jit(solution)/shard_map/ppermute | solution.py:634
  1.2 15.8 %collective-permute-start.1 = (bf16[256,512]{1,0:T(8,128)(2,1)}, bf16[256,512]{1,0:T(8,128)(2,1)S(1)}, u32[]{:S(2)}, u32[]{:S(2)}) collective-permute-start(bf16[256,512]{1,0:T(8,128)(2,1)} %bitcast.14), channel_id=1, source_target_pairs={{0,2},{1,3},{2,0},{3,1},{4,6},{5,7},{6,4},{7,5},{8,10},{9,11},{10,... | collective-permute-start | bytes 786440 | tf_op jit(solution)/shard_map/ppermute | solution.py:634
  3.7 14.2 %collective-permute-start.3 = (bf16[256,512]{1,0:T(8,128)(2,1)}, bf16[256,512]{1,0:T(8,128)(2,1)S(1)}, u32[]{:S(2)}, u32[]{:S(2)}) collective-permute-start(bf16[256,512]{1,0:T(8,128)(2,1)} %bitcast.15), channel_id=1, source_target_pairs={{0,4},{1,5},{2,6},{3,7},{4,0},{5,1},{6,2},{7,3},{8,12},{9,13},{10,... | collective-permute-start | bytes 786440 | tf_op jit(solution)/shard_map/ppermute | solution.py:634
  5.2 12.7 %collective-permute-start.5 = (bf16[256,512]{1,0:T(8,128)(2,1)}, bf16[256,512]{1,0:T(8,128)(2,1)S(1)}, u32[]{:S(2)}, u32[]{:S(2)}) collective-permute-start(bf16[256,512]{1,0:T(8,128)(2,1)} %bitcast.16), channel_id=1, source_target_pairs={{0,6},{1,7},{2,4},{3,5},{4,2},{5,3},{6,0},{7,1},{8,14},{9,15},{10,... | collective-permute-start | bytes 786440 | tf_op jit(solution)/shard_map/ppermute | solution.py:634
  6.0 1.0 copy-start.3
  7.0 1.0 copy-start.4
  8.0 1.0 copy-start.5
  9.0 0.9 copy-start.7
  10.0 0.7 copy-start.9
  10.6 0.7 copy-start.11
  13.7 4.8 %copy-start.12 = (bf16[512]{0:T(512)(128)(2,1)S(1)}, bf16[512]{0:T(512)(128)(2,1)}, u32[]{:S(2)}) copy-start(bf16[512]{0:T(512)(128)(2,1)} %param.20) | copy-start | bytes 3076
  13.7 6.2 %copy-start.10 = (s32[1,16]{1,0:T(1,128)S(1)}, s32[1,16]{1,0:T(1,128)}, u32[]{:S(2)}) copy-start(s32[1,16]{1,0:T(1,128)} %param.24) | copy-start | bytes 196
  17.0 1.6 %collective-permute-start.2 = (bf16[256,512]{1,0:T(8,128)(2,1)S(1)}, bf16[256,512]{1,0:T(8,128)(2,1)S(1)}, u32[]{:S(2)}, u32[]{:S(2)}) collective-permute-start(bf16[256,512]{1,0:T(8,128)(2,1)S(1)} %collective-permute-done.1.refs_0_), channel_id=1, source_target_pairs={{0,1},{1,0},{2,3},{3,2},{4,5},{5,4},{6,7},{7,6},{8,9},{9,8},{10,11... | collective-permute-start | bytes 786440 | tf_op jit(solution)/shard_map/ppermute | solution.py:634
  17.9 1.5 %collective-permute-start.4 = (bf16[256,512]{1,0:T(8,128)(2,1)S(1)}, bf16[256,512]{1,0:T(8,128)(2,1)S(1)}, u32[]{:S(2)}, u32[]{:S(2)}) collective-permute-start(bf16[256,512]{1,0:T(8,128)(2,1)S(1)} %collective-permute-done.3.refs_2_), channel_id=1, source_target_pairs={{0,1},{1,0},{2,3},{3,2},{4,5},{5,4},{6,7},{7,6},{8,9},{9,8},{10,11... | collective-permute-start | bytes 786440 | tf_op jit(solution)/shard_map/ppermute | solution.py:634
  17.9 1.9 %collective-permute-start.6 = (bf16[256,512]{1,0:T(8,128)(2,1)S(1)}, bf16[256,512]{1,0:T(8,128)(2,1)S(1)}, u32[]{:S(2)}, u32[]{:S(2)}) collective-permute-start(bf16[256,512]{1,0:T(8,128)(2,1)S(1)} %collective-permute-done.5.refs_4_), channel_id=1, source_target_pairs={{0,1},{1,0},{2,3},{3,2},{4,5},{5,4},{6,7},{7,6},{8,9},{9,8},{10,11... | collective-permute-start | bytes 786440 | tf_op jit(solution)/shard_map/ppermute | solution.py:634
  18.5 7.5 %copy-start = (bf16[512,1024]{1,0:T(8,128)(2,1)S(1)}, bf16[512,1024]{1,0:T(8,128)(2,1)}, u32[]{:S(2)}) copy-start(bf16[512,1024]{1,0:T(8,128)(2,1)} %wg.1) | copy-start | bytes 3145732
  18.5 7.5 %copy-start.1 = (bf16[512,1024]{1,0:T(8,128)(2,1)S(1)}, bf16[512,1024]{1,0:T(8,128)(2,1)}, u32[]{:S(2)}) copy-start(bf16[512,1024]{1,0:T(8,128)(2,1)} %wu.1) | copy-start | bytes 3145732
  18.5 7.5 %copy-start.2 = (bf16[1024,512]{1,0:T(8,128)(2,1)S(1)}, bf16[1024,512]{1,0:T(8,128)(2,1)}, u32[]{:S(2)}) copy-start(bf16[1024,512]{1,0:T(8,128)(2,1)} %wd.1) | copy-start | bytes 3145732
  18.5 7.5 %copy-start.6 = (bf16[384,512]{1,0:T(8,128)(2,1)S(1)}, bf16[384,512]{1,0:T(8,128)(2,1)}, u32[]{:S(2)}) copy-start(bf16[384,512]{1,0:T(8,128)(2,1)} %wo.1) | copy-start | bytes 1179652
  18.5 7.5 %copy-start.8 = (bf16[1,256,512]{2,1,0:T(8,128)(2,1)S(1)}, bf16[1,256,512]{2,1,0:T(8,128)(2,1)}, u32[]{:S(2)}) copy-start(bf16[1,256,512]{2,1,0:T(8,128)(2,1)} %param.25) | copy-start | bytes 786436
  31.9 3.4 %collective-permute-start.7 = (bf16[768,1024]{1,0:T(8,128)(2,1)S(1)}, bf16[768,1024]{1,0:T(8,128)(2,1)S(1)}, u32[]{:S(2)}, u32[]{:S(2)}) collective-permute-start(bf16[768,1024]{1,0:T(8,128)(2,1)S(1)} %get-tuple-element.159), channel_id=1, source_target_pairs={{0,1},{1,0},{2,3},{3,2},{4,5},{5,4},{6,7},{7,6},{8,9},{9,8},{10,11... | collective-permute-start | bytes 4718600 | tf_op jit(solution)/shard_map/ppermute | solution.py:634
  36.3 12.4 %collective-permute-start.8 = (bf16[192,1024]{1,0:T(8,128)(2,1)S(1)}, bf16[192,1024]{1,0:T(8,128)(2,1)S(1)}, u32[]{:S(2)}, u32[]{:S(2)}) collective-permute-start(bf16[192,1024]{1,0:T(8,128)(2,1)S(1)} %get-tuple-element.181), channel_id=1, source_target_pairs={{0,2},{1,3},{2,0},{3,1},{4,6},{5,7},{6,4},{7,5},{8,10},{9,11},{10,... | collective-permute-start | bytes 1179656 | tf_op jit(solution)/shard_map/ppermute | solution.py:634
  37.7 11.1 %collective-permute-start.9 = (bf16[192,1024]{1,0:T(8,128)(2,1)S(1)}, bf16[192,1024]{1,0:T(8,128)(2,1)S(1)}, u32[]{:S(2)}, u32[]{:S(2)}) collective-permute-start(bf16[192,1024]{1,0:T(8,128)(2,1)S(1)} %get-tuple-element.183), channel_id=1, source_target_pairs={{0,4},{1,5},{2,6},{3,7},{4,0},{5,1},{6,2},{7,3},{8,12},{9,13},{10,... | collective-permute-start | bytes 1179656 | tf_op jit(solution)/shard_map/ppermute | solution.py:634
  48.8 3.5 %collective-permute-start.10 = (bf16[784,512]{1,0:T(8,128)(2,1)S(1)}, bf16[784,512]{1,0:T(8,128)(2,1)S(1)}, u32[]{:S(2)}, u32[]{:S(2)}) collective-permute-start(bf16[784,512]{1,0:T(8,128)(2,1)S(1)} %get-tuple-element.188), channel_id=1, source_target_pairs={{0,1},{1,0},{2,3},{3,2},{4,5},{5,4},{6,7},{7,6},{8,9},{9,8},{10,11... | collective-permute-start | bytes 2408456 | tf_op jit(solution)/shard_map/ppermute | solution.py:634
  48.8 22.4 %collective-permute-start.17 = (bf16[4,512,256]{2,1,0:T(8,128)(2,1)S(1)}, bf16[4,512,256]{2,1,0:T(8,128)(2,1)S(1)}, u32[]{:S(2)}, u32[]{:S(2)}) collective-permute-start(bf16[4,512,256]{2,1,0:T(8,128)(2,1)S(1)} %get-tuple-element.207), channel_id=1, source_target_pairs={{0,1},{1,0},{2,3},{3,2},{4,5},{5,4},{6,7},{7,6},{8,9},{9,8},{10,11... | collective-permute-start | bytes 3145736 | tf_op jit(solution)/shard_map/ppermute | solution.py:634
  50.1 6.9 %collective-permute-start.11 = (bf16[96,1024]{1,0:T(8,128)(2,1)S(1)}, bf16[96,1024]{1,0:T(8,128)(2,1)S(1)}, u32[]{:S(2)}, u32[]{:S(2)}) collective-permute-start(bf16[96,1024]{1,0:T(8,128)(2,1)S(1)} %get-tuple-element.191), channel_id=1, source_target_pairs={{0,4},{1,5},{2,6},{3,7},{4,0},{5,1},{6,2},{7,3},{8,12},{9,13},{10,... | collective-permute-start | bytes 589832 | tf_op jit(solution)/shard_map/ppermute | solution.py:634
  51.7 6.5 %collective-permute-start.12 = (bf16[96,1024]{1,0:T(8,128)(2,1)S(1)}, bf16[96,1024]{1,0:T(8,128)(2,1)S(1)}, u32[]{:S(2)}, u32[]{:S(2)}) collective-permute-start(bf16[96,1024]{1,0:T(8,128)(2,1)S(1)} %get-tuple-element.192), channel_id=1, source_target_pairs={{0,2},{1,3},{2,0},{3,1},{4,6},{5,7},{6,4},{7,5},{8,10},{9,11},{10,... | collective-permute-start | bytes 589832 | tf_op jit(solution)/shard_map/ppermute | solution.py:634
  58.9 5.7 %collective-permute-start.13 = (bf16[96,1024]{1,0:T(8,128)(2,1)S(1)}, bf16[96,1024]{1,0:T(8,128)(2,1)S(1)}, u32[]{:S(2)}, u32[]{:S(2)}) collective-permute-start(bf16[96,1024]{1,0:T(8,128)(2,1)S(1)} %get-tuple-element.197), channel_id=1, source_target_pairs={{0,8},{8,0},{16,24},{24,16},{1,9},{9,1},{17,25},{25,17},{2,10},{10... | collective-permute-start | bytes 589832 | tf_op jit(solution)/shard_map/ppermute | solution.py:634
  60.5 8.0 %collective-permute-start.14 = (bf16[208,512]{1,0:T(8,128)(2,1)S(1)}, bf16[208,512]{1,0:T(8,128)(2,1)S(1)}, u32[]{:S(2)}, u32[]{:S(2)}) collective-permute-start(bf16[208,512]{1,0:T(8,128)(2,1)S(1)} %get-tuple-element.199), channel_id=1, source_target_pairs={{0,2},{1,3},{2,0},{3,1},{4,6},{5,7},{6,4},{7,5},{8,10},{9,11},{10,... | collective-permute-start | bytes 638984 | tf_op jit(solution)/shard_map/ppermute | solution.py:634
  61.1 10.0 %collective-permute-start.15 = (bf16[208,512]{1,0:T(8,128)(2,1)S(1)}, bf16[208,512]{1,0:T(8,128)(2,1)S(1)}, u32[]{:S(2)}, u32[]{:S(2)}) collective-permute-start(bf16[208,512]{1,0:T(8,128)(2,1)S(1)} %get-tuple-element.200), channel_id=1, source_target_pairs={{0,4},{1,5},{2,6},{3,7},{4,0},{5,1},{6,2},{7,3},{8,12},{9,13},{10,... | collective-permute-start | bytes 638984 | tf_op jit(solution)/shard_map/ppermute | solution.py:634
  61.7 9.4 %collective-permute-start.16 = (bf16[208,512]{1,0:T(8,128)(2,1)S(1)}, bf16[208,512]{1,0:T(8,128)(2,1)S(1)}, u32[]{:S(2)}, u32[]{:S(2)}) collective-permute-start(bf16[208,512]{1,0:T(8,128)(2,1)S(1)} %get-tuple-element.201), channel_id=1, source_target_pairs={{0,6},{1,7},{2,4},{3,5},{4,2},{5,3},{6,0},{7,1},{8,14},{9,15},{10,... | collective-permute-start | bytes 638984 | tf_op jit(solution)/shard_map/ppermute | solution.py:634
  65.2 9.7 %collective-permute-start.20 = (bf16[96,1024]{1,0:T(8,128)(2,1)S(1)}, bf16[96,1024]{1,0:T(8,128)(2,1)S(1)}, u32[]{:S(2)}, u32[]{:S(2)}) collective-permute-start(bf16[96,1024]{1,0:T(8,128)(2,1)S(1)} %add_parts.13.refs_0_), channel_id=1, source_target_pairs={{0,16},{8,24},{16,0},{24,8},{1,17},{9,25},{17,1},{25,9},{2,18},{10... | collective-permute-start | bytes 589832 | tf_op jit(solution)/shard_map/ppermute | solution.py:634
  72.1 15.6 %collective-permute-start.23 = (bf16[512,256]{1,0:T(8,128)(2,1)S(1)}, bf16[512,256]{1,0:T(8,128)(2,1)S(1)}, u32[]{:S(2)}, u32[]{:S(2)}) collective-permute-start(bf16[512,256]{1,0:T(8,128)(2,1)S(1)} %get-tuple-element.217), channel_id=1, source_target_pairs={{0,6},{1,7},{2,4},{3,5},{4,2},{5,3},{6,0},{7,1},{8,14},{9,15},{10,... | collective-permute-start | bytes 786440 | tf_op jit(solution)/shard_map/ppermute | solution.py:634
  75.5 7.0 %collective-permute-start.21 = (bf16[96,1024]{1,0:T(8,128)(2,1)S(1)}, bf16[96,1024]{1,0:T(8,128)(2,1)S(1)}, u32[]{:S(2)}, u32[]{:S(2)}) collective-permute-start(bf16[96,1024]{1,0:T(8,128)(2,1)S(1)} %add_parts.15.mine), channel_id=1, source_target_pairs={{0,8},{8,0},{16,24},{24,16},{1,9},{9,1},{17,25},{25,17},{2,10},{10... | collective-permute-start | bytes 589832 | tf_op jit(solution)/shard_map/ppermute | solution.py:634
  76.2 12.9 %collective-permute-start.18 = (bf16[512,256]{1,0:T(8,128)(2,1)S(1)}, bf16[512,256]{1,0:T(8,128)(2,1)S(1)}, u32[]{:S(2)}, u32[]{:S(2)}) collective-permute-start(bf16[512,256]{1,0:T(8,128)(2,1)S(1)} %get-tuple-element.210), channel_id=1, source_target_pairs={{0,2},{1,3},{2,0},{3,1},{4,6},{5,7},{6,4},{7,5},{8,10},{9,11},{10,... | collective-permute-start | bytes 786440 | tf_op jit(solution)/shard_map/ppermute | solution.py:634
  76.8 12.2 %collective-permute-start.19 = (bf16[512,256]{1,0:T(8,128)(2,1)S(1)}, bf16[512,256]{1,0:T(8,128)(2,1)S(1)}, u32[]{:S(2)}, u32[]{:S(2)}) collective-permute-start(bf16[512,256]{1,0:T(8,128)(2,1)S(1)} %get-tuple-element.211), channel_id=1, source_target_pairs={{0,4},{1,5},{2,6},{3,7},{4,0},{5,1},{6,2},{7,3},{8,12},{9,13},{10,... | collective-permute-start | bytes 786440 | tf_op jit(solution)/shard_map/ppermute | solution.py:634
  77.5 6.2 %collective-permute-start.22 = (bf16[112,512]{1,0:T(8,128)(2,1)S(1)}, bf16[112,512]{1,0:T(8,128)(2,1)S(1)}, u32[]{:S(2)}, u32[]{:S(2)}) collective-permute-start(bf16[112,512]{1,0:T(8,128)(2,1)S(1)} %get-tuple-element.215), channel_id=1, source_target_pairs={{0,8},{8,0},{16,24},{24,16},{1,9},{9,1},{17,25},{25,17},{2,10},{10... | collective-permute-start | bytes 344072 | tf_op jit(solution)/shard_map/ppermute | solution.py:634
  84.2 7.0 %collective-permute-start.24 = (bf16[112,512]{1,0:T(8,128)(2,1)S(1)}, bf16[112,512]{1,0:T(8,128)(2,1)S(1)}, u32[]{:S(2)}, u32[]{:S(2)}) collective-permute-start(bf16[112,512]{1,0:T(8,128)(2,1)S(1)} %add_parts.16.refs_0_), channel_id=1, source_target_pairs={{0,16},{8,24},{16,0},{24,8},{1,17},{9,25},{17,1},{25,9},{2,18},{10... | collective-permute-start | bytes 344072 | tf_op jit(solution)/shard_map/ppermute | solution.py:634
  86.5 8.9 %collective-permute-start.25 = (bf16[96,1024]{1,0:T(8,128)(2,1)S(1)}, bf16[96,1024]{1,0:T(8,128)(2,1)S(1)}, u32[]{:S(2)}, u32[]{:S(2)}) collective-permute-start(bf16[96,1024]{1,0:T(8,128)(2,1)S(1)} %get-tuple-element.214.a), channel_id=1, source_target_pairs={{0,4},{1,5},{2,6},{3,7},{4,0},{5,1},{6,2},{7,3},{8,12},{9,13},{10,... | collective-permute-start | bytes 589832 | tf_op jit(solution)/shard_map/ppermute | solution.py:634
  87.7 7.8 %collective-permute-start.26 = (bf16[96,1024]{1,0:T(8,128)(2,1)S(1)}, bf16[96,1024]{1,0:T(8,128)(2,1)S(1)}, u32[]{:S(2)}, u32[]{:S(2)}) collective-permute-start(bf16[96,1024]{1,0:T(8,128)(2,1)S(1)} %get-tuple-element.226.c), channel_id=1, source_target_pairs={{0,2},{1,3},{2,0},{3,1},{4,6},{5,7},{6,4},{7,5},{8,10},{9,11},{10,... | collective-permute-start | bytes 589832 | tf_op jit(solution)/shard_map/ppermute | solution.py:634
  91.8 4.8 %collective-permute-start.27 = (bf16[96,512]{1,0:T(8,128)(2,1)S(1)}, bf16[96,512]{1,0:T(8,128)(2,1)S(1)}, u32[]{:S(2)}, u32[]{:S(2)}) collective-permute-start(bf16[96,512]{1,0:T(8,128)(2,1)S(1)} %slice.8.refs_0_), channel_id=1, source_target_pairs={{0,2},{1,3},{2,0},{3,1},{4,6},{5,7},{6,4},{7,5},{8,10},{9,11},{10,... | collective-permute-start | bytes 294920 | tf_op jit(solution)/shard_map/ppermute | solution.py:634
  92.5 4.6 %collective-permute-start.28 = (bf16[96,512]{1,0:T(8,128)(2,1)S(1)}, bf16[96,512]{1,0:T(8,128)(2,1)S(1)}, u32[]{:S(2)}, u32[]{:S(2)}) collective-permute-start(bf16[96,512]{1,0:T(8,128)(2,1)S(1)} %slice.8.refs_0_), channel_id=1, source_target_pairs={{0,4},{1,5},{2,6},{3,7},{4,0},{5,1},{6,2},{7,3},{8,12},{9,13},{10,... | collective-permute-start | bytes 294920 | tf_op jit(solution)/shard_map/ppermute | solution.py:634
  93.7 5.5 %collective-permute-start.29 = (bf16[96,512]{1,0:T(8,128)(2,1)S(1)}, bf16[96,512]{1,0:T(8,128)(2,1)S(1)}, u32[]{:S(2)}, u32[]{:S(2)}) collective-permute-start(bf16[96,512]{1,0:T(8,128)(2,1)S(1)} %slice.8.refs_0_), channel_id=1, source_target_pairs={{0,6},{1,7},{2,4},{3,5},{4,2},{5,3},{6,0},{7,1},{8,14},{9,15},{10,... | collective-permute-start | bytes 294920 | tf_op jit(solution)/shard_map/ppermute | solution.py:634
  96.1 6.3 %collective-permute-start.30 = (bf16[192,1024]{1,0:T(8,128)(2,1)S(1)}, bf16[192,1024]{1,0:T(8,128)(2,1)S(1)}, u32[]{:S(2)}, u32[]{:S(2)}) collective-permute-start(bf16[192,1024]{1,0:T(8,128)(2,1)S(1)} %get-tuple-element.229.refs_0_), channel_id=1, source_target_pairs={{0,1},{1,0},{2,3},{3,2},{4,5},{5,4},{6,7},{7,6},{8,9},{9,8},{10,11... | collective-permute-start | bytes 1179656 | tf_op jit(solution)/shard_map/ppermute | solution.py:634
  96.2 6.3 %collective-permute-start.31 = (bf16[192,1024]{1,0:T(8,128)(2,1)S(1)}, bf16[192,1024]{1,0:T(8,128)(2,1)S(1)}, u32[]{:S(2)}, u32[]{:S(2)}) collective-permute-start(bf16[192,1024]{1,0:T(8,128)(2,1)S(1)} %get-tuple-element.230.refs_1_), channel_id=1, source_target_pairs={{0,1},{1,0},{2,3},{3,2},{4,5},{5,4},{6,7},{7,6},{8,9},{9,8},{10,11... | collective-permute-start | bytes 1179656 | tf_op jit(solution)/shard_map/ppermute | solution.py:634
  99.8 8.6 %collective-permute-start.32 = (bf16[384,512]{1,0:T(8,128)(2,1)S(1)}, bf16[384,512]{1,0:T(8,128)(2,1)S(1)}, u32[]{:S(2)}, u32[]{:S(2)}) collective-permute-start(bf16[384,512]{1,0:T(8,128)(2,1)S(1)} %stack.21.refs_4_), channel_id=1, source_target_pairs={{0,8},{8,0},{16,24},{24,16},{1,9},{9,1},{17,25},{25,17},{2,10},{10... | collective-permute-start | bytes 1179656 | tf_op jit(solution)/shard_map/ppermute | solution.py:634
  100.9 8.0 %collective-permute-start.33 = (bf16[192,1024]{1,0:T(8,128)(2,1)S(1)}, bf16[192,1024]{1,0:T(8,128)(2,1)S(1)}, u32[]{:S(2)}, u32[]{:S(2)}) collective-permute-start(bf16[192,1024]{1,0:T(8,128)(2,1)S(1)} %get-tuple-element.229.refs_0_), channel_id=1, source_target_pairs={{0,2},{1,3},{2,0},{3,1},{4,6},{5,7},{6,4},{7,5},{8,10},{9,11},{10,... | collective-permute-start | bytes 1179656 | tf_op jit(solution)/shard_map/ppermute | solution.py:634
  101.5 8.1 %collective-permute-start.34 = (bf16[192,1024]{1,0:T(8,128)(2,1)S(1)}, bf16[192,1024]{1,0:T(8,128)(2,1)S(1)}, u32[]{:S(2)}, u32[]{:S(2)}) collective-permute-start(bf16[192,1024]{1,0:T(8,128)(2,1)S(1)} %get-tuple-element.230.refs_1_), channel_id=1, source_target_pairs={{0,4},{1,5},{2,6},{3,7},{4,0},{5,1},{6,2},{7,3},{8,12},{9,13},{10,... | collective-permute-start | bytes 1179656 | tf_op jit(solution)/shard_map/ppermute | solution.py:634
  109.6 1.7 %collective-permute-start.35 = (bf16[192,1024]{1,0:T(8,128)(2,1)S(1)}, bf16[192,1024]{1,0:T(8,128)(2,1)S(1)}, u32[]{:S(2)}, u32[]{:S(2)}) collective-permute-start(bf16[192,1024]{1,0:T(8,128)(2,1)S(1)} %collective-permute-done.33.refs_0_), channel_id=1, source_target_pairs={{0,1},{1,0},{2,3},{3,2},{4,5},{5,4},{6,7},{7,6},{8,9},{9,8},{10,11... | collective-permute-start | bytes 1179656 | tf_op jit(solution)/shard_map/ppermute | solution.py:634
  109.6 2.3 %collective-permute-start.36 = (bf16[192,1024]{1,0:T(8,128)(2,1)S(1)}, bf16[192,1024]{1,0:T(8,128)(2,1)S(1)}, u32[]{:S(2)}, u32[]{:S(2)}) collective-permute-start(bf16[192,1024]{1,0:T(8,128)(2,1)S(1)} %collective-permute-done.34.refs_1_), channel_id=1, source_target_pairs={{0,1},{1,0},{2,3},{3,2},{4,5},{5,4},{6,7},{7,6},{8,9},{9,8},{10,11... | collective-permute-start | bytes 1179656 | tf_op jit(solution)/shard_map/ppermute | solution.py:634
  110.1 2.3 %collective-permute-start.37 = (bf16[384,512]{1,0:T(8,128)(2,1)S(1)}, bf16[384,512]{1,0:T(8,128)(2,1)S(1)}, u32[]{:S(2)}, u32[]{:S(2)}) collective-permute-start(bf16[384,512]{1,0:T(8,128)(2,1)S(1)} %stack.21.refs_4_), channel_id=1, source_target_pairs={{0,1},{1,0},{2,3},{3,2},{4,5},{5,4},{6,7},{7,6},{8,9},{9,8},{10,11... | collective-permute-start | bytes 1179656 | tf_op jit(solution)/shard_map/ppermute | solution.py:634
  110.1 2.9 %collective-permute-start.38 = (bf16[384,512]{1,0:T(8,128)(2,1)S(1)}, bf16[384,512]{1,0:T(8,128)(2,1)S(1)}, u32[]{:S(2)}, u32[]{:S(2)}) collective-permute-start(bf16[384,512]{1,0:T(8,128)(2,1)S(1)} %collective-permute-done.32.refs_5_), channel_id=1, source_target_pairs={{0,1},{1,0},{2,3},{3,2},{4,5},{5,4},{6,7},{7,6},{8,9},{9,8},{10,11... | collective-permute-start | bytes 1179656 | tf_op jit(solution)/shard_map/ppermute | solution.py:634

commit v5 on v4

--- a/solution.py
+++ b/solution.py
@@ -12,9 +12,10 @@
 LEFT, RIGHT, ONES = 17, 18, 19
 PIECE = 32
 FFN_CHUNKS = 1
-STEPS = """
-    a_chips f_rows f_z0 a_rows d_slots f_z1 f_pick a_z0 d:3 d_out a_z1 f_join a_stack f_near small a_swap f_swap last
-"""
+STEPS = (
+    "a_chips", "f_rows", "f_z0", "a_rows", "d_slots", "f_z1", "f_pick", "a_z0", "d:3", "d_out", "a_z1",
+    "f_join", "a_stack", "f_near", "small", "a_swap", "f_swap", "own", "last",
+)
 SMALL = 16
 VMEM = 24 * 1024 * 1024
 MUCH = 56 * 1024 * 1024
@@ -92,11 +93,12 @@
     return pltpu.roll(pair, 64, 1)
 
 
-def prepare_kernel(ids, lens, gain, table, x, wq, wk, wv, q, ext, bands, wt, line, x_here, wq_here, wk_here, wv_here, sems):
-    pairs = ((x, x_here), (wq, wq_here), (wk, wk_here), (wv, wv_here))
-    copies = [pltpu.make_async_copy(a, b, sems.at[i]) for i, (a, b) in enumerate(pairs)]
-    for copy in copies:
-        copy.start()
+def prepare_kernel(ids, lens, gain, table, x, w3, q, ext, bands, wt, line, x_here, wq, wk, wv):
+    w = wq.shape[1]
+    for k, ref in enumerate((wq, wk, wv)):
+        ref[...] = w3[:, k * w : (k + 1) * w]
+        wt[k * w : (k + 1) * w] = ref[...].astype(f32).T.astype(bf16)
+    x_here[...] = x[...]
     t = x.shape[0]
     heads, buckets = table.shape
     low, high = segment_bounds(lens)
@@ -114,13 +116,8 @@
         for r in range(3):
             bands[h, r] = band[:, r * t : (r + 1) * t].astype(bf16)
         bands[h, 3] = jnp.zeros((t, t), bf16)
-    for copy in copies:
-        copy.wait()
-    n1 = rms(x_here[...].astype(f32), gain[...].astype(f32)).astype(bf16)
-    q[...] = nn(n1, wq_here[...]).astype(bf16)
-    w = wq.shape[1]
-    for k, ref in enumerate((wq_here, wk_here, wv_here)):
-        wt[k * w : (k + 1) * w] = ref[...].astype(f32).T.astype(bf16)
+    n1 = rms(x[...].astype(f32), gain[...].astype(f32)).astype(bf16)
+    q[...] = nn(n1, wq[...]).astype(bf16)
 
 
 def prepare(ids, lens, x, gain, table, wq, wk, wv):
@@ -130,7 +127,7 @@
         prepare_kernel, "prepare", 4,
         [shape(t, w), shape(t, 128, dtype=f32), shape(heads, 4, t, t), shape(3 * w, d), shape(8, 4 * t, dtype=f32),
          shape(t, d), shape(d, w), shape(d, w), shape(d, w)],
-        (ids, lens), (gain, table, x, wq, wk, wv), anywhere=4, scratch=[pltpu.SemaphoreType.DMA((4,))],
+        (ids, lens), (gain, table, x, jnp.concatenate([wq, wk, wv], axis=1)),
     )
 
 
@@ -146,20 +143,23 @@
     return low, jnp.where(lane == lens.shape[0], 2**30, high)
 
 
-def attend_kernel(n, first, count, ids, lens, *refs):
-    x = refs[:count]
-    gain, wk, wv, q, ext, bands, line, n1, e, acc, stat = refs[count : count + 11]
+def attend_kernel(n, first, count, pieces, ids, lens, *refs):
+    x, refs = refs[:pieces], refs[pieces:]
+    gain, wk, wv, q, ext, bands, line, n1, e, acc, stat = refs[:11]
     pairs = q.shape[1] // 128
-    kv, p = refs[count + 11 : count + 11 + pairs], refs[count + 11 + pairs : -1]
+    kv, p = refs[11 : 11 + pairs], refs[11 + pairs : -1]
     s = refs[-1]
     me = ids[0]
-    t = x[0].shape[0]
+    t = q.shape[0]
     low, high = segment_bounds(lens)
     row = iota((t, 128), 0)
     lanes = iota((t, 128), 1)
+    begin = 0
+    for ref in x:
+        n1[begin : begin + ref.shape[0]] = rms(ref[...].astype(f32), gain[...].astype(f32)).astype(bf16)
+        begin += ref.shape[0]
     for i in range(count):
         at = slice(i * t, (i + 1) * t)
-        n1[at] = rms(x[i][...].astype(f32), gain[...].astype(f32)).astype(bf16)
         block = me ^ (first + i)
         pos = row + block * t
         away = block - me
@@ -203,8 +203,9 @@
         more = nn(raised, keys_of(h, i))
         return more if out is None else out + more
 
-    for i in range(count):
-        project(0, i)
+    for g in range(pairs):
+        for i in range(count):
+            project(g, i)
     stats = jnp.zeros((t, 128), f32)
     last = None
     sums = []
@@ -216,8 +217,6 @@
                 top = score(h, i, qa, top)
             if h > 0:
                 out = mix(h - 1, i, last, out)
-            if h % 2 == 1 and h // 2 + 1 < pairs:
-                project(h // 2 + 1, i)
         if h > 0:
             stats = jnp.where(lanes == h - 1, last, stats)
             stats = jnp.where(lanes == 7 + h, out[:, 128 + ONES : 129 + ONES], stats)
@@ -231,11 +230,12 @@
 
 def attend(n, first, ids, lens, blocks, gain, wk, wv, q, ext, bands, line):
     count = len(blocks)
-    t, d = blocks[0].shape
+    blocks = [piece for block in blocks for piece in block]
+    t, d = q.shape[0], wk.shape[0]
     pairs = wk.shape[1] // 128
     c = count * t
     out = call(
-        partial(attend_kernel, n, first, count), "attend", 2 * count,
+        partial(attend_kernel, n, first, count, len(blocks)), "attend", 2 * count,
         [shape(c, d), shape(c, 128), shape(t, wk.shape[1], dtype=f32), shape(t, 128, dtype=f32)]
         + [shape(2, c, 128)] * pairs + [shape(2, t, c)] * pairs,
         (ids, lens), (*blocks, gain, wk, wv, q, ext, bands, line), scratch=[pltpu.VMEM((2, t, c), f32)], much=n > 8,
@@ -281,6 +281,7 @@
         pos = ids[0] * t + rows.start + iota((chunk, 1), 0)
         v["g"] = cot[rows].astype(f32) * (pos < last).astype(f32)
         gb_all[rows] = v["g"].astype(bf16)
+        v["du"] = nt(gb_all[rows], wd[...]).astype(bf16).astype(f32)
 
     def norm(v):
         rows = v["rows"]
@@ -292,7 +293,6 @@
     def project(v):
         rows = v["rows"]
         v["gate"], v["up"] = nn(n2_all[rows], wg[...]), nn(n2_all[rows], wu[...])
-        v["du"] = nt(gb_all[rows], wd[...]).astype(bf16).astype(f32)
 
     def activate(v):
         rows, gate, up = v["rows"], v["gate"], v["up"]
@@ -308,11 +308,11 @@
 
     def down(v):
         rows = v["rows"]
-        out[rows] = (v["h1"] + nn(u_all[rows], wd[...])).astype(bf16)
         v["dn2"] = nt(dg_all[rows], wg[...]) + nt(du_all[rows], wu[...])
 
     def norm_back(v):
         rows, dn2, hat, s2 = v["rows"], v["dn2"], v["hat"], v["s2"]
+        out[rows] = (v["h1"] + nn(u_all[rows], wd[...])).astype(bf16)
         v["gn"] = jnp.sum(dn2 * hat, axis=0, keepdims=True)
         scaled = dn2 * g2
         dh1 = v["g"] + s2 * (scaled - hat * jnp.mean(hat * scaled, axis=-1, keepdims=True))
@@ -346,7 +346,7 @@
         for c, v in enumerate(work):
             if 0 <= step - c < len(stages):
                 stages[step - c](v)
-        if step == 3 + FFN_CHUNKS - 1:
+        if step == len(stages) + FFN_CHUNKS - 2:
             weights_kernel()
     gn[...] = sum(v["gn"] for v in work)
     gwo[...] = tn(mixed_all[...], dh_all[...]).astype(bf16)
@@ -679,7 +679,7 @@
     x, y = ids[2] % 2, ids[2] // 2
     rows = 3 * PIECE
     copies = []
-    for c, pair in ((ids[1], parts[:2]), (1 - ids[1], parts[2:])):
+    for c, *pair in parts:
         for half, first, second in ((0, x, y), (1, y, x)):
             for b in range(2):
                 k = len(copies) // 4
@@ -694,26 +694,40 @@
 
 
 def unpack_near_kernel(ids, *refs):
-    for copy in write_ffn(0, ids, refs[:4], *refs[4:]):
+    for copy in write_ffn(0, ids, ((ids[1], *refs[:2]), (1 - ids[1], *refs[2:4])), *refs[4:]):
         copy.wait()
 
 
-def unpack_far_kernel(pieces, ids, *refs):
-    parts, stacks = refs[:4], refs[4:8]
-    gate, up, down, *attention, full, sems, both, wide, tall, sem2 = refs[8 + 3 :]
-    copies = write_ffn(1, ids, parts, gate, up, down, full, sems)
-    size = both.shape[0] // 2
-    rows = stacks[0].shape[0] // pieces
+def unpack_half_kernel(other, filled, chips, ids, *refs):
+    (x, y, *stacks), refs = refs[:4], refs[4 + filled :]
+    gate, up, down, gq, gk, gv, go, full, sems, both, wide, tall, sem2 = refs
+    core = ids[1] ^ other
+    copies = write_ffn(1, ids, ((core, x, y),), gate, up, down, full, sems)
+    rows = stacks[0].shape[0] // chips
     for k, stack in enumerate(stacks):
-        for a in range(pieces):
-            where = (ids[1] ^ (k // 2)) * size + ((ids[2] ^ a) * 2 + ((ids[3] % 2) ^ (k % 2))) * rows
+        for a in range(chips):
+            where = ((ids[2] ^ a) * 2 + ((ids[3] % 2) ^ k)) * rows
             both[pl.ds(pl.multiple_of(where, 16), rows)] = stack[a * rows : (a + 1) * rows]
     w = wide.shape[2]
-    tall[...] = both[3 * w :].astype(f32)
-    send_out(copies, tall, attention[3], sem2.at[3])
-    for k in range(3):
-        wide[k] = both[k * w : (k + 1) * w].astype(f32).T
-        send_out(copies, wide.at[k], attention[k], sem2.at[k])
+
+    def finish(matrices):
+        moves = []
+        for i, (ref, turned) in enumerate(matrices):
+            value = both[i * w : (i + 1) * w].astype(f32)
+            source = wide.at[i] if turned else tall
+            source[...] = value.T if turned else value
+            send_out(moves, source, ref, sem2.at[i])
+        for copy in moves:
+            copy.wait()
+
+    @pl.when(core == 0)
+    def _():
+        finish(((gq, True), (gk, True)))
+
+    @pl.when(core == 1)
+    def _():
+        finish(((gv, True), (go, False)))
+
     for copy in copies:
         copy.wait()
 
@@ -791,24 +805,28 @@
     gain1 = norm_attn.reshape(1, d)
     gain2 = norm_ffn.reshape(1, d)
 
-    blocks = [None] * n
-    blocks[0], blocks[1] = x, swap(x, "seq", 1)
+    blocks = [[x], [swap(x, "seq", 1)]] + [None] * (n - 2)
     for j in range(2, n, 2):
-        blocks[j] = swap(x, "seq", j)
+        if n != 8 or j != 6:
+            blocks[j] = [swap(x, "seq", j)]
     q, ext, bands, wt, line, x, wq, wk, wv = prepare(
         ids, lens, x, gain1, bucket_bias_table.T, query_weight, key_weight, value_weight
     )
-    blocks[0] = x
-    cuts = [0, 2, *range(8, n, 8), n]
+    blocks[0] = [x]
+    cuts = [0, 2, 6, *range(8, n, 8), n]
 
     def phase(a, b):
         return attend(n, a, ids, lens, blocks[a:b], gain1, wk, wv, q, ext, bands, line)
 
-    parts = [phase(0, 2)]
-    for j in range(2, n, 2):
-        blocks[j] = order(parts[0]["acc"], blocks[j])
-        blocks[j + 1] = swap(blocks[j], "seq", 1)
-    parts += [phase(a, b) for a, b in zip(cuts[1:-1], cuts[2:], strict=True)]
+    parts = []
+    for a, b in zip(cuts[:-1], cuts[1:], strict=True):
+        for j in range(a, b, 2):
+            if j:
+                blocks[j] = [order(parts[-1]["acc"], v) for v in blocks[j]]
+                blocks[j + 1] = [swap(v, "seq", 1) for v in blocks[j]]
+        if n == 8 and a == 2:
+            blocks[6] = [swap(blocks[4][0][: t // 2], "seq", 2), swap(blocks[2][0][t // 2 :], "seq", 4)]
+        parts.append(phase(a, b))
     output, dh, do, scale, gwo, keep, send, gn = feed_forward(
         ids, lens, gain2, x, out_weight, gate_weight, expansion_matrix, down_weight, cot, parts
     )
@@ -923,14 +941,20 @@
             live["afar"] = swap(live["a"], "seq", 1)
             return None
 
+        def unpack_half(other, x, y, first, second, filled):
+            return unpack(
+                partial(unpack_half_kernel, other, len(filled), half), ids, (x, y, first, second), filled,
+                ffn_out + [shape(d, width, dtype=f32)] * 3 + [shape(width, d, dtype=f32)],
+                [*ffn_scratch, pltpu.VMEM((2 * width, d), bf16), pltpu.VMEM((2, d, width), f32),
+                 pltpu.VMEM((width, d), f32), pltpu.SemaphoreType.DMA((2,))],
+            )
+
+        def own():
+            kept["near"] = unpack_half(0, *live["f"], kept["stack"], live["a"], kept["near"])
+            return kept["near"][0]
+
         def last():
-            kept["out"] = unpack(
-                partial(unpack_far_kernel, half), ids,
-                (*live["f"], *live["far"], kept["stack"], live["a"], live["anear"], live["afar"]), kept["near"],
-                ffn_out + [shape(d, width, dtype=f32)] * 3 + [shape(width, d, dtype=f32)],
-                [*ffn_scratch, pltpu.VMEM((4 * width, d), bf16), pltpu.VMEM((3, d, width), f32),
-                 pltpu.VMEM((width, d), f32), pltpu.SemaphoreType.DMA((4,))],
-            )
+            kept["out"] = unpack_half(1, *live["far"], live["anear"], live["afar"], kept["near"])
             return kept["out"][0]
 
         def d_slots():
@@ -948,13 +972,13 @@
 
         steps = dict(
             f_rows=(f_rows, "f"), f_z0=(partial(f_add, 2), "f"), f_z1=(partial(f_add, 1), "f"), f_pick=(f_pick, "f"),
-            f_join=(f_join, "f"), f_near=(f_near, "near"), f_swap=(f_swap, "f"), last=(last, "far"),
+            f_join=(f_join, "f"), f_near=(f_near, "near"), f_swap=(f_swap, "f"), own=(own, "f"), last=(last, "far"),
             a_chips=(a_chips, "a"), a_rows=(a_rows, "a"), a_z0=(partial(a_add, 2), "a"), a_z1=(partial(a_add, 1), "a"),
             a_stack=(a_stack, "a"), a_swap=(a_swap, "a"),
             d_slots=(d_slots, "d"), d_out=(d_out, "d"), small=(small, None),
         )
         token = f_x
-        for name in STEPS.split():
+        for name in STEPS:
             if ":" in name:
                 stream, j = name.split(":")
                 live[stream][int(j)] = token = order(token, live[stream][int(j)])

time: 117 us -> 113 us (0.966)
  local copies, waits for them, and re-layouts: 6.01 us -> 0.77 us
  waiting for transfers between devices: 26 us -> 21.5 us
  starting transfers between devices: 36.3 us -> 39.7 us
  other arithmetic: 0.08 us -> 1.41 us
    unnamed x26 -> x18, local copies, waits for them, and re-layouts: 5.31 us -> 0.05 us
    ppermute x39 -> x41, waiting for transfers between devices: 26 us -> 21.5 us  [swap(): return lax.ppermute(array, axis, [(i, i ^ j) for i in range(size)])]
    ppermute x39 -> x41, starting transfers between devices: 36.3 us -> 39.7 us  [swap(): return lax.ppermute(array, axis, [(i, i ^ j) for i in range(size)])]
    concatenate x0 -> x1, other arithmetic: none -> 1.34 us  [prepare(): jnp.concatenate([wq, wk, wv], axis=1)]
    pallas_call x2 -> x3, Pallas kernels: 6.27 us -> 7.58 us  [unpack(): pl.pallas_call(kernel, in_specs=[pl.BlockSpec(memory_space=pltpu.SMEM)] +...]
    pallas_call x21 -> x22, Pallas kernels: 41.2 us -> 40.4 us  [call(): pl.pallas_call(kernel, in_specs=[smem] * len(smem_args) + [vmem] * (len(a...]
  transfers between devices with their start and end apart: 39 -> 41, of which waited for: 24 -> 17; matrix products, arithmetic and copies ran while one was open for 1% -> 2% of each run, Pallas kernels for 26% -> 32%
where the time goes in v5:
time: 113 us
  Pallas kernels  48 us (42%)
  starting transfers between devices  39.7 us (35%)
  waiting for transfers between devices  21.5 us (19%)
  other arithmetic  1.41 us (1%)
  between operations  1.28 us (1%)
    pallas_call x22, Pallas kernels, call(): pl.pallas_call(kernel, in_specs=[smem] * len(smem_args) + [vmem] * (len(a...  40.4 us
    ppermute x41, starting transfers between devices, swap(): return lax.ppermute(array, axis, [(i, i ^ j) for i in range(size)])  39.7 us
    ppermute x41, waiting for transfers between devices, swap(): return lax.ppermute(array, axis, [(i, i ^ j) for i in range(size)])  21.5 us
    pallas_call x3, Pallas kernels, unpack(): pl.pallas_call(kernel, in_specs=[pl.BlockSpec(memory_space=pltpu.SMEM)] +...  7.58 us
  transfers between devices with their start and end apart: 41, of which 17 were waited for; matrix products, arithmetic and copies ran while one was open for 2% of the time, Pallas kernels for 32%

profile of v5, /device:TPU:0, one launch (start us, length us, event | category | flops | bytes accessed | tf_op | source)
XLA Modules:
  0.0 112.7 jit_solution(11288446697422760962)
XLA Ops:
  0.7 3.0 %collective-permute-start.3 = (bf16[256,512]{1,0:T(8,128)(2,1)}, bf16[256,512]{1,0:T(8,128)(2,1)S(1)}, u32[]{:S(2)}, u32[]{:S(2)}) collective-permute-start(bf16[256,512]{1,0:T(8,128)(2,1)} %bitcast.13), channel_id=1, source_target_pairs={{0,4},{1,5},{2,6},{3,7},{4,0},{5,1},{6,2},{7,3},{8,12},{9,13},{10,... | collective-permute-start | bytes 786440 | tf_op jit(solution)/shard_map/ppermute | solution.py:634
  3.7 1.5 %collective-permute-start.1 = (bf16[256,512]{1,0:T(8,128)(2,1)}, bf16[256,512]{1,0:T(8,128)(2,1)S(1)}, u32[]{:S(2)}, u32[]{:S(2)}) collective-permute-start(bf16[256,512]{1,0:T(8,128)(2,1)} %bitcast.14), channel_id=1, source_target_pairs={{0,2},{1,3},{2,0},{3,1},{4,6},{5,7},{6,4},{7,5},{8,10},{9,11},{10,... | collective-permute-start | bytes 786440 | tf_op jit(solution)/shard_map/ppermute | solution.py:634
  5.2 0.7 reshape.55.gain.refs_2_.refs_4_.refs_18_.refs_7_
  6.0 1.3 %pad_maximum_fusion.w3 = bf16[512,1152]{1,0:T(8,128)(2,1)S(1)} fusion(bf16[512,384]{1,0:T(8,128)(2,1)} %param.17, bf16[512,384]{1,0:T(8,128)(2,1)} %param.16, bf16[512,384]{1,0:T(8,128)(2,1)} %param.15), kind=kLoop, calls=%fused_computation | loop fusion | flops 3538944 | bytes 2359296 | tf_op jit(solution)/shard_map/concatenate | solution.py:130
  7.3 1.6 %prepare.1 = (bf16[256,384]{1,0:T(8,128)(2,1)S(1)}, f32[256,128]{1,0:T(8,128)S(1)}, bf16[6,4,256,256]{3,2,1,0:T(8,128)(2,1)S(1)}, bf16[1152,512]{1,0:T(8,128)(2,...) custom-call(s32[4]{0:T(128)S(1)} %pad_add_fusion.ids, ...), custom_call_target="tpu_custom_call" | custom-call | flops 4000000 | bytes 8000 | tf_op jit(solution)/shard_map/prepare/pallas_call | solution.py:72
  9.0 2.8 %attend.3 = (bf16[512,512]{1,0:T(8,128)(2,1)S(1)}, bf16[512,128]{1,0:T(8,128)(2,1)S(1)}, f32[256,384]{1,0:T(8,128)S(1)}, f32[256,128]{1,0:T(8,128)S(1)}, bf16[2,...) custom-call(s32[4]{0:T(128)S(1)} %pad_add_fusion.ids, ...), custom_call_target="tpu_custom_call" | custom-call | flops 4000000 | bytes 8000 | tf_op jit(solution)/shard_map/attend/pallas_call | solution.py:72
  12.5 0.6 collective-permute-start.6
  13.1 1.3 %collective-permute-start.5 = (bf16[128,512]{1,0:T(8,128)(2,1)S(1)}, bf16[128,512]{1,0:T(8,128)(2,1)S(1)}, u32[]{:S(2)}, u32[]{:S(2)}) collective-permute-start(bf16[128,512]{1,0:T(8,128)(2,1)S(1)} %slice.12), channel_id=1, source_target_pairs={{0,2},{1,3},{2,0},{3,1},{4,6},{5,7},{6,4},{7,5},{8,10},{9,11},{10,... | collective-permute-start | bytes 393224 | tf_op jit(solution)/shard_map/ppermute | solution.py:634
  14.4 4.3 %attend.4 = (bf16[1024,512]{1,0:T(8,128)(2,1)S(1)}, bf16[1024,128]{1,0:T(8,128)(2,1)S(1)}, f32[256,384]{1,0:T(8,128)S(1)}, f32[256,128]{1,0:T(8,128)S(1)}, bf16[...) custom-call(s32[4]{0:T(128)S(1)} %pad_add_fusion.ids, ...), custom_call_target="tpu_custom_call" | custom-call | flops 8000000 | bytes 16000 | tf_op jit(solution)/shard_map/attend/pallas_call | solution.py:72
  19.3 0.8 collective-permute-done.7.refs_2_
  20.3 2.7 %attend.5 = (bf16[512,512]{1,0:T(8,128)(2,1)S(1)}, bf16[512,128]{1,0:T(8,128)(2,1)S(1)}, f32[256,384]{1,0:T(8,128)S(1)}, f32[256,128]{1,0:T(8,128)S(1)}, bf16[2,...) custom-call(s32[4]{0:T(128)S(1)} %pad_add_fusion.ids, ...), custom_call_target="tpu_custom_call" | custom-call | flops 4000000 | bytes 8000 | tf_op jit(solution)/shard_map/attend/pallas_call | solution.py:72
  23.0 5.3 %feed_forward.1 = (bf16[256,512]{1,0:T(8,128)(2,1)}, f32[256,512]{1,0:T(8,128)S(1)}, bf16[256,384]{1,0:T(8,128)(2,1)S(1)}, f32[256,128]{1,0:T(8,128)S(1)}, bf16[...) custom-call(s32[4]{0:T(128)S(1)} %pad_add_fusion.ids, ...), custom_call_target="tpu_custom_call" | custom-call | flops 8000000 | bytes 16000 | tf_op jit(solution)/shard_map/feed_forward/pallas_call | solution.py:72
  28.7 3.3 %attend_back.1 = (bf16[128,2048]{1,0:T(8,128)(2,1)S(1)}, bf16[128,2048]{1,0:T(8,128)(2,1)S(1)}, bf16[256,128]{1,0:T(8,128)(2,1)S(1)}, f32[8,1152]{1,0:T(8,128)S(1)}) custom-call(s32[4]{0:T(128)S(1)} %pad_add_fusion.ids, bf16[256,384]{1,0:T(8,128)(2,1)S(1)} %get-tuple-element.157.refs_5_.refs_7_.q.refs_0_, ...), custom_call_target="tpu_custom_call" | custom-call | flops 4000000 | bytes 8000 | tf_op jit(solution)/shard_map/attend_back/pallas_call | solution.py:72
  32.0 0.9 add_parts.9
  32.9 0.8 collective-permute-start.10
  33.8 1.5 %collective-permute-start.11 = (bf16[192,1024]{1,0:T(8,128)(2,1)S(1)}, bf16[192,1024]{1,0:T(8,128)(2,1)S(1)}, u32[]{:S(2)}, u32[]{:S(2)}) collective-permute-start(bf16[192,1024]{1,0:T(8,128)(2,1)S(1)} %get-tuple-element.214), channel_id=1, source_target_pairs={{0,4},{1,5},{2,6},{3,7},{4,0},{5,1},{6,2},{7,3},{8,12},{9,13},{10,... | collective-permute-start | bytes 1179656 | tf_op jit(solution)/shard_map/ppermute | solution.py:634
  35.3 9.5 %rest_back.1 = (bf16[4,512,256]{2,1,0:T(8,128)(2,1)S(1)}, bf16[4,512,256]{2,1,0:T(8,128)(2,1)S(1)}, f32[256,512]{1,0:T(8,128)S(1)}, bf16[784,512]{1,0:T(8,128)(2,1)S(1)}, bf16[784,512]{1,0:T(8,128)(2,1)S(1)}) custom-call(s32[4]{0:T(128)S(1)} %pad_add_fusion.ids, bf16[256,384]{1,0:T(8,128)(2,1)S(1)} %get-tuple-element.157.refs_5_.refs_7_.q.refs_0_, ...), custom_call_target="tpu_custom_call" | custom-call | flops 10000000 | bytes 20000 | tf_op jit(solution)/shard_map/rest_back/pallas_call | solution.py:72
  45.4 0.7 add_parts.10
  46.1 1.4 %collective-permute-start.13 = (bf16[96,1024]{1,0:T(8,128)(2,1)S(1)}, bf16[96,1024]{1,0:T(8,128)(2,1)S(1)}, u32[]{:S(2)}, u32[]{:S(2)}) collective-permute-start(bf16[96,1024]{1,0:T(8,128)(2,1)S(1)} %get-tuple-element.222), channel_id=1, source_target_pairs={{0,4},{1,5},{2,6},{3,7},{4,0},{5,1},{6,2},{7,3},{8,12},{9,13},{10,... | collective-permute-start | bytes 589832 | tf_op jit(solution)/shard_map/ppermute | solution.py:634
  47.5 1.2 %collective-permute-start.14 = (bf16[96,1024]{1,0:T(8,128)(2,1)S(1)}, bf16[96,1024]{1,0:T(8,128)(2,1)S(1)}, u32[]{:S(2)}, u32[]{:S(2)}) collective-permute-start(bf16[96,1024]{1,0:T(8,128)(2,1)S(1)} %get-tuple-element.223), channel_id=1, source_target_pairs={{0,2},{1,3},{2,0},{3,1},{4,6},{5,7},{6,4},{7,5},{8,10},{9,11},{10,... | collective-permute-start | bytes 589832 | tf_op jit(solution)/shard_map/ppermute | solution.py:634
  48.8 0.7 add_parts.11
  49.5 3.5 %collective-permute-done.13.recv_x = bf16[96,1024]{1,0:T(8,128)(2,1)S(1)} collective-permute-done((bf16[96,1024]{1,0:T(8,128)(2,1)S(1)}, bf16[96,1024]{1,0:T(8,128)(2,1)S(1)}, u32[]{:S(2)}, u32[]{:S(2)}) %collective-permute-start.13) | collective-permute-done | bytes 196640 | tf_op jit(solution)/shard_map/ppermute | solution.py:634
  53.1 1.0 collective-permute-done.14.recv_y
  54.1 0.7 add_parts.12
  54.7 1.6 %collective-permute-start.15 = (bf16[96,1024]{1,0:T(8,128)(2,1)S(1)}, bf16[96,1024]{1,0:T(8,128)(2,1)S(1)}, u32[]{:S(2)}, u32[]{:S(2)}) collective-permute-start(bf16[96,1024]{1,0:T(8,128)(2,1)S(1)} %get-tuple-element.228), channel_id=1, source_target_pairs={{0,8},{8,0},{16,24},{24,16},{1,9},{9,1},{17,25},{25,17},{2,10},{10... | collective-permute-start | bytes 589832 | tf_op jit(solution)/shard_map/ppermute | solution.py:634
  56.4 1.2 %collective-permute-start.16 = (bf16[208,512]{1,0:T(8,128)(2,1)S(1)}, bf16[208,512]{1,0:T(8,128)(2,1)S(1)}, u32[]{:S(2)}, u32[]{:S(2)}) collective-permute-start(bf16[208,512]{1,0:T(8,128)(2,1)S(1)} %get-tuple-element.230), channel_id=1, source_target_pairs={{0,2},{1,3},{2,0},{3,1},{4,6},{5,7},{6,4},{7,5},{8,10},{9,11},{10,... | collective-permute-start | bytes 638984 | tf_op jit(solution)/shard_map/ppermute | solution.py:634
  57.6 0.7 collective-permute-start.17
  58.4 1.5 %collective-permute-start.18 = (bf16[208,512]{1,0:T(8,128)(2,1)S(1)}, bf16[208,512]{1,0:T(8,128)(2,1)S(1)}, u32[]{:S(2)}, u32[]{:S(2)}) collective-permute-start(bf16[208,512]{1,0:T(8,128)(2,1)S(1)} %get-tuple-element.232), channel_id=1, source_target_pairs={{0,6},{1,7},{2,4},{3,5},{4,2},{5,3},{6,0},{7,1},{8,14},{9,15},{10,... | collective-permute-start | bytes 638984 | tf_op jit(solution)/shard_map/ppermute | solution.py:634
  59.9 0.6 collective-permute-done.15.refs_1_
  60.5 0.6 add_parts.13.refs_0_
  61.1 2.7 %collective-permute-start.22 = (bf16[96,1024]{1,0:T(8,128)(2,1)S(1)}, bf16[96,1024]{1,0:T(8,128)(2,1)S(1)}, u32[]{:S(2)}, u32[]{:S(2)}) collective-permute-start(bf16[96,1024]{1,0:T(8,128)(2,1)S(1)} %add_parts.13.refs_0_), channel_id=1, source_target_pairs={{0,16},{8,24},{16,0},{24,8},{1,17},{9,25},{17,1},{25,9},{2,18},{10... | collective-permute-start | bytes 589832 | tf_op jit(solution)/shard_map/ppermute | solution.py:634
  63.7 0.6 collective-permute-done.16.refs_1_
  64.4 3.2 %collective-permute-done.17.refs_2_ = bf16[208,512]{1,0:T(8,128)(2,1)S(1)} collective-permute-done((bf16[208,512]{1,0:T(8,128)(2,1)S(1)}, bf16[208,512]{1,0:T(8,128)(2,1)S(1)}, u32[]{:S(2)}, u32[]{:S(2)}) %collective-permute-start.17) | collective-permute-done | bytes 213024 | tf_op jit(solution)/shard_map/ppermute | solution.py:634
  67.7 0.8 add_slots.1
  68.5 1.2 %collective-permute-start.25 = (bf16[512,256]{1,0:T(8,128)(2,1)S(1)}, bf16[512,256]{1,0:T(8,128)(2,1)S(1)}, u32[]{:S(2)}, u32[]{:S(2)}) collective-permute-start(bf16[512,256]{1,0:T(8,128)(2,1)S(1)} %get-tuple-element.248), channel_id=1, source_target_pairs={{0,6},{1,7},{2,4},{3,5},{4,2},{5,3},{6,0},{7,1},{8,14},{9,15},{10,... | collective-permute-start | bytes 786440 | tf_op jit(solution)/shard_map/ppermute | solution.py:634
  69.8 1.0 collective-permute-done.22.refs_1_
  70.7 0.6 add_parts.15.mine
  71.3 0.7 collective-permute-start.23
  72.1 1.2 %collective-permute-start.20 = (bf16[512,256]{1,0:T(8,128)(2,1)S(1)}, bf16[512,256]{1,0:T(8,128)(2,1)S(1)}, u32[]{:S(2)}, u32[]{:S(2)}) collective-permute-start(bf16[512,256]{1,0:T(8,128)(2,1)S(1)} %get-tuple-element.241), channel_id=1, source_target_pairs={{0,2},{1,3},{2,0},{3,1},{4,6},{5,7},{6,4},{7,5},{8,10},{9,11},{10,... | collective-permute-start | bytes 786440 | tf_op jit(solution)/shard_map/ppermute | solution.py:634
  73.3 0.8 collective-permute-start.21
  74.1 1.4 %collective-permute-start.24 = (bf16[112,512]{1,0:T(8,128)(2,1)S(1)}, bf16[112,512]{1,0:T(8,128)(2,1)S(1)}, u32[]{:S(2)}, u32[]{:S(2)}) collective-permute-start(bf16[112,512]{1,0:T(8,128)(2,1)S(1)} %get-tuple-element.246), channel_id=1, source_target_pairs={{0,8},{8,0},{16,24},{24,16},{1,9},{9,1},{17,25},{25,17},{2,10},{10... | collective-permute-start | bytes 344072 | tf_op jit(solution)/shard_map/ppermute | solution.py:634
  75.5 2.8 %collective-permute-done.23.other = bf16[96,1024]{1,0:T(8,128)(2,1)S(1)} collective-permute-done((bf16[96,1024]{1,0:T(8,128)(2,1)S(1)}, bf16[96,1024]{1,0:T(8,128)(2,1)S(1)}, u32[]{:S(2)}, u32[]{:S(2)}) %collective-permute-start.23) | collective-permute-done | bytes 196640 | tf_op jit(solution)/shard_map/ppermute | solution.py:634
  78.3 0.6 pick.1
  79.0 0.6 collective-permute-done.24.refs_1_
  80.1 2.9 %collective-permute-start.26 = (bf16[112,512]{1,0:T(8,128)(2,1)S(1)}, bf16[112,512]{1,0:T(8,128)(2,1)S(1)}, u32[]{:S(2)}, u32[]{:S(2)}) collective-permute-start(bf16[112,512]{1,0:T(8,128)(2,1)S(1)} %add_parts.16.refs_0_), channel_id=1, source_target_pairs={{0,16},{8,24},{16,0},{24,8},{1,17},{9,25},{17,1},{25,9},{2,18},{10... | collective-permute-start | bytes 344072 | tf_op jit(solution)/shard_map/ppermute | solution.py:634
  83.0 0.8 collective-permute-start.28
  83.8 1.2 %collective-permute-start.27 = (bf16[96,1024]{1,0:T(8,128)(2,1)S(1)}, bf16[96,1024]{1,0:T(8,128)(2,1)S(1)}, u32[]{:S(2)}, u32[]{:S(2)}) collective-permute-start(bf16[96,1024]{1,0:T(8,128)(2,1)S(1)} %get-tuple-element.245.a), channel_id=1, source_target_pairs={{0,4},{1,5},{2,6},{3,7},{4,0},{5,1},{6,2},{7,3},{8,12},{9,13},{10,... | collective-permute-start | bytes 589832 | tf_op jit(solution)/shard_map/ppermute | solution.py:634
  85.0 1.8 %input_grad.1 = f32[256,512]{1,0:T(8,128)} custom-call(s32[4]{0:T(128)S(1)} %pad_add_fusion.ids, bf16[512,256]{1,0:T(8,128)(2,1)S(1)} %get-tuple-element.250.refs_0_, bf16[512,256]{1,0:T(8,128)(2,1)S(1)} %collective-permute-done.20.refs_1_, bf16[512,256]{1,0:T(8,128)(2,1)S(1)} %collective-permute-done.21.refs_2_, ...), custom_call_target="tpu_custom_call" | custom-call | flops 2000000 | bytes 4000 | tf_op jit(solution)/shard_map/input_grad/pallas_call | solution.py:72
  87.7 1.6 %collective-permute-start.31 = (bf16[96,512]{1,0:T(8,128)(2,1)S(1)}, bf16[96,512]{1,0:T(8,128)(2,1)S(1)}, u32[]{:S(2)}, u32[]{:S(2)}) collective-permute-start(bf16[96,512]{1,0:T(8,128)(2,1)S(1)} %slice.16.refs_0_), channel_id=1, source_target_pairs={{0,6},{1,7},{2,4},{3,5},{4,2},{5,3},{6,0},{7,1},{8,14},{9,15},{10,... | collective-permute-start | bytes 294920 | tf_op jit(solution)/shard_map/ppermute | solution.py:634
  89.3 1.2 %collective-permute-start.30 = (bf16[96,512]{1,0:T(8,128)(2,1)S(1)}, bf16[96,512]{1,0:T(8,128)(2,1)S(1)}, u32[]{:S(2)}, u32[]{:S(2)}) collective-permute-start(bf16[96,512]{1,0:T(8,128)(2,1)S(1)} %slice.16.refs_0_), channel_id=1, source_target_pairs={{0,4},{1,5},{2,6},{3,7},{4,0},{5,1},{6,2},{7,3},{8,12},{9,13},{10,... | collective-permute-start | bytes 294920 | tf_op jit(solution)/shard_map/ppermute | solution.py:634
  90.5 0.8 collective-permute-start.29
  91.3 0.6 join.1
  92.4 0.9 collective-permute-done.31.refs_3_
  93.3 1.0 collective-permute-done.30.refs_2_
  94.3 0.8 collective-permute-done.29.refs_1_
  96.2 1.2 %collective-permute-start.36 = (bf16[192,1024]{1,0:T(8,128)(2,1)S(1)}, bf16[192,1024]{1,0:T(8,128)(2,1)S(1)}, u32[]{:S(2)}, u32[]{:S(2)}) collective-permute-start(bf16[192,1024]{1,0:T(8,128)(2,1)S(1)} %get-tuple-element.261.refs_1_), channel_id=1, source_target_pairs={{0,4},{1,5},{2,6},{3,7},{4,0},{5,1},{6,2},{7,3},{8,12},{9,13},{10,... | collective-permute-start | bytes 1179656 | tf_op jit(solution)/shard_map/ppermute | solution.py:634
  97.4 1.2 %collective-permute-start.35 = (bf16[192,1024]{1,0:T(8,128)(2,1)S(1)}, bf16[192,1024]{1,0:T(8,128)(2,1)S(1)}, u32[]{:S(2)}, u32[]{:S(2)}) collective-permute-start(bf16[192,1024]{1,0:T(8,128)(2,1)S(1)} %get-tuple-element.260.refs_0_), channel_id=1, source_target_pairs={{0,2},{1,3},{2,0},{3,1},{4,6},{5,7},{6,4},{7,5},{8,10},{9,11},{10,... | collective-permute-start | bytes 1179656 | tf_op jit(solution)/shard_map/ppermute | solution.py:634
  98.6 2.5 %unpack.3 = (f32[512,1024]{1,0:T(8,128)}, f32[512,1024]{1,0:T(8,128)}, f32[1024,512]{1,0:T(8,128)}) custom-call(s32[4]{0:T(128)S(1)} %pad_add_fusion.ids, bf16[192,1024]{1,0:T(8,128)(2,1)S(1)} %get-tuple-element.260.refs_0_, bf16[192,1024]{1,0:T(8,128)(2,1)S(1)} %get-tuple-element.261.refs_1_, bf16[192,1024]{1,0:T(8,128)(2,1)S(1)} %collective-permute-done.32.refs_2_, ...), custom_call_target="tpu_custom_call" | custom-call | flops 1000 | bytes 1000 | tf_op jit(solution)/shard_map/unpack/pallas_call | solution.py:737
  101.1 1.1 %unpack_small.1 = (f32[1,512]{1,0:T(1,128)}, f32[1,512]{1,0:T(1,128)}, f32[6,32]{1,0:T(8,128)}) custom-call(s32[4]{0:T(128)S(1)} %pad_add_fusion.ids, bf16[16,512]{1,0:T(8,128)(2,1)S(1)} %slice.15.tail), custom_call_target="tpu_custom_call" | custom-call | flops 1000000 | bytes 2000 | tf_op jit(solution)/shard_map/unpack_small/pallas_call | solution.py:72
  102.3 2.1 %collective-permute-done.34.refs_3_ = bf16[384,512]{1,0:T(8,128)(2,1)S(1)} collective-permute-done((bf16[384,512]{1,0:T(8,128)(2,1)S(1)}, bf16[384,512]{1,0:T(8,128)(2,1)S(1)}, u32[]{:S(2)}, u32[]{:S(2)}) %collective-permute-start.34) | collective-permute-done | bytes 393248 | tf_op jit(solution)/shard_map/ppermute | solution.py:634
  104.3 1.5 %collective-permute-done.36.refs_1_ = bf16[192,1024]{1,0:T(8,128)(2,1)S(1)} collective-permute-done((bf16[192,1024]{1,0:T(8,128)(2,1)S(1)}, bf16[192,1024]{1,0:T(8,128)(2,1)S(1)}, u32[]{:S(2)}, u32[]{:S(2)}) %collective-permute-start.36) | collective-permute-done | bytes 393248 | tf_op jit(solution)/shard_map/ppermute | solution.py:634
  105.8 0.6 collective-permute-done.35.refs_0_
  107.4 2.5 %unpack.4 = (f32[512,1024]{1,0:T(8,128)}, f32[512,1024]{1,0:T(8,128)}, f32[1024,512]{1,0:T(8,128)}, f32[512,384]{1,0:T(8,128)}, f32[512,384]{1,0:T(8,128)}, /*index=5*/f32[512,384]{1,0:T(8,128)}, f32[384,512]{1,0:T(8,128)}) custom-call(s32[4]{0:T(128)S(1)} %pad_add_fusion.ids, ...), custom_call_target="tpu_custom_call", output_to_operand_aliasing={{0}: (5, {}), {1}: (6, {}), {2}: (7, {})} | custom-call | flops 1000 | bytes 1000 | tf_op jit(solution)/shard_map/unpack/pallas_call | solution.py:737
  110.0 2.6 %unpack.5 = (f32[512,1024]{1,0:T(8,128)}, f32[512,1024]{1,0:T(8,128)}, f32[1024,512]{1,0:T(8,128)}, f32[512,384]{1,0:T(8,128)}, f32[512,384]{1,0:T(8,128)}, /*index=5*/f32[512,384]{1,0:T(8,128)}, f32[384,512]{1,0:T(8,128)}) custom-call(s32[4]{0:T(128)S(1)} %pad_add_fusion.ids, ...), custom_call_target="tpu_custom_call", output_to_operand_aliasing={{0}: (5, {}), {1}: (6, {}), {2}: (7, {}), {3}: (8, {}), {4}... | custom-call | flops 1000 | bytes 1000 | tf_op jit(solution)/shard_map/unpack/pallas_call | solution.py:737
  (70 shorter events, 6.9 us)
Async XLA Ops:
  0.6 6.7 %copy-start.4 = (bf16[1,256,512]{2,1,0:T(8,128)(2,1)S(1)}, bf16[1,256,512]{2,1,0:T(8,128)(2,1)}, u32[]{:S(2)}) copy-start(bf16[1,256,512]{2,1,0:T(8,128)(2,1)} %param.13) | copy-start | bytes 786436
  0.7 6.7 %copy-start.6 = (s32[1,16]{1,0:T(1,128)S(1)}, s32[1,16]{1,0:T(1,128)}, u32[]{:S(2)}) copy-start(s32[1,16]{1,0:T(1,128)} %param.24) | copy-start | bytes 196
  0.7 6.7 %copy-start.7 = (bf16[32,6]{0,1:T(8,128)(2,1)S(1)}, bf16[32,6]{0,1:T(8,128)(2,1)}, u32[]{:S(2)}) copy-start(bf16[32,6]{0,1:T(8,128)(2,1)} %param.19) | copy-start | bytes 1156
  0.7 11.1 %collective-permute-start.3 = (bf16[256,512]{1,0:T(8,128)(2,1)}, bf16[256,512]{1,0:T(8,128)(2,1)S(1)}, u32[]{:S(2)}, u32[]{:S(2)}) collective-permute-start(bf16[256,512]{1,0:T(8,128)(2,1)} %bitcast.13), channel_id=1, source_target_pairs={{0,4},{1,5},{2,6},{3,7},{4,0},{5,1},{6,2},{7,3},{8,12},{9,13},{10,... | collective-permute-start | bytes 786440 | tf_op jit(solution)/shard_map/ppermute | solution.py:634
  3.7 8.1 %collective-permute-start.1 = (bf16[256,512]{1,0:T(8,128)(2,1)}, bf16[256,512]{1,0:T(8,128)(2,1)S(1)}, u32[]{:S(2)}, u32[]{:S(2)}) collective-permute-start(bf16[256,512]{1,0:T(8,128)(2,1)} %bitcast.14), channel_id=1, source_target_pairs={{0,2},{1,3},{2,0},{3,1},{4,6},{5,7},{6,4},{7,5},{8,10},{9,11},{10,... | collective-permute-start | bytes 786440 | tf_op jit(solution)/shard_map/ppermute | solution.py:634
  5.2 3.8 %collective-permute-start = (bf16[256,512]{1,0:T(8,128)(2,1)}, bf16[256,512]{1,0:T(8,128)(2,1)S(1)}, u32[]{:S(2)}, u32[]{:S(2)}) collective-permute-start(bf16[256,512]{1,0:T(8,128)(2,1)} %bitcast.15), channel_id=1, source_target_pairs={{0,1},{1,0},{2,3},{3,2},{4,5},{5,4},{6,7},{7,6},{8,9},{9,8},{10,11... | collective-permute-start | bytes 786440 | tf_op jit(solution)/shard_map/ppermute | solution.py:634
  11.8 2.6 %collective-permute-start.2 = (bf16[256,512]{1,0:T(8,128)(2,1)S(1)}, bf16[256,512]{1,0:T(8,128)(2,1)S(1)}, u32[]{:S(2)}, u32[]{:S(2)}) collective-permute-start(bf16[256,512]{1,0:T(8,128)(2,1)S(1)} %collective-permute-done.1.refs_0_), channel_id=1, source_target_pairs={{0,1},{1,0},{2,3},{3,2},{4,5},{5,4},{6,7},{7,6},{8,9},{9,8},{10,11... | collective-permute-start | bytes 786440 | tf_op jit(solution)/shard_map/ppermute | solution.py:634
  12.4 2.0 %collective-permute-start.4 = (bf16[256,512]{1,0:T(8,128)(2,1)S(1)}, bf16[256,512]{1,0:T(8,128)(2,1)S(1)}, u32[]{:S(2)}, u32[]{:S(2)}) collective-permute-start(bf16[256,512]{1,0:T(8,128)(2,1)S(1)} %collective-permute-done.3.refs_2_), channel_id=1, source_target_pairs={{0,1},{1,0},{2,3},{3,2},{4,5},{5,4},{6,7},{7,6},{8,9},{9,8},{10,11... | collective-permute-start | bytes 786440 | tf_op jit(solution)/shard_map/ppermute | solution.py:634
  12.5 6.2 %collective-permute-start.6 = (bf16[128,512]{1,0:T(8,128)(2,1)S(1)}, bf16[128,512]{1,0:T(8,128)(2,1)S(1)}, u32[]{:S(2)}, u32[]{:S(2)}) collective-permute-start(bf16[128,512]{1,0:T(8,128)(2,1)S(1)} %slice.13), channel_id=1, source_target_pairs={{0,4},{1,5},{2,6},{3,7},{4,0},{5,1},{6,2},{7,3},{8,12},{9,13},{10,... | collective-permute-start | bytes 393224 | tf_op jit(solution)/shard_map/ppermute | solution.py:634
  13.0 6.2 %copy-start.8 = (bf16[512]{0:T(512)(128)(2,1)S(1)}, bf16[512]{0:T(512)(128)(2,1)}, u32[]{:S(2)}) copy-start(bf16[512]{0:T(512)(128)(2,1)} %param.20) | copy-start | bytes 3076
  13.1 5.6 %collective-permute-start.5 = (bf16[128,512]{1,0:T(8,128)(2,1)S(1)}, bf16[128,512]{1,0:T(8,128)(2,1)S(1)}, u32[]{:S(2)}, u32[]{:S(2)}) collective-permute-start(bf16[128,512]{1,0:T(8,128)(2,1)S(1)} %slice.12), channel_id=1, source_target_pairs={{0,2},{1,3},{2,0},{3,1},{4,6},{5,7},{6,4},{7,5},{8,10},{9,11},{10,... | collective-permute-start | bytes 393224 | tf_op jit(solution)/shard_map/ppermute | solution.py:634
  18.7 1.4 %collective-permute-start.7 = (bf16[128,512]{1,0:T(8,128)(2,1)S(1)}, bf16[128,512]{1,0:T(8,128)(2,1)S(1)}, u32[]{:S(2)}, u32[]{:S(2)}) collective-permute-start(bf16[128,512]{1,0:T(8,128)(2,1)S(1)} %collective-permute-done.5.refs_0_), channel_id=1, source_target_pairs={{0,1},{1,0},{2,3},{3,2},{4,5},{5,4},{6,7},{7,6},{8,9},{9,8},{10,11... | collective-permute-start | bytes 393224 | tf_op jit(solution)/shard_map/ppermute | solution.py:634
  18.7 1.5 %collective-permute-start.8 = (bf16[128,512]{1,0:T(8,128)(2,1)S(1)}, bf16[128,512]{1,0:T(8,128)(2,1)S(1)}, u32[]{:S(2)}, u32[]{:S(2)}) collective-permute-start(bf16[128,512]{1,0:T(8,128)(2,1)S(1)} %collective-permute-done.6.refs_1_), channel_id=1, source_target_pairs={{0,1},{1,0},{2,3},{3,2},{4,5},{5,4},{6,7},{7,6},{8,9},{9,8},{10,11... | collective-permute-start | bytes 393224 | tf_op jit(solution)/shard_map/ppermute | solution.py:634
  19.2 3.7 %copy-start = (bf16[512,1024]{1,0:T(8,128)(2,1)S(1)}, bf16[512,1024]{1,0:T(8,128)(2,1)}, u32[]{:S(2)}) copy-start(bf16[512,1024]{1,0:T(8,128)(2,1)} %wg.1) | copy-start | bytes 3145732
  19.2 3.7 %copy-start.1 = (bf16[512,1024]{1,0:T(8,128)(2,1)S(1)}, bf16[512,1024]{1,0:T(8,128)(2,1)}, u32[]{:S(2)}) copy-start(bf16[512,1024]{1,0:T(8,128)(2,1)} %wu.1) | copy-start | bytes 3145732
  19.2 3.7 %copy-start.2 = (bf16[1024,512]{1,0:T(8,128)(2,1)S(1)}, bf16[1024,512]{1,0:T(8,128)(2,1)}, u32[]{:S(2)}) copy-start(bf16[1024,512]{1,0:T(8,128)(2,1)} %wd.1) | copy-start | bytes 3145732
  19.3 3.7 %copy-start.3 = (bf16[384,512]{1,0:T(8,128)(2,1)S(1)}, bf16[384,512]{1,0:T(8,128)(2,1)}, u32[]{:S(2)}) copy-start(bf16[384,512]{1,0:T(8,128)(2,1)} %wo.1) | copy-start | bytes 1179652
  19.3 3.7 %copy-start.5 = (bf16[1,256,512]{2,1,0:T(8,128)(2,1)S(1)}, bf16[1,256,512]{2,1,0:T(8,128)(2,1)}, u32[]{:S(2)}) copy-start(bf16[1,256,512]{2,1,0:T(8,128)(2,1)} %param.25) | copy-start | bytes 786436
  28.3 3.7 %collective-permute-start.9 = (bf16[768,1024]{1,0:T(8,128)(2,1)S(1)}, bf16[768,1024]{1,0:T(8,128)(2,1)S(1)}, u32[]{:S(2)}, u32[]{:S(2)}) collective-permute-start(bf16[768,1024]{1,0:T(8,128)(2,1)S(1)} %get-tuple-element.185), channel_id=1, source_target_pairs={{0,1},{1,0},{2,3},{3,2},{4,5},{5,4},{6,7},{7,6},{8,9},{9,8},{10,11... | collective-permute-start | bytes 4718600 | tf_op jit(solution)/shard_map/ppermute | solution.py:634
  32.9 11.8 %collective-permute-start.10 = (bf16[192,1024]{1,0:T(8,128)(2,1)S(1)}, bf16[192,1024]{1,0:T(8,128)(2,1)S(1)}, u32[]{:S(2)}, u32[]{:S(2)}) collective-permute-start(bf16[192,1024]{1,0:T(8,128)(2,1)S(1)} %get-tuple-element.212), channel_id=1, source_target_pairs={{0,2},{1,3},{2,0},{3,1},{4,6},{5,7},{6,4},{7,5},{8,10},{9,11},{10,... | collective-permute-start | bytes 1179656 | tf_op jit(solution)/shard_map/ppermute | solution.py:634
  33.8 11.0 %collective-permute-start.11 = (bf16[192,1024]{1,0:T(8,128)(2,1)S(1)}, bf16[192,1024]{1,0:T(8,128)(2,1)S(1)}, u32[]{:S(2)}, u32[]{:S(2)}) collective-permute-start(bf16[192,1024]{1,0:T(8,128)(2,1)S(1)} %get-tuple-element.214), channel_id=1, source_target_pairs={{0,4},{1,5},{2,6},{3,7},{4,0},{5,1},{6,2},{7,3},{8,12},{9,13},{10,... | collective-permute-start | bytes 1179656 | tf_op jit(solution)/shard_map/ppermute | solution.py:634
  44.8 4.0 %collective-permute-start.12 = (bf16[784,512]{1,0:T(8,128)(2,1)S(1)}, bf16[784,512]{1,0:T(8,128)(2,1)S(1)}, u32[]{:S(2)}, u32[]{:S(2)}) collective-permute-start(bf16[784,512]{1,0:T(8,128)(2,1)S(1)} %get-tuple-element.219), channel_id=1, source_target_pairs={{0,1},{1,0},{2,3},{3,2},{4,5},{5,4},{6,7},{7,6},{8,9},{9,8},{10,11... | collective-permute-start | bytes 2408456 | tf_op jit(solution)/shard_map/ppermute | solution.py:634
  44.9 22.9 %collective-permute-start.19 = (bf16[4,512,256]{2,1,0:T(8,128)(2,1)S(1)}, bf16[4,512,256]{2,1,0:T(8,128)(2,1)S(1)}, u32[]{:S(2)}, u32[]{:S(2)}) collective-permute-start(bf16[4,512,256]{2,1,0:T(8,128)(2,1)S(1)} %get-tuple-element.238), channel_id=1, source_target_pairs={{0,1},{1,0},{2,3},{3,2},{4,5},{5,4},{6,7},{7,6},{8,9},{9,8},{10,11... | collective-permute-start | bytes 3145736 | tf_op jit(solution)/shard_map/ppermute | solution.py:634
  46.1 7.0 %collective-permute-start.13 = (bf16[96,1024]{1,0:T(8,128)(2,1)S(1)}, bf16[96,1024]{1,0:T(8,128)(2,1)S(1)}, u32[]{:S(2)}, u32[]{:S(2)}) collective-permute-start(bf16[96,1024]{1,0:T(8,128)(2,1)S(1)} %get-tuple-element.222), channel_id=1, source_target_pairs={{0,4},{1,5},{2,6},{3,7},{4,0},{5,1},{6,2},{7,3},{8,12},{9,13},{10,... | collective-permute-start | bytes 589832 | tf_op jit(solution)/shard_map/ppermute | solution.py:634
  47.5 6.5 %collective-permute-start.14 = (bf16[96,1024]{1,0:T(8,128)(2,1)S(1)}, bf16[96,1024]{1,0:T(8,128)(2,1)S(1)}, u32[]{:S(2)}, u32[]{:S(2)}) collective-permute-start(bf16[96,1024]{1,0:T(8,128)(2,1)S(1)} %get-tuple-element.223), channel_id=1, source_target_pairs={{0,2},{1,3},{2,0},{3,1},{4,6},{5,7},{6,4},{7,5},{8,10},{9,11},{10,... | collective-permute-start | bytes 589832 | tf_op jit(solution)/shard_map/ppermute | solution.py:634
  54.7 5.7 %collective-permute-start.15 = (bf16[96,1024]{1,0:T(8,128)(2,1)S(1)}, bf16[96,1024]{1,0:T(8,128)(2,1)S(1)}, u32[]{:S(2)}, u32[]{:S(2)}) collective-permute-start(bf16[96,1024]{1,0:T(8,128)(2,1)S(1)} %get-tuple-element.228), channel_id=1, source_target_pairs={{0,8},{8,0},{16,24},{24,16},{1,9},{9,1},{17,25},{25,17},{2,10},{10... | collective-permute-start | bytes 589832 | tf_op jit(solution)/shard_map/ppermute | solution.py:634
  56.4 8.0 %collective-permute-start.16 = (bf16[208,512]{1,0:T(8,128)(2,1)S(1)}, bf16[208,512]{1,0:T(8,128)(2,1)S(1)}, u32[]{:S(2)}, u32[]{:S(2)}) collective-permute-start(bf16[208,512]{1,0:T(8,128)(2,1)S(1)} %get-tuple-element.230), channel_id=1, source_target_pairs={{0,2},{1,3},{2,0},{3,1},{4,6},{5,7},{6,4},{7,5},{8,10},{9,11},{10,... | collective-permute-start | bytes 638984 | tf_op jit(solution)/shard_map/ppermute | solution.py:634
  57.6 10.0 %collective-permute-start.17 = (bf16[208,512]{1,0:T(8,128)(2,1)S(1)}, bf16[208,512]{1,0:T(8,128)(2,1)S(1)}, u32[]{:S(2)}, u32[]{:S(2)}) collective-permute-start(bf16[208,512]{1,0:T(8,128)(2,1)S(1)} %get-tuple-element.231), channel_id=1, source_target_pairs={{0,4},{1,5},{2,6},{3,7},{4,0},{5,1},{6,2},{7,3},{8,12},{9,13},{10,... | collective-permute-start | bytes 638984 | tf_op jit(solution)/shard_map/ppermute | solution.py:634
  58.4 9.3 %collective-permute-start.18 = (bf16[208,512]{1,0:T(8,128)(2,1)S(1)}, bf16[208,512]{1,0:T(8,128)(2,1)S(1)}, u32[]{:S(2)}, u32[]{:S(2)}) collective-permute-start(bf16[208,512]{1,0:T(8,128)(2,1)S(1)} %get-tuple-element.232), channel_id=1, source_target_pairs={{0,6},{1,7},{2,4},{3,5},{4,2},{5,3},{6,0},{7,1},{8,14},{9,15},{10,... | collective-permute-start | bytes 638984 | tf_op jit(solution)/shard_map/ppermute | solution.py:634
  61.1 9.7 %collective-permute-start.22 = (bf16[96,1024]{1,0:T(8,128)(2,1)S(1)}, bf16[96,1024]{1,0:T(8,128)(2,1)S(1)}, u32[]{:S(2)}, u32[]{:S(2)}) collective-permute-start(bf16[96,1024]{1,0:T(8,128)(2,1)S(1)} %add_parts.13.refs_0_), channel_id=1, source_target_pairs={{0,16},{8,24},{16,0},{24,8},{1,17},{9,25},{17,1},{25,9},{2,18},{10... | collective-permute-start | bytes 589832 | tf_op jit(solution)/shard_map/ppermute | solution.py:634
  68.5 15.2 %collective-permute-start.25 = (bf16[512,256]{1,0:T(8,128)(2,1)S(1)}, bf16[512,256]{1,0:T(8,128)(2,1)S(1)}, u32[]{:S(2)}, u32[]{:S(2)}) collective-permute-start(bf16[512,256]{1,0:T(8,128)(2,1)S(1)} %get-tuple-element.248), channel_id=1, source_target_pairs={{0,6},{1,7},{2,4},{3,5},{4,2},{5,3},{6,0},{7,1},{8,14},{9,15},{10,... | collective-permute-start | bytes 786440 | tf_op jit(solution)/shard_map/ppermute | solution.py:634
  71.3 7.0 %collective-permute-start.23 = (bf16[96,1024]{1,0:T(8,128)(2,1)S(1)}, bf16[96,1024]{1,0:T(8,128)(2,1)S(1)}, u32[]{:S(2)}, u32[]{:S(2)}) collective-permute-start(bf16[96,1024]{1,0:T(8,128)(2,1)S(1)} %add_parts.15.mine), channel_id=1, source_target_pairs={{0,8},{8,0},{16,24},{24,16},{1,9},{9,1},{17,25},{25,17},{2,10},{10... | collective-permute-start | bytes 589832 | tf_op jit(solution)/shard_map/ppermute | solution.py:634
  72.1 12.9 %collective-permute-start.20 = (bf16[512,256]{1,0:T(8,128)(2,1)S(1)}, bf16[512,256]{1,0:T(8,128)(2,1)S(1)}, u32[]{:S(2)}, u32[]{:S(2)}) collective-permute-start(bf16[512,256]{1,0:T(8,128)(2,1)S(1)} %get-tuple-element.241), channel_id=1, source_target_pairs={{0,2},{1,3},{2,0},{3,1},{4,6},{5,7},{6,4},{7,5},{8,10},{9,11},{10,... | collective-permute-start | bytes 786440 | tf_op jit(solution)/shard_map/ppermute | solution.py:634
  73.3 11.7 %collective-permute-start.21 = (bf16[512,256]{1,0:T(8,128)(2,1)S(1)}, bf16[512,256]{1,0:T(8,128)(2,1)S(1)}, u32[]{:S(2)}, u32[]{:S(2)}) collective-permute-start(bf16[512,256]{1,0:T(8,128)(2,1)S(1)} %get-tuple-element.242), channel_id=1, source_target_pairs={{0,4},{1,5},{2,6},{3,7},{4,0},{5,1},{6,2},{7,3},{8,12},{9,13},{10,... | collective-permute-start | bytes 786440 | tf_op jit(solution)/shard_map/ppermute | solution.py:634
  74.1 5.4 %collective-permute-start.24 = (bf16[112,512]{1,0:T(8,128)(2,1)S(1)}, bf16[112,512]{1,0:T(8,128)(2,1)S(1)}, u32[]{:S(2)}, u32[]{:S(2)}) collective-permute-start(bf16[112,512]{1,0:T(8,128)(2,1)S(1)} %get-tuple-element.246), channel_id=1, source_target_pairs={{0,8},{8,0},{16,24},{24,16},{1,9},{9,1},{17,25},{25,17},{2,10},{10... | collective-permute-start | bytes 344072 | tf_op jit(solution)/shard_map/ppermute | solution.py:634
  80.1 7.0 %collective-permute-start.26 = (bf16[112,512]{1,0:T(8,128)(2,1)S(1)}, bf16[112,512]{1,0:T(8,128)(2,1)S(1)}, u32[]{:S(2)}, u32[]{:S(2)}) collective-permute-start(bf16[112,512]{1,0:T(8,128)(2,1)S(1)} %add_parts.16.refs_0_), channel_id=1, source_target_pairs={{0,16},{8,24},{16,0},{24,8},{1,17},{9,25},{17,1},{25,9},{2,18},{10... | collective-permute-start | bytes 344072 | tf_op jit(solution)/shard_map/ppermute | solution.py:634
  83.0 8.3 %collective-permute-start.28 = (bf16[96,1024]{1,0:T(8,128)(2,1)S(1)}, bf16[96,1024]{1,0:T(8,128)(2,1)S(1)}, u32[]{:S(2)}, u32[]{:S(2)}) collective-permute-start(bf16[96,1024]{1,0:T(8,128)(2,1)S(1)} %get-tuple-element.257.c), channel_id=1, source_target_pairs={{0,2},{1,3},{2,0},{3,1},{4,6},{5,7},{6,4},{7,5},{8,10},{9,11},{10,... | collective-permute-start | bytes 589832 | tf_op jit(solution)/shard_map/ppermute | solution.py:634
  83.8 7.5 %collective-permute-start.27 = (bf16[96,1024]{1,0:T(8,128)(2,1)S(1)}, bf16[96,1024]{1,0:T(8,128)(2,1)S(1)}, u32[]{:S(2)}, u32[]{:S(2)}) collective-permute-start(bf16[96,1024]{1,0:T(8,128)(2,1)S(1)} %get-tuple-element.245.a), channel_id=1, source_target_pairs={{0,4},{1,5},{2,6},{3,7},{4,0},{5,1},{6,2},{7,3},{8,12},{9,13},{10,... | collective-permute-start | bytes 589832 | tf_op jit(solution)/shard_map/ppermute | solution.py:634
  87.7 5.6 %collective-permute-start.31 = (bf16[96,512]{1,0:T(8,128)(2,1)S(1)}, bf16[96,512]{1,0:T(8,128)(2,1)S(1)}, u32[]{:S(2)}, u32[]{:S(2)}) collective-permute-start(bf16[96,512]{1,0:T(8,128)(2,1)S(1)} %slice.16.refs_0_), channel_id=1, source_target_pairs={{0,6},{1,7},{2,4},{3,5},{4,2},{5,3},{6,0},{7,1},{8,14},{9,15},{10,... | collective-permute-start | bytes 294920 | tf_op jit(solution)/shard_map/ppermute | solution.py:634
  89.3 5.0 %collective-permute-start.30 = (bf16[96,512]{1,0:T(8,128)(2,1)S(1)}, bf16[96,512]{1,0:T(8,128)(2,1)S(1)}, u32[]{:S(2)}, u32[]{:S(2)}) collective-permute-start(bf16[96,512]{1,0:T(8,128)(2,1)S(1)} %slice.16.refs_0_), channel_id=1, source_target_pairs={{0,4},{1,5},{2,6},{3,7},{4,0},{5,1},{6,2},{7,3},{8,12},{9,13},{10,... | collective-permute-start | bytes 294920 | tf_op jit(solution)/shard_map/ppermute | solution.py:634
  90.5 4.6 %collective-permute-start.29 = (bf16[96,512]{1,0:T(8,128)(2,1)S(1)}, bf16[96,512]{1,0:T(8,128)(2,1)S(1)}, u32[]{:S(2)}, u32[]{:S(2)}) collective-permute-start(bf16[96,512]{1,0:T(8,128)(2,1)S(1)} %slice.16.refs_0_), channel_id=1, source_target_pairs={{0,2},{1,3},{2,0},{3,1},{4,6},{5,7},{6,4},{7,5},{8,10},{9,11},{10,... | collective-permute-start | bytes 294920 | tf_op jit(solution)/shard_map/ppermute | solution.py:634
  91.9 6.8 %collective-permute-start.33 = (bf16[192,1024]{1,0:T(8,128)(2,1)S(1)}, bf16[192,1024]{1,0:T(8,128)(2,1)S(1)}, u32[]{:S(2)}, u32[]{:S(2)}) collective-permute-start(bf16[192,1024]{1,0:T(8,128)(2,1)S(1)} %get-tuple-element.261.refs_1_), channel_id=1, source_target_pairs={{0,1},{1,0},{2,3},{3,2},{4,5},{5,4},{6,7},{7,6},{8,9},{9,8},{10,11... | collective-permute-start | bytes 1179656 | tf_op jit(solution)/shard_map/ppermute | solution.py:634
  91.9 6.7 %collective-permute-start.32 = (bf16[192,1024]{1,0:T(8,128)(2,1)S(1)}, bf16[192,1024]{1,0:T(8,128)(2,1)S(1)}, u32[]{:S(2)}, u32[]{:S(2)}) collective-permute-start(bf16[192,1024]{1,0:T(8,128)(2,1)S(1)} %get-tuple-element.260.refs_0_), channel_id=1, source_target_pairs={{0,1},{1,0},{2,3},{3,2},{4,5},{5,4},{6,7},{7,6},{8,9},{9,8},{10,11... | collective-permute-start | bytes 1179656 | tf_op jit(solution)/shard_map/ppermute | solution.py:634
  95.7 8.7 %collective-permute-start.34 = (bf16[384,512]{1,0:T(8,128)(2,1)S(1)}, bf16[384,512]{1,0:T(8,128)(2,1)S(1)}, u32[]{:S(2)}, u32[]{:S(2)}) collective-permute-start(bf16[384,512]{1,0:T(8,128)(2,1)S(1)} %stack.21.refs_2_), channel_id=1, source_target_pairs={{0,8},{8,0},{16,24},{24,16},{1,9},{9,1},{17,25},{25,17},{2,10},{10... | collective-permute-start | bytes 1179656 | tf_op jit(solution)/shard_map/ppermute | solution.py:634
  96.2 9.6 %collective-permute-start.36 = (bf16[192,1024]{1,0:T(8,128)(2,1)S(1)}, bf16[192,1024]{1,0:T(8,128)(2,1)S(1)}, u32[]{:S(2)}, u32[]{:S(2)}) collective-permute-start(bf16[192,1024]{1,0:T(8,128)(2,1)S(1)} %get-tuple-element.261.refs_1_), channel_id=1, source_target_pairs={{0,4},{1,5},{2,6},{3,7},{4,0},{5,1},{6,2},{7,3},{8,12},{9,13},{10,... | collective-permute-start | bytes 1179656 | tf_op jit(solution)/shard_map/ppermute | solution.py:634
  97.4 9.0 %collective-permute-start.35 = (bf16[192,1024]{1,0:T(8,128)(2,1)S(1)}, bf16[192,1024]{1,0:T(8,128)(2,1)S(1)}, u32[]{:S(2)}, u32[]{:S(2)}) collective-permute-start(bf16[192,1024]{1,0:T(8,128)(2,1)S(1)} %get-tuple-element.260.refs_0_), channel_id=1, source_target_pairs={{0,2},{1,3},{2,0},{3,1},{4,6},{5,7},{6,4},{7,5},{8,10},{9,11},{10,... | collective-permute-start | bytes 1179656 | tf_op jit(solution)/shard_map/ppermute | solution.py:634
  106.4 3.6 %collective-permute-start.37 = (bf16[192,1024]{1,0:T(8,128)(2,1)S(1)}, bf16[192,1024]{1,0:T(8,128)(2,1)S(1)}, u32[]{:S(2)}, u32[]{:S(2)}) collective-permute-start(bf16[192,1024]{1,0:T(8,128)(2,1)S(1)} %collective-permute-done.35.refs_0_), channel_id=1, source_target_pairs={{0,1},{1,0},{2,3},{3,2},{4,5},{5,4},{6,7},{7,6},{8,9},{9,8},{10,11... | collective-permute-start | bytes 1179656 | tf_op jit(solution)/shard_map/ppermute | solution.py:634
  106.4 3.6 %collective-permute-start.38 = (bf16[192,1024]{1,0:T(8,128)(2,1)S(1)}, bf16[192,1024]{1,0:T(8,128)(2,1)S(1)}, u32[]{:S(2)}, u32[]{:S(2)}) collective-permute-start(bf16[192,1024]{1,0:T(8,128)(2,1)S(1)} %collective-permute-done.36.refs_1_), channel_id=1, source_target_pairs={{0,1},{1,0},{2,3},{3,2},{4,5},{5,4},{6,7},{7,6},{8,9},{9,8},{10,11... | collective-permute-start | bytes 1179656 | tf_op jit(solution)/shard_map/ppermute | solution.py:634
  106.9 3.1 %collective-permute-start.39 = (bf16[384,512]{1,0:T(8,128)(2,1)S(1)}, bf16[384,512]{1,0:T(8,128)(2,1)S(1)}, u32[]{:S(2)}, u32[]{:S(2)}) collective-permute-start(bf16[384,512]{1,0:T(8,128)(2,1)S(1)} %stack.21.refs_2_), channel_id=1, source_target_pairs={{0,1},{1,0},{2,3},{3,2},{4,5},{5,4},{6,7},{7,6},{8,9},{9,8},{10,11... | collective-permute-start | bytes 1179656 | tf_op jit(solution)/shard_map/ppermute | solution.py:634
  106.9 3.1 %collective-permute-start.40 = (bf16[384,512]{1,0:T(8,128)(2,1)S(1)}, bf16[384,512]{1,0:T(8,128)(2,1)S(1)}, u32[]{:S(2)}, u32[]{:S(2)}) collective-permute-start(bf16[384,512]{1,0:T(8,128)(2,1)S(1)} %collective-permute-done.34.refs_3_), channel_id=1, source_target_pairs={{0,1},{1,0},{2,3},{3,2},{4,5},{5,4},{6,7},{7,6},{8,9},{9,8},{10,11... | collective-permute-start | bytes 1179656 | tf_op jit(solution)/shard_map/ppermute | solution.py:634

commit v6 on v5

--- a/solution.py
+++ b/solution.py
@@ -14,7 +14,7 @@
 FFN_CHUNKS = 1
 STEPS = (
     "a_chips", "f_rows", "f_z0", "a_rows", "d_slots", "f_z1", "f_pick", "a_z0", "d:3", "d_out", "a_z1",
-    "f_join", "a_stack", "f_near", "small", "a_swap", "f_swap", "own", "last",
+    "f_join", "a_stack", "small", "f_near", "f_swap", "a_swap", "own", "last",
 )
 SMALL = 16
 VMEM = 24 * 1024 * 1024

time: 113 us -> 112 us (level)
  transfers between devices with their start and end apart: 41 -> 41, of which waited for: 17 -> 15; matrix products, arithmetic and copies ran while one was open for 2% -> 2% of each run, Pallas kernels for 32% -> 33%
where the time goes in v6:
time: 112 us
  Pallas kernels  48 us (43%)
  starting transfers between devices  39.2 us (35%)
  waiting for transfers between devices  21 us (19%)
  other arithmetic  1.41 us (1%)
  between operations  1.28 us (1%)
    pallas_call x22, Pallas kernels, call(): pl.pallas_call(kernel, in_specs=[smem] * len(smem_args) + [vmem] * (len(a...  40.4 us
    ppermute x41, starting transfers between devices, swap(): return lax.ppermute(array, axis, [(i, i ^ j) for i in range(size)])  39.2 us
    ppermute x41, waiting for transfers between devices, swap(): return lax.ppermute(array, axis, [(i, i ^ j) for i in range(size)])  21 us
    pallas_call x3, Pallas kernels, unpack(): pl.pallas_call(kernel, in_specs=[pl.BlockSpec(memory_space=pltpu.SMEM)] +...  7.58 us
  transfers between devices with their start and end apart: 41, of which 15 were waited for; matrix products, arithmetic and copies ran while one was open for 2% of the time, Pallas kernels for 33%

profile of v6, /device:TPU:0, one launch (start us, length us, event | category | flops | bytes accessed | tf_op | source)
XLA Modules:
  0.0 111.7 jit_solution(307290283707652063)
XLA Ops:
  0.7 3.0 %collective-permute-start.3 = (bf16[256,512]{1,0:T(8,128)(2,1)}, bf16[256,512]{1,0:T(8,128)(2,1)S(1)}, u32[]{:S(2)}, u32[]{:S(2)}) collective-permute-start(bf16[256,512]{1,0:T(8,128)(2,1)} %bitcast.13), channel_id=1, source_target_pairs={{0,4},{1,5},{2,6},{3,7},{4,0},{5,1},{6,2},{7,3},{8,12},{9,13},{10,... | collective-permute-start | bytes 786440 | tf_op jit(solution)/shard_map/ppermute | solution.py:634
  3.7 1.5 %collective-permute-start.1 = (bf16[256,512]{1,0:T(8,128)(2,1)}, bf16[256,512]{1,0:T(8,128)(2,1)S(1)}, u32[]{:S(2)}, u32[]{:S(2)}) collective-permute-start(bf16[256,512]{1,0:T(8,128)(2,1)} %bitcast.14), channel_id=1, source_target_pairs={{0,2},{1,3},{2,0},{3,1},{4,6},{5,7},{6,4},{7,5},{8,10},{9,11},{10,... | collective-permute-start | bytes 786440 | tf_op jit(solution)/shard_map/ppermute | solution.py:634
  5.2 0.7 reshape.55.gain.refs_2_.refs_4_.refs_18_.refs_7_
  6.0 1.3 %pad_maximum_fusion.w3 = bf16[512,1152]{1,0:T(8,128)(2,1)S(1)} fusion(bf16[512,384]{1,0:T(8,128)(2,1)} %param.17, bf16[512,384]{1,0:T(8,128)(2,1)} %param.16, bf16[512,384]{1,0:T(8,128)(2,1)} %param.15), kind=kLoop, calls=%fused_computation | loop fusion | flops 3538944 | bytes 2359296 | tf_op jit(solution)/shard_map/concatenate | solution.py:130
  7.3 1.6 %prepare.1 = (bf16[256,384]{1,0:T(8,128)(2,1)S(1)}, f32[256,128]{1,0:T(8,128)S(1)}, bf16[6,4,256,256]{3,2,1,0:T(8,128)(2,1)S(1)}, bf16[1152,512]{1,0:T(8,128)(2,...) custom-call(s32[4]{0:T(128)S(1)} %pad_add_fusion.ids, ...), custom_call_target="tpu_custom_call" | custom-call | flops 4000000 | bytes 8000 | tf_op jit(solution)/shard_map/prepare/pallas_call | solution.py:72
  9.0 2.8 %attend.3 = (bf16[512,512]{1,0:T(8,128)(2,1)S(1)}, bf16[512,128]{1,0:T(8,128)(2,1)S(1)}, f32[256,384]{1,0:T(8,128)S(1)}, f32[256,128]{1,0:T(8,128)S(1)}, bf16[2,...) custom-call(s32[4]{0:T(128)S(1)} %pad_add_fusion.ids, ...), custom_call_target="tpu_custom_call" | custom-call | flops 4000000 | bytes 8000 | tf_op jit(solution)/shard_map/attend/pallas_call | solution.py:72
  12.5 0.6 collective-permute-start.6
  13.1 1.3 %collective-permute-start.5 = (bf16[128,512]{1,0:T(8,128)(2,1)S(1)}, bf16[128,512]{1,0:T(8,128)(2,1)S(1)}, u32[]{:S(2)}, u32[]{:S(2)}) collective-permute-start(bf16[128,512]{1,0:T(8,128)(2,1)S(1)} %slice.12), channel_id=1, source_target_pairs={{0,2},{1,3},{2,0},{3,1},{4,6},{5,7},{6,4},{7,5},{8,10},{9,11},{10,... | collective-permute-start | bytes 393224 | tf_op jit(solution)/shard_map/ppermute | solution.py:634
  14.4 4.3 %attend.4 = (bf16[1024,512]{1,0:T(8,128)(2,1)S(1)}, bf16[1024,128]{1,0:T(8,128)(2,1)S(1)}, f32[256,384]{1,0:T(8,128)S(1)}, f32[256,128]{1,0:T(8,128)S(1)}, bf16[...) custom-call(s32[4]{0:T(128)S(1)} %pad_add_fusion.ids, ...), custom_call_target="tpu_custom_call" | custom-call | flops 8000000 | bytes 16000 | tf_op jit(solution)/shard_map/attend/pallas_call | solution.py:72
  19.3 0.8 collective-permute-done.7.refs_2_
  20.3 2.7 %attend.5 = (bf16[512,512]{1,0:T(8,128)(2,1)S(1)}, bf16[512,128]{1,0:T(8,128)(2,1)S(1)}, f32[256,384]{1,0:T(8,128)S(1)}, f32[256,128]{1,0:T(8,128)S(1)}, bf16[2,...) custom-call(s32[4]{0:T(128)S(1)} %pad_add_fusion.ids, ...), custom_call_target="tpu_custom_call" | custom-call | flops 4000000 | bytes 8000 | tf_op jit(solution)/shard_map/attend/pallas_call | solution.py:72
  23.0 5.3 %feed_forward.1 = (bf16[256,512]{1,0:T(8,128)(2,1)}, f32[256,512]{1,0:T(8,128)S(1)}, bf16[256,384]{1,0:T(8,128)(2,1)S(1)}, f32[256,128]{1,0:T(8,128)S(1)}, bf16[...) custom-call(s32[4]{0:T(128)S(1)} %pad_add_fusion.ids, ...), custom_call_target="tpu_custom_call" | custom-call | flops 8000000 | bytes 16000 | tf_op jit(solution)/shard_map/feed_forward/pallas_call | solution.py:72
  28.7 3.3 %attend_back.1 = (bf16[128,2048]{1,0:T(8,128)(2,1)S(1)}, bf16[128,2048]{1,0:T(8,128)(2,1)S(1)}, bf16[256,128]{1,0:T(8,128)(2,1)S(1)}, f32[8,1152]{1,0:T(8,128)S(1)}) custom-call(s32[4]{0:T(128)S(1)} %pad_add_fusion.ids, bf16[256,384]{1,0:T(8,128)(2,1)S(1)} %get-tuple-element.157.refs_5_.refs_7_.q.refs_0_, ...), custom_call_target="tpu_custom_call" | custom-call | flops 4000000 | bytes 8000 | tf_op jit(solution)/shard_map/attend_back/pallas_call | solution.py:72
  32.0 0.9 add_parts.9
  32.9 0.8 collective-permute-start.10
  33.8 1.5 %collective-permute-start.11 = (bf16[192,1024]{1,0:T(8,128)(2,1)S(1)}, bf16[192,1024]{1,0:T(8,128)(2,1)S(1)}, u32[]{:S(2)}, u32[]{:S(2)}) collective-permute-start(bf16[192,1024]{1,0:T(8,128)(2,1)S(1)} %get-tuple-element.214), channel_id=1, source_target_pairs={{0,4},{1,5},{2,6},{3,7},{4,0},{5,1},{6,2},{7,3},{8,12},{9,13},{10,... | collective-permute-start | bytes 1179656 | tf_op jit(solution)/shard_map/ppermute | solution.py:634
  35.3 9.5 %rest_back.1 = (bf16[4,512,256]{2,1,0:T(8,128)(2,1)S(1)}, bf16[4,512,256]{2,1,0:T(8,128)(2,1)S(1)}, f32[256,512]{1,0:T(8,128)S(1)}, bf16[784,512]{1,0:T(8,128)(2,1)S(1)}, bf16[784,512]{1,0:T(8,128)(2,1)S(1)}) custom-call(s32[4]{0:T(128)S(1)} %pad_add_fusion.ids, bf16[256,384]{1,0:T(8,128)(2,1)S(1)} %get-tuple-element.157.refs_5_.refs_7_.q.refs_0_, ...), custom_call_target="tpu_custom_call" | custom-call | flops 10000000 | bytes 20000 | tf_op jit(solution)/shard_map/rest_back/pallas_call | solution.py:72
  45.4 0.7 add_parts.10
  46.1 1.4 %collective-permute-start.13 = (bf16[96,1024]{1,0:T(8,128)(2,1)S(1)}, bf16[96,1024]{1,0:T(8,128)(2,1)S(1)}, u32[]{:S(2)}, u32[]{:S(2)}) collective-permute-start(bf16[96,1024]{1,0:T(8,128)(2,1)S(1)} %get-tuple-element.222), channel_id=1, source_target_pairs={{0,4},{1,5},{2,6},{3,7},{4,0},{5,1},{6,2},{7,3},{8,12},{9,13},{10,... | collective-permute-start | bytes 589832 | tf_op jit(solution)/shard_map/ppermute | solution.py:634
  47.5 1.2 %collective-permute-start.14 = (bf16[96,1024]{1,0:T(8,128)(2,1)S(1)}, bf16[96,1024]{1,0:T(8,128)(2,1)S(1)}, u32[]{:S(2)}, u32[]{:S(2)}) collective-permute-start(bf16[96,1024]{1,0:T(8,128)(2,1)S(1)} %get-tuple-element.223), channel_id=1, source_target_pairs={{0,2},{1,3},{2,0},{3,1},{4,6},{5,7},{6,4},{7,5},{8,10},{9,11},{10,... | collective-permute-start | bytes 589832 | tf_op jit(solution)/shard_map/ppermute | solution.py:634
  48.8 0.7 add_parts.11
  49.5 3.5 %collective-permute-done.13.recv_x = bf16[96,1024]{1,0:T(8,128)(2,1)S(1)} collective-permute-done((bf16[96,1024]{1,0:T(8,128)(2,1)S(1)}, bf16[96,1024]{1,0:T(8,128)(2,1)S(1)}, u32[]{:S(2)}, u32[]{:S(2)}) %collective-permute-start.13) | collective-permute-done | bytes 196640 | tf_op jit(solution)/shard_map/ppermute | solution.py:634
  53.1 1.0 collective-permute-done.14.recv_y
  54.1 0.7 add_parts.12
  54.7 1.6 %collective-permute-start.15 = (bf16[96,1024]{1,0:T(8,128)(2,1)S(1)}, bf16[96,1024]{1,0:T(8,128)(2,1)S(1)}, u32[]{:S(2)}, u32[]{:S(2)}) collective-permute-start(bf16[96,1024]{1,0:T(8,128)(2,1)S(1)} %get-tuple-element.228), channel_id=1, source_target_pairs={{0,8},{8,0},{16,24},{24,16},{1,9},{9,1},{17,25},{25,17},{2,10},{10... | collective-permute-start | bytes 589832 | tf_op jit(solution)/shard_map/ppermute | solution.py:634
  56.4 1.2 %collective-permute-start.16 = (bf16[208,512]{1,0:T(8,128)(2,1)S(1)}, bf16[208,512]{1,0:T(8,128)(2,1)S(1)}, u32[]{:S(2)}, u32[]{:S(2)}) collective-permute-start(bf16[208,512]{1,0:T(8,128)(2,1)S(1)} %get-tuple-element.230), channel_id=1, source_target_pairs={{0,2},{1,3},{2,0},{3,1},{4,6},{5,7},{6,4},{7,5},{8,10},{9,11},{10,... | collective-permute-start | bytes 638984 | tf_op jit(solution)/shard_map/ppermute | solution.py:634
  57.6 0.7 collective-permute-start.17
  58.4 1.5 %collective-permute-start.18 = (bf16[208,512]{1,0:T(8,128)(2,1)S(1)}, bf16[208,512]{1,0:T(8,128)(2,1)S(1)}, u32[]{:S(2)}, u32[]{:S(2)}) collective-permute-start(bf16[208,512]{1,0:T(8,128)(2,1)S(1)} %get-tuple-element.232), channel_id=1, source_target_pairs={{0,6},{1,7},{2,4},{3,5},{4,2},{5,3},{6,0},{7,1},{8,14},{9,15},{10,... | collective-permute-start | bytes 638984 | tf_op jit(solution)/shard_map/ppermute | solution.py:634
  59.9 0.6 collective-permute-done.15.refs_1_
  60.5 0.6 add_parts.13.refs_0_
  61.1 2.7 %collective-permute-start.22 = (bf16[96,1024]{1,0:T(8,128)(2,1)S(1)}, bf16[96,1024]{1,0:T(8,128)(2,1)S(1)}, u32[]{:S(2)}, u32[]{:S(2)}) collective-permute-start(bf16[96,1024]{1,0:T(8,128)(2,1)S(1)} %add_parts.13.refs_0_), channel_id=1, source_target_pairs={{0,16},{8,24},{16,0},{24,8},{1,17},{9,25},{17,1},{25,9},{2,18},{10... | collective-permute-start | bytes 589832 | tf_op jit(solution)/shard_map/ppermute | solution.py:634
  63.7 0.6 collective-permute-done.16.refs_1_
  64.4 3.2 %collective-permute-done.17.refs_2_ = bf16[208,512]{1,0:T(8,128)(2,1)S(1)} collective-permute-done((bf16[208,512]{1,0:T(8,128)(2,1)S(1)}, bf16[208,512]{1,0:T(8,128)(2,1)S(1)}, u32[]{:S(2)}, u32[]{:S(2)}) %collective-permute-start.17) | collective-permute-done | bytes 213024 | tf_op jit(solution)/shard_map/ppermute | solution.py:634
  67.7 0.8 add_slots.1
  68.5 1.2 %collective-permute-start.25 = (bf16[512,256]{1,0:T(8,128)(2,1)S(1)}, bf16[512,256]{1,0:T(8,128)(2,1)S(1)}, u32[]{:S(2)}, u32[]{:S(2)}) collective-permute-start(bf16[512,256]{1,0:T(8,128)(2,1)S(1)} %get-tuple-element.248), channel_id=1, source_target_pairs={{0,6},{1,7},{2,4},{3,5},{4,2},{5,3},{6,0},{7,1},{8,14},{9,15},{10,... | collective-permute-start | bytes 786440 | tf_op jit(solution)/shard_map/ppermute | solution.py:634
  69.8 1.0 collective-permute-done.22.refs_1_
  70.7 0.6 add_parts.15.mine
  71.3 0.7 collective-permute-start.23
  72.1 1.2 %collective-permute-start.20 = (bf16[512,256]{1,0:T(8,128)(2,1)S(1)}, bf16[512,256]{1,0:T(8,128)(2,1)S(1)}, u32[]{:S(2)}, u32[]{:S(2)}) collective-permute-start(bf16[512,256]{1,0:T(8,128)(2,1)S(1)} %get-tuple-element.241), channel_id=1, source_target_pairs={{0,2},{1,3},{2,0},{3,1},{4,6},{5,7},{6,4},{7,5},{8,10},{9,11},{10,... | collective-permute-start | bytes 786440 | tf_op jit(solution)/shard_map/ppermute | solution.py:634
  73.3 0.8 collective-permute-start.21
  74.1 1.4 %collective-permute-start.24 = (bf16[112,512]{1,0:T(8,128)(2,1)S(1)}, bf16[112,512]{1,0:T(8,128)(2,1)S(1)}, u32[]{:S(2)}, u32[]{:S(2)}) collective-permute-start(bf16[112,512]{1,0:T(8,128)(2,1)S(1)} %get-tuple-element.246), channel_id=1, source_target_pairs={{0,8},{8,0},{16,24},{24,16},{1,9},{9,1},{17,25},{25,17},{2,10},{10... | collective-permute-start | bytes 344072 | tf_op jit(solution)/shard_map/ppermute | solution.py:634
  75.5 2.8 %collective-permute-done.23.other = bf16[96,1024]{1,0:T(8,128)(2,1)S(1)} collective-permute-done((bf16[96,1024]{1,0:T(8,128)(2,1)S(1)}, bf16[96,1024]{1,0:T(8,128)(2,1)S(1)}, u32[]{:S(2)}, u32[]{:S(2)}) %collective-permute-start.23) | collective-permute-done | bytes 196640 | tf_op jit(solution)/shard_map/ppermute | solution.py:634
  78.3 0.6 pick.1
  79.0 0.6 collective-permute-done.24.refs_1_
  79.5 0.6 add_parts.16.refs_0_
  80.1 2.9 %collective-permute-start.26 = (bf16[112,512]{1,0:T(8,128)(2,1)S(1)}, bf16[112,512]{1,0:T(8,128)(2,1)S(1)}, u32[]{:S(2)}, u32[]{:S(2)}) collective-permute-start(bf16[112,512]{1,0:T(8,128)(2,1)S(1)} %add_parts.16.refs_0_), channel_id=1, source_target_pairs={{0,16},{8,24},{16,0},{24,8},{1,17},{9,25},{17,1},{25,9},{2,18},{10... | collective-permute-start | bytes 344072 | tf_op jit(solution)/shard_map/ppermute | solution.py:634
  83.0 0.8 collective-permute-start.28
  83.8 1.2 %collective-permute-start.27 = (bf16[96,1024]{1,0:T(8,128)(2,1)S(1)}, bf16[96,1024]{1,0:T(8,128)(2,1)S(1)}, u32[]{:S(2)}, u32[]{:S(2)}) collective-permute-start(bf16[96,1024]{1,0:T(8,128)(2,1)S(1)} %get-tuple-element.245.a), channel_id=1, source_target_pairs={{0,4},{1,5},{2,6},{3,7},{4,0},{5,1},{6,2},{7,3},{8,12},{9,13},{10,... | collective-permute-start | bytes 589832 | tf_op jit(solution)/shard_map/ppermute | solution.py:634
  85.0 1.8 %input_grad.1 = f32[256,512]{1,0:T(8,128)} custom-call(s32[4]{0:T(128)S(1)} %pad_add_fusion.ids, bf16[512,256]{1,0:T(8,128)(2,1)S(1)} %get-tuple-element.250.refs_0_, bf16[512,256]{1,0:T(8,128)(2,1)S(1)} %collective-permute-done.20.refs_1_, bf16[512,256]{1,0:T(8,128)(2,1)S(1)} %collective-permute-done.21.refs_2_, ...), custom_call_target="tpu_custom_call" | custom-call | flops 2000000 | bytes 4000 | tf_op jit(solution)/shard_map/input_grad/pallas_call | solution.py:72
  87.7 1.6 %collective-permute-start.31 = (bf16[96,512]{1,0:T(8,128)(2,1)S(1)}, bf16[96,512]{1,0:T(8,128)(2,1)S(1)}, u32[]{:S(2)}, u32[]{:S(2)}) collective-permute-start(bf16[96,512]{1,0:T(8,128)(2,1)S(1)} %slice.16.refs_0_), channel_id=1, source_target_pairs={{0,6},{1,7},{2,4},{3,5},{4,2},{5,3},{6,0},{7,1},{8,14},{9,15},{10,... | collective-permute-start | bytes 294920 | tf_op jit(solution)/shard_map/ppermute | solution.py:634
  89.3 1.2 %collective-permute-start.30 = (bf16[96,512]{1,0:T(8,128)(2,1)S(1)}, bf16[96,512]{1,0:T(8,128)(2,1)S(1)}, u32[]{:S(2)}, u32[]{:S(2)}) collective-permute-start(bf16[96,512]{1,0:T(8,128)(2,1)S(1)} %slice.16.refs_0_), channel_id=1, source_target_pairs={{0,4},{1,5},{2,6},{3,7},{4,0},{5,1},{6,2},{7,3},{8,12},{9,13},{10,... | collective-permute-start | bytes 294920 | tf_op jit(solution)/shard_map/ppermute | solution.py:634
  90.5 0.8 collective-permute-start.29
  91.3 0.6 join.1
  92.4 0.9 collective-permute-done.31.refs_3_
  93.3 1.1 collective-permute-start.35
  94.4 1.2 %collective-permute-start.34 = (bf16[192,1024]{1,0:T(8,128)(2,1)S(1)}, bf16[192,1024]{1,0:T(8,128)(2,1)S(1)}, u32[]{:S(2)}, u32[]{:S(2)}) collective-permute-start(bf16[192,1024]{1,0:T(8,128)(2,1)S(1)} %get-tuple-element.260.refs_0_), channel_id=1, source_target_pairs={{0,2},{1,3},{2,0},{3,1},{4,6},{5,7},{6,4},{7,5},{8,10},{9,11},{10,... | collective-permute-start | bytes 1179656 | tf_op jit(solution)/shard_map/ppermute | solution.py:634
  96.1 0.7 collective-permute-start.36
  96.9 1.1 %unpack_small.1 = (f32[1,512]{1,0:T(1,128)}, f32[1,512]{1,0:T(1,128)}, f32[6,32]{1,0:T(8,128)}) custom-call(s32[4]{0:T(128)S(1)} %pad_add_fusion.ids, bf16[16,512]{1,0:T(8,128)(2,1)S(1)} %slice.15.tail), custom_call_target="tpu_custom_call" | custom-call | flops 1000000 | bytes 2000 | tf_op jit(solution)/shard_map/unpack_small/pallas_call | solution.py:72
  98.0 2.5 %unpack.3 = (f32[512,1024]{1,0:T(8,128)}, f32[512,1024]{1,0:T(8,128)}, f32[1024,512]{1,0:T(8,128)}) custom-call(s32[4]{0:T(128)S(1)} %pad_add_fusion.ids, bf16[192,1024]{1,0:T(8,128)(2,1)S(1)} %get-tuple-element.260.refs_0_, bf16[192,1024]{1,0:T(8,128)(2,1)S(1)} %get-tuple-element.267.refs_1_, bf16[192,1024]{1,0:T(8,128)(2,1)S(1)} %collective-permute-done.32.refs_2_, ...), custom_call_target="tpu_custom_call" | custom-call | flops 1000 | bytes 1000 | tf_op jit(solution)/shard_map/unpack/pallas_call | solution.py:737
  100.5 3.0 %collective-permute-done.35.refs_1_ = bf16[192,1024]{1,0:T(8,128)(2,1)S(1)} collective-permute-done((bf16[192,1024]{1,0:T(8,128)(2,1)S(1)}, bf16[192,1024]{1,0:T(8,128)(2,1)S(1)}, u32[]{:S(2)}, u32[]{:S(2)}) %collective-permute-start.35) | collective-permute-done | bytes 393248 | tf_op jit(solution)/shard_map/ppermute | solution.py:634
  103.5 1.2 %collective-permute-done.34.refs_0_ = bf16[192,1024]{1,0:T(8,128)(2,1)S(1)} collective-permute-done((bf16[192,1024]{1,0:T(8,128)(2,1)S(1)}, bf16[192,1024]{1,0:T(8,128)(2,1)S(1)}, u32[]{:S(2)}, u32[]{:S(2)}) %collective-permute-start.34) | collective-permute-done | bytes 393248 | tf_op jit(solution)/shard_map/ppermute | solution.py:634
  105.3 1.1 collective-permute-done.36.refs_3_
  106.3 2.5 %unpack.4 = (f32[512,1024]{1,0:T(8,128)}, f32[512,1024]{1,0:T(8,128)}, f32[1024,512]{1,0:T(8,128)}, f32[512,384]{1,0:T(8,128)}, f32[512,384]{1,0:T(8,128)}, /*index=5*/f32[512,384]{1,0:T(8,128)}, f32[384,512]{1,0:T(8,128)}) custom-call(s32[4]{0:T(128)S(1)} %pad_add_fusion.ids, ...), custom_call_target="tpu_custom_call", output_to_operand_aliasing={{0}: (5, {}), {1}: (6, {}), {2}: (7, {})} | custom-call | flops 1000 | bytes 1000 | tf_op jit(solution)/shard_map/unpack/pallas_call | solution.py:737
  108.9 2.6 %unpack.5 = (f32[512,1024]{1,0:T(8,128)}, f32[512,1024]{1,0:T(8,128)}, f32[1024,512]{1,0:T(8,128)}, f32[512,384]{1,0:T(8,128)}, f32[512,384]{1,0:T(8,128)}, /*index=5*/f32[512,384]{1,0:T(8,128)}, f32[384,512]{1,0:T(8,128)}) custom-call(s32[4]{0:T(128)S(1)} %pad_add_fusion.ids, ...), custom_call_target="tpu_custom_call", output_to_operand_aliasing={{0}: (5, {}), {1}: (6, {}), {2}: (7, {}), {3}: (8, {}), {4}... | custom-call | flops 1000 | bytes 1000 | tf_op jit(solution)/shard_map/unpack/pallas_call | solution.py:737
  (70 shorter events, 5.3 us)
Async XLA Ops:
  0.6 6.7 %copy-start.4 = (bf16[1,256,512]{2,1,0:T(8,128)(2,1)S(1)}, bf16[1,256,512]{2,1,0:T(8,128)(2,1)}, u32[]{:S(2)}) copy-start(bf16[1,256,512]{2,1,0:T(8,128)(2,1)} %param.13) | copy-start | bytes 786436
  0.7 6.7 %copy-start.6 = (s32[1,16]{1,0:T(1,128)S(1)}, s32[1,16]{1,0:T(1,128)}, u32[]{:S(2)}) copy-start(s32[1,16]{1,0:T(1,128)} %param.24) | copy-start | bytes 196
  0.7 6.7 %copy-start.7 = (bf16[32,6]{0,1:T(8,128)(2,1)S(1)}, bf16[32,6]{0,1:T(8,128)(2,1)}, u32[]{:S(2)}) copy-start(bf16[32,6]{0,1:T(8,128)(2,1)} %param.19) | copy-start | bytes 1156
  0.7 11.1 %collective-permute-start.3 = (bf16[256,512]{1,0:T(8,128)(2,1)}, bf16[256,512]{1,0:T(8,128)(2,1)S(1)}, u32[]{:S(2)}, u32[]{:S(2)}) collective-permute-start(bf16[256,512]{1,0:T(8,128)(2,1)} %bitcast.13), channel_id=1, source_target_pairs={{0,4},{1,5},{2,6},{3,7},{4,0},{5,1},{6,2},{7,3},{8,12},{9,13},{10,... | collective-permute-start | bytes 786440 | tf_op jit(solution)/shard_map/ppermute | solution.py:634
  3.7 8.1 %collective-permute-start.1 = (bf16[256,512]{1,0:T(8,128)(2,1)}, bf16[256,512]{1,0:T(8,128)(2,1)S(1)}, u32[]{:S(2)}, u32[]{:S(2)}) collective-permute-start(bf16[256,512]{1,0:T(8,128)(2,1)} %bitcast.14), channel_id=1, source_target_pairs={{0,2},{1,3},{2,0},{3,1},{4,6},{5,7},{6,4},{7,5},{8,10},{9,11},{10,... | collective-permute-start | bytes 786440 | tf_op jit(solution)/shard_map/ppermute | solution.py:634
  5.2 3.8 %collective-permute-start = (bf16[256,512]{1,0:T(8,128)(2,1)}, bf16[256,512]{1,0:T(8,128)(2,1)S(1)}, u32[]{:S(2)}, u32[]{:S(2)}) collective-permute-start(bf16[256,512]{1,0:T(8,128)(2,1)} %bitcast.15), channel_id=1, source_target_pairs={{0,1},{1,0},{2,3},{3,2},{4,5},{5,4},{6,7},{7,6},{8,9},{9,8},{10,11... | collective-permute-start | bytes 786440 | tf_op jit(solution)/shard_map/ppermute | solution.py:634
  11.8 2.6 %collective-permute-start.2 = (bf16[256,512]{1,0:T(8,128)(2,1)S(1)}, bf16[256,512]{1,0:T(8,128)(2,1)S(1)}, u32[]{:S(2)}, u32[]{:S(2)}) collective-permute-start(bf16[256,512]{1,0:T(8,128)(2,1)S(1)} %collective-permute-done.1.refs_0_), channel_id=1, source_target_pairs={{0,1},{1,0},{2,3},{3,2},{4,5},{5,4},{6,7},{7,6},{8,9},{9,8},{10,11... | collective-permute-start | bytes 786440 | tf_op jit(solution)/shard_map/ppermute | solution.py:634
  12.4 2.0 %collective-permute-start.4 = (bf16[256,512]{1,0:T(8,128)(2,1)S(1)}, bf16[256,512]{1,0:T(8,128)(2,1)S(1)}, u32[]{:S(2)}, u32[]{:S(2)}) collective-permute-start(bf16[256,512]{1,0:T(8,128)(2,1)S(1)} %collective-permute-done.3.refs_2_), channel_id=1, source_target_pairs={{0,1},{1,0},{2,3},{3,2},{4,5},{5,4},{6,7},{7,6},{8,9},{9,8},{10,11... | collective-permute-start | bytes 786440 | tf_op jit(solution)/shard_map/ppermute | solution.py:634
  12.5 6.2 %collective-permute-start.6 = (bf16[128,512]{1,0:T(8,128)(2,1)S(1)}, bf16[128,512]{1,0:T(8,128)(2,1)S(1)}, u32[]{:S(2)}, u32[]{:S(2)}) collective-permute-start(bf16[128,512]{1,0:T(8,128)(2,1)S(1)} %slice.13), channel_id=1, source_target_pairs={{0,4},{1,5},{2,6},{3,7},{4,0},{5,1},{6,2},{7,3},{8,12},{9,13},{10,... | collective-permute-start | bytes 393224 | tf_op jit(solution)/shard_map/ppermute | solution.py:634
  13.0 6.2 %copy-start.8 = (bf16[512]{0:T(512)(128)(2,1)S(1)}, bf16[512]{0:T(512)(128)(2,1)}, u32[]{:S(2)}) copy-start(bf16[512]{0:T(512)(128)(2,1)} %param.20) | copy-start | bytes 3076
  13.1 5.6 %collective-permute-start.5 = (bf16[128,512]{1,0:T(8,128)(2,1)S(1)}, bf16[128,512]{1,0:T(8,128)(2,1)S(1)}, u32[]{:S(2)}, u32[]{:S(2)}) collective-permute-start(bf16[128,512]{1,0:T(8,128)(2,1)S(1)} %slice.12), channel_id=1, source_target_pairs={{0,2},{1,3},{2,0},{3,1},{4,6},{5,7},{6,4},{7,5},{8,10},{9,11},{10,... | collective-permute-start | bytes 393224 | tf_op jit(solution)/shard_map/ppermute | solution.py:634
  18.7 1.4 %collective-permute-start.7 = (bf16[128,512]{1,0:T(8,128)(2,1)S(1)}, bf16[128,512]{1,0:T(8,128)(2,1)S(1)}, u32[]{:S(2)}, u32[]{:S(2)}) collective-permute-start(bf16[128,512]{1,0:T(8,128)(2,1)S(1)} %collective-permute-done.5.refs_0_), channel_id=1, source_target_pairs={{0,1},{1,0},{2,3},{3,2},{4,5},{5,4},{6,7},{7,6},{8,9},{9,8},{10,11... | collective-permute-start | bytes 393224 | tf_op jit(solution)/shard_map/ppermute | solution.py:634
  18.7 1.5 %collective-permute-start.8 = (bf16[128,512]{1,0:T(8,128)(2,1)S(1)}, bf16[128,512]{1,0:T(8,128)(2,1)S(1)}, u32[]{:S(2)}, u32[]{:S(2)}) collective-permute-start(bf16[128,512]{1,0:T(8,128)(2,1)S(1)} %collective-permute-done.6.refs_1_), channel_id=1, source_target_pairs={{0,1},{1,0},{2,3},{3,2},{4,5},{5,4},{6,7},{7,6},{8,9},{9,8},{10,11... | collective-permute-start | bytes 393224 | tf_op jit(solution)/shard_map/ppermute | solution.py:634
  19.2 3.7 %copy-start = (bf16[512,1024]{1,0:T(8,128)(2,1)S(1)}, bf16[512,1024]{1,0:T(8,128)(2,1)}, u32[]{:S(2)}) copy-start(bf16[512,1024]{1,0:T(8,128)(2,1)} %wg.1) | copy-start | bytes 3145732
  19.2 3.7 %copy-start.1 = (bf16[512,1024]{1,0:T(8,128)(2,1)S(1)}, bf16[512,1024]{1,0:T(8,128)(2,1)}, u32[]{:S(2)}) copy-start(bf16[512,1024]{1,0:T(8,128)(2,1)} %wu.1) | copy-start | bytes 3145732
  19.2 3.7 %copy-start.2 = (bf16[1024,512]{1,0:T(8,128)(2,1)S(1)}, bf16[1024,512]{1,0:T(8,128)(2,1)}, u32[]{:S(2)}) copy-start(bf16[1024,512]{1,0:T(8,128)(2,1)} %wd.1) | copy-start | bytes 3145732
  19.3 3.7 %copy-start.3 = (bf16[384,512]{1,0:T(8,128)(2,1)S(1)}, bf16[384,512]{1,0:T(8,128)(2,1)}, u32[]{:S(2)}) copy-start(bf16[384,512]{1,0:T(8,128)(2,1)} %wo.1) | copy-start | bytes 1179652
  19.3 3.7 %copy-start.5 = (bf16[1,256,512]{2,1,0:T(8,128)(2,1)S(1)}, bf16[1,256,512]{2,1,0:T(8,128)(2,1)}, u32[]{:S(2)}) copy-start(bf16[1,256,512]{2,1,0:T(8,128)(2,1)} %param.25) | copy-start | bytes 786436
  28.3 3.7 %collective-permute-start.9 = (bf16[768,1024]{1,0:T(8,128)(2,1)S(1)}, bf16[768,1024]{1,0:T(8,128)(2,1)S(1)}, u32[]{:S(2)}, u32[]{:S(2)}) collective-permute-start(bf16[768,1024]{1,0:T(8,128)(2,1)S(1)} %get-tuple-element.185), channel_id=1, source_target_pairs={{0,1},{1,0},{2,3},{3,2},{4,5},{5,4},{6,7},{7,6},{8,9},{9,8},{10,11... | collective-permute-start | bytes 4718600 | tf_op jit(solution)/shard_map/ppermute | solution.py:634
  32.9 11.8 %collective-permute-start.10 = (bf16[192,1024]{1,0:T(8,128)(2,1)S(1)}, bf16[192,1024]{1,0:T(8,128)(2,1)S(1)}, u32[]{:S(2)}, u32[]{:S(2)}) collective-permute-start(bf16[192,1024]{1,0:T(8,128)(2,1)S(1)} %get-tuple-element.212), channel_id=1, source_target_pairs={{0,2},{1,3},{2,0},{3,1},{4,6},{5,7},{6,4},{7,5},{8,10},{9,11},{10,... | collective-permute-start | bytes 1179656 | tf_op jit(solution)/shard_map/ppermute | solution.py:634
  33.8 11.0 %collective-permute-start.11 = (bf16[192,1024]{1,0:T(8,128)(2,1)S(1)}, bf16[192,1024]{1,0:T(8,128)(2,1)S(1)}, u32[]{:S(2)}, u32[]{:S(2)}) collective-permute-start(bf16[192,1024]{1,0:T(8,128)(2,1)S(1)} %get-tuple-element.214), channel_id=1, source_target_pairs={{0,4},{1,5},{2,6},{3,7},{4,0},{5,1},{6,2},{7,3},{8,12},{9,13},{10,... | collective-permute-start | bytes 1179656 | tf_op jit(solution)/shard_map/ppermute | solution.py:634
  44.8 4.0 %collective-permute-start.12 = (bf16[784,512]{1,0:T(8,128)(2,1)S(1)}, bf16[784,512]{1,0:T(8,128)(2,1)S(1)}, u32[]{:S(2)}, u32[]{:S(2)}) collective-permute-start(bf16[784,512]{1,0:T(8,128)(2,1)S(1)} %get-tuple-element.219), channel_id=1, source_target_pairs={{0,1},{1,0},{2,3},{3,2},{4,5},{5,4},{6,7},{7,6},{8,9},{9,8},{10,11... | collective-permute-start | bytes 2408456 | tf_op jit(solution)/shard_map/ppermute | solution.py:634
  44.9 22.9 %collective-permute-start.19 = (bf16[4,512,256]{2,1,0:T(8,128)(2,1)S(1)}, bf16[4,512,256]{2,1,0:T(8,128)(2,1)S(1)}, u32[]{:S(2)}, u32[]{:S(2)}) collective-permute-start(bf16[4,512,256]{2,1,0:T(8,128)(2,1)S(1)} %get-tuple-element.238), channel_id=1, source_target_pairs={{0,1},{1,0},{2,3},{3,2},{4,5},{5,4},{6,7},{7,6},{8,9},{9,8},{10,11... | collective-permute-start | bytes 3145736 | tf_op jit(solution)/shard_map/ppermute | solution.py:634
  46.1 7.0 %collective-permute-start.13 = (bf16[96,1024]{1,0:T(8,128)(2,1)S(1)}, bf16[96,1024]{1,0:T(8,128)(2,1)S(1)}, u32[]{:S(2)}, u32[]{:S(2)}) collective-permute-start(bf16[96,1024]{1,0:T(8,128)(2,1)S(1)} %get-tuple-element.222), channel_id=1, source_target_pairs={{0,4},{1,5},{2,6},{3,7},{4,0},{5,1},{6,2},{7,3},{8,12},{9,13},{10,... | collective-permute-start | bytes 589832 | tf_op jit(solution)/shard_map/ppermute | solution.py:634
  47.5 6.5 %collective-permute-start.14 = (bf16[96,1024]{1,0:T(8,128)(2,1)S(1)}, bf16[96,1024]{1,0:T(8,128)(2,1)S(1)}, u32[]{:S(2)}, u32[]{:S(2)}) collective-permute-start(bf16[96,1024]{1,0:T(8,128)(2,1)S(1)} %get-tuple-element.223), channel_id=1, source_target_pairs={{0,2},{1,3},{2,0},{3,1},{4,6},{5,7},{6,4},{7,5},{8,10},{9,11},{10,... | collective-permute-start | bytes 589832 | tf_op jit(solution)/shard_map/ppermute | solution.py:634
  54.7 5.7 %collective-permute-start.15 = (bf16[96,1024]{1,0:T(8,128)(2,1)S(1)}, bf16[96,1024]{1,0:T(8,128)(2,1)S(1)}, u32[]{:S(2)}, u32[]{:S(2)}) collective-permute-start(bf16[96,1024]{1,0:T(8,128)(2,1)S(1)} %get-tuple-element.228), channel_id=1, source_target_pairs={{0,8},{8,0},{16,24},{24,16},{1,9},{9,1},{17,25},{25,17},{2,10},{10... | collective-permute-start | bytes 589832 | tf_op jit(solution)/shard_map/ppermute | solution.py:634
  56.4 8.0 %collective-permute-start.16 = (bf16[208,512]{1,0:T(8,128)(2,1)S(1)}, bf16[208,512]{1,0:T(8,128)(2,1)S(1)}, u32[]{:S(2)}, u32[]{:S(2)}) collective-permute-start(bf16[208,512]{1,0:T(8,128)(2,1)S(1)} %get-tuple-element.230), channel_id=1, source_target_pairs={{0,2},{1,3},{2,0},{3,1},{4,6},{5,7},{6,4},{7,5},{8,10},{9,11},{10,... | collective-permute-start | bytes 638984 | tf_op jit(solution)/shard_map/ppermute | solution.py:634
  57.6 10.0 %collective-permute-start.17 = (bf16[208,512]{1,0:T(8,128)(2,1)S(1)}, bf16[208,512]{1,0:T(8,128)(2,1)S(1)}, u32[]{:S(2)}, u32[]{:S(2)}) collective-permute-start(bf16[208,512]{1,0:T(8,128)(2,1)S(1)} %get-tuple-element.231), channel_id=1, source_target_pairs={{0,4},{1,5},{2,6},{3,7},{4,0},{5,1},{6,2},{7,3},{8,12},{9,13},{10,... | collective-permute-start | bytes 638984 | tf_op jit(solution)/shard_map/ppermute | solution.py:634
  58.4 9.3 %collective-permute-start.18 = (bf16[208,512]{1,0:T(8,128)(2,1)S(1)}, bf16[208,512]{1,0:T(8,128)(2,1)S(1)}, u32[]{:S(2)}, u32[]{:S(2)}) collective-permute-start(bf16[208,512]{1,0:T(8,128)(2,1)S(1)} %get-tuple-element.232), channel_id=1, source_target_pairs={{0,6},{1,7},{2,4},{3,5},{4,2},{5,3},{6,0},{7,1},{8,14},{9,15},{10,... | collective-permute-start | bytes 638984 | tf_op jit(solution)/shard_map/ppermute | solution.py:634
  61.1 9.7 %collective-permute-start.22 = (bf16[96,1024]{1,0:T(8,128)(2,1)S(1)}, bf16[96,1024]{1,0:T(8,128)(2,1)S(1)}, u32[]{:S(2)}, u32[]{:S(2)}) collective-permute-start(bf16[96,1024]{1,0:T(8,128)(2,1)S(1)} %add_parts.13.refs_0_), channel_id=1, source_target_pairs={{0,16},{8,24},{16,0},{24,8},{1,17},{9,25},{17,1},{25,9},{2,18},{10... | collective-permute-start | bytes 589832 | tf_op jit(solution)/shard_map/ppermute | solution.py:634
  68.5 15.2 %collective-permute-start.25 = (bf16[512,256]{1,0:T(8,128)(2,1)S(1)}, bf16[512,256]{1,0:T(8,128)(2,1)S(1)}, u32[]{:S(2)}, u32[]{:S(2)}) collective-permute-start(bf16[512,256]{1,0:T(8,128)(2,1)S(1)} %get-tuple-element.248), channel_id=1, source_target_pairs={{0,6},{1,7},{2,4},{3,5},{4,2},{5,3},{6,0},{7,1},{8,14},{9,15},{10,... | collective-permute-start | bytes 786440 | tf_op jit(solution)/shard_map/ppermute | solution.py:634
  71.3 7.0 %collective-permute-start.23 = (bf16[96,1024]{1,0:T(8,128)(2,1)S(1)}, bf16[96,1024]{1,0:T(8,128)(2,1)S(1)}, u32[]{:S(2)}, u32[]{:S(2)}) collective-permute-start(bf16[96,1024]{1,0:T(8,128)(2,1)S(1)} %add_parts.15.mine), channel_id=1, source_target_pairs={{0,8},{8,0},{16,24},{24,16},{1,9},{9,1},{17,25},{25,17},{2,10},{10... | collective-permute-start | bytes 589832 | tf_op jit(solution)/shard_map/ppermute | solution.py:634
  72.1 12.9 %collective-permute-start.20 = (bf16[512,256]{1,0:T(8,128)(2,1)S(1)}, bf16[512,256]{1,0:T(8,128)(2,1)S(1)}, u32[]{:S(2)}, u32[]{:S(2)}) collective-permute-start(bf16[512,256]{1,0:T(8,128)(2,1)S(1)} %get-tuple-element.241), channel_id=1, source_target_pairs={{0,2},{1,3},{2,0},{3,1},{4,6},{5,7},{6,4},{7,5},{8,10},{9,11},{10,... | collective-permute-start | bytes 786440 | tf_op jit(solution)/shard_map/ppermute | solution.py:634
  73.3 11.7 %collective-permute-start.21 = (bf16[512,256]{1,0:T(8,128)(2,1)S(1)}, bf16[512,256]{1,0:T(8,128)(2,1)S(1)}, u32[]{:S(2)}, u32[]{:S(2)}) collective-permute-start(bf16[512,256]{1,0:T(8,128)(2,1)S(1)} %get-tuple-element.242), channel_id=1, source_target_pairs={{0,4},{1,5},{2,6},{3,7},{4,0},{5,1},{6,2},{7,3},{8,12},{9,13},{10,... | collective-permute-start | bytes 786440 | tf_op jit(solution)/shard_map/ppermute | solution.py:634
  74.1 5.4 %collective-permute-start.24 = (bf16[112,512]{1,0:T(8,128)(2,1)S(1)}, bf16[112,512]{1,0:T(8,128)(2,1)S(1)}, u32[]{:S(2)}, u32[]{:S(2)}) collective-permute-start(bf16[112,512]{1,0:T(8,128)(2,1)S(1)} %get-tuple-element.246), channel_id=1, source_target_pairs={{0,8},{8,0},{16,24},{24,16},{1,9},{9,1},{17,25},{25,17},{2,10},{10... | collective-permute-start | bytes 344072 | tf_op jit(solution)/shard_map/ppermute | solution.py:634
  80.1 7.0 %collective-permute-start.26 = (bf16[112,512]{1,0:T(8,128)(2,1)S(1)}, bf16[112,512]{1,0:T(8,128)(2,1)S(1)}, u32[]{:S(2)}, u32[]{:S(2)}) collective-permute-start(bf16[112,512]{1,0:T(8,128)(2,1)S(1)} %add_parts.16.refs_0_), channel_id=1, source_target_pairs={{0,16},{8,24},{16,0},{24,8},{1,17},{9,25},{17,1},{25,9},{2,18},{10... | collective-permute-start | bytes 344072 | tf_op jit(solution)/shard_map/ppermute | solution.py:634
  83.0 8.3 %collective-permute-start.28 = (bf16[96,1024]{1,0:T(8,128)(2,1)S(1)}, bf16[96,1024]{1,0:T(8,128)(2,1)S(1)}, u32[]{:S(2)}, u32[]{:S(2)}) collective-permute-start(bf16[96,1024]{1,0:T(8,128)(2,1)S(1)} %get-tuple-element.257.c), channel_id=1, source_target_pairs={{0,2},{1,3},{2,0},{3,1},{4,6},{5,7},{6,4},{7,5},{8,10},{9,11},{10,... | collective-permute-start | bytes 589832 | tf_op jit(solution)/shard_map/ppermute | solution.py:634
  83.8 7.5 %collective-permute-start.27 = (bf16[96,1024]{1,0:T(8,128)(2,1)S(1)}, bf16[96,1024]{1,0:T(8,128)(2,1)S(1)}, u32[]{:S(2)}, u32[]{:S(2)}) collective-permute-start(bf16[96,1024]{1,0:T(8,128)(2,1)S(1)} %get-tuple-element.245.a), channel_id=1, source_target_pairs={{0,4},{1,5},{2,6},{3,7},{4,0},{5,1},{6,2},{7,3},{8,12},{9,13},{10,... | collective-permute-start | bytes 589832 | tf_op jit(solution)/shard_map/ppermute | solution.py:634
  87.7 5.6 %collective-permute-start.31 = (bf16[96,512]{1,0:T(8,128)(2,1)S(1)}, bf16[96,512]{1,0:T(8,128)(2,1)S(1)}, u32[]{:S(2)}, u32[]{:S(2)}) collective-permute-start(bf16[96,512]{1,0:T(8,128)(2,1)S(1)} %slice.16.refs_0_), channel_id=1, source_target_pairs={{0,6},{1,7},{2,4},{3,5},{4,2},{5,3},{6,0},{7,1},{8,14},{9,15},{10,... | collective-permute-start | bytes 294920 | tf_op jit(solution)/shard_map/ppermute | solution.py:634
  89.3 5.1 %collective-permute-start.30 = (bf16[96,512]{1,0:T(8,128)(2,1)S(1)}, bf16[96,512]{1,0:T(8,128)(2,1)S(1)}, u32[]{:S(2)}, u32[]{:S(2)}) collective-permute-start(bf16[96,512]{1,0:T(8,128)(2,1)S(1)} %slice.16.refs_0_), channel_id=1, source_target_pairs={{0,4},{1,5},{2,6},{3,7},{4,0},{5,1},{6,2},{7,3},{8,12},{9,13},{10,... | collective-permute-start | bytes 294920 | tf_op jit(solution)/shard_map/ppermute | solution.py:634
  90.5 5.1 %collective-permute-start.29 = (bf16[96,512]{1,0:T(8,128)(2,1)S(1)}, bf16[96,512]{1,0:T(8,128)(2,1)S(1)}, u32[]{:S(2)}, u32[]{:S(2)}) collective-permute-start(bf16[96,512]{1,0:T(8,128)(2,1)S(1)} %slice.16.refs_0_), channel_id=1, source_target_pairs={{0,2},{1,3},{2,0},{3,1},{4,6},{5,7},{6,4},{7,5},{8,10},{9,11},{10,... | collective-permute-start | bytes 294920 | tf_op jit(solution)/shard_map/ppermute | solution.py:634
  91.9 6.2 %collective-permute-start.33 = (bf16[192,1024]{1,0:T(8,128)(2,1)S(1)}, bf16[192,1024]{1,0:T(8,128)(2,1)S(1)}, u32[]{:S(2)}, u32[]{:S(2)}) collective-permute-start(bf16[192,1024]{1,0:T(8,128)(2,1)S(1)} %get-tuple-element.267.refs_1_), channel_id=1, source_target_pairs={{0,1},{1,0},{2,3},{3,2},{4,5},{5,4},{6,7},{7,6},{8,9},{9,8},{10,11... | collective-permute-start | bytes 1179656 | tf_op jit(solution)/shard_map/ppermute | solution.py:634
  91.9 6.1 %collective-permute-start.32 = (bf16[192,1024]{1,0:T(8,128)(2,1)S(1)}, bf16[192,1024]{1,0:T(8,128)(2,1)S(1)}, u32[]{:S(2)}, u32[]{:S(2)}) collective-permute-start(bf16[192,1024]{1,0:T(8,128)(2,1)S(1)} %get-tuple-element.260.refs_0_), channel_id=1, source_target_pairs={{0,1},{1,0},{2,3},{3,2},{4,5},{5,4},{6,7},{7,6},{8,9},{9,8},{10,11... | collective-permute-start | bytes 1179656 | tf_op jit(solution)/shard_map/ppermute | solution.py:634
  93.3 10.2 %collective-permute-start.35 = (bf16[192,1024]{1,0:T(8,128)(2,1)S(1)}, bf16[192,1024]{1,0:T(8,128)(2,1)S(1)}, u32[]{:S(2)}, u32[]{:S(2)}) collective-permute-start(bf16[192,1024]{1,0:T(8,128)(2,1)S(1)} %get-tuple-element.267.refs_1_), channel_id=1, source_target_pairs={{0,4},{1,5},{2,6},{3,7},{4,0},{5,1},{6,2},{7,3},{8,12},{9,13},{10,... | collective-permute-start | bytes 1179656 | tf_op jit(solution)/shard_map/ppermute | solution.py:634
  94.4 10.4 %collective-permute-start.34 = (bf16[192,1024]{1,0:T(8,128)(2,1)S(1)}, bf16[192,1024]{1,0:T(8,128)(2,1)S(1)}, u32[]{:S(2)}, u32[]{:S(2)}) collective-permute-start(bf16[192,1024]{1,0:T(8,128)(2,1)S(1)} %get-tuple-element.260.refs_0_), channel_id=1, source_target_pairs={{0,2},{1,3},{2,0},{3,1},{4,6},{5,7},{6,4},{7,5},{8,10},{9,11},{10,... | collective-permute-start | bytes 1179656 | tf_op jit(solution)/shard_map/ppermute | solution.py:634
  96.1 10.2 %collective-permute-start.36 = (bf16[384,512]{1,0:T(8,128)(2,1)S(1)}, bf16[384,512]{1,0:T(8,128)(2,1)S(1)}, u32[]{:S(2)}, u32[]{:S(2)}) collective-permute-start(bf16[384,512]{1,0:T(8,128)(2,1)S(1)} %stack.21.refs_2_), channel_id=1, source_target_pairs={{0,8},{8,0},{16,24},{24,16},{1,9},{9,1},{17,25},{25,17},{2,10},{10... | collective-permute-start | bytes 1179656 | tf_op jit(solution)/shard_map/ppermute | solution.py:634
  98.0 10.9 %collective-permute-start.39 = (bf16[384,512]{1,0:T(8,128)(2,1)S(1)}, bf16[384,512]{1,0:T(8,128)(2,1)S(1)}, u32[]{:S(2)}, u32[]{:S(2)}) collective-permute-start(bf16[384,512]{1,0:T(8,128)(2,1)S(1)} %stack.21.refs_2_), channel_id=1, source_target_pairs={{0,1},{1,0},{2,3},{3,2},{4,5},{5,4},{6,7},{7,6},{8,9},{9,8},{10,11... | collective-permute-start | bytes 1179656 | tf_op jit(solution)/shard_map/ppermute | solution.py:634
  104.8 4.1 %collective-permute-start.37 = (bf16[192,1024]{1,0:T(8,128)(2,1)S(1)}, bf16[192,1024]{1,0:T(8,128)(2,1)S(1)}, u32[]{:S(2)}, u32[]{:S(2)}) collective-permute-start(bf16[192,1024]{1,0:T(8,128)(2,1)S(1)} %collective-permute-done.34.refs_0_), channel_id=1, source_target_pairs={{0,1},{1,0},{2,3},{3,2},{4,5},{5,4},{6,7},{7,6},{8,9},{9,8},{10,11... | collective-permute-start | bytes 1179656 | tf_op jit(solution)/shard_map/ppermute | solution.py:634
  104.8 4.1 %collective-permute-start.38 = (bf16[192,1024]{1,0:T(8,128)(2,1)S(1)}, bf16[192,1024]{1,0:T(8,128)(2,1)S(1)}, u32[]{:S(2)}, u32[]{:S(2)}) collective-permute-start(bf16[192,1024]{1,0:T(8,128)(2,1)S(1)} %collective-permute-done.35.refs_1_), channel_id=1, source_target_pairs={{0,1},{1,0},{2,3},{3,2},{4,5},{5,4},{6,7},{7,6},{8,9},{9,8},{10,11... | collective-permute-start | bytes 1179656 | tf_op jit(solution)/shard_map/ppermute | solution.py:634
  106.3 2.6 %collective-permute-start.40 = (bf16[384,512]{1,0:T(8,128)(2,1)S(1)}, bf16[384,512]{1,0:T(8,128)(2,1)S(1)}, u32[]{:S(2)}, u32[]{:S(2)}) collective-permute-start(bf16[384,512]{1,0:T(8,128)(2,1)S(1)} %collective-permute-done.36.refs_3_), channel_id=1, source_target_pairs={{0,1},{1,0},{2,3},{3,2},{4,5},{5,4},{6,7},{7,6},{8,9},{9,8},{10,11... | collective-permute-start | bytes 1179656 | tf_op jit(solution)/shard_map/ppermute | solution.py:634

commit v7 on v6

--- a/solution.py
+++ b/solution.py
@@ -442,8 +442,9 @@
             later = start(k2, s2, ops[k2])
         accs[k] = finish(k, s, ops[k], d_prob, accs[k])
         d_prob = later
-        if s == len(slots) - 1:
-            bias(k, accs[k])
+        if s == 3 and k > 0:
+            bias(k - 1, accs[k - 1])
+    bias(2 * size - 1, accs[2 * size - 1])
     for g in range(size):
         dq[:, g * 128 : g * 128 + 128] = jnp.where(lower, accs[2 * g][:, :128], accs[2 * g + 1][:, :128]).astype(bf16)
 
@@ -560,23 +561,25 @@
     )
 
 
+def add_all(refs, at):
+    if len(refs) == 2:
+        return refs[0][at] + refs[1][at]
+    return sum(ref[at].astype(f32) for ref in refs).astype(bf16)
+
+
 def split_kernel(which, count, extra, ids, *refs):
     inputs, outs = refs[:-count], refs[-count:]
     rows = (inputs[0].shape[0] - extra) // count
     own = ids[which]
     for j in range(count):
         at = pl.ds(pl.multiple_of((own ^ j) * rows, 16), rows)
-        total = inputs[0][at].astype(f32)
-        for ref in inputs[1:]:
-            total = total + ref[at].astype(f32)
-        outs[j][:rows] = total.astype(bf16)
+        total = add_all(inputs, at)
+        outs[j][:rows] = total
     if extra:
         at = pl.ds(rows * count, extra)
-        total = inputs[0][at].astype(f32)
-        for ref in inputs[1:]:
-            total = total + ref[at].astype(f32)
+        total = add_all(inputs, at)
         for j in range(count):
-            outs[j][rows:] = total.astype(bf16)
+            outs[j][rows:] = total
 
 
 def add_and_split(which, count, extra, ids, *arrays):
@@ -590,7 +593,7 @@
     for half, own in ((0, ids[2] % 2), (1, ids[2] // 2)):
         for j in range(2):
             at = pl.ds(pl.multiple_of((2 * half + (own ^ j)) * rows, 16), rows)
-            outs[2 * half + j][...] = (keep[at].astype(f32) + recv[at].astype(f32)).astype(bf16)
+            outs[2 * half + j][...] = keep[at] + recv[at]
 
 
 def by_next_chip_kernel(ids, keep_x, recv_x, keep_y, recv_y, *outs):
@@ -598,7 +601,7 @@
     for half, own, a, b in ((0, ids[2] // 2, keep_x, recv_x), (1, ids[2] % 2, keep_y, recv_y)):
         for j in range(2):
             at = pl.ds(pl.multiple_of((own ^ j) * rows, 16), rows)
-            outs[2 * half + j][...] = (a[at].astype(f32) + b[at].astype(f32)).astype(bf16)
+            outs[2 * half + j][...] = a[at] + b[at]
 
 
 def by_row_kernel(ids, keep_x, recv_x, keep_y, recv_y, mine, other):

time: 112 us -> 112 us (level)
  no operation moved by 1% of the time
where the time goes in v7:
time: 112 us; the launch traced here: 111 us
  Pallas kernels  47.5 us (42%)
  starting transfers between devices  39.2 us (35%)
  waiting for transfers between devices  21.2 us (19%)
  other arithmetic  1.41 us (1%)
  between operations  1.28 us (1%)
    pallas_call x22, Pallas kernels, call(): pl.pallas_call(kernel, in_specs=[smem] * len(smem_args) + [vmem] * (len(a...  39.9 us
    ppermute x41, starting transfers between devices, swap(): return lax.ppermute(array, axis, [(i, i ^ j) for i in range(size)])  39.2 us
    ppermute x41, waiting for transfers between devices, swap(): return lax.ppermute(array, axis, [(i, i ^ j) for i in range(size)])  21.2 us
    pallas_call x3, Pallas kernels, unpack(): pl.pallas_call(kernel, in_specs=[pl.BlockSpec(memory_space=pltpu.SMEM)] +...  7.58 us
  transfers between devices with their start and end apart: 41, of which 15 were waited for; matrix products, arithmetic and copies ran while one was open for 2% of the time, Pallas kernels for 33%

profile of v7, /device:TPU:0, one launch (start us, length us, event | category | flops | bytes accessed | tf_op | source)
XLA Modules:
  0.0 111.3 jit_solution(9741364611783378478)
XLA Ops:
  0.7 3.0 %collective-permute-start.3 = (bf16[256,512]{1,0:T(8,128)(2,1)}, bf16[256,512]{1,0:T(8,128)(2,1)S(1)}, u32[]{:S(2)}, u32[]{:S(2)}) collective-permute-start(bf16[256,512]{1,0:T(8,128)(2,1)} %bitcast.13), channel_id=1, source_target_pairs={{0,4},{1,5},{2,6},{3,7},{4,0},{5,1},{6,2},{7,3},{8,12},{9,13},{10,... | collective-permute-start | bytes 786440 | tf_op jit(solution)/shard_map/ppermute | solution.py:637
  3.7 1.5 %collective-permute-start.1 = (bf16[256,512]{1,0:T(8,128)(2,1)}, bf16[256,512]{1,0:T(8,128)(2,1)S(1)}, u32[]{:S(2)}, u32[]{:S(2)}) collective-permute-start(bf16[256,512]{1,0:T(8,128)(2,1)} %bitcast.14), channel_id=1, source_target_pairs={{0,2},{1,3},{2,0},{3,1},{4,6},{5,7},{6,4},{7,5},{8,10},{9,11},{10,... | collective-permute-start | bytes 786440 | tf_op jit(solution)/shard_map/ppermute | solution.py:637
  5.2 0.7 reshape.55.gain.refs_2_.refs_4_.refs_18_.refs_7_
  6.0 1.3 %pad_maximum_fusion.w3 = bf16[512,1152]{1,0:T(8,128)(2,1)S(1)} fusion(bf16[512,384]{1,0:T(8,128)(2,1)} %param.17, bf16[512,384]{1,0:T(8,128)(2,1)} %param.16, bf16[512,384]{1,0:T(8,128)(2,1)} %param.15), kind=kLoop, calls=%fused_computation | loop fusion | flops 3538944 | bytes 2359296 | tf_op jit(solution)/shard_map/concatenate | solution.py:130
  7.3 1.6 %prepare.1 = (bf16[256,384]{1,0:T(8,128)(2,1)S(1)}, f32[256,128]{1,0:T(8,128)S(1)}, bf16[6,4,256,256]{3,2,1,0:T(8,128)(2,1)S(1)}, bf16[1152,512]{1,0:T(8,128)(2,...) custom-call(s32[4]{0:T(128)S(1)} %pad_add_fusion.ids, ...), custom_call_target="tpu_custom_call" | custom-call | flops 4000000 | bytes 8000 | tf_op jit(solution)/shard_map/prepare/pallas_call | solution.py:72
  9.0 2.8 %attend.3 = (bf16[512,512]{1,0:T(8,128)(2,1)S(1)}, bf16[512,128]{1,0:T(8,128)(2,1)S(1)}, f32[256,384]{1,0:T(8,128)S(1)}, f32[256,128]{1,0:T(8,128)S(1)}, bf16[2,...) custom-call(s32[4]{0:T(128)S(1)} %pad_add_fusion.ids, ...), custom_call_target="tpu_custom_call" | custom-call | flops 4000000 | bytes 8000 | tf_op jit(solution)/shard_map/attend/pallas_call | solution.py:72
  12.5 0.6 collective-permute-start.6
  13.1 1.3 %collective-permute-start.5 = (bf16[128,512]{1,0:T(8,128)(2,1)S(1)}, bf16[128,512]{1,0:T(8,128)(2,1)S(1)}, u32[]{:S(2)}, u32[]{:S(2)}) collective-permute-start(bf16[128,512]{1,0:T(8,128)(2,1)S(1)} %slice.12), channel_id=1, source_target_pairs={{0,2},{1,3},{2,0},{3,1},{4,6},{5,7},{6,4},{7,5},{8,10},{9,11},{10,... | collective-permute-start | bytes 393224 | tf_op jit(solution)/shard_map/ppermute | solution.py:637
  14.4 4.3 %attend.4 = (bf16[1024,512]{1,0:T(8,128)(2,1)S(1)}, bf16[1024,128]{1,0:T(8,128)(2,1)S(1)}, f32[256,384]{1,0:T(8,128)S(1)}, f32[256,128]{1,0:T(8,128)S(1)}, bf16[...) custom-call(s32[4]{0:T(128)S(1)} %pad_add_fusion.ids, ...), custom_call_target="tpu_custom_call" | custom-call | flops 8000000 | bytes 16000 | tf_op jit(solution)/shard_map/attend/pallas_call | solution.py:72
  19.3 0.8 collective-permute-done.7.refs_2_
  20.3 2.7 %attend.5 = (bf16[512,512]{1,0:T(8,128)(2,1)S(1)}, bf16[512,128]{1,0:T(8,128)(2,1)S(1)}, f32[256,384]{1,0:T(8,128)S(1)}, f32[256,128]{1,0:T(8,128)S(1)}, bf16[2,...) custom-call(s32[4]{0:T(128)S(1)} %pad_add_fusion.ids, ...), custom_call_target="tpu_custom_call" | custom-call | flops 4000000 | bytes 8000 | tf_op jit(solution)/shard_map/attend/pallas_call | solution.py:72
  23.0 5.3 %feed_forward.1 = (bf16[256,512]{1,0:T(8,128)(2,1)}, f32[256,512]{1,0:T(8,128)S(1)}, bf16[256,384]{1,0:T(8,128)(2,1)S(1)}, f32[256,128]{1,0:T(8,128)S(1)}, bf16[...) custom-call(s32[4]{0:T(128)S(1)} %pad_add_fusion.ids, ...), custom_call_target="tpu_custom_call" | custom-call | flops 8000000 | bytes 16000 | tf_op jit(solution)/shard_map/feed_forward/pallas_call | solution.py:72
  28.7 3.3 %attend_back.1 = (bf16[128,2048]{1,0:T(8,128)(2,1)S(1)}, bf16[128,2048]{1,0:T(8,128)(2,1)S(1)}, bf16[256,128]{1,0:T(8,128)(2,1)S(1)}, f32[8,1152]{1,0:T(8,128)S(1)}) custom-call(s32[4]{0:T(128)S(1)} %pad_add_fusion.ids, bf16[256,384]{1,0:T(8,128)(2,1)S(1)} %get-tuple-element.157.refs_5_.refs_7_.q.refs_0_, ...), custom_call_target="tpu_custom_call" | custom-call | flops 4000000 | bytes 8000 | tf_op jit(solution)/shard_map/attend_back/pallas_call | solution.py:72
  32.0 0.7 add_parts.9
  32.7 0.8 collective-permute-start.10
  33.5 1.5 %collective-permute-start.11 = (bf16[192,1024]{1,0:T(8,128)(2,1)S(1)}, bf16[192,1024]{1,0:T(8,128)(2,1)S(1)}, u32[]{:S(2)}, u32[]{:S(2)}) collective-permute-start(bf16[192,1024]{1,0:T(8,128)(2,1)S(1)} %get-tuple-element.214), channel_id=1, source_target_pairs={{0,4},{1,5},{2,6},{3,7},{4,0},{5,1},{6,2},{7,3},{8,12},{9,13},{10,... | collective-permute-start | bytes 1179656 | tf_op jit(solution)/shard_map/ppermute | solution.py:637
  35.1 9.4 %rest_back.1 = (bf16[4,512,256]{2,1,0:T(8,128)(2,1)S(1)}, bf16[4,512,256]{2,1,0:T(8,128)(2,1)S(1)}, f32[256,512]{1,0:T(8,128)S(1)}, bf16[784,512]{1,0:T(8,128)(2,1)S(1)}, bf16[784,512]{1,0:T(8,128)(2,1)S(1)}) custom-call(s32[4]{0:T(128)S(1)} %pad_add_fusion.ids, bf16[256,384]{1,0:T(8,128)(2,1)S(1)} %get-tuple-element.157.refs_5_.refs_7_.q.refs_0_, ...), custom_call_target="tpu_custom_call" | custom-call | flops 10000000 | bytes 20000 | tf_op jit(solution)/shard_map/rest_back/pallas_call | solution.py:72
  45.1 0.6 add_parts.10
  45.8 1.5 %collective-permute-start.13 = (bf16[96,1024]{1,0:T(8,128)(2,1)S(1)}, bf16[96,1024]{1,0:T(8,128)(2,1)S(1)}, u32[]{:S(2)}, u32[]{:S(2)}) collective-permute-start(bf16[96,1024]{1,0:T(8,128)(2,1)S(1)} %get-tuple-element.222), channel_id=1, source_target_pairs={{0,4},{1,5},{2,6},{3,7},{4,0},{5,1},{6,2},{7,3},{8,12},{9,13},{10,... | collective-permute-start | bytes 589832 | tf_op jit(solution)/shard_map/ppermute | solution.py:637
  47.2 1.2 %collective-permute-start.14 = (bf16[96,1024]{1,0:T(8,128)(2,1)S(1)}, bf16[96,1024]{1,0:T(8,128)(2,1)S(1)}, u32[]{:S(2)}, u32[]{:S(2)}) collective-permute-start(bf16[96,1024]{1,0:T(8,128)(2,1)S(1)} %get-tuple-element.223), channel_id=1, source_target_pairs={{0,2},{1,3},{2,0},{3,1},{4,6},{5,7},{6,4},{7,5},{8,10},{9,11},{10,... | collective-permute-start | bytes 589832 | tf_op jit(solution)/shard_map/ppermute | solution.py:637
  48.5 0.6 add_parts.11
  49.1 3.6 %collective-permute-done.13.recv_x = bf16[96,1024]{1,0:T(8,128)(2,1)S(1)} collective-permute-done((bf16[96,1024]{1,0:T(8,128)(2,1)S(1)}, bf16[96,1024]{1,0:T(8,128)(2,1)S(1)}, u32[]{:S(2)}, u32[]{:S(2)}) %collective-permute-start.13) | collective-permute-done | bytes 196640 | tf_op jit(solution)/shard_map/ppermute | solution.py:637
  52.7 1.0 collective-permute-done.14.recv_y
  53.8 0.7 add_parts.12
  54.4 1.6 %collective-permute-start.15 = (bf16[96,1024]{1,0:T(8,128)(2,1)S(1)}, bf16[96,1024]{1,0:T(8,128)(2,1)S(1)}, u32[]{:S(2)}, u32[]{:S(2)}) collective-permute-start(bf16[96,1024]{1,0:T(8,128)(2,1)S(1)} %get-tuple-element.228), channel_id=1, source_target_pairs={{0,8},{8,0},{16,24},{24,16},{1,9},{9,1},{17,25},{25,17},{2,10},{10... | collective-permute-start | bytes 589832 | tf_op jit(solution)/shard_map/ppermute | solution.py:637
  56.1 1.2 %collective-permute-start.16 = (bf16[208,512]{1,0:T(8,128)(2,1)S(1)}, bf16[208,512]{1,0:T(8,128)(2,1)S(1)}, u32[]{:S(2)}, u32[]{:S(2)}) collective-permute-start(bf16[208,512]{1,0:T(8,128)(2,1)S(1)} %get-tuple-element.230), channel_id=1, source_target_pairs={{0,2},{1,3},{2,0},{3,1},{4,6},{5,7},{6,4},{7,5},{8,10},{9,11},{10,... | collective-permute-start | bytes 638984 | tf_op jit(solution)/shard_map/ppermute | solution.py:637
  57.3 0.7 collective-permute-start.17
  58.0 1.6 %collective-permute-start.18 = (bf16[208,512]{1,0:T(8,128)(2,1)S(1)}, bf16[208,512]{1,0:T(8,128)(2,1)S(1)}, u32[]{:S(2)}, u32[]{:S(2)}) collective-permute-start(bf16[208,512]{1,0:T(8,128)(2,1)S(1)} %get-tuple-element.232), channel_id=1, source_target_pairs={{0,6},{1,7},{2,4},{3,5},{4,2},{5,3},{6,0},{7,1},{8,14},{9,15},{10,... | collective-permute-start | bytes 638984 | tf_op jit(solution)/shard_map/ppermute | solution.py:637
  59.6 0.6 collective-permute-done.15.refs_1_
  60.2 0.6 add_parts.13.refs_0_
  60.7 2.7 %collective-permute-start.22 = (bf16[96,1024]{1,0:T(8,128)(2,1)S(1)}, bf16[96,1024]{1,0:T(8,128)(2,1)S(1)}, u32[]{:S(2)}, u32[]{:S(2)}) collective-permute-start(bf16[96,1024]{1,0:T(8,128)(2,1)S(1)} %add_parts.13.refs_0_), channel_id=1, source_target_pairs={{0,16},{8,24},{16,0},{24,8},{1,17},{9,25},{17,1},{25,9},{2,18},{10... | collective-permute-start | bytes 589832 | tf_op jit(solution)/shard_map/ppermute | solution.py:637
  63.4 0.7 collective-permute-done.16.refs_1_
  64.1 3.2 %collective-permute-done.17.refs_2_ = bf16[208,512]{1,0:T(8,128)(2,1)S(1)} collective-permute-done((bf16[208,512]{1,0:T(8,128)(2,1)S(1)}, bf16[208,512]{1,0:T(8,128)(2,1)S(1)}, u32[]{:S(2)}, u32[]{:S(2)}) %collective-permute-start.17) | collective-permute-done | bytes 213024 | tf_op jit(solution)/shard_map/ppermute | solution.py:637
  67.4 0.8 add_slots.1
  68.2 1.2 %collective-permute-start.25 = (bf16[512,256]{1,0:T(8,128)(2,1)S(1)}, bf16[512,256]{1,0:T(8,128)(2,1)S(1)}, u32[]{:S(2)}, u32[]{:S(2)}) collective-permute-start(bf16[512,256]{1,0:T(8,128)(2,1)S(1)} %get-tuple-element.248), channel_id=1, source_target_pairs={{0,6},{1,7},{2,4},{3,5},{4,2},{5,3},{6,0},{7,1},{8,14},{9,15},{10,... | collective-permute-start | bytes 786440 | tf_op jit(solution)/shard_map/ppermute | solution.py:637
  69.5 0.9 collective-permute-done.22.refs_1_
  70.4 0.6 add_parts.15.mine
  71.0 0.7 collective-permute-start.23
  71.7 1.2 %collective-permute-start.20 = (bf16[512,256]{1,0:T(8,128)(2,1)S(1)}, bf16[512,256]{1,0:T(8,128)(2,1)S(1)}, u32[]{:S(2)}, u32[]{:S(2)}) collective-permute-start(bf16[512,256]{1,0:T(8,128)(2,1)S(1)} %get-tuple-element.241), channel_id=1, source_target_pairs={{0,2},{1,3},{2,0},{3,1},{4,6},{5,7},{6,4},{7,5},{8,10},{9,11},{10,... | collective-permute-start | bytes 786440 | tf_op jit(solution)/shard_map/ppermute | solution.py:637
  73.0 0.8 collective-permute-start.21
  73.7 1.4 %collective-permute-start.24 = (bf16[112,512]{1,0:T(8,128)(2,1)S(1)}, bf16[112,512]{1,0:T(8,128)(2,1)S(1)}, u32[]{:S(2)}, u32[]{:S(2)}) collective-permute-start(bf16[112,512]{1,0:T(8,128)(2,1)S(1)} %get-tuple-element.246), channel_id=1, source_target_pairs={{0,8},{8,0},{16,24},{24,16},{1,9},{9,1},{17,25},{25,17},{2,10},{10... | collective-permute-start | bytes 344072 | tf_op jit(solution)/shard_map/ppermute | solution.py:637
  75.1 2.9 %collective-permute-done.23.other = bf16[96,1024]{1,0:T(8,128)(2,1)S(1)} collective-permute-done((bf16[96,1024]{1,0:T(8,128)(2,1)S(1)}, bf16[96,1024]{1,0:T(8,128)(2,1)S(1)}, u32[]{:S(2)}, u32[]{:S(2)}) %collective-permute-start.23) | collective-permute-done | bytes 196640 | tf_op jit(solution)/shard_map/ppermute | solution.py:637
  77.9 0.6 pick.1
  78.6 0.6 collective-permute-done.24.refs_1_
  79.7 2.8 %collective-permute-start.26 = (bf16[112,512]{1,0:T(8,128)(2,1)S(1)}, bf16[112,512]{1,0:T(8,128)(2,1)S(1)}, u32[]{:S(2)}, u32[]{:S(2)}) collective-permute-start(bf16[112,512]{1,0:T(8,128)(2,1)S(1)} %add_parts.16.refs_0_), channel_id=1, source_target_pairs={{0,16},{8,24},{16,0},{24,8},{1,17},{9,25},{17,1},{25,9},{2,18},{10... | collective-permute-start | bytes 344072 | tf_op jit(solution)/shard_map/ppermute | solution.py:637
  82.5 0.8 collective-permute-start.28
  83.3 1.2 %collective-permute-start.27 = (bf16[96,1024]{1,0:T(8,128)(2,1)S(1)}, bf16[96,1024]{1,0:T(8,128)(2,1)S(1)}, u32[]{:S(2)}, u32[]{:S(2)}) collective-permute-start(bf16[96,1024]{1,0:T(8,128)(2,1)S(1)} %get-tuple-element.245.a), channel_id=1, source_target_pairs={{0,4},{1,5},{2,6},{3,7},{4,0},{5,1},{6,2},{7,3},{8,12},{9,13},{10,... | collective-permute-start | bytes 589832 | tf_op jit(solution)/shard_map/ppermute | solution.py:637
  84.6 1.8 %input_grad.1 = f32[256,512]{1,0:T(8,128)} custom-call(s32[4]{0:T(128)S(1)} %pad_add_fusion.ids, bf16[512,256]{1,0:T(8,128)(2,1)S(1)} %get-tuple-element.250.refs_0_, bf16[512,256]{1,0:T(8,128)(2,1)S(1)} %collective-permute-done.20.refs_1_, bf16[512,256]{1,0:T(8,128)(2,1)S(1)} %collective-permute-done.21.refs_2_, ...), custom_call_target="tpu_custom_call" | custom-call | flops 2000000 | bytes 4000 | tf_op jit(solution)/shard_map/input_grad/pallas_call | solution.py:72
  87.3 1.6 %collective-permute-start.31 = (bf16[96,512]{1,0:T(8,128)(2,1)S(1)}, bf16[96,512]{1,0:T(8,128)(2,1)S(1)}, u32[]{:S(2)}, u32[]{:S(2)}) collective-permute-start(bf16[96,512]{1,0:T(8,128)(2,1)S(1)} %slice.16.refs_0_), channel_id=1, source_target_pairs={{0,6},{1,7},{2,4},{3,5},{4,2},{5,3},{6,0},{7,1},{8,14},{9,15},{10,... | collective-permute-start | bytes 294920 | tf_op jit(solution)/shard_map/ppermute | solution.py:637
  88.9 1.2 %collective-permute-start.30 = (bf16[96,512]{1,0:T(8,128)(2,1)S(1)}, bf16[96,512]{1,0:T(8,128)(2,1)S(1)}, u32[]{:S(2)}, u32[]{:S(2)}) collective-permute-start(bf16[96,512]{1,0:T(8,128)(2,1)S(1)} %slice.16.refs_0_), channel_id=1, source_target_pairs={{0,4},{1,5},{2,6},{3,7},{4,0},{5,1},{6,2},{7,3},{8,12},{9,13},{10,... | collective-permute-start | bytes 294920 | tf_op jit(solution)/shard_map/ppermute | solution.py:637
  90.1 0.8 collective-permute-start.29
  90.9 0.6 join.1
  92.0 0.9 collective-permute-done.31.refs_3_
  92.9 1.1 collective-permute-start.35
  94.0 1.2 %collective-permute-start.34 = (bf16[192,1024]{1,0:T(8,128)(2,1)S(1)}, bf16[192,1024]{1,0:T(8,128)(2,1)S(1)}, u32[]{:S(2)}, u32[]{:S(2)}) collective-permute-start(bf16[192,1024]{1,0:T(8,128)(2,1)S(1)} %get-tuple-element.260.refs_0_), channel_id=1, source_target_pairs={{0,2},{1,3},{2,0},{3,1},{4,6},{5,7},{6,4},{7,5},{8,10},{9,11},{10,... | collective-permute-start | bytes 1179656 | tf_op jit(solution)/shard_map/ppermute | solution.py:637
  95.2 0.6 stack.21.refs_2_
  95.8 0.7 collective-permute-start.36
  96.5 1.1 %unpack_small.1 = (f32[1,512]{1,0:T(1,128)}, f32[1,512]{1,0:T(1,128)}, f32[6,32]{1,0:T(8,128)}) custom-call(s32[4]{0:T(128)S(1)} %pad_add_fusion.ids, bf16[16,512]{1,0:T(8,128)(2,1)S(1)} %slice.15.tail), custom_call_target="tpu_custom_call" | custom-call | flops 1000000 | bytes 2000 | tf_op jit(solution)/shard_map/unpack_small/pallas_call | solution.py:72
  97.6 2.5 %unpack.3 = (f32[512,1024]{1,0:T(8,128)}, f32[512,1024]{1,0:T(8,128)}, f32[1024,512]{1,0:T(8,128)}) custom-call(s32[4]{0:T(128)S(1)} %pad_add_fusion.ids, bf16[192,1024]{1,0:T(8,128)(2,1)S(1)} %get-tuple-element.260.refs_0_, bf16[192,1024]{1,0:T(8,128)(2,1)S(1)} %get-tuple-element.267.refs_1_, bf16[192,1024]{1,0:T(8,128)(2,1)S(1)} %collective-permute-done.32.refs_2_, ...), custom_call_target="tpu_custom_call" | custom-call | flops 1000 | bytes 1000 | tf_op jit(solution)/shard_map/unpack/pallas_call | solution.py:740
  100.1 3.0 %collective-permute-done.35.refs_1_ = bf16[192,1024]{1,0:T(8,128)(2,1)S(1)} collective-permute-done((bf16[192,1024]{1,0:T(8,128)(2,1)S(1)}, bf16[192,1024]{1,0:T(8,128)(2,1)S(1)}, u32[]{:S(2)}, u32[]{:S(2)}) %collective-permute-start.35) | collective-permute-done | bytes 393248 | tf_op jit(solution)/shard_map/ppermute | solution.py:637
  103.1 1.2 %collective-permute-done.34.refs_0_ = bf16[192,1024]{1,0:T(8,128)(2,1)S(1)} collective-permute-done((bf16[192,1024]{1,0:T(8,128)(2,1)S(1)}, bf16[192,1024]{1,0:T(8,128)(2,1)S(1)}, u32[]{:S(2)}, u32[]{:S(2)}) %collective-permute-start.34) | collective-permute-done | bytes 393248 | tf_op jit(solution)/shard_map/ppermute | solution.py:637
  104.9 1.1 collective-permute-done.36.refs_3_
  106.0 2.5 %unpack.4 = (f32[512,1024]{1,0:T(8,128)}, f32[512,1024]{1,0:T(8,128)}, f32[1024,512]{1,0:T(8,128)}, f32[512,384]{1,0:T(8,128)}, f32[512,384]{1,0:T(8,128)}, /*index=5*/f32[512,384]{1,0:T(8,128)}, f32[384,512]{1,0:T(8,128)}) custom-call(s32[4]{0:T(128)S(1)} %pad_add_fusion.ids, ...), custom_call_target="tpu_custom_call", output_to_operand_aliasing={{0}: (5, {}), {1}: (6, {}), {2}: (7, {})} | custom-call | flops 1000 | bytes 1000 | tf_op jit(solution)/shard_map/unpack/pallas_call | solution.py:740
  108.6 2.6 %unpack.5 = (f32[512,1024]{1,0:T(8,128)}, f32[512,1024]{1,0:T(8,128)}, f32[1024,512]{1,0:T(8,128)}, f32[512,384]{1,0:T(8,128)}, f32[512,384]{1,0:T(8,128)}, /*index=5*/f32[512,384]{1,0:T(8,128)}, f32[384,512]{1,0:T(8,128)}) custom-call(s32[4]{0:T(128)S(1)} %pad_add_fusion.ids, ...), custom_call_target="tpu_custom_call", output_to_operand_aliasing={{0}: (5, {}), {1}: (6, {}), {2}: (7, {}), {3}: (8, {}), {4}... | custom-call | flops 1000 | bytes 1000 | tf_op jit(solution)/shard_map/unpack/pallas_call | solution.py:740
  (70 shorter events, 5.2 us)
Async XLA Ops:
  0.6 6.7 %copy-start.4 = (bf16[1,256,512]{2,1,0:T(8,128)(2,1)S(1)}, bf16[1,256,512]{2,1,0:T(8,128)(2,1)}, u32[]{:S(2)}) copy-start(bf16[1,256,512]{2,1,0:T(8,128)(2,1)} %param.13) | copy-start | bytes 786436
  0.7 6.7 %copy-start.6 = (s32[1,16]{1,0:T(1,128)S(1)}, s32[1,16]{1,0:T(1,128)}, u32[]{:S(2)}) copy-start(s32[1,16]{1,0:T(1,128)} %param.24) | copy-start | bytes 196
  0.7 6.7 %copy-start.7 = (bf16[32,6]{0,1:T(8,128)(2,1)S(1)}, bf16[32,6]{0,1:T(8,128)(2,1)}, u32[]{:S(2)}) copy-start(bf16[32,6]{0,1:T(8,128)(2,1)} %param.19) | copy-start | bytes 1156
  0.7 11.1 %collective-permute-start.3 = (bf16[256,512]{1,0:T(8,128)(2,1)}, bf16[256,512]{1,0:T(8,128)(2,1)S(1)}, u32[]{:S(2)}, u32[]{:S(2)}) collective-permute-start(bf16[256,512]{1,0:T(8,128)(2,1)} %bitcast.13), channel_id=1, source_target_pairs={{0,4},{1,5},{2,6},{3,7},{4,0},{5,1},{6,2},{7,3},{8,12},{9,13},{10,... | collective-permute-start | bytes 786440 | tf_op jit(solution)/shard_map/ppermute | solution.py:637
  3.7 8.1 %collective-permute-start.1 = (bf16[256,512]{1,0:T(8,128)(2,1)}, bf16[256,512]{1,0:T(8,128)(2,1)S(1)}, u32[]{:S(2)}, u32[]{:S(2)}) collective-permute-start(bf16[256,512]{1,0:T(8,128)(2,1)} %bitcast.14), channel_id=1, source_target_pairs={{0,2},{1,3},{2,0},{3,1},{4,6},{5,7},{6,4},{7,5},{8,10},{9,11},{10,... | collective-permute-start | bytes 786440 | tf_op jit(solution)/shard_map/ppermute | solution.py:637
  5.2 3.8 %collective-permute-start = (bf16[256,512]{1,0:T(8,128)(2,1)}, bf16[256,512]{1,0:T(8,128)(2,1)S(1)}, u32[]{:S(2)}, u32[]{:S(2)}) collective-permute-start(bf16[256,512]{1,0:T(8,128)(2,1)} %bitcast.15), channel_id=1, source_target_pairs={{0,1},{1,0},{2,3},{3,2},{4,5},{5,4},{6,7},{7,6},{8,9},{9,8},{10,11... | collective-permute-start | bytes 786440 | tf_op jit(solution)/shard_map/ppermute | solution.py:637
  11.8 2.6 %collective-permute-start.2 = (bf16[256,512]{1,0:T(8,128)(2,1)S(1)}, bf16[256,512]{1,0:T(8,128)(2,1)S(1)}, u32[]{:S(2)}, u32[]{:S(2)}) collective-permute-start(bf16[256,512]{1,0:T(8,128)(2,1)S(1)} %collective-permute-done.1.refs_0_), channel_id=1, source_target_pairs={{0,1},{1,0},{2,3},{3,2},{4,5},{5,4},{6,7},{7,6},{8,9},{9,8},{10,11... | collective-permute-start | bytes 786440 | tf_op jit(solution)/shard_map/ppermute | solution.py:637
  12.4 2.0 %collective-permute-start.4 = (bf16[256,512]{1,0:T(8,128)(2,1)S(1)}, bf16[256,512]{1,0:T(8,128)(2,1)S(1)}, u32[]{:S(2)}, u32[]{:S(2)}) collective-permute-start(bf16[256,512]{1,0:T(8,128)(2,1)S(1)} %collective-permute-done.3.refs_2_), channel_id=1, source_target_pairs={{0,1},{1,0},{2,3},{3,2},{4,5},{5,4},{6,7},{7,6},{8,9},{9,8},{10,11... | collective-permute-start | bytes 786440 | tf_op jit(solution)/shard_map/ppermute | solution.py:637
  12.5 6.2 %collective-permute-start.6 = (bf16[128,512]{1,0:T(8,128)(2,1)S(1)}, bf16[128,512]{1,0:T(8,128)(2,1)S(1)}, u32[]{:S(2)}, u32[]{:S(2)}) collective-permute-start(bf16[128,512]{1,0:T(8,128)(2,1)S(1)} %slice.13), channel_id=1, source_target_pairs={{0,4},{1,5},{2,6},{3,7},{4,0},{5,1},{6,2},{7,3},{8,12},{9,13},{10,... | collective-permute-start | bytes 393224 | tf_op jit(solution)/shard_map/ppermute | solution.py:637
  13.0 6.2 %copy-start.8 = (bf16[512]{0:T(512)(128)(2,1)S(1)}, bf16[512]{0:T(512)(128)(2,1)}, u32[]{:S(2)}) copy-start(bf16[512]{0:T(512)(128)(2,1)} %param.20) | copy-start | bytes 3076
  13.1 5.6 %collective-permute-start.5 = (bf16[128,512]{1,0:T(8,128)(2,1)S(1)}, bf16[128,512]{1,0:T(8,128)(2,1)S(1)}, u32[]{:S(2)}, u32[]{:S(2)}) collective-permute-start(bf16[128,512]{1,0:T(8,128)(2,1)S(1)} %slice.12), channel_id=1, source_target_pairs={{0,2},{1,3},{2,0},{3,1},{4,6},{5,7},{6,4},{7,5},{8,10},{9,11},{10,... | collective-permute-start | bytes 393224 | tf_op jit(solution)/shard_map/ppermute | solution.py:637
  18.7 1.4 %collective-permute-start.7 = (bf16[128,512]{1,0:T(8,128)(2,1)S(1)}, bf16[128,512]{1,0:T(8,128)(2,1)S(1)}, u32[]{:S(2)}, u32[]{:S(2)}) collective-permute-start(bf16[128,512]{1,0:T(8,128)(2,1)S(1)} %collective-permute-done.5.refs_0_), channel_id=1, source_target_pairs={{0,1},{1,0},{2,3},{3,2},{4,5},{5,4},{6,7},{7,6},{8,9},{9,8},{10,11... | collective-permute-start | bytes 393224 | tf_op jit(solution)/shard_map/ppermute | solution.py:637
  18.7 1.5 %collective-permute-start.8 = (bf16[128,512]{1,0:T(8,128)(2,1)S(1)}, bf16[128,512]{1,0:T(8,128)(2,1)S(1)}, u32[]{:S(2)}, u32[]{:S(2)}) collective-permute-start(bf16[128,512]{1,0:T(8,128)(2,1)S(1)} %collective-permute-done.6.refs_1_), channel_id=1, source_target_pairs={{0,1},{1,0},{2,3},{3,2},{4,5},{5,4},{6,7},{7,6},{8,9},{9,8},{10,11... | collective-permute-start | bytes 393224 | tf_op jit(solution)/shard_map/ppermute | solution.py:637
  19.2 3.7 %copy-start = (bf16[512,1024]{1,0:T(8,128)(2,1)S(1)}, bf16[512,1024]{1,0:T(8,128)(2,1)}, u32[]{:S(2)}) copy-start(bf16[512,1024]{1,0:T(8,128)(2,1)} %wg.1) | copy-start | bytes 3145732
  19.2 3.7 %copy-start.1 = (bf16[512,1024]{1,0:T(8,128)(2,1)S(1)}, bf16[512,1024]{1,0:T(8,128)(2,1)}, u32[]{:S(2)}) copy-start(bf16[512,1024]{1,0:T(8,128)(2,1)} %wu.1) | copy-start | bytes 3145732
  19.2 3.7 %copy-start.2 = (bf16[1024,512]{1,0:T(8,128)(2,1)S(1)}, bf16[1024,512]{1,0:T(8,128)(2,1)}, u32[]{:S(2)}) copy-start(bf16[1024,512]{1,0:T(8,128)(2,1)} %wd.1) | copy-start | bytes 3145732
  19.3 3.7 %copy-start.3 = (bf16[384,512]{1,0:T(8,128)(2,1)S(1)}, bf16[384,512]{1,0:T(8,128)(2,1)}, u32[]{:S(2)}) copy-start(bf16[384,512]{1,0:T(8,128)(2,1)} %wo.1) | copy-start | bytes 1179652
  19.3 3.7 %copy-start.5 = (bf16[1,256,512]{2,1,0:T(8,128)(2,1)S(1)}, bf16[1,256,512]{2,1,0:T(8,128)(2,1)}, u32[]{:S(2)}) copy-start(bf16[1,256,512]{2,1,0:T(8,128)(2,1)} %param.25) | copy-start | bytes 786436
  28.3 3.7 %collective-permute-start.9 = (bf16[768,1024]{1,0:T(8,128)(2,1)S(1)}, bf16[768,1024]{1,0:T(8,128)(2,1)S(1)}, u32[]{:S(2)}, u32[]{:S(2)}) collective-permute-start(bf16[768,1024]{1,0:T(8,128)(2,1)S(1)} %get-tuple-element.185), channel_id=1, source_target_pairs={{0,1},{1,0},{2,3},{3,2},{4,5},{5,4},{6,7},{7,6},{8,9},{9,8},{10,11... | collective-permute-start | bytes 4718600 | tf_op jit(solution)/shard_map/ppermute | solution.py:637
  32.7 11.8 %collective-permute-start.10 = (bf16[192,1024]{1,0:T(8,128)(2,1)S(1)}, bf16[192,1024]{1,0:T(8,128)(2,1)S(1)}, u32[]{:S(2)}, u32[]{:S(2)}) collective-permute-start(bf16[192,1024]{1,0:T(8,128)(2,1)S(1)} %get-tuple-element.212), channel_id=1, source_target_pairs={{0,2},{1,3},{2,0},{3,1},{4,6},{5,7},{6,4},{7,5},{8,10},{9,11},{10,... | collective-permute-start | bytes 1179656 | tf_op jit(solution)/shard_map/ppermute | solution.py:637
  33.5 11.0 %collective-permute-start.11 = (bf16[192,1024]{1,0:T(8,128)(2,1)S(1)}, bf16[192,1024]{1,0:T(8,128)(2,1)S(1)}, u32[]{:S(2)}, u32[]{:S(2)}) collective-permute-start(bf16[192,1024]{1,0:T(8,128)(2,1)S(1)} %get-tuple-element.214), channel_id=1, source_target_pairs={{0,4},{1,5},{2,6},{3,7},{4,0},{5,1},{6,2},{7,3},{8,12},{9,13},{10,... | collective-permute-start | bytes 1179656 | tf_op jit(solution)/shard_map/ppermute | solution.py:637
  44.5 3.9 %collective-permute-start.12 = (bf16[784,512]{1,0:T(8,128)(2,1)S(1)}, bf16[784,512]{1,0:T(8,128)(2,1)S(1)}, u32[]{:S(2)}, u32[]{:S(2)}) collective-permute-start(bf16[784,512]{1,0:T(8,128)(2,1)S(1)} %get-tuple-element.219), channel_id=1, source_target_pairs={{0,1},{1,0},{2,3},{3,2},{4,5},{5,4},{6,7},{7,6},{8,9},{9,8},{10,11... | collective-permute-start | bytes 2408456 | tf_op jit(solution)/shard_map/ppermute | solution.py:637
  44.6 22.8 %collective-permute-start.19 = (bf16[4,512,256]{2,1,0:T(8,128)(2,1)S(1)}, bf16[4,512,256]{2,1,0:T(8,128)(2,1)S(1)}, u32[]{:S(2)}, u32[]{:S(2)}) collective-permute-start(bf16[4,512,256]{2,1,0:T(8,128)(2,1)S(1)} %get-tuple-element.238), channel_id=1, source_target_pairs={{0,1},{1,0},{2,3},{3,2},{4,5},{5,4},{6,7},{7,6},{8,9},{9,8},{10,11... | collective-permute-start | bytes 3145736 | tf_op jit(solution)/shard_map/ppermute | solution.py:637
  45.8 7.0 %collective-permute-start.13 = (bf16[96,1024]{1,0:T(8,128)(2,1)S(1)}, bf16[96,1024]{1,0:T(8,128)(2,1)S(1)}, u32[]{:S(2)}, u32[]{:S(2)}) collective-permute-start(bf16[96,1024]{1,0:T(8,128)(2,1)S(1)} %get-tuple-element.222), channel_id=1, source_target_pairs={{0,4},{1,5},{2,6},{3,7},{4,0},{5,1},{6,2},{7,3},{8,12},{9,13},{10,... | collective-permute-start | bytes 589832 | tf_op jit(solution)/shard_map/ppermute | solution.py:637
  47.2 6.5 %collective-permute-start.14 = (bf16[96,1024]{1,0:T(8,128)(2,1)S(1)}, bf16[96,1024]{1,0:T(8,128)(2,1)S(1)}, u32[]{:S(2)}, u32[]{:S(2)}) collective-permute-start(bf16[96,1024]{1,0:T(8,128)(2,1)S(1)} %get-tuple-element.223), channel_id=1, source_target_pairs={{0,2},{1,3},{2,0},{3,1},{4,6},{5,7},{6,4},{7,5},{8,10},{9,11},{10,... | collective-permute-start | bytes 589832 | tf_op jit(solution)/shard_map/ppermute | solution.py:637
  54.4 5.7 %collective-permute-start.15 = (bf16[96,1024]{1,0:T(8,128)(2,1)S(1)}, bf16[96,1024]{1,0:T(8,128)(2,1)S(1)}, u32[]{:S(2)}, u32[]{:S(2)}) collective-permute-start(bf16[96,1024]{1,0:T(8,128)(2,1)S(1)} %get-tuple-element.228), channel_id=1, source_target_pairs={{0,8},{8,0},{16,24},{24,16},{1,9},{9,1},{17,25},{25,17},{2,10},{10... | collective-permute-start | bytes 589832 | tf_op jit(solution)/shard_map/ppermute | solution.py:637
  56.1 8.0 %collective-permute-start.16 = (bf16[208,512]{1,0:T(8,128)(2,1)S(1)}, bf16[208,512]{1,0:T(8,128)(2,1)S(1)}, u32[]{:S(2)}, u32[]{:S(2)}) collective-permute-start(bf16[208,512]{1,0:T(8,128)(2,1)S(1)} %get-tuple-element.230), channel_id=1, source_target_pairs={{0,2},{1,3},{2,0},{3,1},{4,6},{5,7},{6,4},{7,5},{8,10},{9,11},{10,... | collective-permute-start | bytes 638984 | tf_op jit(solution)/shard_map/ppermute | solution.py:637
  57.3 10.0 %collective-permute-start.17 = (bf16[208,512]{1,0:T(8,128)(2,1)S(1)}, bf16[208,512]{1,0:T(8,128)(2,1)S(1)}, u32[]{:S(2)}, u32[]{:S(2)}) collective-permute-start(bf16[208,512]{1,0:T(8,128)(2,1)S(1)} %get-tuple-element.231), channel_id=1, source_target_pairs={{0,4},{1,5},{2,6},{3,7},{4,0},{5,1},{6,2},{7,3},{8,12},{9,13},{10,... | collective-permute-start | bytes 638984 | tf_op jit(solution)/shard_map/ppermute | solution.py:637
  58.0 9.3 %collective-permute-start.18 = (bf16[208,512]{1,0:T(8,128)(2,1)S(1)}, bf16[208,512]{1,0:T(8,128)(2,1)S(1)}, u32[]{:S(2)}, u32[]{:S(2)}) collective-permute-start(bf16[208,512]{1,0:T(8,128)(2,1)S(1)} %get-tuple-element.232), channel_id=1, source_target_pairs={{0,6},{1,7},{2,4},{3,5},{4,2},{5,3},{6,0},{7,1},{8,14},{9,15},{10,... | collective-permute-start | bytes 638984 | tf_op jit(solution)/shard_map/ppermute | solution.py:637
  60.7 9.7 %collective-permute-start.22 = (bf16[96,1024]{1,0:T(8,128)(2,1)S(1)}, bf16[96,1024]{1,0:T(8,128)(2,1)S(1)}, u32[]{:S(2)}, u32[]{:S(2)}) collective-permute-start(bf16[96,1024]{1,0:T(8,128)(2,1)S(1)} %add_parts.13.refs_0_), channel_id=1, source_target_pairs={{0,16},{8,24},{16,0},{24,8},{1,17},{9,25},{17,1},{25,9},{2,18},{10... | collective-permute-start | bytes 589832 | tf_op jit(solution)/shard_map/ppermute | solution.py:637
  68.2 15.1 %collective-permute-start.25 = (bf16[512,256]{1,0:T(8,128)(2,1)S(1)}, bf16[512,256]{1,0:T(8,128)(2,1)S(1)}, u32[]{:S(2)}, u32[]{:S(2)}) collective-permute-start(bf16[512,256]{1,0:T(8,128)(2,1)S(1)} %get-tuple-element.248), channel_id=1, source_target_pairs={{0,6},{1,7},{2,4},{3,5},{4,2},{5,3},{6,0},{7,1},{8,14},{9,15},{10,... | collective-permute-start | bytes 786440 | tf_op jit(solution)/shard_map/ppermute | solution.py:637
  71.0 7.0 %collective-permute-start.23 = (bf16[96,1024]{1,0:T(8,128)(2,1)S(1)}, bf16[96,1024]{1,0:T(8,128)(2,1)S(1)}, u32[]{:S(2)}, u32[]{:S(2)}) collective-permute-start(bf16[96,1024]{1,0:T(8,128)(2,1)S(1)} %add_parts.15.mine), channel_id=1, source_target_pairs={{0,8},{8,0},{16,24},{24,16},{1,9},{9,1},{17,25},{25,17},{2,10},{10... | collective-permute-start | bytes 589832 | tf_op jit(solution)/shard_map/ppermute | solution.py:637
  71.7 12.9 %collective-permute-start.20 = (bf16[512,256]{1,0:T(8,128)(2,1)S(1)}, bf16[512,256]{1,0:T(8,128)(2,1)S(1)}, u32[]{:S(2)}, u32[]{:S(2)}) collective-permute-start(bf16[512,256]{1,0:T(8,128)(2,1)S(1)} %get-tuple-element.241), channel_id=1, source_target_pairs={{0,2},{1,3},{2,0},{3,1},{4,6},{5,7},{6,4},{7,5},{8,10},{9,11},{10,... | collective-permute-start | bytes 786440 | tf_op jit(solution)/shard_map/ppermute | solution.py:637
  73.0 11.6 %collective-permute-start.21 = (bf16[512,256]{1,0:T(8,128)(2,1)S(1)}, bf16[512,256]{1,0:T(8,128)(2,1)S(1)}, u32[]{:S(2)}, u32[]{:S(2)}) collective-permute-start(bf16[512,256]{1,0:T(8,128)(2,1)S(1)} %get-tuple-element.242), channel_id=1, source_target_pairs={{0,4},{1,5},{2,6},{3,7},{4,0},{5,1},{6,2},{7,3},{8,12},{9,13},{10,... | collective-permute-start | bytes 786440 | tf_op jit(solution)/shard_map/ppermute | solution.py:637
  73.7 5.4 %collective-permute-start.24 = (bf16[112,512]{1,0:T(8,128)(2,1)S(1)}, bf16[112,512]{1,0:T(8,128)(2,1)S(1)}, u32[]{:S(2)}, u32[]{:S(2)}) collective-permute-start(bf16[112,512]{1,0:T(8,128)(2,1)S(1)} %get-tuple-element.246), channel_id=1, source_target_pairs={{0,8},{8,0},{16,24},{24,16},{1,9},{9,1},{17,25},{25,17},{2,10},{10... | collective-permute-start | bytes 344072 | tf_op jit(solution)/shard_map/ppermute | solution.py:637
  79.7 7.0 %collective-permute-start.26 = (bf16[112,512]{1,0:T(8,128)(2,1)S(1)}, bf16[112,512]{1,0:T(8,128)(2,1)S(1)}, u32[]{:S(2)}, u32[]{:S(2)}) collective-permute-start(bf16[112,512]{1,0:T(8,128)(2,1)S(1)} %add_parts.16.refs_0_), channel_id=1, source_target_pairs={{0,16},{8,24},{16,0},{24,8},{1,17},{9,25},{17,1},{25,9},{2,18},{10... | collective-permute-start | bytes 344072 | tf_op jit(solution)/shard_map/ppermute | solution.py:637
  82.5 8.3 %collective-permute-start.28 = (bf16[96,1024]{1,0:T(8,128)(2,1)S(1)}, bf16[96,1024]{1,0:T(8,128)(2,1)S(1)}, u32[]{:S(2)}, u32[]{:S(2)}) collective-permute-start(bf16[96,1024]{1,0:T(8,128)(2,1)S(1)} %get-tuple-element.257.c), channel_id=1, source_target_pairs={{0,2},{1,3},{2,0},{3,1},{4,6},{5,7},{6,4},{7,5},{8,10},{9,11},{10,... | collective-permute-start | bytes 589832 | tf_op jit(solution)/shard_map/ppermute | solution.py:637
  83.3 7.5 %collective-permute-start.27 = (bf16[96,1024]{1,0:T(8,128)(2,1)S(1)}, bf16[96,1024]{1,0:T(8,128)(2,1)S(1)}, u32[]{:S(2)}, u32[]{:S(2)}) collective-permute-start(bf16[96,1024]{1,0:T(8,128)(2,1)S(1)} %get-tuple-element.245.a), channel_id=1, source_target_pairs={{0,4},{1,5},{2,6},{3,7},{4,0},{5,1},{6,2},{7,3},{8,12},{9,13},{10,... | collective-permute-start | bytes 589832 | tf_op jit(solution)/shard_map/ppermute | solution.py:637
  87.3 5.6 %collective-permute-start.31 = (bf16[96,512]{1,0:T(8,128)(2,1)S(1)}, bf16[96,512]{1,0:T(8,128)(2,1)S(1)}, u32[]{:S(2)}, u32[]{:S(2)}) collective-permute-start(bf16[96,512]{1,0:T(8,128)(2,1)S(1)} %slice.16.refs_0_), channel_id=1, source_target_pairs={{0,6},{1,7},{2,4},{3,5},{4,2},{5,3},{6,0},{7,1},{8,14},{9,15},{10,... | collective-permute-start | bytes 294920 | tf_op jit(solution)/shard_map/ppermute | solution.py:637
  88.9 5.1 %collective-permute-start.30 = (bf16[96,512]{1,0:T(8,128)(2,1)S(1)}, bf16[96,512]{1,0:T(8,128)(2,1)S(1)}, u32[]{:S(2)}, u32[]{:S(2)}) collective-permute-start(bf16[96,512]{1,0:T(8,128)(2,1)S(1)} %slice.16.refs_0_), channel_id=1, source_target_pairs={{0,4},{1,5},{2,6},{3,7},{4,0},{5,1},{6,2},{7,3},{8,12},{9,13},{10,... | collective-permute-start | bytes 294920 | tf_op jit(solution)/shard_map/ppermute | solution.py:637
  90.1 5.1 %collective-permute-start.29 = (bf16[96,512]{1,0:T(8,128)(2,1)S(1)}, bf16[96,512]{1,0:T(8,128)(2,1)S(1)}, u32[]{:S(2)}, u32[]{:S(2)}) collective-permute-start(bf16[96,512]{1,0:T(8,128)(2,1)S(1)} %slice.16.refs_0_), channel_id=1, source_target_pairs={{0,2},{1,3},{2,0},{3,1},{4,6},{5,7},{6,4},{7,5},{8,10},{9,11},{10,... | collective-permute-start | bytes 294920 | tf_op jit(solution)/shard_map/ppermute | solution.py:637
  91.5 6.2 %collective-permute-start.33 = (bf16[192,1024]{1,0:T(8,128)(2,1)S(1)}, bf16[192,1024]{1,0:T(8,128)(2,1)S(1)}, u32[]{:S(2)}, u32[]{:S(2)}) collective-permute-start(bf16[192,1024]{1,0:T(8,128)(2,1)S(1)} %get-tuple-element.267.refs_1_), channel_id=1, source_target_pairs={{0,1},{1,0},{2,3},{3,2},{4,5},{5,4},{6,7},{7,6},{8,9},{9,8},{10,11... | collective-permute-start | bytes 1179656 | tf_op jit(solution)/shard_map/ppermute | solution.py:637
  91.5 6.1 %collective-permute-start.32 = (bf16[192,1024]{1,0:T(8,128)(2,1)S(1)}, bf16[192,1024]{1,0:T(8,128)(2,1)S(1)}, u32[]{:S(2)}, u32[]{:S(2)}) collective-permute-start(bf16[192,1024]{1,0:T(8,128)(2,1)S(1)} %get-tuple-element.260.refs_0_), channel_id=1, source_target_pairs={{0,1},{1,0},{2,3},{3,2},{4,5},{5,4},{6,7},{7,6},{8,9},{9,8},{10,11... | collective-permute-start | bytes 1179656 | tf_op jit(solution)/shard_map/ppermute | solution.py:637
  92.9 10.2 %collective-permute-start.35 = (bf16[192,1024]{1,0:T(8,128)(2,1)S(1)}, bf16[192,1024]{1,0:T(8,128)(2,1)S(1)}, u32[]{:S(2)}, u32[]{:S(2)}) collective-permute-start(bf16[192,1024]{1,0:T(8,128)(2,1)S(1)} %get-tuple-element.267.refs_1_), channel_id=1, source_target_pairs={{0,4},{1,5},{2,6},{3,7},{4,0},{5,1},{6,2},{7,3},{8,12},{9,13},{10,... | collective-permute-start | bytes 1179656 | tf_op jit(solution)/shard_map/ppermute | solution.py:637
  94.0 10.4 %collective-permute-start.34 = (bf16[192,1024]{1,0:T(8,128)(2,1)S(1)}, bf16[192,1024]{1,0:T(8,128)(2,1)S(1)}, u32[]{:S(2)}, u32[]{:S(2)}) collective-permute-start(bf16[192,1024]{1,0:T(8,128)(2,1)S(1)} %get-tuple-element.260.refs_0_), channel_id=1, source_target_pairs={{0,2},{1,3},{2,0},{3,1},{4,6},{5,7},{6,4},{7,5},{8,10},{9,11},{10,... | collective-permute-start | bytes 1179656 | tf_op jit(solution)/shard_map/ppermute | solution.py:637
  95.8 10.2 %collective-permute-start.36 = (bf16[384,512]{1,0:T(8,128)(2,1)S(1)}, bf16[384,512]{1,0:T(8,128)(2,1)S(1)}, u32[]{:S(2)}, u32[]{:S(2)}) collective-permute-start(bf16[384,512]{1,0:T(8,128)(2,1)S(1)} %stack.21.refs_2_), channel_id=1, source_target_pairs={{0,8},{8,0},{16,24},{24,16},{1,9},{9,1},{17,25},{25,17},{2,10},{10... | collective-permute-start | bytes 1179656 | tf_op jit(solution)/shard_map/ppermute | solution.py:637
  97.6 10.9 %collective-permute-start.39 = (bf16[384,512]{1,0:T(8,128)(2,1)S(1)}, bf16[384,512]{1,0:T(8,128)(2,1)S(1)}, u32[]{:S(2)}, u32[]{:S(2)}) collective-permute-start(bf16[384,512]{1,0:T(8,128)(2,1)S(1)} %stack.21.refs_2_), channel_id=1, source_target_pairs={{0,1},{1,0},{2,3},{3,2},{4,5},{5,4},{6,7},{7,6},{8,9},{9,8},{10,11... | collective-permute-start | bytes 1179656 | tf_op jit(solution)/shard_map/ppermute | solution.py:637
  104.4 4.2 %collective-permute-start.37 = (bf16[192,1024]{1,0:T(8,128)(2,1)S(1)}, bf16[192,1024]{1,0:T(8,128)(2,1)S(1)}, u32[]{:S(2)}, u32[]{:S(2)}) collective-permute-start(bf16[192,1024]{1,0:T(8,128)(2,1)S(1)} %collective-permute-done.34.refs_0_), channel_id=1, source_target_pairs={{0,1},{1,0},{2,3},{3,2},{4,5},{5,4},{6,7},{7,6},{8,9},{9,8},{10,11... | collective-permute-start | bytes 1179656 | tf_op jit(solution)/shard_map/ppermute | solution.py:637
  104.4 4.2 %collective-permute-start.38 = (bf16[192,1024]{1,0:T(8,128)(2,1)S(1)}, bf16[192,1024]{1,0:T(8,128)(2,1)S(1)}, u32[]{:S(2)}, u32[]{:S(2)}) collective-permute-start(bf16[192,1024]{1,0:T(8,128)(2,1)S(1)} %collective-permute-done.35.refs_1_), channel_id=1, source_target_pairs={{0,1},{1,0},{2,3},{3,2},{4,5},{5,4},{6,7},{7,6},{8,9},{9,8},{10,11... | collective-permute-start | bytes 1179656 | tf_op jit(solution)/shard_map/ppermute | solution.py:637
  106.0 2.6 %collective-permute-start.40 = (bf16[384,512]{1,0:T(8,128)(2,1)S(1)}, bf16[384,512]{1,0:T(8,128)(2,1)S(1)}, u32[]{:S(2)}, u32[]{:S(2)}) collective-permute-start(bf16[384,512]{1,0:T(8,128)(2,1)S(1)} %collective-permute-done.36.refs_3_), channel_id=1, source_target_pairs={{0,1},{1,0},{2,3},{3,2},{4,5},{5,4},{6,7},{7,6},{8,9},{9,8},{10,11... | collective-permute-start | bytes 1179656 | tf_op jit(solution)/shard_map/ppermute | solution.py:637

commit v8 on v7

--- a/solution.py
+++ b/solution.py
@@ -605,18 +605,21 @@
 
 
 def by_row_kernel(ids, keep_x, recv_x, keep_y, recv_y, mine, other):
-    first = keep_x[...].astype(f32) + recv_x[...].astype(f32)
-    second = keep_y[...].astype(f32) + recv_y[...].astype(f32)
-    even = ids[3] % 2 == 0
-    mine[...] = jnp.where(even, first, second).astype(bf16)
-    other[...] = jnp.where(even, second, first).astype(bf16)
+    for parity, first, second in ((0, mine, other), (1, other, mine)):
+
+        @pl.when(ids[3] % 2 == parity)
+        def _(first=first, second=second):
+            first[...] = keep_x[...] + recv_x[...]
+            second[...] = keep_y[...] + recv_y[...]
 
 
 def pick_kernel(ids, mine, other, first, second):
-    even = ids[3] % 2 == 0
-    a, b = mine[...].astype(f32), other[...].astype(f32)
-    first[...] = jnp.where(even, a, b).astype(bf16)
-    second[...] = jnp.where(even, b, a).astype(bf16)
+    for parity, a, b in ((0, mine, other), (1, other, mine)):
+
+        @pl.when(ids[3] % 2 == parity)
+        def _(a=a, b=b):
+            first[...] = a[...]
+            second[...] = b[...]
 
 
 def stack_kernel(ids, *refs):

time: 112 us -> 111 us (level)
  transfers between devices with their start and end apart: 41 -> 41, of which waited for: 15 -> 15; matrix products, arithmetic and copies ran while one was open for 2% -> 2% of each run, Pallas kernels for 33% -> 32%
where the time goes in v8:
time: 111 us
  Pallas kernels  47.4 us (43%)
  starting transfers between devices  39.2 us (35%)
  waiting for transfers between devices  21.2 us (19%)
  other arithmetic  1.41 us (1%)
  between operations  1.28 us (1%)
    pallas_call x22, Pallas kernels, call(): pl.pallas_call(kernel, in_specs=[smem] * len(smem_args) + [vmem] * (len(a...  39.8 us
    ppermute x41, starting transfers between devices, swap(): return lax.ppermute(array, axis, [(i, i ^ j) for i in range(size)])  39.2 us
    ppermute x41, waiting for transfers between devices, swap(): return lax.ppermute(array, axis, [(i, i ^ j) for i in range(size)])  21.2 us
    pallas_call x3, Pallas kernels, unpack(): pl.pallas_call(kernel, in_specs=[pl.BlockSpec(memory_space=pltpu.SMEM)] +...  7.58 us
  transfers between devices with their start and end apart: 41, of which 15 were waited for; matrix products, arithmetic and copies ran while one was open for 2% of the time, Pallas kernels for 32%

profile of v8, /device:TPU:0, one launch (start us, length us, event | category | flops | bytes accessed | tf_op | source)
XLA Modules:
  0.0 111.2 jit_solution(14791231950702185018)
XLA Ops:
  0.7 3.0 %collective-permute-start.3 = (bf16[256,512]{1,0:T(8,128)(2,1)}, bf16[256,512]{1,0:T(8,128)(2,1)S(1)}, u32[]{:S(2)}, u32[]{:S(2)}) collective-permute-start(bf16[256,512]{1,0:T(8,128)(2,1)} %bitcast.13), channel_id=1, source_target_pairs={{0,4},{1,5},{2,6},{3,7},{4,0},{5,1},{6,2},{7,3},{8,12},{9,13},{10,... | collective-permute-start | bytes 786440 | tf_op jit(solution)/shard_map/ppermute | solution.py:640
  3.7 1.5 %collective-permute-start.1 = (bf16[256,512]{1,0:T(8,128)(2,1)}, bf16[256,512]{1,0:T(8,128)(2,1)S(1)}, u32[]{:S(2)}, u32[]{:S(2)}) collective-permute-start(bf16[256,512]{1,0:T(8,128)(2,1)} %bitcast.14), channel_id=1, source_target_pairs={{0,2},{1,3},{2,0},{3,1},{4,6},{5,7},{6,4},{7,5},{8,10},{9,11},{10,... | collective-permute-start | bytes 786440 | tf_op jit(solution)/shard_map/ppermute | solution.py:640
  5.2 0.7 reshape.55.gain.refs_2_.refs_4_.refs_18_.refs_7_
  6.0 1.3 %pad_maximum_fusion.w3 = bf16[512,1152]{1,0:T(8,128)(2,1)S(1)} fusion(bf16[512,384]{1,0:T(8,128)(2,1)} %param.17, bf16[512,384]{1,0:T(8,128)(2,1)} %param.16, bf16[512,384]{1,0:T(8,128)(2,1)} %param.15), kind=kLoop, calls=%fused_computation | loop fusion | flops 3538944 | bytes 2359296 | tf_op jit(solution)/shard_map/concatenate | solution.py:130
  7.3 1.6 %prepare.1 = (bf16[256,384]{1,0:T(8,128)(2,1)S(1)}, f32[256,128]{1,0:T(8,128)S(1)}, bf16[6,4,256,256]{3,2,1,0:T(8,128)(2,1)S(1)}, bf16[1152,512]{1,0:T(8,128)(2,...) custom-call(s32[4]{0:T(128)S(1)} %pad_add_fusion.ids, ...), custom_call_target="tpu_custom_call" | custom-call | flops 4000000 | bytes 8000 | tf_op jit(solution)/shard_map/prepare/pallas_call | solution.py:72
  9.0 2.8 %attend.3 = (bf16[512,512]{1,0:T(8,128)(2,1)S(1)}, bf16[512,128]{1,0:T(8,128)(2,1)S(1)}, f32[256,384]{1,0:T(8,128)S(1)}, f32[256,128]{1,0:T(8,128)S(1)}, bf16[2,...) custom-call(s32[4]{0:T(128)S(1)} %pad_add_fusion.ids, ...), custom_call_target="tpu_custom_call" | custom-call | flops 4000000 | bytes 8000 | tf_op jit(solution)/shard_map/attend/pallas_call | solution.py:72
  12.5 0.6 collective-permute-start.6
  13.1 1.3 %collective-permute-start.5 = (bf16[128,512]{1,0:T(8,128)(2,1)S(1)}, bf16[128,512]{1,0:T(8,128)(2,1)S(1)}, u32[]{:S(2)}, u32[]{:S(2)}) collective-permute-start(bf16[128,512]{1,0:T(8,128)(2,1)S(1)} %slice.12), channel_id=1, source_target_pairs={{0,2},{1,3},{2,0},{3,1},{4,6},{5,7},{6,4},{7,5},{8,10},{9,11},{10,... | collective-permute-start | bytes 393224 | tf_op jit(solution)/shard_map/ppermute | solution.py:640
  14.4 4.3 %attend.4 = (bf16[1024,512]{1,0:T(8,128)(2,1)S(1)}, bf16[1024,128]{1,0:T(8,128)(2,1)S(1)}, f32[256,384]{1,0:T(8,128)S(1)}, f32[256,128]{1,0:T(8,128)S(1)}, bf16[...) custom-call(s32[4]{0:T(128)S(1)} %pad_add_fusion.ids, ...), custom_call_target="tpu_custom_call" | custom-call | flops 8000000 | bytes 16000 | tf_op jit(solution)/shard_map/attend/pallas_call | solution.py:72
  19.3 0.8 collective-permute-done.7.refs_2_
  20.3 2.7 %attend.5 = (bf16[512,512]{1,0:T(8,128)(2,1)S(1)}, bf16[512,128]{1,0:T(8,128)(2,1)S(1)}, f32[256,384]{1,0:T(8,128)S(1)}, f32[256,128]{1,0:T(8,128)S(1)}, bf16[2,...) custom-call(s32[4]{0:T(128)S(1)} %pad_add_fusion.ids, ...), custom_call_target="tpu_custom_call" | custom-call | flops 4000000 | bytes 8000 | tf_op jit(solution)/shard_map/attend/pallas_call | solution.py:72
  23.0 5.3 %feed_forward.1 = (bf16[256,512]{1,0:T(8,128)(2,1)}, f32[256,512]{1,0:T(8,128)S(1)}, bf16[256,384]{1,0:T(8,128)(2,1)S(1)}, f32[256,128]{1,0:T(8,128)S(1)}, bf16[...) custom-call(s32[4]{0:T(128)S(1)} %pad_add_fusion.ids, ...), custom_call_target="tpu_custom_call" | custom-call | flops 8000000 | bytes 16000 | tf_op jit(solution)/shard_map/feed_forward/pallas_call | solution.py:72
  28.7 3.3 %attend_back.1 = (bf16[128,2048]{1,0:T(8,128)(2,1)S(1)}, bf16[128,2048]{1,0:T(8,128)(2,1)S(1)}, bf16[256,128]{1,0:T(8,128)(2,1)S(1)}, f32[8,1152]{1,0:T(8,128)S(1)}) custom-call(s32[4]{0:T(128)S(1)} %pad_add_fusion.ids, bf16[256,384]{1,0:T(8,128)(2,1)S(1)} %get-tuple-element.157.refs_5_.refs_7_.q.refs_0_, ...), custom_call_target="tpu_custom_call" | custom-call | flops 4000000 | bytes 8000 | tf_op jit(solution)/shard_map/attend_back/pallas_call | solution.py:72
  32.0 0.7 add_parts.9
  32.7 0.8 collective-permute-start.10
  33.5 1.5 %collective-permute-start.11 = (bf16[192,1024]{1,0:T(8,128)(2,1)S(1)}, bf16[192,1024]{1,0:T(8,128)(2,1)S(1)}, u32[]{:S(2)}, u32[]{:S(2)}) collective-permute-start(bf16[192,1024]{1,0:T(8,128)(2,1)S(1)} %get-tuple-element.214), channel_id=1, source_target_pairs={{0,4},{1,5},{2,6},{3,7},{4,0},{5,1},{6,2},{7,3},{8,12},{9,13},{10,... | collective-permute-start | bytes 1179656 | tf_op jit(solution)/shard_map/ppermute | solution.py:640
  35.1 9.4 %rest_back.1 = (bf16[4,512,256]{2,1,0:T(8,128)(2,1)S(1)}, bf16[4,512,256]{2,1,0:T(8,128)(2,1)S(1)}, f32[256,512]{1,0:T(8,128)S(1)}, bf16[784,512]{1,0:T(8,128)(2,1)S(1)}, bf16[784,512]{1,0:T(8,128)(2,1)S(1)}) custom-call(s32[4]{0:T(128)S(1)} %pad_add_fusion.ids, bf16[256,384]{1,0:T(8,128)(2,1)S(1)} %get-tuple-element.157.refs_5_.refs_7_.q.refs_0_, ...), custom_call_target="tpu_custom_call" | custom-call | flops 10000000 | bytes 20000 | tf_op jit(solution)/shard_map/rest_back/pallas_call | solution.py:72
  45.1 0.6 add_parts.10
  45.8 1.5 %collective-permute-start.13 = (bf16[96,1024]{1,0:T(8,128)(2,1)S(1)}, bf16[96,1024]{1,0:T(8,128)(2,1)S(1)}, u32[]{:S(2)}, u32[]{:S(2)}) collective-permute-start(bf16[96,1024]{1,0:T(8,128)(2,1)S(1)} %get-tuple-element.222), channel_id=1, source_target_pairs={{0,4},{1,5},{2,6},{3,7},{4,0},{5,1},{6,2},{7,3},{8,12},{9,13},{10,... | collective-permute-start | bytes 589832 | tf_op jit(solution)/shard_map/ppermute | solution.py:640
  47.2 1.2 %collective-permute-start.14 = (bf16[96,1024]{1,0:T(8,128)(2,1)S(1)}, bf16[96,1024]{1,0:T(8,128)(2,1)S(1)}, u32[]{:S(2)}, u32[]{:S(2)}) collective-permute-start(bf16[96,1024]{1,0:T(8,128)(2,1)S(1)} %get-tuple-element.223), channel_id=1, source_target_pairs={{0,2},{1,3},{2,0},{3,1},{4,6},{5,7},{6,4},{7,5},{8,10},{9,11},{10,... | collective-permute-start | bytes 589832 | tf_op jit(solution)/shard_map/ppermute | solution.py:640
  48.5 0.6 add_parts.11
  49.1 3.6 %collective-permute-done.13.recv_x = bf16[96,1024]{1,0:T(8,128)(2,1)S(1)} collective-permute-done((bf16[96,1024]{1,0:T(8,128)(2,1)S(1)}, bf16[96,1024]{1,0:T(8,128)(2,1)S(1)}, u32[]{:S(2)}, u32[]{:S(2)}) %collective-permute-start.13) | collective-permute-done | bytes 196640 | tf_op jit(solution)/shard_map/ppermute | solution.py:640
  52.7 1.0 collective-permute-done.14.recv_y
  53.8 0.6 add_parts.12
  54.4 1.6 %collective-permute-start.15 = (bf16[96,1024]{1,0:T(8,128)(2,1)S(1)}, bf16[96,1024]{1,0:T(8,128)(2,1)S(1)}, u32[]{:S(2)}, u32[]{:S(2)}) collective-permute-start(bf16[96,1024]{1,0:T(8,128)(2,1)S(1)} %get-tuple-element.228), channel_id=1, source_target_pairs={{0,8},{8,0},{16,24},{24,16},{1,9},{9,1},{17,25},{25,17},{2,10},{10... | collective-permute-start | bytes 589832 | tf_op jit(solution)/shard_map/ppermute | solution.py:640
  56.0 1.2 %collective-permute-start.16 = (bf16[208,512]{1,0:T(8,128)(2,1)S(1)}, bf16[208,512]{1,0:T(8,128)(2,1)S(1)}, u32[]{:S(2)}, u32[]{:S(2)}) collective-permute-start(bf16[208,512]{1,0:T(8,128)(2,1)S(1)} %get-tuple-element.230), channel_id=1, source_target_pairs={{0,2},{1,3},{2,0},{3,1},{4,6},{5,7},{6,4},{7,5},{8,10},{9,11},{10,... | collective-permute-start | bytes 638984 | tf_op jit(solution)/shard_map/ppermute | solution.py:640
  57.3 0.7 collective-permute-start.17
  57.9 1.6 %collective-permute-start.18 = (bf16[208,512]{1,0:T(8,128)(2,1)S(1)}, bf16[208,512]{1,0:T(8,128)(2,1)S(1)}, u32[]{:S(2)}, u32[]{:S(2)}) collective-permute-start(bf16[208,512]{1,0:T(8,128)(2,1)S(1)} %get-tuple-element.232), channel_id=1, source_target_pairs={{0,6},{1,7},{2,4},{3,5},{4,2},{5,3},{6,0},{7,1},{8,14},{9,15},{10,... | collective-permute-start | bytes 638984 | tf_op jit(solution)/shard_map/ppermute | solution.py:640
  59.5 0.6 collective-permute-done.15.refs_1_
  60.1 0.6 add_parts.13.refs_0_
  60.7 2.7 %collective-permute-start.22 = (bf16[96,1024]{1,0:T(8,128)(2,1)S(1)}, bf16[96,1024]{1,0:T(8,128)(2,1)S(1)}, u32[]{:S(2)}, u32[]{:S(2)}) collective-permute-start(bf16[96,1024]{1,0:T(8,128)(2,1)S(1)} %add_parts.13.refs_0_), channel_id=1, source_target_pairs={{0,16},{8,24},{16,0},{24,8},{1,17},{9,25},{17,1},{25,9},{2,18},{10... | collective-permute-start | bytes 589832 | tf_op jit(solution)/shard_map/ppermute | solution.py:640
  63.3 0.7 collective-permute-done.16.refs_1_
  64.0 3.2 %collective-permute-done.17.refs_2_ = bf16[208,512]{1,0:T(8,128)(2,1)S(1)} collective-permute-done((bf16[208,512]{1,0:T(8,128)(2,1)S(1)}, bf16[208,512]{1,0:T(8,128)(2,1)S(1)}, u32[]{:S(2)}, u32[]{:S(2)}) %collective-permute-start.17) | collective-permute-done | bytes 213024 | tf_op jit(solution)/shard_map/ppermute | solution.py:640
  67.4 0.8 add_slots.1
  68.2 1.2 %collective-permute-start.25 = (bf16[512,256]{1,0:T(8,128)(2,1)S(1)}, bf16[512,256]{1,0:T(8,128)(2,1)S(1)}, u32[]{:S(2)}, u32[]{:S(2)}) collective-permute-start(bf16[512,256]{1,0:T(8,128)(2,1)S(1)} %get-tuple-element.248), channel_id=1, source_target_pairs={{0,6},{1,7},{2,4},{3,5},{4,2},{5,3},{6,0},{7,1},{8,14},{9,15},{10,... | collective-permute-start | bytes 786440 | tf_op jit(solution)/shard_map/ppermute | solution.py:640
  69.4 0.9 collective-permute-done.22.refs_1_
  70.3 0.6 add_parts.15.mine
  70.9 0.7 collective-permute-start.23
  71.7 1.2 %collective-permute-start.20 = (bf16[512,256]{1,0:T(8,128)(2,1)S(1)}, bf16[512,256]{1,0:T(8,128)(2,1)S(1)}, u32[]{:S(2)}, u32[]{:S(2)}) collective-permute-start(bf16[512,256]{1,0:T(8,128)(2,1)S(1)} %get-tuple-element.241), channel_id=1, source_target_pairs={{0,2},{1,3},{2,0},{3,1},{4,6},{5,7},{6,4},{7,5},{8,10},{9,11},{10,... | collective-permute-start | bytes 786440 | tf_op jit(solution)/shard_map/ppermute | solution.py:640
  72.9 0.8 collective-permute-start.21
  73.7 1.4 %collective-permute-start.24 = (bf16[112,512]{1,0:T(8,128)(2,1)S(1)}, bf16[112,512]{1,0:T(8,128)(2,1)S(1)}, u32[]{:S(2)}, u32[]{:S(2)}) collective-permute-start(bf16[112,512]{1,0:T(8,128)(2,1)S(1)} %get-tuple-element.246), channel_id=1, source_target_pairs={{0,8},{8,0},{16,24},{24,16},{1,9},{9,1},{17,25},{25,17},{2,10},{10... | collective-permute-start | bytes 344072 | tf_op jit(solution)/shard_map/ppermute | solution.py:640
  75.0 2.9 %collective-permute-done.23.other = bf16[96,1024]{1,0:T(8,128)(2,1)S(1)} collective-permute-done((bf16[96,1024]{1,0:T(8,128)(2,1)S(1)}, bf16[96,1024]{1,0:T(8,128)(2,1)S(1)}, u32[]{:S(2)}, u32[]{:S(2)}) %collective-permute-start.23) | collective-permute-done | bytes 196640 | tf_op jit(solution)/shard_map/ppermute | solution.py:640
  77.9 0.6 pick.1
  78.5 0.6 collective-permute-done.24.refs_1_
  79.7 2.8 %collective-permute-start.26 = (bf16[112,512]{1,0:T(8,128)(2,1)S(1)}, bf16[112,512]{1,0:T(8,128)(2,1)S(1)}, u32[]{:S(2)}, u32[]{:S(2)}) collective-permute-start(bf16[112,512]{1,0:T(8,128)(2,1)S(1)} %add_parts.16.refs_0_), channel_id=1, source_target_pairs={{0,16},{8,24},{16,0},{24,8},{1,17},{9,25},{17,1},{25,9},{2,18},{10... | collective-permute-start | bytes 344072 | tf_op jit(solution)/shard_map/ppermute | solution.py:640
  82.5 0.8 collective-permute-start.28
  83.3 1.2 %collective-permute-start.27 = (bf16[96,1024]{1,0:T(8,128)(2,1)S(1)}, bf16[96,1024]{1,0:T(8,128)(2,1)S(1)}, u32[]{:S(2)}, u32[]{:S(2)}) collective-permute-start(bf16[96,1024]{1,0:T(8,128)(2,1)S(1)} %get-tuple-element.245.a), channel_id=1, source_target_pairs={{0,4},{1,5},{2,6},{3,7},{4,0},{5,1},{6,2},{7,3},{8,12},{9,13},{10,... | collective-permute-start | bytes 589832 | tf_op jit(solution)/shard_map/ppermute | solution.py:640
  84.5 1.8 %input_grad.1 = f32[256,512]{1,0:T(8,128)} custom-call(s32[4]{0:T(128)S(1)} %pad_add_fusion.ids, bf16[512,256]{1,0:T(8,128)(2,1)S(1)} %get-tuple-element.250.refs_0_, bf16[512,256]{1,0:T(8,128)(2,1)S(1)} %collective-permute-done.20.refs_1_, bf16[512,256]{1,0:T(8,128)(2,1)S(1)} %collective-permute-done.21.refs_2_, ...), custom_call_target="tpu_custom_call" | custom-call | flops 2000000 | bytes 4000 | tf_op jit(solution)/shard_map/input_grad/pallas_call | solution.py:72
  87.2 1.6 %collective-permute-start.31 = (bf16[96,512]{1,0:T(8,128)(2,1)S(1)}, bf16[96,512]{1,0:T(8,128)(2,1)S(1)}, u32[]{:S(2)}, u32[]{:S(2)}) collective-permute-start(bf16[96,512]{1,0:T(8,128)(2,1)S(1)} %slice.16.refs_0_), channel_id=1, source_target_pairs={{0,6},{1,7},{2,4},{3,5},{4,2},{5,3},{6,0},{7,1},{8,14},{9,15},{10,... | collective-permute-start | bytes 294920 | tf_op jit(solution)/shard_map/ppermute | solution.py:640
  88.8 1.2 %collective-permute-start.30 = (bf16[96,512]{1,0:T(8,128)(2,1)S(1)}, bf16[96,512]{1,0:T(8,128)(2,1)S(1)}, u32[]{:S(2)}, u32[]{:S(2)}) collective-permute-start(bf16[96,512]{1,0:T(8,128)(2,1)S(1)} %slice.16.refs_0_), channel_id=1, source_target_pairs={{0,4},{1,5},{2,6},{3,7},{4,0},{5,1},{6,2},{7,3},{8,12},{9,13},{10,... | collective-permute-start | bytes 294920 | tf_op jit(solution)/shard_map/ppermute | solution.py:640
  90.0 0.8 collective-permute-start.29
  90.8 0.6 join.1
  92.0 0.9 collective-permute-done.31.refs_3_
  92.9 1.1 collective-permute-start.35
  93.9 1.2 %collective-permute-start.34 = (bf16[192,1024]{1,0:T(8,128)(2,1)S(1)}, bf16[192,1024]{1,0:T(8,128)(2,1)S(1)}, u32[]{:S(2)}, u32[]{:S(2)}) collective-permute-start(bf16[192,1024]{1,0:T(8,128)(2,1)S(1)} %get-tuple-element.260.refs_0_), channel_id=1, source_target_pairs={{0,2},{1,3},{2,0},{3,1},{4,6},{5,7},{6,4},{7,5},{8,10},{9,11},{10,... | collective-permute-start | bytes 1179656 | tf_op jit(solution)/shard_map/ppermute | solution.py:640
  95.1 0.6 stack.21.refs_2_
  95.7 0.7 collective-permute-start.36
  96.4 1.1 %unpack_small.1 = (f32[1,512]{1,0:T(1,128)}, f32[1,512]{1,0:T(1,128)}, f32[6,32]{1,0:T(8,128)}) custom-call(s32[4]{0:T(128)S(1)} %pad_add_fusion.ids, bf16[16,512]{1,0:T(8,128)(2,1)S(1)} %slice.15.tail), custom_call_target="tpu_custom_call" | custom-call | flops 1000000 | bytes 2000 | tf_op jit(solution)/shard_map/unpack_small/pallas_call | solution.py:72
  97.6 2.5 %unpack.3 = (f32[512,1024]{1,0:T(8,128)}, f32[512,1024]{1,0:T(8,128)}, f32[1024,512]{1,0:T(8,128)}) custom-call(s32[4]{0:T(128)S(1)} %pad_add_fusion.ids, bf16[192,1024]{1,0:T(8,128)(2,1)S(1)} %get-tuple-element.260.refs_0_, bf16[192,1024]{1,0:T(8,128)(2,1)S(1)} %get-tuple-element.267.refs_1_, bf16[192,1024]{1,0:T(8,128)(2,1)S(1)} %collective-permute-done.32.refs_2_, ...), custom_call_target="tpu_custom_call" | custom-call | flops 1000 | bytes 1000 | tf_op jit(solution)/shard_map/unpack/pallas_call | solution.py:743
  100.1 3.0 %collective-permute-done.35.refs_1_ = bf16[192,1024]{1,0:T(8,128)(2,1)S(1)} collective-permute-done((bf16[192,1024]{1,0:T(8,128)(2,1)S(1)}, bf16[192,1024]{1,0:T(8,128)(2,1)S(1)}, u32[]{:S(2)}, u32[]{:S(2)}) %collective-permute-start.35) | collective-permute-done | bytes 393248 | tf_op jit(solution)/shard_map/ppermute | solution.py:640
  103.1 1.2 %collective-permute-done.34.refs_0_ = bf16[192,1024]{1,0:T(8,128)(2,1)S(1)} collective-permute-done((bf16[192,1024]{1,0:T(8,128)(2,1)S(1)}, bf16[192,1024]{1,0:T(8,128)(2,1)S(1)}, u32[]{:S(2)}, u32[]{:S(2)}) %collective-permute-start.34) | collective-permute-done | bytes 393248 | tf_op jit(solution)/shard_map/ppermute | solution.py:640
  104.8 1.1 collective-permute-done.36.refs_3_
  105.9 2.5 %unpack.4 = (f32[512,1024]{1,0:T(8,128)}, f32[512,1024]{1,0:T(8,128)}, f32[1024,512]{1,0:T(8,128)}, f32[512,384]{1,0:T(8,128)}, f32[512,384]{1,0:T(8,128)}, /*index=5*/f32[512,384]{1,0:T(8,128)}, f32[384,512]{1,0:T(8,128)}) custom-call(s32[4]{0:T(128)S(1)} %pad_add_fusion.ids, ...), custom_call_target="tpu_custom_call", output_to_operand_aliasing={{0}: (5, {}), {1}: (6, {}), {2}: (7, {})} | custom-call | flops 1000 | bytes 1000 | tf_op jit(solution)/shard_map/unpack/pallas_call | solution.py:743
  108.5 2.6 %unpack.5 = (f32[512,1024]{1,0:T(8,128)}, f32[512,1024]{1,0:T(8,128)}, f32[1024,512]{1,0:T(8,128)}, f32[512,384]{1,0:T(8,128)}, f32[512,384]{1,0:T(8,128)}, /*index=5*/f32[512,384]{1,0:T(8,128)}, f32[384,512]{1,0:T(8,128)}) custom-call(s32[4]{0:T(128)S(1)} %pad_add_fusion.ids, ...), custom_call_target="tpu_custom_call", output_to_operand_aliasing={{0}: (5, {}), {1}: (6, {}), {2}: (7, {}), {3}: (8, {}), {4}... | custom-call | flops 1000 | bytes 1000 | tf_op jit(solution)/shard_map/unpack/pallas_call | solution.py:743
  (70 shorter events, 5.2 us)
Async XLA Ops:
  0.6 6.7 %copy-start.4 = (bf16[1,256,512]{2,1,0:T(8,128)(2,1)S(1)}, bf16[1,256,512]{2,1,0:T(8,128)(2,1)}, u32[]{:S(2)}) copy-start(bf16[1,256,512]{2,1,0:T(8,128)(2,1)} %param.13) | copy-start | bytes 786436
  0.7 6.7 %copy-start.6 = (s32[1,16]{1,0:T(1,128)S(1)}, s32[1,16]{1,0:T(1,128)}, u32[]{:S(2)}) copy-start(s32[1,16]{1,0:T(1,128)} %param.24) | copy-start | bytes 196
  0.7 6.7 %copy-start.7 = (bf16[32,6]{0,1:T(8,128)(2,1)S(1)}, bf16[32,6]{0,1:T(8,128)(2,1)}, u32[]{:S(2)}) copy-start(bf16[32,6]{0,1:T(8,128)(2,1)} %param.19) | copy-start | bytes 1156
  0.7 11.1 %collective-permute-start.3 = (bf16[256,512]{1,0:T(8,128)(2,1)}, bf16[256,512]{1,0:T(8,128)(2,1)S(1)}, u32[]{:S(2)}, u32[]{:S(2)}) collective-permute-start(bf16[256,512]{1,0:T(8,128)(2,1)} %bitcast.13), channel_id=1, source_target_pairs={{0,4},{1,5},{2,6},{3,7},{4,0},{5,1},{6,2},{7,3},{8,12},{9,13},{10,... | collective-permute-start | bytes 786440 | tf_op jit(solution)/shard_map/ppermute | solution.py:640
  3.7 8.1 %collective-permute-start.1 = (bf16[256,512]{1,0:T(8,128)(2,1)}, bf16[256,512]{1,0:T(8,128)(2,1)S(1)}, u32[]{:S(2)}, u32[]{:S(2)}) collective-permute-start(bf16[256,512]{1,0:T(8,128)(2,1)} %bitcast.14), channel_id=1, source_target_pairs={{0,2},{1,3},{2,0},{3,1},{4,6},{5,7},{6,4},{7,5},{8,10},{9,11},{10,... | collective-permute-start | bytes 786440 | tf_op jit(solution)/shard_map/ppermute | solution.py:640
  5.2 3.8 %collective-permute-start = (bf16[256,512]{1,0:T(8,128)(2,1)}, bf16[256,512]{1,0:T(8,128)(2,1)S(1)}, u32[]{:S(2)}, u32[]{:S(2)}) collective-permute-start(bf16[256,512]{1,0:T(8,128)(2,1)} %bitcast.15), channel_id=1, source_target_pairs={{0,1},{1,0},{2,3},{3,2},{4,5},{5,4},{6,7},{7,6},{8,9},{9,8},{10,11... | collective-permute-start | bytes 786440 | tf_op jit(solution)/shard_map/ppermute | solution.py:640
  11.8 2.6 %collective-permute-start.2 = (bf16[256,512]{1,0:T(8,128)(2,1)S(1)}, bf16[256,512]{1,0:T(8,128)(2,1)S(1)}, u32[]{:S(2)}, u32[]{:S(2)}) collective-permute-start(bf16[256,512]{1,0:T(8,128)(2,1)S(1)} %collective-permute-done.1.refs_0_), channel_id=1, source_target_pairs={{0,1},{1,0},{2,3},{3,2},{4,5},{5,4},{6,7},{7,6},{8,9},{9,8},{10,11... | collective-permute-start | bytes 786440 | tf_op jit(solution)/shard_map/ppermute | solution.py:640
  12.4 2.0 %collective-permute-start.4 = (bf16[256,512]{1,0:T(8,128)(2,1)S(1)}, bf16[256,512]{1,0:T(8,128)(2,1)S(1)}, u32[]{:S(2)}, u32[]{:S(2)}) collective-permute-start(bf16[256,512]{1,0:T(8,128)(2,1)S(1)} %collective-permute-done.3.refs_2_), channel_id=1, source_target_pairs={{0,1},{1,0},{2,3},{3,2},{4,5},{5,4},{6,7},{7,6},{8,9},{9,8},{10,11... | collective-permute-start | bytes 786440 | tf_op jit(solution)/shard_map/ppermute | solution.py:640
  12.5 6.2 %collective-permute-start.6 = (bf16[128,512]{1,0:T(8,128)(2,1)S(1)}, bf16[128,512]{1,0:T(8,128)(2,1)S(1)}, u32[]{:S(2)}, u32[]{:S(2)}) collective-permute-start(bf16[128,512]{1,0:T(8,128)(2,1)S(1)} %slice.13), channel_id=1, source_target_pairs={{0,4},{1,5},{2,6},{3,7},{4,0},{5,1},{6,2},{7,3},{8,12},{9,13},{10,... | collective-permute-start | bytes 393224 | tf_op jit(solution)/shard_map/ppermute | solution.py:640
  13.0 6.2 %copy-start.8 = (bf16[512]{0:T(512)(128)(2,1)S(1)}, bf16[512]{0:T(512)(128)(2,1)}, u32[]{:S(2)}) copy-start(bf16[512]{0:T(512)(128)(2,1)} %param.20) | copy-start | bytes 3076
  13.1 5.6 %collective-permute-start.5 = (bf16[128,512]{1,0:T(8,128)(2,1)S(1)}, bf16[128,512]{1,0:T(8,128)(2,1)S(1)}, u32[]{:S(2)}, u32[]{:S(2)}) collective-permute-start(bf16[128,512]{1,0:T(8,128)(2,1)S(1)} %slice.12), channel_id=1, source_target_pairs={{0,2},{1,3},{2,0},{3,1},{4,6},{5,7},{6,4},{7,5},{8,10},{9,11},{10,... | collective-permute-start | bytes 393224 | tf_op jit(solution)/shard_map/ppermute | solution.py:640
  18.7 1.4 %collective-permute-start.7 = (bf16[128,512]{1,0:T(8,128)(2,1)S(1)}, bf16[128,512]{1,0:T(8,128)(2,1)S(1)}, u32[]{:S(2)}, u32[]{:S(2)}) collective-permute-start(bf16[128,512]{1,0:T(8,128)(2,1)S(1)} %collective-permute-done.5.refs_0_), channel_id=1, source_target_pairs={{0,1},{1,0},{2,3},{3,2},{4,5},{5,4},{6,7},{7,6},{8,9},{9,8},{10,11... | collective-permute-start | bytes 393224 | tf_op jit(solution)/shard_map/ppermute | solution.py:640
  18.7 1.5 %collective-permute-start.8 = (bf16[128,512]{1,0:T(8,128)(2,1)S(1)}, bf16[128,512]{1,0:T(8,128)(2,1)S(1)}, u32[]{:S(2)}, u32[]{:S(2)}) collective-permute-start(bf16[128,512]{1,0:T(8,128)(2,1)S(1)} %collective-permute-done.6.refs_1_), channel_id=1, source_target_pairs={{0,1},{1,0},{2,3},{3,2},{4,5},{5,4},{6,7},{7,6},{8,9},{9,8},{10,11... | collective-permute-start | bytes 393224 | tf_op jit(solution)/shard_map/ppermute | solution.py:640
  19.2 3.7 %copy-start = (bf16[512,1024]{1,0:T(8,128)(2,1)S(1)}, bf16[512,1024]{1,0:T(8,128)(2,1)}, u32[]{:S(2)}) copy-start(bf16[512,1024]{1,0:T(8,128)(2,1)} %wg.1) | copy-start | bytes 3145732
  19.2 3.7 %copy-start.1 = (bf16[512,1024]{1,0:T(8,128)(2,1)S(1)}, bf16[512,1024]{1,0:T(8,128)(2,1)}, u32[]{:S(2)}) copy-start(bf16[512,1024]{1,0:T(8,128)(2,1)} %wu.1) | copy-start | bytes 3145732
  19.2 3.7 %copy-start.2 = (bf16[1024,512]{1,0:T(8,128)(2,1)S(1)}, bf16[1024,512]{1,0:T(8,128)(2,1)}, u32[]{:S(2)}) copy-start(bf16[1024,512]{1,0:T(8,128)(2,1)} %wd.1) | copy-start | bytes 3145732
  19.3 3.7 %copy-start.3 = (bf16[384,512]{1,0:T(8,128)(2,1)S(1)}, bf16[384,512]{1,0:T(8,128)(2,1)}, u32[]{:S(2)}) copy-start(bf16[384,512]{1,0:T(8,128)(2,1)} %wo.1) | copy-start | bytes 1179652
  19.3 3.7 %copy-start.5 = (bf16[1,256,512]{2,1,0:T(8,128)(2,1)S(1)}, bf16[1,256,512]{2,1,0:T(8,128)(2,1)}, u32[]{:S(2)}) copy-start(bf16[1,256,512]{2,1,0:T(8,128)(2,1)} %param.25) | copy-start | bytes 786436
  28.3 3.7 %collective-permute-start.9 = (bf16[768,1024]{1,0:T(8,128)(2,1)S(1)}, bf16[768,1024]{1,0:T(8,128)(2,1)S(1)}, u32[]{:S(2)}, u32[]{:S(2)}) collective-permute-start(bf16[768,1024]{1,0:T(8,128)(2,1)S(1)} %get-tuple-element.185), channel_id=1, source_target_pairs={{0,1},{1,0},{2,3},{3,2},{4,5},{5,4},{6,7},{7,6},{8,9},{9,8},{10,11... | collective-permute-start | bytes 4718600 | tf_op jit(solution)/shard_map/ppermute | solution.py:640
  32.7 11.8 %collective-permute-start.10 = (bf16[192,1024]{1,0:T(8,128)(2,1)S(1)}, bf16[192,1024]{1,0:T(8,128)(2,1)S(1)}, u32[]{:S(2)}, u32[]{:S(2)}) collective-permute-start(bf16[192,1024]{1,0:T(8,128)(2,1)S(1)} %get-tuple-element.212), channel_id=1, source_target_pairs={{0,2},{1,3},{2,0},{3,1},{4,6},{5,7},{6,4},{7,5},{8,10},{9,11},{10,... | collective-permute-start | bytes 1179656 | tf_op jit(solution)/shard_map/ppermute | solution.py:640
  33.5 11.0 %collective-permute-start.11 = (bf16[192,1024]{1,0:T(8,128)(2,1)S(1)}, bf16[192,1024]{1,0:T(8,128)(2,1)S(1)}, u32[]{:S(2)}, u32[]{:S(2)}) collective-permute-start(bf16[192,1024]{1,0:T(8,128)(2,1)S(1)} %get-tuple-element.214), channel_id=1, source_target_pairs={{0,4},{1,5},{2,6},{3,7},{4,0},{5,1},{6,2},{7,3},{8,12},{9,13},{10,... | collective-permute-start | bytes 1179656 | tf_op jit(solution)/shard_map/ppermute | solution.py:640
  44.5 3.9 %collective-permute-start.12 = (bf16[784,512]{1,0:T(8,128)(2,1)S(1)}, bf16[784,512]{1,0:T(8,128)(2,1)S(1)}, u32[]{:S(2)}, u32[]{:S(2)}) collective-permute-start(bf16[784,512]{1,0:T(8,128)(2,1)S(1)} %get-tuple-element.219), channel_id=1, source_target_pairs={{0,1},{1,0},{2,3},{3,2},{4,5},{5,4},{6,7},{7,6},{8,9},{9,8},{10,11... | collective-permute-start | bytes 2408456 | tf_op jit(solution)/shard_map/ppermute | solution.py:640
  44.6 22.8 %collective-permute-start.19 = (bf16[4,512,256]{2,1,0:T(8,128)(2,1)S(1)}, bf16[4,512,256]{2,1,0:T(8,128)(2,1)S(1)}, u32[]{:S(2)}, u32[]{:S(2)}) collective-permute-start(bf16[4,512,256]{2,1,0:T(8,128)(2,1)S(1)} %get-tuple-element.238), channel_id=1, source_target_pairs={{0,1},{1,0},{2,3},{3,2},{4,5},{5,4},{6,7},{7,6},{8,9},{9,8},{10,11... | collective-permute-start | bytes 3145736 | tf_op jit(solution)/shard_map/ppermute | solution.py:640
  45.8 7.0 %collective-permute-start.13 = (bf16[96,1024]{1,0:T(8,128)(2,1)S(1)}, bf16[96,1024]{1,0:T(8,128)(2,1)S(1)}, u32[]{:S(2)}, u32[]{:S(2)}) collective-permute-start(bf16[96,1024]{1,0:T(8,128)(2,1)S(1)} %get-tuple-element.222), channel_id=1, source_target_pairs={{0,4},{1,5},{2,6},{3,7},{4,0},{5,1},{6,2},{7,3},{8,12},{9,13},{10,... | collective-permute-start | bytes 589832 | tf_op jit(solution)/shard_map/ppermute | solution.py:640
  47.2 6.5 %collective-permute-start.14 = (bf16[96,1024]{1,0:T(8,128)(2,1)S(1)}, bf16[96,1024]{1,0:T(8,128)(2,1)S(1)}, u32[]{:S(2)}, u32[]{:S(2)}) collective-permute-start(bf16[96,1024]{1,0:T(8,128)(2,1)S(1)} %get-tuple-element.223), channel_id=1, source_target_pairs={{0,2},{1,3},{2,0},{3,1},{4,6},{5,7},{6,4},{7,5},{8,10},{9,11},{10,... | collective-permute-start | bytes 589832 | tf_op jit(solution)/shard_map/ppermute | solution.py:640
  54.4 5.7 %collective-permute-start.15 = (bf16[96,1024]{1,0:T(8,128)(2,1)S(1)}, bf16[96,1024]{1,0:T(8,128)(2,1)S(1)}, u32[]{:S(2)}, u32[]{:S(2)}) collective-permute-start(bf16[96,1024]{1,0:T(8,128)(2,1)S(1)} %get-tuple-element.228), channel_id=1, source_target_pairs={{0,8},{8,0},{16,24},{24,16},{1,9},{9,1},{17,25},{25,17},{2,10},{10... | collective-permute-start | bytes 589832 | tf_op jit(solution)/shard_map/ppermute | solution.py:640
  56.0 8.0 %collective-permute-start.16 = (bf16[208,512]{1,0:T(8,128)(2,1)S(1)}, bf16[208,512]{1,0:T(8,128)(2,1)S(1)}, u32[]{:S(2)}, u32[]{:S(2)}) collective-permute-start(bf16[208,512]{1,0:T(8,128)(2,1)S(1)} %get-tuple-element.230), channel_id=1, source_target_pairs={{0,2},{1,3},{2,0},{3,1},{4,6},{5,7},{6,4},{7,5},{8,10},{9,11},{10,... | collective-permute-start | bytes 638984 | tf_op jit(solution)/shard_map/ppermute | solution.py:640
  57.3 10.0 %collective-permute-start.17 = (bf16[208,512]{1,0:T(8,128)(2,1)S(1)}, bf16[208,512]{1,0:T(8,128)(2,1)S(1)}, u32[]{:S(2)}, u32[]{:S(2)}) collective-permute-start(bf16[208,512]{1,0:T(8,128)(2,1)S(1)} %get-tuple-element.231), channel_id=1, source_target_pairs={{0,4},{1,5},{2,6},{3,7},{4,0},{5,1},{6,2},{7,3},{8,12},{9,13},{10,... | collective-permute-start | bytes 638984 | tf_op jit(solution)/shard_map/ppermute | solution.py:640
  57.9 9.3 %collective-permute-start.18 = (bf16[208,512]{1,0:T(8,128)(2,1)S(1)}, bf16[208,512]{1,0:T(8,128)(2,1)S(1)}, u32[]{:S(2)}, u32[]{:S(2)}) collective-permute-start(bf16[208,512]{1,0:T(8,128)(2,1)S(1)} %get-tuple-element.232), channel_id=1, source_target_pairs={{0,6},{1,7},{2,4},{3,5},{4,2},{5,3},{6,0},{7,1},{8,14},{9,15},{10,... | collective-permute-start | bytes 638984 | tf_op jit(solution)/shard_map/ppermute | solution.py:640
  60.7 9.7 %collective-permute-start.22 = (bf16[96,1024]{1,0:T(8,128)(2,1)S(1)}, bf16[96,1024]{1,0:T(8,128)(2,1)S(1)}, u32[]{:S(2)}, u32[]{:S(2)}) collective-permute-start(bf16[96,1024]{1,0:T(8,128)(2,1)S(1)} %add_parts.13.refs_0_), channel_id=1, source_target_pairs={{0,16},{8,24},{16,0},{24,8},{1,17},{9,25},{17,1},{25,9},{2,18},{10... | collective-permute-start | bytes 589832 | tf_op jit(solution)/shard_map/ppermute | solution.py:640
  68.2 15.1 %collective-permute-start.25 = (bf16[512,256]{1,0:T(8,128)(2,1)S(1)}, bf16[512,256]{1,0:T(8,128)(2,1)S(1)}, u32[]{:S(2)}, u32[]{:S(2)}) collective-permute-start(bf16[512,256]{1,0:T(8,128)(2,1)S(1)} %get-tuple-element.248), channel_id=1, source_target_pairs={{0,6},{1,7},{2,4},{3,5},{4,2},{5,3},{6,0},{7,1},{8,14},{9,15},{10,... | collective-permute-start | bytes 786440 | tf_op jit(solution)/shard_map/ppermute | solution.py:640
  70.9 7.0 %collective-permute-start.23 = (bf16[96,1024]{1,0:T(8,128)(2,1)S(1)}, bf16[96,1024]{1,0:T(8,128)(2,1)S(1)}, u32[]{:S(2)}, u32[]{:S(2)}) collective-permute-start(bf16[96,1024]{1,0:T(8,128)(2,1)S(1)} %add_parts.15.mine), channel_id=1, source_target_pairs={{0,8},{8,0},{16,24},{24,16},{1,9},{9,1},{17,25},{25,17},{2,10},{10... | collective-permute-start | bytes 589832 | tf_op jit(solution)/shard_map/ppermute | solution.py:640
  71.7 12.9 %collective-permute-start.20 = (bf16[512,256]{1,0:T(8,128)(2,1)S(1)}, bf16[512,256]{1,0:T(8,128)(2,1)S(1)}, u32[]{:S(2)}, u32[]{:S(2)}) collective-permute-start(bf16[512,256]{1,0:T(8,128)(2,1)S(1)} %get-tuple-element.241), channel_id=1, source_target_pairs={{0,2},{1,3},{2,0},{3,1},{4,6},{5,7},{6,4},{7,5},{8,10},{9,11},{10,... | collective-permute-start | bytes 786440 | tf_op jit(solution)/shard_map/ppermute | solution.py:640
  72.9 11.6 %collective-permute-start.21 = (bf16[512,256]{1,0:T(8,128)(2,1)S(1)}, bf16[512,256]{1,0:T(8,128)(2,1)S(1)}, u32[]{:S(2)}, u32[]{:S(2)}) collective-permute-start(bf16[512,256]{1,0:T(8,128)(2,1)S(1)} %get-tuple-element.242), channel_id=1, source_target_pairs={{0,4},{1,5},{2,6},{3,7},{4,0},{5,1},{6,2},{7,3},{8,12},{9,13},{10,... | collective-permute-start | bytes 786440 | tf_op jit(solution)/shard_map/ppermute | solution.py:640
  73.7 5.4 %collective-permute-start.24 = (bf16[112,512]{1,0:T(8,128)(2,1)S(1)}, bf16[112,512]{1,0:T(8,128)(2,1)S(1)}, u32[]{:S(2)}, u32[]{:S(2)}) collective-permute-start(bf16[112,512]{1,0:T(8,128)(2,1)S(1)} %get-tuple-element.246), channel_id=1, source_target_pairs={{0,8},{8,0},{16,24},{24,16},{1,9},{9,1},{17,25},{25,17},{2,10},{10... | collective-permute-start | bytes 344072 | tf_op jit(solution)/shard_map/ppermute | solution.py:640
  79.7 7.0 %collective-permute-start.26 = (bf16[112,512]{1,0:T(8,128)(2,1)S(1)}, bf16[112,512]{1,0:T(8,128)(2,1)S(1)}, u32[]{:S(2)}, u32[]{:S(2)}) collective-permute-start(bf16[112,512]{1,0:T(8,128)(2,1)S(1)} %add_parts.16.refs_0_), channel_id=1, source_target_pairs={{0,16},{8,24},{16,0},{24,8},{1,17},{9,25},{17,1},{25,9},{2,18},{10... | collective-permute-start | bytes 344072 | tf_op jit(solution)/shard_map/ppermute | solution.py:640
  82.5 8.3 %collective-permute-start.28 = (bf16[96,1024]{1,0:T(8,128)(2,1)S(1)}, bf16[96,1024]{1,0:T(8,128)(2,1)S(1)}, u32[]{:S(2)}, u32[]{:S(2)}) collective-permute-start(bf16[96,1024]{1,0:T(8,128)(2,1)S(1)} %get-tuple-element.257.c), channel_id=1, source_target_pairs={{0,2},{1,3},{2,0},{3,1},{4,6},{5,7},{6,4},{7,5},{8,10},{9,11},{10,... | collective-permute-start | bytes 589832 | tf_op jit(solution)/shard_map/ppermute | solution.py:640
  83.3 7.5 %collective-permute-start.27 = (bf16[96,1024]{1,0:T(8,128)(2,1)S(1)}, bf16[96,1024]{1,0:T(8,128)(2,1)S(1)}, u32[]{:S(2)}, u32[]{:S(2)}) collective-permute-start(bf16[96,1024]{1,0:T(8,128)(2,1)S(1)} %get-tuple-element.245.a), channel_id=1, source_target_pairs={{0,4},{1,5},{2,6},{3,7},{4,0},{5,1},{6,2},{7,3},{8,12},{9,13},{10,... | collective-permute-start | bytes 589832 | tf_op jit(solution)/shard_map/ppermute | solution.py:640
  87.2 5.6 %collective-permute-start.31 = (bf16[96,512]{1,0:T(8,128)(2,1)S(1)}, bf16[96,512]{1,0:T(8,128)(2,1)S(1)}, u32[]{:S(2)}, u32[]{:S(2)}) collective-permute-start(bf16[96,512]{1,0:T(8,128)(2,1)S(1)} %slice.16.refs_0_), channel_id=1, source_target_pairs={{0,6},{1,7},{2,4},{3,5},{4,2},{5,3},{6,0},{7,1},{8,14},{9,15},{10,... | collective-permute-start | bytes 294920 | tf_op jit(solution)/shard_map/ppermute | solution.py:640
  88.8 5.1 %collective-permute-start.30 = (bf16[96,512]{1,0:T(8,128)(2,1)S(1)}, bf16[96,512]{1,0:T(8,128)(2,1)S(1)}, u32[]{:S(2)}, u32[]{:S(2)}) collective-permute-start(bf16[96,512]{1,0:T(8,128)(2,1)S(1)} %slice.16.refs_0_), channel_id=1, source_target_pairs={{0,4},{1,5},{2,6},{3,7},{4,0},{5,1},{6,2},{7,3},{8,12},{9,13},{10,... | collective-permute-start | bytes 294920 | tf_op jit(solution)/shard_map/ppermute | solution.py:640
  90.0 5.1 %collective-permute-start.29 = (bf16[96,512]{1,0:T(8,128)(2,1)S(1)}, bf16[96,512]{1,0:T(8,128)(2,1)S(1)}, u32[]{:S(2)}, u32[]{:S(2)}) collective-permute-start(bf16[96,512]{1,0:T(8,128)(2,1)S(1)} %slice.16.refs_0_), channel_id=1, source_target_pairs={{0,2},{1,3},{2,0},{3,1},{4,6},{5,7},{6,4},{7,5},{8,10},{9,11},{10,... | collective-permute-start | bytes 294920 | tf_op jit(solution)/shard_map/ppermute | solution.py:640
  91.4 6.2 %collective-permute-start.33 = (bf16[192,1024]{1,0:T(8,128)(2,1)S(1)}, bf16[192,1024]{1,0:T(8,128)(2,1)S(1)}, u32[]{:S(2)}, u32[]{:S(2)}) collective-permute-start(bf16[192,1024]{1,0:T(8,128)(2,1)S(1)} %get-tuple-element.267.refs_1_), channel_id=1, source_target_pairs={{0,1},{1,0},{2,3},{3,2},{4,5},{5,4},{6,7},{7,6},{8,9},{9,8},{10,11... | collective-permute-start | bytes 1179656 | tf_op jit(solution)/shard_map/ppermute | solution.py:640
  91.5 6.1 %collective-permute-start.32 = (bf16[192,1024]{1,0:T(8,128)(2,1)S(1)}, bf16[192,1024]{1,0:T(8,128)(2,1)S(1)}, u32[]{:S(2)}, u32[]{:S(2)}) collective-permute-start(bf16[192,1024]{1,0:T(8,128)(2,1)S(1)} %get-tuple-element.260.refs_0_), channel_id=1, source_target_pairs={{0,1},{1,0},{2,3},{3,2},{4,5},{5,4},{6,7},{7,6},{8,9},{9,8},{10,11... | collective-permute-start | bytes 1179656 | tf_op jit(solution)/shard_map/ppermute | solution.py:640
  92.9 10.2 %collective-permute-start.35 = (bf16[192,1024]{1,0:T(8,128)(2,1)S(1)}, bf16[192,1024]{1,0:T(8,128)(2,1)S(1)}, u32[]{:S(2)}, u32[]{:S(2)}) collective-permute-start(bf16[192,1024]{1,0:T(8,128)(2,1)S(1)} %get-tuple-element.267.refs_1_), channel_id=1, source_target_pairs={{0,4},{1,5},{2,6},{3,7},{4,0},{5,1},{6,2},{7,3},{8,12},{9,13},{10,... | collective-permute-start | bytes 1179656 | tf_op jit(solution)/shard_map/ppermute | solution.py:640
  93.9 10.4 %collective-permute-start.34 = (bf16[192,1024]{1,0:T(8,128)(2,1)S(1)}, bf16[192,1024]{1,0:T(8,128)(2,1)S(1)}, u32[]{:S(2)}, u32[]{:S(2)}) collective-permute-start(bf16[192,1024]{1,0:T(8,128)(2,1)S(1)} %get-tuple-element.260.refs_0_), channel_id=1, source_target_pairs={{0,2},{1,3},{2,0},{3,1},{4,6},{5,7},{6,4},{7,5},{8,10},{9,11},{10,... | collective-permute-start | bytes 1179656 | tf_op jit(solution)/shard_map/ppermute | solution.py:640
  95.7 10.2 %collective-permute-start.36 = (bf16[384,512]{1,0:T(8,128)(2,1)S(1)}, bf16[384,512]{1,0:T(8,128)(2,1)S(1)}, u32[]{:S(2)}, u32[]{:S(2)}) collective-permute-start(bf16[384,512]{1,0:T(8,128)(2,1)S(1)} %stack.21.refs_2_), channel_id=1, source_target_pairs={{0,8},{8,0},{16,24},{24,16},{1,9},{9,1},{17,25},{25,17},{2,10},{10... | collective-permute-start | bytes 1179656 | tf_op jit(solution)/shard_map/ppermute | solution.py:640
  97.6 10.9 %collective-permute-start.39 = (bf16[384,512]{1,0:T(8,128)(2,1)S(1)}, bf16[384,512]{1,0:T(8,128)(2,1)S(1)}, u32[]{:S(2)}, u32[]{:S(2)}) collective-permute-start(bf16[384,512]{1,0:T(8,128)(2,1)S(1)} %stack.21.refs_2_), channel_id=1, source_target_pairs={{0,1},{1,0},{2,3},{3,2},{4,5},{5,4},{6,7},{7,6},{8,9},{9,8},{10,11... | collective-permute-start | bytes 1179656 | tf_op jit(solution)/shard_map/ppermute | solution.py:640
  104.3 4.2 %collective-permute-start.37 = (bf16[192,1024]{1,0:T(8,128)(2,1)S(1)}, bf16[192,1024]{1,0:T(8,128)(2,1)S(1)}, u32[]{:S(2)}, u32[]{:S(2)}) collective-permute-start(bf16[192,1024]{1,0:T(8,128)(2,1)S(1)} %collective-permute-done.34.refs_0_), channel_id=1, source_target_pairs={{0,1},{1,0},{2,3},{3,2},{4,5},{5,4},{6,7},{7,6},{8,9},{9,8},{10,11... | collective-permute-start | bytes 1179656 | tf_op jit(solution)/shard_map/ppermute | solution.py:640
  104.3 4.2 %collective-permute-start.38 = (bf16[192,1024]{1,0:T(8,128)(2,1)S(1)}, bf16[192,1024]{1,0:T(8,128)(2,1)S(1)}, u32[]{:S(2)}, u32[]{:S(2)}) collective-permute-start(bf16[192,1024]{1,0:T(8,128)(2,1)S(1)} %collective-permute-done.35.refs_1_), channel_id=1, source_target_pairs={{0,1},{1,0},{2,3},{3,2},{4,5},{5,4},{6,7},{7,6},{8,9},{9,8},{10,11... | collective-permute-start | bytes 1179656 | tf_op jit(solution)/shard_map/ppermute | solution.py:640
  105.9 2.6 %collective-permute-start.40 = (bf16[384,512]{1,0:T(8,128)(2,1)S(1)}, bf16[384,512]{1,0:T(8,128)(2,1)S(1)}, u32[]{:S(2)}, u32[]{:S(2)}) collective-permute-start(bf16[384,512]{1,0:T(8,128)(2,1)S(1)} %collective-permute-done.36.refs_3_), channel_id=1, source_target_pairs={{0,1},{1,0},{2,3},{3,2},{4,5},{5,4},{6,7},{7,6},{8,9},{9,8},{10,11... | collective-permute-start | bytes 1179656 | tf_op jit(solution)/shard_map/ppermute | solution.py:640
